TPU v7x, 32 devices: a whole 2x2x4 slice. The times are simulated.
32 devices in a mesh: wide: 8 (over z, core), narrow: 4 (over y, x).
Axes of the slice: x: 2, y: 2, z: 4, core: 2. Of those that a mesh axis runs over, the one named last changes fastest.
Arguments:
- tokens: bfloat16 [8, 1024, 2048], P('narrow', 'wide'), may hold values from -6 to 6
- lengths: int32 [8], P('narrow'), may hold values from 128 to 1024, as said below
- cotangent: bfloat16 [8, 1024, 2048], P('narrow', 'wide'), may hold values from -6 to 6
- first_gain: float32 [2048], replicated, may hold values from 0.5 to 1.5
- proj_in: bfloat16 [2, 2048, 2560], P(None, 'narrow', 'wide'), may hold values from -0.125 to 0.125
- conv_weight: float32 [4, 2560], P(None, 'wide'), may hold values from -3 to 3
- conv_bias: float32 [2560], P('wide'), may hold values from -3 to 3
- rate_weight: bfloat16 [16, 160, 160], P('wide'), may hold values from -0.5 to 0.5
- rate_bias: float32 [2560], P('wide'), may hold values from -4 to 4
- input_weight: bfloat16 [16, 160, 160], P('wide'), may hold values from -0.5 to 0.5
- input_bias: float32 [2560], P('wide'), may hold values from -4 to 4
- decay_param: float32 [2560], P('wide'), may hold values from 4.3 to 9
- proj_out: bfloat16 [2560, 2048], P('wide', 'narrow'), may hold values from -0.3125 to 0.3125
- second_gain: float32 [2048], replicated, may hold values from 0.5 to 1.5
- mlp_in: bfloat16 [2, 2048, 6144], P(None, 'narrow', 'wide'), may hold values from -0.125 to 0.125
- mlp_down: bfloat16 [6144, 2048], P('wide', 'narrow'), may hold values from -0.109375 to 0.109375
Outputs:
- output: bfloat16 [8, 1024, 2048], P('narrow', 'wide')
- grad_tokens: bfloat16 [8, 1024, 2048], P('narrow', 'wide')
- final_state: float32 [8, 2560], P('narrow', 'wide')
- conv_state: float32 [8, 3, 2560], P('narrow', None, 'wide')
- grad_first_gain: float32 [2048], replicated
- grad_proj_in: float32 [2, 2048, 2560], P(None, 'narrow', 'wide')
- grad_conv_weight: float32 [4, 2560], P(None, 'wide')
- grad_conv_bias: float32 [2560], P('wide')
- grad_rate_weight: float32 [16, 160, 160], P('wide')
- grad_rate_bias: float32 [2560], P('wide')
- grad_input_weight: float32 [16, 160, 160], P('wide')
- grad_input_bias: float32 [2560], P('wide')
- grad_decay_param: float32 [2560], P('wide')
- grad_proj_out: float32 [2560, 2048], P('wide', 'narrow')
- grad_second_gain: float32 [2048], replicated
- grad_mlp_in: float32 [2, 2048, 6144], P(None, 'narrow', 'wide')
- grad_mlp_down: float32 [6144, 2048], P('wide', 'narrow')
Inputs may be any that keep to these rules, and one draw needn't show every extreme that they name: `lengths`: in every aligned group of 2 consecutive sequences at least one has length 1024.
All inputs are finite; a program needn't handle non-finite values.
Results may differ from a plain program's by a relative error of at most 0.0086.
Values may be sent and summed in bfloat16 or wider, within the bound.
No kernel may reach another device: no remote copies, remote signals or barrier semaphores. Data moves between devices by JAX's collectives and lax.ppermute only.
A program may use at most 320 MiB of HBM per device.

v0:
```python
from functools import partial

import jax
import jax.numpy as jnp
from jax import lax
from jax.sharding import PartitionSpec as P

decay_scale = 8.0
norm_eps = 1e-06
span_block = 16


def rms_scale(values, norm_gain):
    return (
        values * lax.rsqrt(jnp.mean(values * values, axis=-1, keepdims=True) + norm_eps) * norm_gain
    )


def lagged(values, offset):
    return jnp.pad(values, ((0, 0), (offset, 0), (0, 0)))[:, : values.shape[1]]


def linear_combine(earlier, latter):
    return (earlier[0] * latter[0], latter[0] * earlier[1] + latter[1])


def blocked_scan(log_steps, drives):
    seq_count, seq_len, channels = drives.shape
    block_total = seq_len // span_block
    logs_shaped = log_steps.reshape(seq_count, block_total, span_block, channels)
    drive_shaped = drives.reshape(seq_count, block_total, span_block, channels)
    running = jnp.cumsum(logs_shaped, axis=2)
    lower = (jnp.arange(span_block)[:, None] >= jnp.arange(span_block)[None, :]).astype(
        jnp.float32
    )[:, :, None]
    spread = (running[:, :, :, None, :] - running[:, :, None, :, :]) * lower
    factors = jnp.exp(spread) * lower
    within = jnp.sum(factors * drive_shaped[:, :, None, :, :], axis=3)
    block_decay = jnp.exp(running[:, :, -1])
    block_end = within[:, :, -1]
    carried, ends = lax.associative_scan(linear_combine, (block_decay, block_end), axis=1)
    incoming = jnp.concatenate((jnp.zeros_like(ends[:, :1]), ends[:, :-1]), axis=1)
    states = within + jnp.exp(running) * incoming[:, :, None, :]
    return states.reshape(seq_count, seq_len, channels)


def mixer_core(
    y_branch,
    x_branch,
    conv_weight,
    conv_bias,
    rate_weight,
    rate_bias,
    input_weight,
    input_bias,
    decay_param,
    mask_f,
    lengths,
):
    convolved = conv_bias + conv_weight[0] * x_branch
    for offset in range(1, 4):
        convolved = convolved + conv_weight[offset] * lagged(x_branch, offset)
    seq_count, seq_len, channels = convolved.shape
    block_count = rate_weight.shape[0]
    block_width = rate_weight.shape[1]
    blocked = convolved.reshape(seq_count, seq_len, block_count, block_width)
    rate_pre = jnp.einsum("stnc,ncd->stnd", blocked, rate_weight, precision=lax.Precision.HIGHEST)
    in_pre = jnp.einsum("stnc,ncd->stnd", blocked, input_weight, precision=lax.Precision.HIGHEST)
    rate_gate = jax.nn.sigmoid(rate_pre.reshape(seq_count, seq_len, channels) + rate_bias)
    in_gate = jax.nn.sigmoid(in_pre.reshape(seq_count, seq_len, channels) + input_bias)
    log_decay = -decay_scale * jax.nn.softplus(-decay_param) * rate_gate
    drive_term = jnp.sqrt(-jnp.expm1(2.0 * log_decay)) * in_gate * convolved * mask_f
    states = blocked_scan(log_decay * mask_f, drive_term)
    mixer_out = jax.nn.gelu(y_branch) * states
    positions = lengths[:, None] - 3 + jnp.arange(3, dtype=jnp.int32)[None, :]
    conv_state = jnp.take_along_axis(x_branch, positions[:, :, None], axis=1)
    return (mixer_out, states[:, -1], conv_state)


def gated_unit(gate_pre, up_pre):
    return jax.nn.gelu(gate_pre) * up_pre


def gather_rows(values):
    whole = lax.all_gather(values, "wide", axis=1, tiled=True)
    return whole.reshape(-1, whole.shape[-1])


def whole_weight(weight):
    return lax.all_gather(weight, "narrow", axis=1, tiled=True)


def forward_in(rows_b, weight):
    return (
        jnp.einsum(
            "gd,kdc->kgc",
            rows_b,
            lax.all_gather(weight, "narrow", axis=1, tiled=True),
            preferred_element_type=jnp.float32,
        ),
        weight,
    )


def forward_out(hidden_b, weight, seq_count, full_len):
    whole = whole_weight(weight)
    shaped = hidden_b.reshape(seq_count, full_len, hidden_b.shape[-1])
    summed = lax.psum_scatter(
        jnp.einsum("stc,cd->tsd", shaped, whole, preferred_element_type=jnp.float32),
        "wide",
        scatter_dimension=0,
        tiled=True,
    )
    return (jnp.transpose(summed, (1, 0, 2)), weight)


def backward_in(grads_b, held, seq_count, full_len):
    whole = whole_weight(held)
    shaped = grads_b.reshape(grads_b.shape[0], seq_count, full_len, grads_b.shape[-1])
    summed = lax.psum_scatter(
        jnp.einsum("kstc,kdc->tsd", shaped, whole, preferred_element_type=jnp.float32),
        "wide",
        scatter_dimension=0,
        tiled=True,
    )
    return jnp.transpose(summed, (1, 0, 2))


def backward_out(grads_b, held):
    contract = (((1,), (1,)), ((), ()))
    return lax.dot_general(
        grads_b,
        lax.all_gather(held, "narrow", axis=1, tiled=True),
        contract,
        preferred_element_type=jnp.float32,
    )


def weight_grads(rows_b, grads_b, hidden_b, back_rows):
    grad_in = jnp.einsum("gd,kgc->kdc", rows_b, grads_b, preferred_element_type=jnp.float32)
    grad_out = lax.dot_general(
        hidden_b, back_rows, (((0,), (0,)), ((), ())), preferred_element_type=jnp.float32
    )
    return (
        lax.psum_scatter(grad_in, "narrow", scatter_dimension=1, tiled=True),
        lax.psum_scatter(grad_out, "narrow", scatter_dimension=1, tiled=True),
    )


def body(
    tokens,
    lengths,
    cotangent,
    first_gain,
    proj_in,
    conv_weight,
    conv_bias,
    rate_weight,
    rate_bias,
    input_weight,
    input_bias,
    decay_param,
    proj_out,
    second_gain,
    mlp_in,
    mlp_down,
):
    seq_count, local_len, model_width = tokens.shape
    full_len = local_len * lax.axis_size("wide")
    row_count = seq_count * full_len
    positions = lax.axis_index("wide") * local_len + jnp.arange(local_len, dtype=jnp.int32)
    local_mask = (positions[None, :] < lengths[:, None]).astype(jnp.float32)[:, :, None]
    whole_mask = (jnp.arange(full_len, dtype=jnp.int32)[None, :] < lengths[:, None]).astype(
        jnp.float32
    )[:, :, None]
    tokens_f = tokens.astype(jnp.float32)
    norm_in, norm_in_back = jax.vjp(rms_scale, tokens_f, first_gain)
    rows_first = gather_rows(norm_in.astype(jnp.bfloat16))
    pre_mix, held_mix_in = forward_in(rows_first, proj_in)
    channels = pre_mix.shape[2]
    branch_y = pre_mix[0].reshape(seq_count, full_len, channels)
    branch_x = pre_mix[1].reshape(seq_count, full_len, channels)
    core = partial(mixer_core, mask_f=whole_mask, lengths=lengths)
    (mixer_out, final_state, conv_state), core_back = jax.vjp(
        core,
        branch_y,
        branch_x,
        conv_weight,
        conv_bias,
        rate_weight.astype(jnp.float32),
        rate_bias,
        input_weight.astype(jnp.float32),
        input_bias,
        decay_param,
    )
    mixer_b = mixer_out.reshape(row_count, channels).astype(jnp.bfloat16)
    mix_sum, held_mix_out = forward_out(mixer_b, proj_out, seq_count, full_len)
    resid = tokens_f + mix_sum
    norm_mid, norm_mid_back = jax.vjp(rms_scale, resid, second_gain)
    rows_second = gather_rows(norm_mid.astype(jnp.bfloat16))
    pre_mlp, held_mlp_in = forward_in(rows_second, mlp_in)
    hidden, gated_back = jax.vjp(gated_unit, pre_mlp[0], pre_mlp[1])
    hidden_b = hidden.astype(jnp.bfloat16)
    mlp_sum, held_mlp_out = forward_out(hidden_b, mlp_down, seq_count, full_len)
    output = (resid + mlp_sum).astype(jnp.bfloat16)
    out_grad = cotangent.astype(jnp.float32) * local_mask
    back_second = gather_rows(out_grad.astype(jnp.bfloat16))
    hidden_grad = backward_out(back_second, held_mlp_out)
    gate_grad, up_grad = gated_back(hidden_grad)
    mlp_grads_b = jnp.stack((gate_grad, up_grad)).astype(jnp.bfloat16)
    mid_sum = backward_in(mlp_grads_b, held_mlp_in, seq_count, full_len)
    grad_mlp_in, grad_mlp_down = weight_grads(rows_second, mlp_grads_b, hidden_b, back_second)
    resid_from_norm, gain_two_part = norm_mid_back(mid_sum)
    resid_grad = out_grad + resid_from_norm
    back_first = gather_rows(resid_grad.astype(jnp.bfloat16))
    mixer_grad = backward_out(back_first, held_mix_out)
    core_grads = core_back(
        (
            mixer_grad.reshape(seq_count, full_len, channels),
            jnp.zeros_like(final_state),
            jnp.zeros_like(conv_state),
        )
    )
    mix_grads_b = jnp.stack(
        (core_grads[0].reshape(row_count, channels), core_grads[1].reshape(row_count, channels))
    ).astype(jnp.bfloat16)
    in_sum = backward_in(mix_grads_b, held_mix_in, seq_count, full_len)
    grad_proj_in, grad_proj_out = weight_grads(rows_first, mix_grads_b, mixer_b, back_first)
    tokens_from_norm, gain_one_part = norm_in_back(in_sum)
    grad_tokens = (resid_grad + tokens_from_norm).astype(jnp.bfloat16)
    channel_grads = lax.psum(
        (
            core_grads[2],
            core_grads[3],
            core_grads[4],
            core_grads[5],
            core_grads[6],
            core_grads[7],
            core_grads[8],
        ),
        "narrow",
    )
    gain_grads = lax.psum((gain_one_part, gain_two_part), ("wide", "narrow"))
    return (
        output,
        grad_tokens,
        final_state,
        conv_state,
        gain_grads[0],
        grad_proj_in,
        channel_grads[0],
        channel_grads[1],
        channel_grads[2],
        channel_grads[3],
        channel_grads[4],
        channel_grads[5],
        channel_grads[6],
        grad_proj_out,
        gain_grads[1],
        grad_mlp_in,
        grad_mlp_down,
    )


def solution(mesh):
    return jax.shard_map(
        body,
        mesh=mesh,
        in_specs=(
            P("narrow", "wide", None),
            P("narrow"),
            P("narrow", "wide", None),
            P(),
            P(None, "narrow", "wide"),
            P(None, "wide"),
            P("wide"),
            P("wide", None, None),
            P("wide"),
            P("wide", None, None),
            P("wide"),
            P("wide"),
            P("wide", "narrow"),
            P(),
            P(None, "narrow", "wide"),
            P("wide", "narrow"),
        ),
        out_specs=(
            P("narrow", "wide", None),
            P("narrow", "wide", None),
            P("narrow", "wide"),
            P("narrow", None, "wide"),
            P(),
            P(None, "narrow", "wide"),
            P(None, "wide"),
            P("wide"),
            P("wide", None, None),
            P("wide"),
            P("wide", None, None),
            P("wide"),
            P("wide"),
            P("wide", "narrow"),
            P(),
            P(None, "narrow", "wide"),
            P("wide", "narrow"),
        ),
        check_vma=False,
    )
```

profile of v0, /device:TPU:0, one launch (start us, length us, event | category | flops | bytes accessed | tf_op | source)
XLA Modules:
  0.0 1902.6 jit_solution(10188909834763674770)
XLA Ops:
  14.9 37.2 %all-gather.11.cloned.1.call-done = bf16[2,2048,320]{1,2,0:T(8,128)(2,1)} async-done(((bf16[2,512,320]{1,2,0:T(8,128)(2,1)}), bf16[2,2048,320]{1,2,0:T(8,128)(2,1)}) %all-gather.11.cloned.1.call-update) | async-done | bytes 2621456 | tf_op jit(solution)/shard_map/all_gather | solution.py:98
  52.1 84.3 %all-gather.9.cloned.1.call-done = bf16[2,1024,2048]{2,1,0:T(8,128)(2,1)} async-done(((bf16[2,128,2048]{2,1,0:T(8,128)(2,1)}), bf16[2,1024,2048]{2,1,0:T(8,128)(2,1)}) %all-gather.9.cloned.1.call-update) | async-done | bytes 8388624 | tf_op jit(solution)/shard_map/all_gather | solution.py:85
  136.4 8.8 convolution_bitcast_fusion.6
  145.3 3.5 fusion.194
  149.7 3.7 reshape_squeeze.7
  162.0 6.8 copy.142
  174.8 5.1 multiply_multiply_fusion.9
  182.5 5.1 reshape.547
  191.5 22.5 %multiply_reduce_fusion.1 = f32[2,64,16,320]{3,2,1,0:T(8,128)S(1)} fusion(f32[2,64,16,320]{3,2,1,0:T(8,128)S(1)} %bitcast.270, f32[16,16]{1,0:T(8,128)S(1)} %fusion.145, f32[2,64,16,320]{3,2,1,0:T(8,128)S(1)} %copy.144), kind=kLoop, calls=%fused_computation.4 | loop fusion | flops 51773440 | bytes 7865344 | tf_op jit(solution)/shard_map/jvp()/reduce_sum | solution.py:38
  308.0 3.5 copy.154
  311.5 3.4 copy.155
  314.9 4.8 reshape_squeeze.6
  319.7 14.2 convolution_bitcast_fusion.3
  334.5 166.3 %reduce-scatter.9.cloned.1.call-done = f32[128,2,2048]{2,0,1:T(8,128)} async-done(((f32[1024,2,2048]{2,0,1:T(8,128)}), f32[128,2,2048]{2,0,1:T(8,128)}) %reduce-scatter.9.cloned.1.call-update) | async-done | bytes 2097168 | tf_op jit(solution)/shard_map/reduce_scatter | solution.py:108
  510.5 60.6 %all-gather.17.cloned.1.call-done = bf16[2,2048,768]{2,1,0:T(8,128)(2,1)} async-done(((bf16[2,512,768]{2,1,0:T(8,128)(2,1)}), bf16[2,2048,768]{2,1,0:T(8,128)(2,1)}) %all-gather.17.cloned.1.call-update) | async-done | bytes 6291472 | tf_op jit(solution)/shard_map/all_gather | solution.py:98
  571.1 84.1 %all-gather.15.cloned.1.call-done = bf16[2,1024,2048]{2,1,0:T(8,128)(2,1)} async-done(((bf16[2,128,2048]{2,1,0:T(8,128)(2,1)}), bf16[2,1024,2048]{2,1,0:T(8,128)(2,1)}) %all-gather.15.cloned.1.call-update) | async-done | bytes 8388624 | tf_op jit(solution)/shard_map/all_gather | solution.py:85
  655.2 19.4 %convolution_bitcast_fusion.4 = f32[2,2048,768]{2,1,0:T(8,128)} fusion(bf16[2048,2048,1]{1,0,2:T(8,128)(2,1)} %bitcast.294, bf16[2,2048,768]{2,1,0:T(8,128)(2,1)} %all-gather.17.cloned.1.call-done), kind=kOutput, calls=%fused_computation.58 | convolution fusion | flops 12884901888 | bytes 27262976 | tf_op jit(solution)/shard_map/gd,kdc->kgc/dot_general | solution.py:95
  674.7 24.8 %all-gather.19.cloned.1.call-done = bf16[768,2048]{1,0:T(8,128)(2,1)} async-done(((bf16[768,512]{1,0:T(8,128)(2,1)}), bf16[768,2048]{1,0:T(8,128)(2,1)}) %all-gather.19.cloned.1.call-update) | async-done | bytes 3145744 | tf_op jit(solution)/shard_map/all_gather | solution.py:90
  699.4 84.3 %all-gather.21.cloned.1.call-done = bf16[2,1024,2048]{2,1,0:T(8,128)(2,1)} async-done(((bf16[2,128,2048]{2,1,0:T(8,128)(2,1)}), bf16[2,1024,2048]{2,1,0:T(8,128)(2,1)}) %all-gather.21.cloned.1.call-update) | async-done | bytes 8388624 | tf_op jit(solution)/shard_map/all_gather | solution.py:85
  783.7 16.6 fusion.9
  803.1 16.2 convolution_bitcast_fusion.2
  819.3 166.9 %reduce-scatter.13.cloned.1.call-done = f32[128,2,2048]{2,0,1:T(8,128)} async-done(((f32[1024,2,2048]{2,0,1:T(8,128)}), f32[128,2,2048]{2,0,1:T(8,128)}) %reduce-scatter.13.cloned.1.call-update) | async-done | bytes 2097168 | tf_op jit(solution)/shard_map/reduce_scatter | solution.py:120
  986.2 3.5 fusion.114
  993.3 19.3 %fusion.40 = f32[2,2048,768]{1,2,0:T(8,128)} fusion(bf16[2048,2048,1]{1,0,2:T(8,128)(2,1)} %bitcast.295, bf16[1,2048,768]{2,1,0:T(8,128)(2,1)} %bitcast.299, bf16[1,2048,768]{2,1,0:T(8,128)(2,1)} %bitcast.297), kind=kOutput, calls=%fused_computation.57 | convolution fusion | flops 12888047616 | bytes 27262976 | tf_op jit(solution)/shard_map/gd,kgc->kdc/dot_general | solution.py:140
  1019.9 53.9 %all-gather.23.cloned.1.call-done = bf16[2,1024,2048]{2,1,0:T(8,128)(2,1)} async-done(((bf16[2,128,2048]{2,1,0:T(8,128)(2,1)}), bf16[2,1024,2048]{2,1,0:T(8,128)(2,1)}) %all-gather.23.cloned.1.call-update) | async-done | bytes 8388624 | tf_op jit(solution)/shard_map/all_gather | solution.py:85
  1073.8 12.0 fusion.69
  1085.9 4.0 copy.160
  1202.9 3.5 copy.163
  1206.5 42.0 %fusion.2 = (f32[2,64,16,320]{3,2,1,0:T(8,128)}, f32[2,64,16,320]{3,2,1,0:T(8,128)}, f32[2,64,16,320]{3,2,1,0:T(8,128)}) fusion(f32[2,64,16,320]{3,2,1,0:T(8,128)} %copy.163, f32[2,64,16,320]{3,2,1,0:T(8,128)} %bitcast.269, f32[16,16]{1,0:T(8,128)S(1)} %copy-done.75, f32[2,64,16,320]{3,2,1,0:T(8,128)} %copy-done.18), kind=kLoop, calls=%fused_computation.8 | loop fusion | flops 113377280 | bytes 15729664 | tf_op jit(solution)/shard_map/transpose(jvp())/reduce_sum | solution.py:36
  1248.6 6.0 fusion.47
  1254.5 3.5 copy.170
  1258.0 3.7 copy.171
  1261.7 5.0 reshape.562
  1268.9 6.9 copy.183
  1275.9 7.5 fusion.70
  1288.8 4.7 add_reduce_fusion
  1300.6 6.7 multiply_reduce_fusion.7
  1312.1 12.3 convolution_bitcast_fusion.1
  1324.5 8.1 fusion.193
  1332.6 13.7 convolution_bitcast_fusion
  1346.4 14.8 fusion.44
  1361.2 3.6 copy.185
  1364.8 5.2 convolution_bitcast_fusion.8
  1370.0 3.3 convolution_bitcast_fusion.7
  1373.4 9.8 fusion.125
  1391.4 9.9 convolution_bitcast_fusion.5
  1403.0 3.5 copy.179
  1406.5 3.5 copy.180
  1410.8 3.4 copy.176
  1414.2 5.0 reshape.558
  1419.2 3.4 reshape.559
  1425.2 3.8 copy.188
  1429.0 5.5 copy.182
  1434.7 5.1 reshape.561
  1442.1 7.0 multiply_reduce_fusion.4
  1449.3 16.1 all-reduce.70
  1465.5 26.3 %reduce-scatter.15.cloned.1.call-done = f32[128,2,2048]{2,0,1:T(8,128)} async-done(((f32[1024,2,2048]{2,0,1:T(8,128)}), f32[128,2,2048]{2,0,1:T(8,128)}) %reduce-scatter.15.cloned.1.call-update) | async-done | bytes 2097168 | tf_op jit(solution)/shard_map/reduce_scatter | solution.py:120
  1494.1 39.6 %all-reduce.69 = (f32[2048]{0:T(1024)}, f32[2048]{0:T(1024)}) all-reduce(f32[2048]{0:T(1024)S(1)} %get-tuple-element.76, f32[2048]{0:T(1024)S(1)} %copy-done.76), channel_id=1, replica_groups=mesh['wide'=8,'narrow'=4] {'wide','narrow'}, use_global_device_ids=true, to_apply=%region_17.18 | all-reduce | flops 4096 | bytes 32768 | tf_op jit(solution)/shard_map/psum | solution.py:243
  1533.7 128.1 %reduce-scatter.11.cloned.1.call-done = f32[128,2,2048]{2,0,1:T(8,128)} async-done(((f32[1024,2,2048]{2,0,1:T(8,128)}), f32[128,2,2048]{2,0,1:T(8,128)}) %reduce-scatter.11.cloned.1.call-update) | async-done | bytes 2097168 | tf_op jit(solution)/shard_map/reduce_scatter | solution.py:108
  1661.8 5.8 fusion.111
  1667.7 66.1 %reduce-scatter.23.cloned.1.call-done = f32[768,512]{1,0:T(8,128)} async-done(((f32[768,2048]{1,0:T(8,128)}), f32[768,512]{1,0:T(8,128)}) %reduce-scatter.23.cloned.1.call-update) | async-done | bytes 1572880 | tf_op jit(solution)/shard_map/reduce_scatter | solution.py:146
  1733.8 50.5 %all-reduce.74.cloned.1.call-done = (f32[2,160,160]{2,1,0:T(8,128)}, f32[2,160,160]{2,1,0:T(8,128)}) async-done(((f32[2,160,160]{2,1,0:T(8,128)}, f32[2,160,160]{2,1,0:T(8,128)}), (f32[2,160,160]{2,1,0:T(8,128)}, f32[2,160,160]{2,1,0:T(8,128)})) %all-reduce.74.cloned.1.call-update) | async-done | bytes 409616 | tf_op jit(solution)/shard_map/psum | solution.py:231
  1784.4 43.0 %reduce-scatter.19.cloned.1.call-done = f32[320,512]{1,0:T(8,128)} async-done(((f32[320,2048]{1,0:T(8,128)}), f32[320,512]{1,0:T(8,128)}) %reduce-scatter.19.cloned.1.call-update) | async-done | bytes 655376 | tf_op jit(solution)/shard_map/reduce_scatter | solution.py:146
  1827.4 64.9 %reduce-scatter.17.cloned.1.call-done = f32[2,512,320]{1,2,0:T(8,128)} async-done(((f32[2,2048,320]{1,2,0:T(8,128)}), f32[2,512,320]{1,2,0:T(8,128)}) %reduce-scatter.17.cloned.1.call-update) | async-done | bytes 1310736 | tf_op jit(solution)/shard_map/reduce_scatter | solution.py:145
  (469 shorter events, 301.4 us)
Async XLA Ops:
  7.2 161.6 %copy-start = (bf16[2,160,160]{2,1,0:T(8,128)(2,1)S(1)}, bf16[2,160,160]{2,1,0:T(8,128)(2,1)}, u32[]{:S(2)}) copy-start(bf16[2,160,160]{2,1,0:T(8,128)(2,1)} %param.25) | copy-start | bytes 307204
  7.2 6.8 copy-start.100
  7.2 6.9 copy-start.98
  7.2 6.9 copy-start.101
  7.2 44.9 %all-gather.11.cloned.1.call-start = ((), (), s32[]{:S(2)}) async-start(), calls=%async_computation.9 | async-start | bytes 3276800 | tf_op jit(solution)/shard_map/all_gather | solution.py:98
  8.0 128.4 %all-gather.9.cloned.1.call-start = ((), (), s32[]{:S(2)}) async-start(), calls=%async_computation.8 | async-start | bytes 9437184 | tf_op jit(solution)/shard_map/all_gather | solution.py:85
  13.2 306.5 %all-gather.13.cloned.1.call-start = ((), (), s32[]{:S(2)}) async-start(), calls=%async_computation.10 | async-start | bytes 1638400 | tf_op jit(solution)/shard_map/all_gather | solution.py:90
  13.9 486.9 %reduce-scatter.9.cloned.1.call-start = ((), (), s32[]{:S(2)}) async-start(), calls=%async_computation.11 | async-start | bytes 18874368 | tf_op jit(solution)/shard_map/reduce_scatter | solution.py:108
  14.0 177.4 %copy-start.74 = (f32[16,16]{1,0:T(8,128)}, f32[16,16]{1,0:T(8,128)S(1)}, u32[]{:S(2)}) copy-start(f32[16,16]{1,0:T(8,128)S(1)} %fusion.145) | copy-start | bytes 3076
  14.1 157.8 %copy-start.63 = (f32[320]{0:T(512)}, f32[320]{0:T(512)S(1)}, u32[]{:S(2)}) copy-start(f32[320]{0:T(512)S(1)} %get-tuple-element.78) | copy-start | bytes 3844
  14.1 157.8 %copy-start.65 = (f32[320]{0:T(512)}, f32[320]{0:T(512)S(1)}, u32[]{:S(2)}) copy-start(f32[320]{0:T(512)S(1)} %get-tuple-element.80) | copy-start | bytes 3844
  14.1 157.8 %copy-start.67 = (f32[320]{0:T(512)}, f32[320]{0:T(512)S(1)}, u32[]{:S(2)}) copy-start(f32[320]{0:T(512)S(1)} %get-tuple-element.81) | copy-start | bytes 3844
  14.1 157.8 %copy-start.69 = (f32[320]{0:T(512)}, f32[320]{0:T(512)S(1)}, u32[]{:S(2)}) copy-start(f32[320]{0:T(512)S(1)} %get-tuple-element.79) | copy-start | bytes 3844
  14.2 173.4 %copy-start.57 = (f32[320]{0:T(512)}, f32[320]{0:T(512)S(1)}, u32[]{:S(2)}) copy-start(f32[320]{0:T(512)S(1)} %broadcast_multiply_fusion.3) | copy-start | bytes 3844
  14.8 157.1 %copy-start.55 = (f32[2,1024]{1,0:T(2,128)}, f32[2,1024]{1,0:T(2,128)S(1)}, u32[]{:S(2)}) copy-start(f32[2,1024]{1,0:T(2,128)S(1)} %get-tuple-element.171) | copy-start | bytes 24580
  145.3 4.4 copy-start.33
  157.3 11.6 copy-start.1
  170.4 4.4 copy-start.36
  171.9 8.1 copy-start.15
  191.4 22.6 %copy-start.18 = (f32[2,64,16,320]{3,2,1,0:T(8,128)}, f32[2,64,16,320]{3,2,1,0:T(8,128)S(1)}, u32[]{:S(2)}) copy-start(f32[2,64,16,320]{3,2,1,0:T(8,128)S(1)} %copy.144) | copy-start | bytes 7864324
  219.7 71.4 %copy-start.43 = (f32[2,32,320]{2,1,0:T(8,128)}, f32[2,32,320]{2,1,0:T(8,128)S(1)}, u32[]{:S(2)}) copy-start(f32[2,32,320]{2,1,0:T(8,128)S(1)} %slice.243) | copy-start | bytes 245764
  333.9 237.2 %all-gather.17.cloned.1.call-start = ((), (), s32[]{:S(2)}) async-start(), calls=%async_computation.13 | async-start | bytes 7864320 | tf_op jit(solution)/shard_map/all_gather | solution.py:98
  334.5 320.7 %all-gather.15.cloned.1.call-start = ((), (), s32[]{:S(2)}) async-start(), calls=%async_computation.12 | async-start | bytes 9437184 | tf_op jit(solution)/shard_map/all_gather | solution.py:85
  505.7 193.8 %all-gather.19.cloned.1.call-start = ((), (), s32[]{:S(2)}) async-start(), calls=%async_computation.14 | async-start | bytes 3932160 | tf_op jit(solution)/shard_map/all_gather | solution.py:90
  506.4 277.3 %all-gather.21.cloned.1.call-start = ((), (), s32[]{:S(2)}) async-start(), calls=%async_computation.16 | async-start | bytes 9437184 | tf_op jit(solution)/shard_map/all_gather | solution.py:85
  510.4 475.8 %reduce-scatter.13.cloned.1.call-start = ((), (), s32[]{:S(2)}) async-start(), calls=%async_computation.17 | async-start | bytes 18874368 | tf_op jit(solution)/shard_map/reduce_scatter | solution.py:120
  783.7 19.4 %copy-start.108 = (bf16[2,2048,768]{2,1,0:T(8,128)(2,1)S(1)}, bf16[2,2048,768]{2,1,0:T(8,128)(2,1)}, u32[]{:S(2)}) copy-start(bf16[2,2048,768]{2,1,0:T(8,128)(2,1)} %all-gather.17.cloned.1.call-done) | copy-start | bytes 18874372
  819.3 254.6 %all-gather.23.cloned.1.call-start = ((), (), s32[]{:S(2)}) async-start(), calls=%async_computation.18 | async-start | bytes 9437184 | tf_op jit(solution)/shard_map/all_gather | solution.py:85
  993.3 432.0 %reduce-scatter.21.cloned.1.call-start = ((), (), s32[]{:S(2)}) async-start(), calls=%async_computation.22 | async-start | bytes 15728640 | tf_op jit(solution)/shard_map/reduce_scatter | solution.py:145
  1012.7 479.1 %reduce-scatter.15.cloned.1.call-start = ((), (), s32[]{:S(2)}) async-start(), calls=%async_computation.19 | async-start | bytes 18874368 | tf_op jit(solution)/shard_map/reduce_scatter | solution.py:120
  1101.2 82.0 %copy-start.42 = (f32[2,32,320]{2,1,0:T(8,128)S(1)}, f32[2,32,320]{2,1,0:T(8,128)}, u32[]{:S(2)}) copy-start(f32[2,32,320]{2,1,0:T(8,128)} %slice.240) | copy-start | bytes 245764
  1206.5 42.0 %copy-start.11 = (f32[2,1024,320]{2,1,0:T(8,128)S(1)}, f32[2,1024,320]{2,1,0:T(8,128)}, u32[]{:S(2)}) copy-start(f32[2,1024,320]{2,1,0:T(8,128)} %copy.160) | copy-start | bytes 7864324
  1206.5 42.0 %copy-start.40 = (f32[2,64,320]{2,1,0:T(8,128)S(1)}, f32[2,64,320]{2,1,0:T(8,128)}, u32[]{:S(2)}) copy-start(f32[2,64,320]{2,1,0:T(8,128)} %copy-done.39) | copy-start | bytes 491524
  1268.9 7.0 copy-start.5
  1268.9 7.0 copy-start.56
  1268.9 7.0 copy-start.58
  1268.9 7.0 copy-start.62
  1268.9 7.0 copy-start.64
  1268.9 7.0 copy-start.66
  1268.9 7.0 copy-start.68
  1268.9 7.0 copy-start.70
  1268.9 7.0 copy-start.86
  1275.9 7.6 copy-start.17
  1324.5 337.4 %reduce-scatter.11.cloned.1.call-start = ((), (), s32[]{:S(2)}) async-start(), calls=%async_computation.15 | async-start | bytes 18874368 | tf_op jit(solution)/shard_map/reduce_scatter | solution.py:108
  1346.3 387.5 %reduce-scatter.23.cloned.1.call-start = ((), (), s32[]{:S(2)}) async-start(), calls=%async_computation.23 | async-start | bytes 7864320 | tf_op jit(solution)/shard_map/reduce_scatter | solution.py:146
  1361.2 423.2 %all-reduce.74.cloned.1.call-start = ((), (), s32[]{:S(2)}) async-start(), calls=%async_computation.24 | async-start | bytes 1310720 | tf_op jit(solution)/shard_map/psum | solution.py:231
  1364.8 5.2 copy-start.21
  1373.3 454.0 %reduce-scatter.19.cloned.1.call-start = ((), (), s32[]{:S(2)}) async-start(), calls=%async_computation.21 | async-start | bytes 3276800 | tf_op jit(solution)/shard_map/reduce_scatter | solution.py:146
  1383.2 509.0 %reduce-scatter.17.cloned.1.call-start = ((), (), s32[]{:S(2)}) async-start(), calls=%async_computation.20 | async-start | bytes 6553600 | tf_op jit(solution)/shard_map/reduce_scatter | solution.py:145
  1406.5 4.3 copy-start.24
  1414.2 5.0 copy-start.35
  1429.0 5.5 copy-start.22
  1434.7 5.1 copy-start.10
  1442.1 7.2 copy-start.99
  1442.1 49.7 %copy-start.19 = (bf16[2,128,2048]{2,1,0:T(8,128)(2,1)S(1)}, bf16[2,128,2048]{2,1,0:T(8,128)(2,1)}, u32[]{:S(2)}) copy-start(bf16[2,128,2048]{2,1,0:T(8,128)(2,1)} %param.16) | copy-start | bytes 3145732
  1442.1 49.7 %copy-start.60 = (f32[2048]{0:T(1024)S(1)}, f32[2048]{0:T(1024)}, u32[]{:S(2)}) copy-start(f32[2048]{0:T(1024)} %param.19) | copy-start | bytes 24580
  1442.1 49.7 %copy-start.88 = (f32[2,128]{1,0:T(2,128)S(1)}, f32[2,128]{1,0:T(2,128)}, u32[]{:S(2)}) copy-start(f32[2,128]{1,0:T(2,128)} %copy-done.87) | copy-start | bytes 3076
  1449.1 45.0 %copy-start.76 = (f32[2048]{0:T(1024)S(1)}, f32[2048]{0:T(1024)}, u32[]{:S(2)}) copy-start(f32[2048]{0:T(1024)} %get-tuple-element.74) | copy-start | bytes 24580
  1449.1 84.6 %copy-start.95 = (f32[2,128]{1,0:T(2,128)S(1)}, f32[2,128]{1,0:T(2,128)}, u32[]{:S(2)}) copy-start(f32[2,128]{1,0:T(2,128)} %copy-done.94) | copy-start | bytes 3076
  1449.1 212.7 %copy-start.8 = (f32[2,128,2048]{2,1,0:T(8,128)S(1)}, f32[2,128,2048]{2,1,0:T(8,128)}, u32[]{:S(2)}) copy-start(f32[2,128,2048]{2,1,0:T(8,128)} %copy-done.6) | copy-start | bytes 6291460
  1449.1 212.7 %copy-start.54 = (f32[2048]{0:T(1024)S(1)}, f32[2048]{0:T(1024)}, u32[]{:S(2)}) copy-start(f32[2048]{0:T(1024)} %param.29) | copy-start | bytes 24580
  1449.1 212.7 %copy-start.84 = (f32[2,128]{1,0:T(2,128)S(1)}, f32[2,128]{1,0:T(2,128)}, u32[]{:S(2)}) copy-start(f32[2,128]{1,0:T(2,128)} %copy-done.82) | copy-start | bytes 3076
  1449.1 212.7 %copy-start.91 = (f32[2,128]{1,0:T(2,128)S(1)}, f32[2,128]{1,0:T(2,128)}, u32[]{:S(2)}) copy-start(f32[2,128]{1,0:T(2,128)} %copy-done.89) | copy-start | bytes 3076
  1449.1 212.7 %copy-start.93 = (f32[2,128]{1,0:T(2,128)S(1)}, f32[2,128]{1,0:T(2,128)}, u32[]{:S(2)}) copy-start(f32[2,128]{1,0:T(2,128)} %copy-done.92) | copy-start | bytes 3076
  (64 other events, 141.7 us)
Sparse Core Ops, SparseCore 0:
  9.9 42.1 all-gather.10
  54.3 82.0 all-gather.8
  138.2 27.1 all-gather.12
  334.0 166.7 reduce-scatter.8
  502.5 68.5 all-gather.16
  573.1 82.0 all-gather.14
  657.0 42.3 all-gather.18
  701.6 82.0 all-gather.20
  819.4 166.7 reduce-scatter.12
  993.4 80.4 all-gather.22
  1076.9 119.2 reduce-scatter.20
  1324.6 167.1 reduce-scatter.14
  1494.1 167.6 reduce-scatter.10
  1665.2 68.5 reduce-scatter.22
  1737.3 47.0 all-reduce.73
  1787.8 39.5 reduce-scatter.18
  1830.8 61.4 reduce-scatter.16
where the time goes:
time: 1920 us; the launch traced here: 1900 us
  waiting for transfers between devices  1140 us (59%)
  local copies, waits for them, and re-layouts  305 us (16%)
  other arithmetic  196 us (10%)
  matrix products  185 us (10%)
  blocking collectives  55.8 us (3%)
    all_gather x4, waiting for transfers between devices, gather_rows(): whole = lax.all_gather(values, 'wide', axis=1, tiled=True)  307 us
    reduce_scatter x2, waiting for transfers between devices, forward_out(): lax.psum_scatter(jnp.einsum('stc,cd->tsd', shaped, whole, preferred_eleme...  294 us
    reduce_scatter x2, waiting for transfers between devices, backward_in(): lax.psum_scatter(jnp.einsum('kstc,kdc->tsd', shaped, whole, preferred_ele...  193 us
    reduce_scatter x2, waiting for transfers between devices, weight_grads(): lax.psum_scatter(grad_out, 'narrow', scatter_dimension=1, tiled=True)  109 us
    all_gather x2, waiting for transfers between devices, forward_in(): lax.all_gather(weight, 'narrow', axis=1, tiled=True)  97.8 us
    pad x41, local copies, waits for them, and re-layouts, blocked_scan(): lax.associative_scan(linear_combine, (block_decay, block_end), axis=1)  73.2 us
    reduce_scatter x2, waiting for transfers between devices, weight_grads(): lax.psum_scatter(grad_in, 'narrow', scatter_dimension=1, tiled=True)  64.9 us
    slice x42, local copies, waits for them, and re-layouts, blocked_scan(): lax.associative_scan(linear_combine, (block_decay, block_end), axis=1)  56.3 us
  transfers between devices with their start and end apart: 17, of which 15 were waited for; matrix products, arithmetic and copies ran while one was open for 32% of the time, Pallas kernels for 0%

commit v1 on v0

v1 whole, which is shorter than its diff:
```python
from functools import partial

import jax
import jax.numpy as jnp
from jax import lax
from jax.experimental import pallas as pl
from jax.experimental.pallas import tpu as pltpu
from jax.sharding import PartitionSpec as P

decay_scale = 8.0
norm_eps = 1e-06
gelu_in = 0.7978845608028654
gelu_cube = 0.044715
f32 = jnp.float32
bf16 = jnp.bfloat16


def gelu_tanh(v):
    return jnp.tanh(gelu_in * (v + gelu_cube * v * v * v))


def gelu_pair(v):
    t = gelu_tanh(v)
    half = 0.5 * (1.0 + t)
    slope = half + 0.5 * v * (1.0 - t * t) * (gelu_in + (3.0 * gelu_in * gelu_cube) * v * v)
    return v * half, slope


def one_minus_exp(v, decay):
    series = 1.0 - v * (1.0 / 7.0)
    for order in (6.0, 5.0, 4.0, 3.0, 2.0):
        series = 1.0 - v * (1.0 / order) * series
    return jnp.where(v < 0.3, v * series, 1.0 - decay * decay)


def split_dot(values, weight):
    high = values.astype(bf16)
    low = (values - high.astype(f32)).astype(bf16)
    return jnp.dot(high, weight, preferred_element_type=f32) + jnp.dot(
        low, weight, preferred_element_type=f32
    )


def tile_scan(decay, drive, backward):
    rows, channels = decay.shape
    a = decay.reshape(rows // 8, 8, channels)
    b = drive.reshape(rows // 8, 8, channels)
    row = lax.broadcasted_iota(jnp.int32, (1, 8, channels), 1)
    for step in (1, 2, 4):
        if backward:
            keep, shift = row < 8 - step, 8 - step
        else:
            keep, shift = row >= step, step
        a_moved = jnp.where(keep, pltpu.roll(a, shift, 1), 1.0)
        b_moved = jnp.where(keep, pltpu.roll(b, shift, 1), 0.0)
        b = b + a * b_moved
        a = a * a_moved
    return a, b


def mixer_forward_kernel(
    place, lengths, pre, conv_weight, conv_bias, gate_weight, gate_bias, rate_scale,
    mixed, conv_out, rate_out, in_out, states_out, final_state, conv_state, x_tail, carry,
):
    chunk = pl.program_id(0)
    _, _, _, seq_count, local_len, channels = pre.shape

    @pl.when(chunk == 0)
    def _():
        x_tail[...] = jnp.zeros_like(x_tail)
        carry[...] = jnp.zeros_like(carry)

    convs = []
    for seq in range(seq_count):
        x = pre[0, 1, 0, seq]
        extended = jnp.concatenate((x_tail[seq], x), axis=0)
        conv = conv_bias[...] + conv_weight[0:1] * x
        for lag in range(1, 4):
            conv = conv + conv_weight[lag : lag + 1] * extended[8 - lag : 8 - lag + local_len]
        x_tail[seq] = x[local_len - 8 :]
        convs.append(conv)
        for tap in range(3):
            position = lengths[seq] - 3 + tap

            @pl.when(position // local_len == chunk)
            def _(seq=seq, tap=tap, position=position):
                conv_state[seq, tap : tap + 1] = pre[
                    0, 1, 0, seq, pl.ds(lax.rem(position, local_len), 1)
                ]

    conv_all = jnp.concatenate(convs, axis=0)
    gates = jax.nn.sigmoid(split_dot(conv_all, gate_weight[...]) + gate_bias[...])
    for seq in range(seq_count):
        rows = slice(seq * local_len, (seq + 1) * local_len)
        conv = convs[seq]
        rate_gate = gates[rows, :channels]
        in_gate = gates[rows, channels:]
        step_log = rate_scale[...] * rate_gate
        decay = jnp.exp(-step_log)
        root = jnp.sqrt(one_minus_exp(2.0 * step_log, decay))
        position = chunk * local_len + lax.broadcasted_iota(jnp.int32, (local_len, 1), 0)
        live = position < lengths[seq]
        drive = jnp.where(live, root * in_gate * conv, 0.0)
        a, b = tile_scan(jnp.where(live, decay, 1.0), drive, False)
        last = carry[seq]
        gated, _ = gelu_pair(pre[0, 0, 0, seq])
        tiles = []
        for tile in range(local_len // 8):
            tiles.append(b[tile] + a[tile] * last)
            last = tiles[-1][7:8]
        states = jnp.concatenate(tiles, axis=0)
        states_out[0, 0, seq] = states
        mixed[0, 0, seq] = (gated * states).astype(bf16)
        carry[seq] = last
        final_state[seq : seq + 1] = last
        conv_out[0, 0, seq] = conv
        rate_out[0, 0, seq] = rate_gate
        in_out[0, 0, seq] = in_gate


def mixer_backward_kernel(
    place, lengths, pre, back, conv_in, rate_in, in_in, states_in, conv_weight, gate_back, rate_scale,
    y_grad, x_grad, sums, gate_sums, carry, grad_head,
):
    step = pl.program_id(0)
    chunk = pl.num_programs(0) - 1 - step
    _, _, _, seq_count, local_len, channels = pre.shape

    @pl.when(step == 0)
    def _():
        carry[...] = jnp.zeros_like(carry)
        grad_head[...] = jnp.zeros_like(grad_head)
        sums[...] = jnp.zeros_like(sums)
        gate_sums[...] = jnp.zeros_like(gate_sums)

    rate_pre, in_pre, direct = [], [], []
    decay_sum = jnp.zeros((1, channels), f32)
    for seq in range(seq_count):
        position = chunk * local_len + lax.broadcasted_iota(jnp.int32, (local_len, 1), 0)
        live = position < lengths[seq]
        rate_gate = rate_in[0, 0, seq]
        in_gate = in_in[0, 0, seq]
        conv = conv_in[0, 0, seq]
        states = states_in[0, 0, seq]
        mixer_grad = back[0, 0, seq]
        gated, slope = gelu_pair(pre[0, 0, 0, seq])
        step_log = rate_scale[...] * rate_gate
        decay_raw = jnp.exp(-step_log)
        decay = jnp.where(live, decay_raw, 1.0)
        y_grad[0, 0, seq] = (mixer_grad * states * slope).astype(bf16)
        source = mixer_grad * gated
        a, b = tile_scan(decay, decay * source, True)
        following = carry[seq]
        tiles = []
        for tile in reversed(range(local_len // 8)):
            passed = b[tile] + a[tile] * following
            tiles.append(jnp.concatenate((passed[1:], following), axis=0))
            following = passed[0:1]
        carry[seq] = following
        adjoint = source + jnp.concatenate(tiles[::-1], axis=0)
        adjoint = jnp.where(live, adjoint, 0.0)
        square = one_minus_exp(2.0 * step_log, decay_raw)
        inverse_root = lax.rsqrt(square)
        root = square * inverse_root
        gated_conv = in_gate * conv
        logd_grad = adjoint * (
            states - root * gated_conv - gated_conv * decay_raw * decay_raw * inverse_root
        )
        rate_part = logd_grad * rate_gate
        decay_sum = decay_sum + jnp.sum(rate_part, axis=0, keepdims=True)
        rate_pre.append(-rate_scale[...] * rate_part * (1.0 - rate_gate))
        through = adjoint * root
        in_pre.append(through * gated_conv * (1.0 - in_gate))
        direct.append(through * in_gate)
    rate_all = jnp.concatenate(rate_pre, axis=0)
    in_all = jnp.concatenate(in_pre, axis=0)
    both = jnp.concatenate((rate_all, in_all), axis=1)
    conv_grad = jnp.concatenate(direct, axis=0) + split_dot(both, gate_back[...])
    conv_all = jnp.concatenate([conv_in[0, 0, seq] for seq in range(seq_count)], axis=0)
    gate_sums[...] += lax.dot_general(
        conv_all.astype(bf16), both.astype(bf16), (((0,), (0,)), ((), ())), preferred_element_type=f32
    )
    tap_sums = [jnp.zeros((1, channels), f32) for _ in range(4)]
    for seq in range(seq_count):
        part = conv_grad[seq * local_len : (seq + 1) * local_len]
        extended = jnp.concatenate((part, grad_head[seq]), axis=0)
        x = pre[0, 1, 0, seq]
        total = conv_weight[0:1] * part
        tap_sums[0] = tap_sums[0] + jnp.sum(part * x, axis=0, keepdims=True)
        for lag in range(1, 4):
            moved = extended[lag : lag + local_len]
            total = total + conv_weight[lag : lag + 1] * moved
            tap_sums[lag] = tap_sums[lag] + jnp.sum(moved * x, axis=0, keepdims=True)
        x_grad[0, 0, seq] = total.astype(bf16)
        grad_head[seq] = part[:8]
    sums[0:1] += jnp.sum(rate_all, axis=0, keepdims=True)
    sums[1:2] += jnp.sum(in_all, axis=0, keepdims=True)
    sums[2:3] += decay_sum
    sums[3:4] += jnp.sum(conv_grad, axis=0, keepdims=True)
    for lag in range(4):
        sums[4 + lag : 5 + lag] += tap_sums[lag]


def chunk_place(chunk, place, chips):
    return lax.rem(place[0] - chunk // 2 + chips, chips), lax.rem(chunk + place[1], 2)


def mixer_forward(pre, lengths, place, conv_weight, conv_bias, gate_weight, gate_bias, rate_scale):
    chips, _, _, seq_count, local_len, channels = pre.shape

    def in_map(chunk, place, lengths):
        chip, core = chunk_place(chunk, place, chips)
        return (chip, 0, core, 0, 0, 0)

    def out_map(chunk, place, lengths):
        chip, core = chunk_place(chunk, place, chips)
        return (chip, core, 0, 0, 0)

    def whole(shape):
        return pl.BlockSpec(shape, lambda chunk, place, lengths: (0,) * len(shape))

    block = pl.BlockSpec((1, 1, seq_count, local_len, channels), out_map)
    full = (chips, 2, seq_count, local_len, channels)
    rows = chips * 2 * seq_count * local_len
    return pl.pallas_call(
        mixer_forward_kernel,
        grid_spec=pltpu.PrefetchScalarGridSpec(
            num_scalar_prefetch=2,
            grid=(2 * chips,),
            in_specs=[
                pl.BlockSpec((1, 2, 1, seq_count, local_len, channels), in_map),
                whole(conv_weight.shape),
                whole(conv_bias.shape),
                whole(gate_weight.shape),
                whole(gate_bias.shape),
                whole(rate_scale.shape),
            ],
            out_specs=[block] * 5 + [whole((seq_count, channels)), whole((seq_count, 3, channels))],
            scratch_shapes=[
                pltpu.VMEM((seq_count, 8, channels), f32),
                pltpu.VMEM((seq_count, 1, channels), f32),
            ],
        ),
        out_shape=[jax.ShapeDtypeStruct(full, bf16)]
        + [jax.ShapeDtypeStruct(full, f32)] * 4
        + [
            jax.ShapeDtypeStruct((seq_count, channels), f32),
            jax.ShapeDtypeStruct((seq_count, 3, channels), f32),
        ],
        compiler_params=pltpu.CompilerParams(vmem_limit_bytes=32 << 20),
        cost_estimate=pl.CostEstimate(
            flops=rows * channels * 200, bytes_accessed=rows * channels * 26, transcendentals=0
        ),
        name="mixer_forward",
    )(place, lengths, pre, conv_weight, conv_bias, gate_weight, gate_bias, rate_scale)


def mixer_backward(pre, back, saved, lengths, place, conv_weight, gate_back, rate_scale):
    chips, _, _, seq_count, local_len, channels = pre.shape

    def in_map(step, place, lengths):
        chip, core = chunk_place(2 * chips - 1 - step, place, chips)
        return (chip, 0, core, 0, 0, 0)

    def out_map(step, place, lengths):
        chip, core = chunk_place(2 * chips - 1 - step, place, chips)
        return (chip, core, 0, 0, 0)

    def whole(shape):
        return pl.BlockSpec(shape, lambda step, place, lengths: (0,) * len(shape))

    block = pl.BlockSpec((1, 1, seq_count, local_len, channels), out_map)
    full = (chips, 2, seq_count, local_len, channels)
    rows = chips * 2 * seq_count * local_len
    return pl.pallas_call(
        mixer_backward_kernel,
        grid_spec=pltpu.PrefetchScalarGridSpec(
            num_scalar_prefetch=2,
            grid=(2 * chips,),
            in_specs=[pl.BlockSpec((1, 2, 1, seq_count, local_len, channels), in_map)]
            + [block] * 5
            + [whole(conv_weight.shape), whole(gate_back.shape), whole(rate_scale.shape)],
            out_specs=[block, block, whole((8, channels)), whole((channels, 2 * channels))],
            scratch_shapes=[
                pltpu.VMEM((seq_count, 1, channels), f32),
                pltpu.VMEM((seq_count, 8, channels), f32),
            ],
        ),
        out_shape=[
            jax.ShapeDtypeStruct(full, bf16),
            jax.ShapeDtypeStruct(full, bf16),
            jax.ShapeDtypeStruct((8, channels), f32),
            jax.ShapeDtypeStruct((channels, 2 * channels), f32),
        ],
        compiler_params=pltpu.CompilerParams(vmem_limit_bytes=32 << 20),
        cost_estimate=pl.CostEstimate(
            flops=rows * channels * 300, bytes_accessed=rows * channels * 32, transcendentals=0
        ),
        name="mixer_backward",
    )(place, lengths, pre, back, *saved, conv_weight, gate_back, rate_scale)


def block_diagonal(weight):
    count, width, _ = weight.shape
    rows = [
        jnp.pad(weight[at], ((0, 0), (at * width, (count - 1 - at) * width))) for at in range(count)
    ]
    return jnp.concatenate(rows, axis=0)


def diagonal_blocks(values, count):
    width = values.shape[0] // count
    return jnp.stack(
        [values[at * width : (at + 1) * width, at * width : (at + 1) * width] for at in range(count)]
    )


def narrow_whole(weight):
    return lax.all_gather(weight, "narrow", axis=1, tiled=True)


def narrow_sum(grad):
    return lax.psum_scatter(
        grad.astype(bf16), "narrow", scatter_dimension=1, tiled=True
    ).astype(f32)


def swap_cores(values, wide):
    return lax.ppermute(values, "wide", [(at, at ^ 1) for at in range(wide)])


def next_chip(values, wide):
    return lax.ppermute(values, "wide", [(at, (at + 2) % wide) for at in range(wide)])


def gather_ring(rows, wide):
    held, blocks = rows, []
    for hop in range(wide // 2):
        if hop:
            held = next_chip(held, wide)
        blocks.append(jnp.concatenate((held, swap_cores(held, wide)), axis=0))
    return blocks


def ring_order(chips):
    return list(range(1, chips)) + [0]


class RingSum:
    def __init__(self, wide):
        self.wide = wide
        self.moving = None

    def add(self, block, hop):
        mine, other = jnp.split(block, 2, axis=0)
        total = mine + swap_cores(other.astype(bf16), self.wide).astype(f32)
        if self.moving is not None:
            total = total + self.moving.astype(f32)
        if hop:
            self.moving = next_chip(total.astype(bf16), self.wide)
        return total


def norm_forward(values, gain):
    scale = lax.rsqrt(jnp.mean(values * values, axis=-1, keepdims=True) + norm_eps)
    return scale, (values * scale * gain).astype(bf16)


def norm_backward(values, scale, gain, grad):
    unit = values * scale
    scaled = grad * gain
    back = scale * (scaled - unit * jnp.mean(scaled * unit, axis=-1, keepdims=True))
    return back, jnp.sum(grad * unit, axis=0)


def dot(left, right):
    return jnp.dot(left, right, preferred_element_type=f32)


def dot_nt(left, right):
    return lax.dot_general(left, right, (((1,), (1,)), ((), ())), preferred_element_type=f32)


def dot_tn(left, right):
    return lax.dot_general(left, right, (((0,), (0,)), ((), ())), preferred_element_type=f32)


def body(
    tokens, lengths, cotangent, first_gain, proj_in, conv_weight, conv_bias, rate_weight, rate_bias,
    input_weight, input_bias, decay_param, proj_out, second_gain, mlp_in, mlp_down,
):
    seq_count, local_len, width = tokens.shape
    wide = lax.axis_size("wide")
    chips = wide // 2
    me = lax.axis_index("wide")
    place = jnp.stack((me // 2, me % 2)).astype(jnp.int32)
    channels = proj_in.shape[2]
    gate_count = rate_weight.shape[0]
    block_shape = (2, seq_count, local_len, channels)
    order = ring_order(chips)
    positions = me * local_len + jnp.arange(local_len, dtype=jnp.int32)
    mask = (positions[None, :] < lengths[:, None]).astype(f32).reshape(-1, 1)

    tokens_f = tokens.reshape(-1, width).astype(f32)
    scale_one, norm_in = norm_forward(tokens_f, first_gain)
    out_grad = cotangent.reshape(-1, width).astype(f32) * mask

    whole_in = narrow_whole(proj_in)
    rows_first = gather_ring(norm_in, wide)
    whole_out = narrow_whole(proj_out)
    whole_mlp_in = narrow_whole(mlp_in)
    whole_down = narrow_whole(mlp_down)
    rows_back = gather_ring(out_grad.astype(bf16), wide)

    pre = jnp.stack(
        [
            jnp.stack([dot(rows, whole_in[kind]).reshape(block_shape) for kind in range(2)])
            for rows in rows_first
        ]
    )
    gate_weight = jnp.concatenate((block_diagonal(rate_weight), block_diagonal(input_weight)), axis=1)
    gate_bias = jnp.concatenate((rate_bias, input_bias))[None, :]
    rate_scale = (decay_scale * jax.nn.softplus(-decay_param))[None, :]
    mixed, conv, rate_gate, in_gate, states, final_state, conv_state = mixer_forward(
        pre, lengths, place, conv_weight, conv_bias[None, :], gate_weight, gate_bias, rate_scale
    )
    mixed_rows = mixed.reshape(chips, -1, channels)
    ring = RingSum(wide)
    for hop in order:
        mix_sum = ring.add(dot(mixed_rows[hop], whole_out), hop)
    resid = tokens_f + mix_sum

    scale_two, norm_mid = norm_forward(resid, second_gain)
    rows_second = gather_ring(norm_mid, wide)
    hidden, gate_grads, up_grads = {}, {}, {}
    ring_mid, ring_out = RingSum(wide), RingSum(wide)
    for hop in order:
        gate_pre = dot(rows_second[hop], whole_mlp_in[0])
        up_pre = dot(rows_second[hop], whole_mlp_in[1])
        hidden_grad = dot_nt(rows_back[hop], whole_down)
        gated, slope = gelu_pair(gate_pre)
        hidden[hop] = (gated * up_pre).astype(bf16)
        gate_grads[hop] = (hidden_grad * up_pre * slope).astype(bf16)
        up_grads[hop] = (hidden_grad * gated).astype(bf16)
        mid_sum = ring_mid.add(
            dot_nt(gate_grads[hop], whole_mlp_in[0]) + dot_nt(up_grads[hop], whole_mlp_in[1]), hop
        )
    for hop in order:
        mlp_sum = ring_out.add(dot(hidden[hop], whole_down), hop)
    output = (resid + mlp_sum).astype(bf16)

    from_norm, gain_two = norm_backward(resid, scale_two, second_gain, mid_sum)
    resid_grad = out_grad + from_norm
    rows_resid = gather_ring(resid_grad.astype(bf16), wide)
    all_second = jnp.concatenate(rows_second, axis=0)
    all_back = jnp.concatenate(rows_back, axis=0)
    all_resid = jnp.concatenate(rows_resid, axis=0)

    def joined(parts):
        return jnp.concatenate([parts[hop] for hop in range(chips)], axis=0)

    grad_mlp_in = narrow_sum(
        jnp.stack((dot_tn(all_second, joined(gate_grads)), dot_tn(all_second, joined(up_grads))))
    )
    grad_mlp_down = narrow_sum(dot_tn(joined(hidden), all_back))
    grad_proj_out = narrow_sum(dot_tn(mixed.reshape(-1, channels), all_resid))

    back = jnp.stack([dot_nt(rows, whole_out).reshape(block_shape) for rows in rows_resid])
    y_grad, x_grad, sums, gate_sums = mixer_backward(
        pre, back, (conv, rate_gate, in_gate, states), lengths, place, conv_weight,
        gate_weight.T, rate_scale,
    )
    y_rows = y_grad.reshape(chips, -1, channels)
    x_rows = x_grad.reshape(chips, -1, channels)
    ring_in = RingSum(wide)
    for hop in order:
        in_sum = ring_in.add(dot_nt(y_rows[hop], whole_in[0]) + dot_nt(x_rows[hop], whole_in[1]), hop)
    all_first = jnp.concatenate(rows_first, axis=0)
    grad_proj_in = narrow_sum(
        jnp.stack(
            (
                dot_tn(all_first, y_grad.reshape(-1, channels)),
                dot_tn(all_first, x_grad.reshape(-1, channels)),
            )
        )
    )
    sums = lax.psum(
        (
            sums,
            diagonal_blocks(gate_sums[:, :channels], gate_count),
            diagonal_blocks(gate_sums[:, channels:], gate_count),
        ),
        "narrow",
    )
    sums, grad_rate_weight, grad_input_weight = sums
    from_norm, gain_one = norm_backward(tokens_f, scale_one, first_gain, in_sum)
    grad_tokens = (resid_grad + from_norm).astype(bf16)
    gains = lax.psum((gain_one, gain_two), ("wide", "narrow"))
    return (
        output.reshape(tokens.shape),
        grad_tokens.reshape(tokens.shape),
        final_state,
        conv_state,
        gains[0],
        grad_proj_in,
        sums[4:8],
        sums[3],
        grad_rate_weight,
        sums[0],
        grad_input_weight,
        sums[1],
        sums[2] * decay_scale * jax.nn.sigmoid(-decay_param),
        grad_proj_out,
        gains[1],
        grad_mlp_in,
        grad_mlp_down,
    )


def solution(mesh):
    return jax.shard_map(
        body,
        mesh=mesh,
        in_specs=(
            P("narrow", "wide", None),
            P("narrow"),
            P("narrow", "wide", None),
            P(),
            P(None, "narrow", "wide"),
            P(None, "wide"),
            P("wide"),
            P("wide", None, None),
            P("wide"),
            P("wide", None, None),
            P("wide"),
            P("wide"),
            P("wide", "narrow"),
            P(),
            P(None, "narrow", "wide"),
            P("wide", "narrow"),
        ),
        out_specs=(
            P("narrow", "wide", None),
            P("narrow", "wide", None),
            P("narrow", "wide"),
            P("narrow", None, "wide"),
            P(),
            P(None, "narrow", "wide"),
            P(None, "wide"),
            P("wide"),
            P("wide", None, None),
            P("wide"),
            P("wide", None, None),
            P("wide"),
            P("wide"),
            P("wide", "narrow"),
            P(),
            P(None, "narrow", "wide"),
            P("wide", "narrow"),
        ),
        check_vma=False,
    )
```

time: 1920 us -> 848 us (0.44)
  waiting for transfers between devices: 1140 us -> 424 us
  local copies, waits for them, and re-layouts: 305 us -> 69.8 us
  other arithmetic: 196 us -> 68.7 us
  Pallas kernels: 0 us -> 40 us
  matrix products: 185 us -> 146 us
    reduce_scatter x8 -> x4, waiting for transfers between devices: 662 us -> 0.01 us  [narrow_sum(): lax.psum_scatter(grad.astype(bf16), 'narrow', scatter_dimension=1, tiled=...]
    all_gather x8 -> x4, waiting for transfers between devices: 429 us -> 0.01 us  [narrow_whole(): return lax.all_gather(weight, 'narrow', axis=1, tiled=True)]
    ppermute x0 -> x56, waiting for transfers between devices: none -> 423 us  [the longest x24 423 us: next_chip(): lax.ppermute(values, 'wide', [(at, (at + 2) % wide) for at in range(wide)])]
    reduce_sum x11 -> x4, other arithmetic: 92 us -> 11.6 us  [the longest x2 7.14 us: norm_backward(): return (back, jnp.sum(grad * unit, axis=0))]
    pad x41 -> x0, local copies, waits for them, and re-layouts: 73.2 us -> none  [blocked_scan(): lax.associative_scan(linear_combine, (block_decay, block_end), axis=1)]
    slice x47 -> x6, local copies, waits for them, and re-layouts: 71.2 us -> 2.93 us  [the longest x1 1.05 us: body(): mix_sum = ring.add(dot(mixed_rows[hop], whole_out), hop)]
    psum x1, waiting for transfers between devices: 50.5 us -> 0.01 us  [body(): lax.psum((sums, diagonal_blocks(gate_sums[:, :channels], gate_count), dia...]
    pallas_call x0 -> x2, Pallas kernels: none -> 40 us  [the longest x1 23.2 us: mixer_backward(): pl.pallas_call(mixer_backward_kernel, grid_spec=pltpu.PrefetchScalarGridS...]
  transfers between devices with their start and end apart: 17 -> 65, of which waited for: 15 -> 21; matrix products, arithmetic and copies ran while one was open for 32% -> 31% of each run, Pallas kernels for 0% -> 5%
where the time goes in v1:
time: 848 us; the launch traced here: 839 us
  waiting for transfers between devices  424 us (50%)
  matrix products  146 us (17%)
  local copies, waits for them, and re-layouts  69.8 us (8%)
  other arithmetic  68.7 us (8%)
  blocking collectives  57.2 us (7%)
  Pallas kernels  40 us (5%)
  starting transfers between devices  16.7 us (2%)
  between operations  16.2 us (2%)
    ppermute x24, waiting for transfers between devices, next_chip(): lax.ppermute(values, 'wide', [(at, (at + 2) % wide) for at in range(wide)])  423 us
    dot_general x24, matrix products, dot_nt(): lax.dot_general(left, right, (((1,), (1,)), ((), ())), preferred_element_...  63.4 us
    unnamed x295, local copies, waits for them, and re-layouts  54.4 us
    dot_general x24, matrix products, dot(): return jnp.dot(left, right, preferred_element_type=f32)  45.3 us
    psum x1, blocking collectives, body(): gains = lax.psum((gain_one, gain_two), ('wide', 'narrow'))  39.4 us
    dot_general x6, matrix products, dot_tn(): lax.dot_general(left, right, (((0,), (0,)), ((), ())), preferred_element_...  37.6 us
    pallas_call x1, Pallas kernels, mixer_backward(): pl.pallas_call(mixer_backward_kernel, grid_spec=pltpu.PrefetchScalarGridS...  23.2 us
    psum x1, blocking collectives, body(): lax.psum((sums, diagonal_blocks(gate_sums[:, :channels], gate_count), dia...  17.8 us
  transfers between devices with their start and end apart: 65, of which 21 were waited for; matrix products, arithmetic and copies ran while one was open for 31% of the time, Pallas kernels for 5%

profile of v1, /device:TPU:0, one launch (start us, length us, event | category | flops | bytes accessed | tf_op | source)
XLA Modules:
  0.0 839.3 jit_solution(11473097508803363372)
XLA Ops:
  10.3 2.4 constant_dynamic-update-slice_fusion.13
  12.8 3.0 collective-permute-start.1
  15.8 25.4 %collective-permute-done.1 = bf16[256,2048]{1,0:T(8,128)(2,1)S(1)} collective-permute-done((bf16[256,2048]{1,0:T(8,128)(2,1)}, bf16[256,2048]{1,0:T(8,128)(2,1)S(1)}, u32[]{:S(2)}, u32[]{:S(2)}) %collective-permute-start.1) | collective-permute-done | bytes 1048608 | tf_op jit(solution)/shard_map/ppermute | solution.py:333
  44.0 23.4 %collective-permute-done.3 = bf16[256,2048]{1,0:T(8,128)(2,1)S(1)} collective-permute-done((bf16[256,2048]{1,0:T(8,128)(2,1)S(1)}, bf16[256,2048]{1,0:T(8,128)(2,1)S(1)}, u32[]{:S(2)}, u32[]{:S(2)}) %collective-permute-start.3) | collective-permute-done | bytes 1048608 | tf_op jit(solution)/shard_map/ppermute | solution.py:333
  72.5 3.2 pad_maximum_fusion.4
  77.4 15.3 %collective-permute-done.5 = bf16[256,2048]{1,0:T(8,128)(2,1)} collective-permute-done((bf16[256,2048]{1,0:T(8,128)(2,1)S(1)}, bf16[256,2048]{1,0:T(8,128)(2,1)}, u32[]{:S(2)}, u32[]{:S(2)}) %collective-permute-start.5) | collective-permute-done | bytes 1048608 | tf_op jit(solution)/shard_map/ppermute | solution.py:333
  92.7 2.9 pad_maximum_fusion.6
  95.6 3.4 fusion.179
  112.8 16.8 %mixer_forward.1 = (bf16[4,2,2,128,320]{4,3,2,1,0:T(8,128)(2,1)S(1)}, f32[4,2,2,128,320]{4,3,2,1,0:T(8,128)S(1)}, f32[4,2,2,128,320]{4,3,2,1,0:T(8,128)S(1)}, f3...) custom-call(s32[2]{0:T(128)S(1)} %copy-done.27, ...), custom_call_target="tpu_custom_call" | custom-call | flops 131072000 | bytes 17039360 | tf_op jit(solution)/shard_map/mixer_forward/pallas_call | solution.py:225
  137.5 2.7 fusion.254
  145.4 25.6 %collective-permute-done.30 = bf16[256,2048]{1,0:T(8,128)(2,1)S(1)} collective-permute-done((bf16[256,2048]{1,0:T(8,128)(2,1)}, bf16[256,2048]{1,0:T(8,128)(2,1)S(1)}, u32[]{:S(2)}, u32[]{:S(2)}) %collective-permute-start.30) | collective-permute-done | bytes 1048608 | tf_op jit(solution)/shard_map/ppermute | solution.py:333
  172.5 21.0 %collective-permute-done.11 = bf16[256,2048]{1,0:T(8,128)(2,1)S(1)} collective-permute-done((bf16[256,2048]{1,0:T(8,128)(2,1)S(1)}, bf16[256,2048]{1,0:T(8,128)(2,1)S(1)}, u32[]{:S(2)}, u32[]{:S(2)}) %collective-permute-start.11) | collective-permute-done | bytes 1048608 | tf_op jit(solution)/shard_map/ppermute | solution.py:333
  194.1 21.9 %collective-permute-done.31 = bf16[256,2048]{1,0:T(8,128)(2,1)} collective-permute-done((bf16[256,2048]{1,0:T(8,128)(2,1)S(1)}, bf16[256,2048]{1,0:T(8,128)(2,1)}, u32[]{:S(2)}, u32[]{:S(2)}) %collective-permute-start.31) | collective-permute-done | bytes 1048608 | tf_op jit(solution)/shard_map/ppermute | solution.py:333
  218.6 19.8 %collective-permute-done.12 = bf16[256,2048]{1,0:T(8,128)(2,1)S(1)} collective-permute-done((bf16[256,2048]{1,0:T(8,128)(2,1)S(1)}, bf16[256,2048]{1,0:T(8,128)(2,1)S(1)}, u32[]{:S(2)}, u32[]{:S(2)}) %collective-permute-start.12) | collective-permute-done | bytes 1048608 | tf_op jit(solution)/shard_map/ppermute | solution.py:333
  240.0 2.5 constant_dynamic-update-slice_fusion.36
  244.1 16.9 %collective-permute-done.32 = bf16[256,2048]{1,0:T(8,128)(2,1)} collective-permute-done((bf16[256,2048]{1,0:T(8,128)(2,1)}, bf16[256,2048]{1,0:T(8,128)(2,1)}, u32[]{:S(2)}, u32[]{:S(2)}) %collective-permute-start.32) | collective-permute-done | bytes 1048608 | tf_op jit(solution)/shard_map/ppermute | solution.py:333
  261.0 22.0 %collective-permute-done.13 = bf16[256,2048]{1,0:T(8,128)(2,1)} collective-permute-done((bf16[256,2048]{1,0:T(8,128)(2,1)}, bf16[256,2048]{1,0:T(8,128)(2,1)}, u32[]{:S(2)}, u32[]{:S(2)}) %collective-permute-start.13) | collective-permute-done | bytes 1048608 | tf_op jit(solution)/shard_map/ppermute | solution.py:333
  283.0 2.9 multiply_reduce_fusion.2
  288.9 2.3 constant_dynamic-update-slice_fusion.33
  292.6 2.3 constant_dynamic-update-slice_fusion.31
  296.1 18.2 %collective-permute-done.16 = bf16[256,2048]{1,0:T(8,128)(2,1)} collective-permute-done((bf16[256,2048]{1,0:T(8,128)(2,1)S(1)}, bf16[256,2048]{1,0:T(8,128)(2,1)}, u32[]{:S(2)}, u32[]{:S(2)}) %collective-permute-start.16) | collective-permute-done | bytes 1048608 | tf_op jit(solution)/shard_map/ppermute | solution.py:333
  316.8 2.8 constant_dynamic-update-slice_fusion.27
  319.6 5.6 fusion.134
  325.2 2.9 fusion.135
  328.2 6.3 multiply_convert_fusion.4
  340.0 6.0 fusion.203
  346.0 2.4 constant_dynamic-update-slice_fusion.26
  352.1 3.8 multiply_convert_fusion.1
  363.0 2.4 constant_dynamic-update-slice_fusion.25
  370.8 4.0 multiply_convert_fusion.2
  377.2 4.3 collective-permute-start.39
  381.6 9.5 %collective-permute-done.18 = bf16[256,2048]{1,0:T(8,128)(2,1)S(1)} collective-permute-done((bf16[256,2048]{1,0:T(8,128)(2,1)}, bf16[256,2048]{1,0:T(8,128)(2,1)S(1)}, u32[]{:S(2)}, u32[]{:S(2)}) %collective-permute-start.18) | collective-permute-done | bytes 1048608 | tf_op jit(solution)/shard_map/ppermute | solution.py:333
  391.1 3.8 fusion.201
  394.9 4.1 convolution_add_fusion.5
  400.4 13.1 %collective-permute-done.25 = bf16[256,2048]{1,0:T(8,128)(2,1)S(1)} collective-permute-done((bf16[256,2048]{1,0:T(8,128)(2,1)S(1)}, bf16[256,2048]{1,0:T(8,128)(2,1)S(1)}, u32[]{:S(2)}, u32[]{:S(2)}) %collective-permute-start.25) | collective-permute-done | bytes 1048608 | tf_op jit(solution)/shard_map/ppermute | solution.py:333
  419.4 4.0 multiply_convert_fusion.3
  426.0 10.0 %collective-permute-done.39 = bf16[256,2048]{1,0:T(8,128)(2,1)S(1)} collective-permute-done((bf16[256,2048]{1,0:T(8,128)(2,1)S(1)}, bf16[256,2048]{1,0:T(8,128)(2,1)S(1)}, u32[]{:S(2)}, u32[]{:S(2)}) %collective-permute-start.39) | collective-permute-done | bytes 1048608 | tf_op jit(solution)/shard_map/ppermute | solution.py:333
  440.6 5.1 convolution_add_fusion.7
  447.0 11.5 %collective-permute-done.26 = bf16[256,2048]{1,0:T(8,128)(2,1)S(1)} collective-permute-done((bf16[256,2048]{1,0:T(8,128)(2,1)S(1)}, bf16[256,2048]{1,0:T(8,128)(2,1)S(1)}, u32[]{:S(2)}, u32[]{:S(2)}) %collective-permute-start.26) | collective-permute-done | bytes 1048608 | tf_op jit(solution)/shard_map/ppermute | solution.py:333
  460.2 20.8 %collective-permute-done.40 = bf16[256,2048]{1,0:T(8,128)(2,1)S(1)} collective-permute-done((bf16[256,2048]{1,0:T(8,128)(2,1)S(1)}, bf16[256,2048]{1,0:T(8,128)(2,1)S(1)}, u32[]{:S(2)}, u32[]{:S(2)}) %collective-permute-start.40) | collective-permute-done | bytes 1048608 | tf_op jit(solution)/shard_map/ppermute | solution.py:333
  482.5 8.5 %convolution_convert_fusion = bf16[768,2048]{1,0:T(8,128)(2,1)} fusion(bf16[2048,2048]{1,0:T(8,128)(2,1)S(1)} %bitcast.290, bf16[512,768]{1,0:T(8,128)(2,1)S(1)} %copy-done.123, bf16[512,768]{1,0:T(8,128)(2,1)S(1)} %copy-done.121, bf16[512,768]{1,0:T(8,128)(2,1)S(1)} %get-tuple-element.79, bf16[512,768]{1,0:T(8,128)(2,1)S(1)} %get-tuple-element.76), kind=kOutput, calls=%fused_computation.2 | convolution fusion | flops 6456606720 | bytes 14680064 | tf_op jit(solution)/shard_map/dot_general | solution.py:385
  491.1 34.0 %collective-permute-done.41 = bf16[256,2048]{1,0:T(8,128)(2,1)} collective-permute-done((bf16[256,2048]{1,0:T(8,128)(2,1)}, bf16[256,2048]{1,0:T(8,128)(2,1)}, u32[]{:S(2)}, u32[]{:S(2)}) %collective-permute-start.41) | collective-permute-done | bytes 1048608 | tf_op jit(solution)/shard_map/ppermute | solution.py:333
  525.1 3.9 multiply_reduce_fusion
  529.0 6.0 fusion.88
  539.0 23.6 %collective-permute-done.43 = bf16[256,2048]{1,0:T(8,128)(2,1)S(1)} collective-permute-done((bf16[256,2048]{1,0:T(8,128)(2,1)S(1)}, bf16[256,2048]{1,0:T(8,128)(2,1)S(1)}, u32[]{:S(2)}, u32[]{:S(2)}) %collective-permute-start.43) | collective-permute-done | bytes 1048608 | tf_op jit(solution)/shard_map/ppermute | solution.py:333
  565.7 22.1 %collective-permute-done.45 = bf16[256,2048]{1,0:T(8,128)(2,1)S(1)} collective-permute-done((bf16[256,2048]{1,0:T(8,128)(2,1)S(1)}, bf16[256,2048]{1,0:T(8,128)(2,1)S(1)}, u32[]{:S(2)}, u32[]{:S(2)}) %collective-permute-start.45) | collective-permute-done | bytes 1048608 | tf_op jit(solution)/shard_map/ppermute | solution.py:333
  590.2 21.9 %collective-permute-done.47 = bf16[256,2048]{1,0:T(8,128)(2,1)S(1)} collective-permute-done((bf16[256,2048]{1,0:T(8,128)(2,1)S(1)}, bf16[256,2048]{1,0:T(8,128)(2,1)S(1)}, u32[]{:S(2)}, u32[]{:S(2)}) %collective-permute-start.47) | collective-permute-done | bytes 1048608 | tf_op jit(solution)/shard_map/ppermute | solution.py:333
  616.4 4.0 convolution_convert_fusion.3
  620.7 3.4 fusion.80
  628.9 23.2 %mixer_backward.1 = (bf16[4,2,2,128,320]{4,3,2,1,0:T(8,128)(2,1)S(1)}, bf16[4,2,2,128,320]{4,3,2,1,0:T(8,128)(2,1)S(1)}, f32[8,320]{1,0:T(8,128)S(1)}, f32[320,640]{1,0:T(8,128)S(1)}) custom-call(s32[2]{0:T(128)S(1)} %copy-done.28, s32[2]{0:T(128)S(1)} %copy-done.26, f32[4,2,2,2,128,320]{5,4,3,2,1,0:T(8,128)} %copy-done, ...), custom_call_target="tpu_custom_call" | custom-call | flops 196608000 | bytes 20971520 | tf_op jit(solution)/shard_map/mixer_backward/pallas_call | solution.py:275
  652.1 3.1 fusion.28
  655.2 3.1 fusion.27
  661.7 9.4 %fusion.24 = bf16[1,2048,768]{2,1,0:T(8,128)(2,1)S(1)} fusion(bf16[2048,2048]{1,0:T(8,128)(2,1)} %get-tuple-element.100, bf16[512,768]{1,0:T(8,128)(2,1)S(1)} %copy-done.111, bf16[512,768]{1,0:T(8,128)(2,1)S(1)} %copy-done.109, bf16[512,768]{1,0:T(8,128)(2,1)S(1)} %copy-done.107, bf16[512,768]{1,0:T(8,128)(2,1)S(1)} %copy-done.105), kind=kOutput, calls=%fused_computation.38 | convolution fusion | flops 6456606720 | bytes 14680064 | tf_op jit(solution)/shard_map/dot_general | solution.py:385
  671.2 9.5 %fusion.21 = bf16[1,2048,768]{2,1,0:T(8,128)(2,1)S(1)} fusion(bf16[2048,2048]{1,0:T(8,128)(2,1)} %get-tuple-element.100, bf16[512,768]{1,0:T(8,128)(2,1)S(1)} %copy-done.119, bf16[512,768]{1,0:T(8,128)(2,1)S(1)} %copy-done.117, bf16[512,768]{1,0:T(8,128)(2,1)S(1)} %copy-done.115, bf16[512,768]{1,0:T(8,128)(2,1)S(1)} %copy-done.113), kind=kOutput, calls=%fused_computation.37 | convolution fusion | flops 6456606720 | bytes 14680064 | tf_op jit(solution)/shard_map/dot_general | solution.py:385
  680.7 3.2 pad_maximum_fusion.1
  697.3 24.1 %collective-permute-done.53 = bf16[256,2048]{1,0:T(8,128)(2,1)S(1)} collective-permute-done((bf16[256,2048]{1,0:T(8,128)(2,1)S(1)}, bf16[256,2048]{1,0:T(8,128)(2,1)S(1)}, u32[]{:S(2)}, u32[]{:S(2)}) %collective-permute-start.53) | collective-permute-done | bytes 1048608 | tf_op jit(solution)/shard_map/ppermute | solution.py:333
  725.8 22.7 %collective-permute-done.54 = bf16[256,2048]{1,0:T(8,128)(2,1)S(1)} collective-permute-done((bf16[256,2048]{1,0:T(8,128)(2,1)S(1)}, bf16[256,2048]{1,0:T(8,128)(2,1)S(1)}, u32[]{:S(2)}, u32[]{:S(2)}) %collective-permute-start.54) | collective-permute-done | bytes 1048608 | tf_op jit(solution)/shard_map/ppermute | solution.py:333
  750.6 2.7 convert_element_type.311
  753.3 17.8 %psum.36 = f32[8,320]{1,0:T(8,128)S(1)} all-reduce(f32[8,320]{1,0:T(8,128)S(1)} %get-tuple-element.37), channel_id=1, replica_groups=mesh['wide'=8,'narrow'=4] {'narrow'}, use_global_device_ids=true, to_apply=%region_7.8 | all-reduce | flops 2560 | bytes 20480 | tf_op jit(solution)/shard_map/psum | solution.py:487
  776.6 3.3 fusion.100
  779.9 39.4 %all-reduce.4 = (f32[2048]{0:T(1024)}, f32[2048]{0:T(1024)}) all-reduce(f32[2048]{0:T(1024)S(1)} %get-tuple-element.58, f32[2048]{0:T(1024)S(1)} %get-tuple-element.56), channel_id=1, replica_groups=mesh['wide'=8,'narrow'=4] {'wide','narrow'}, use_global_device_ids=true, to_apply=%region_5.6 | all-reduce | flops 4096 | bytes 32768 | tf_op jit(solution)/shard_map/psum | solution.py:498
  819.3 4.2 fusion.99
  823.5 2.3 convert_element_type.306
  825.8 3.3 convert_element_type.309
  (514 shorter events, 148.2 us)
Async XLA Ops:
  7.2 88.3 %all-gather.5.cloned.1.call-start = ((), (), s32[]{:S(2)}) async-start(), calls=%async_computation.4 | async-start | bytes 3276800 | tf_op jit(solution)/shard_map/all_gather | solution.py:319
  7.9 129.5 %all-gather.7.cloned.1.call-start = ((), (), s32[]{:S(2)}) async-start(), calls=%async_computation.5 | async-start | bytes 1638400 | tf_op jit(solution)/shard_map/all_gather | solution.py:319
  8.7 310.9 %all-gather.9.cloned.1.call-start = ((), (), s32[]{:S(2)}) async-start(), calls=%async_computation.6 | async-start | bytes 7864320 | tf_op jit(solution)/shard_map/all_gather | solution.py:319
  12.8 28.4 %collective-permute-start.1 = (bf16[256,2048]{1,0:T(8,128)(2,1)}, bf16[256,2048]{1,0:T(8,128)(2,1)S(1)}, u32[]{:S(2)}, u32[]{:S(2)}) collective-permute-start(bf16[256,2048]{1,0:T(8,128)(2,1)} %get-tuple-element.121), channel_id=1, source_target_pairs={{0,8},{4,12},{8,16},{12,20},{16,24},{20,28},{24,0},{28,4},{1,9},{5... | collective-permute-start | bytes 3145736 | tf_op jit(solution)/shard_map/ppermute | solution.py:333
  41.2 26.1 %collective-permute-start.3 = (bf16[256,2048]{1,0:T(8,128)(2,1)S(1)}, bf16[256,2048]{1,0:T(8,128)(2,1)S(1)}, u32[]{:S(2)}, u32[]{:S(2)}) collective-permute-start(bf16[256,2048]{1,0:T(8,128)(2,1)S(1)} %collective-permute-done.1), channel_id=1, source_target_pairs={{0,8},{4,12},{8,16},{12,20},{16,24},{20,28},{24,0},{28,4},{1,9},{5... | collective-permute-start | bytes 3145736 | tf_op jit(solution)/shard_map/ppermute | solution.py:333
  41.2 31.3 %collective-permute-start = (bf16[256,2048]{1,0:T(8,128)(2,1)}, bf16[256,2048]{1,0:T(8,128)(2,1)}, u32[]{:S(2)}, u32[]{:S(2)}) collective-permute-start(bf16[256,2048]{1,0:T(8,128)(2,1)} %get-tuple-element.121), channel_id=1, source_target_pairs={{0,4},{4,0},{8,12},{12,8},{16,20},{20,16},{24,28},{28,24},{1,5},{5... | collective-permute-start | bytes 3145736 | tf_op jit(solution)/shard_map/ppermute | solution.py:329
  41.2 287.0 %all-gather.11.cloned.1.call-start = ((), (), s32[]{:S(2)}) async-start(), calls=%async_computation.7 | async-start | bytes 3932160 | tf_op jit(solution)/shard_map/all_gather | solution.py:319
  41.3 34.4 %collective-permute-start.2 = (bf16[256,2048]{1,0:T(8,128)(2,1)S(1)}, bf16[256,2048]{1,0:T(8,128)(2,1)S(1)}, u32[]{:S(2)}, u32[]{:S(2)}) collective-permute-start(bf16[256,2048]{1,0:T(8,128)(2,1)S(1)} %collective-permute-done.1), channel_id=1, source_target_pairs={{0,4},{4,0},{8,12},{12,8},{16,20},{20,16},{24,28},{28,24},{1,5},{5... | collective-permute-start | bytes 3145736 | tf_op jit(solution)/shard_map/ppermute | solution.py:329
  67.3 25.3 %collective-permute-start.5 = (bf16[256,2048]{1,0:T(8,128)(2,1)S(1)}, bf16[256,2048]{1,0:T(8,128)(2,1)}, u32[]{:S(2)}, u32[]{:S(2)}) collective-permute-start(bf16[256,2048]{1,0:T(8,128)(2,1)S(1)} %collective-permute-done.3), channel_id=1, source_target_pairs={{0,8},{4,12},{8,16},{12,20},{16,24},{20,28},{24,0},{28,4},{1,9},{5... | collective-permute-start | bytes 3145736 | tf_op jit(solution)/shard_map/ppermute | solution.py:333
  67.3 25.3 %collective-permute-start.4 = (bf16[256,2048]{1,0:T(8,128)(2,1)S(1)}, bf16[256,2048]{1,0:T(8,128)(2,1)}, u32[]{:S(2)}, u32[]{:S(2)}) collective-permute-start(bf16[256,2048]{1,0:T(8,128)(2,1)S(1)} %collective-permute-done.3), channel_id=1, source_target_pairs={{0,4},{4,0},{8,12},{12,8},{16,20},{20,16},{24,28},{28,24},{1,5},{5... | collective-permute-start | bytes 3145736 | tf_op jit(solution)/shard_map/ppermute | solution.py:329
  92.7 14.6 %collective-permute-start.6 = (bf16[256,2048]{1,0:T(8,128)(2,1)}, bf16[256,2048]{1,0:T(8,128)(2,1)S(1)}, u32[]{:S(2)}, u32[]{:S(2)}) collective-permute-start(bf16[256,2048]{1,0:T(8,128)(2,1)} %collective-permute-done.5), channel_id=1, source_target_pairs={{0,4},{4,0},{8,12},{12,8},{16,20},{20,16},{24,28},{28,24},{1,5},{5... | collective-permute-start | bytes 3145736 | tf_op jit(solution)/shard_map/ppermute | solution.py:329
  140.4 4.6 collective-permute-start.10
  143.0 28.0 %collective-permute-start.30 = (bf16[256,2048]{1,0:T(8,128)(2,1)}, bf16[256,2048]{1,0:T(8,128)(2,1)S(1)}, u32[]{:S(2)}, u32[]{:S(2)}) collective-permute-start(bf16[256,2048]{1,0:T(8,128)(2,1)} %get-tuple-element.123), channel_id=1, source_target_pairs={{0,8},{4,12},{8,16},{12,20},{16,24},{20,28},{24,0},{28,4},{1,9},{5... | collective-permute-start | bytes 3145736 | tf_op jit(solution)/shard_map/ppermute | solution.py:333
  144.5 28.0 %collective-permute-start.9 = (bf16[256,2048]{1,0:T(8,128)(2,1)S(1)}, bf16[256,2048]{1,0:T(8,128)(2,1)S(1)}, u32[]{:S(2)}, u32[]{:S(2)}) collective-permute-start(bf16[256,2048]{1,0:T(8,128)(2,1)S(1)} %split.287), channel_id=1, source_target_pairs={{0,4},{4,0},{8,12},{12,8},{16,20},{20,16},{24,28},{28,24},{1,5},{5... | collective-permute-start | bytes 3145736 | tf_op jit(solution)/shard_map/ppermute | solution.py:329
  145.3 48.2 %collective-permute-start.11 = (bf16[256,2048]{1,0:T(8,128)(2,1)S(1)}, bf16[256,2048]{1,0:T(8,128)(2,1)S(1)}, u32[]{:S(2)}, u32[]{:S(2)}) collective-permute-start(bf16[256,2048]{1,0:T(8,128)(2,1)S(1)} %fusion.49), channel_id=1, source_target_pairs={{0,8},{4,12},{8,16},{12,20},{16,24},{20,28},{24,0},{28,4},{1,9},{5... | collective-permute-start | bytes 3145736 | tf_op jit(solution)/shard_map/ppermute | solution.py:333
  171.0 45.0 %collective-permute-start.31 = (bf16[256,2048]{1,0:T(8,128)(2,1)S(1)}, bf16[256,2048]{1,0:T(8,128)(2,1)}, u32[]{:S(2)}, u32[]{:S(2)}) collective-permute-start(bf16[256,2048]{1,0:T(8,128)(2,1)S(1)} %collective-permute-done.30), channel_id=1, source_target_pairs={{0,8},{4,12},{8,16},{12,20},{16,24},{20,28},{24,0},{28,4},{1,9},{5... | collective-permute-start | bytes 3145736 | tf_op jit(solution)/shard_map/ppermute | solution.py:333
  172.4 46.1 %collective-permute-start.8 = (bf16[256,2048]{1,0:T(8,128)(2,1)S(1)}, bf16[256,2048]{1,0:T(8,128)(2,1)S(1)}, u32[]{:S(2)}, u32[]{:S(2)}) collective-permute-start(bf16[256,2048]{1,0:T(8,128)(2,1)S(1)} %split.288), channel_id=1, source_target_pairs={{0,4},{4,0},{8,12},{12,8},{16,20},{20,16},{24,28},{28,24},{1,5},{5... | collective-permute-start | bytes 3145736 | tf_op jit(solution)/shard_map/ppermute | solution.py:329
  194.0 44.4 %collective-permute-start.12 = (bf16[256,2048]{1,0:T(8,128)(2,1)S(1)}, bf16[256,2048]{1,0:T(8,128)(2,1)S(1)}, u32[]{:S(2)}, u32[]{:S(2)}) collective-permute-start(bf16[256,2048]{1,0:T(8,128)(2,1)S(1)} %fusion.51), channel_id=1, source_target_pairs={{0,8},{4,12},{8,16},{12,20},{16,24},{20,28},{24,0},{28,4},{1,9},{5... | collective-permute-start | bytes 3145736 | tf_op jit(solution)/shard_map/ppermute | solution.py:333
  194.0 46.0 %collective-permute-start.28 = (bf16[256,2048]{1,0:T(8,128)(2,1)}, bf16[256,2048]{1,0:T(8,128)(2,1)}, u32[]{:S(2)}, u32[]{:S(2)}) collective-permute-start(bf16[256,2048]{1,0:T(8,128)(2,1)} %get-tuple-element.123), channel_id=1, source_target_pairs={{0,4},{4,0},{8,12},{12,8},{16,20},{20,16},{24,28},{28,24},{1,5},{5... | collective-permute-start | bytes 3145736 | tf_op jit(solution)/shard_map/ppermute | solution.py:329
  216.0 44.9 %collective-permute-start.32 = (bf16[256,2048]{1,0:T(8,128)(2,1)}, bf16[256,2048]{1,0:T(8,128)(2,1)}, u32[]{:S(2)}, u32[]{:S(2)}) collective-permute-start(bf16[256,2048]{1,0:T(8,128)(2,1)} %collective-permute-done.31), channel_id=1, source_target_pairs={{0,8},{4,12},{8,16},{12,20},{16,24},{20,28},{24,0},{28,4},{1,9},{5... | collective-permute-start | bytes 3145736 | tf_op jit(solution)/shard_map/ppermute | solution.py:333
  218.5 42.4 %collective-permute-start.7 = (bf16[256,2048]{1,0:T(8,128)(2,1)}, bf16[256,2048]{1,0:T(8,128)(2,1)}, u32[]{:S(2)}, u32[]{:S(2)}) collective-permute-start(bf16[256,2048]{1,0:T(8,128)(2,1)} %split.289), channel_id=1, source_target_pairs={{0,4},{4,0},{8,12},{12,8},{16,20},{20,16},{24,28},{28,24},{1,5},{5... | collective-permute-start | bytes 3145736 | tf_op jit(solution)/shard_map/ppermute | solution.py:329
  239.9 43.2 %collective-permute-start.13 = (bf16[256,2048]{1,0:T(8,128)(2,1)}, bf16[256,2048]{1,0:T(8,128)(2,1)}, u32[]{:S(2)}, u32[]{:S(2)}) collective-permute-start(bf16[256,2048]{1,0:T(8,128)(2,1)} %fusion.53), channel_id=1, source_target_pairs={{0,8},{4,12},{8,16},{12,20},{16,24},{20,28},{24,0},{28,4},{1,9},{5... | collective-permute-start | bytes 3145736 | tf_op jit(solution)/shard_map/ppermute | solution.py:333
  239.9 510.7 %reduce-scatter.11.cloned.1.call-start = ((), (), s32[]{:S(2)}) async-start(), calls=%async_computation.11 | async-start | bytes 3932160 | tf_op jit(solution)/shard_map/reduce_scatter | solution.py:323
  239.9 47.8 %collective-permute-start.37 = (bf16[256,2048]{1,0:T(8,128)(2,1)}, bf16[256,2048]{1,0:T(8,128)(2,1)S(1)}, u32[]{:S(2)}, u32[]{:S(2)}) collective-permute-start(bf16[256,2048]{1,0:T(8,128)(2,1)} %copy-done.64), channel_id=1, source_target_pairs={{0,4},{4,0},{8,12},{12,8},{16,20},{20,16},{24,28},{28,24},{1,5},{5... | collective-permute-start | bytes 3145736 | tf_op jit(solution)/shard_map/ppermute | solution.py:329
  243.6 47.6 %collective-permute-start.35 = (bf16[256,2048]{1,0:T(8,128)(2,1)}, bf16[256,2048]{1,0:T(8,128)(2,1)S(1)}, u32[]{:S(2)}, u32[]{:S(2)}) collective-permute-start(bf16[256,2048]{1,0:T(8,128)(2,1)} %collective-permute-done.31), channel_id=1, source_target_pairs={{0,4},{4,0},{8,12},{12,8},{16,20},{20,16},{24,28},{28,24},{1,5},{5... | collective-permute-start | bytes 3145736 | tf_op jit(solution)/shard_map/ppermute | solution.py:329
  261.0 33.9 %collective-permute-start.33 = (bf16[256,2048]{1,0:T(8,128)(2,1)}, bf16[256,2048]{1,0:T(8,128)(2,1)S(1)}, u32[]{:S(2)}, u32[]{:S(2)}) collective-permute-start(bf16[256,2048]{1,0:T(8,128)(2,1)} %collective-permute-done.32), channel_id=1, source_target_pairs={{0,4},{4,0},{8,12},{12,8},{16,20},{20,16},{24,28},{28,24},{1,5},{5... | collective-permute-start | bytes 3145736 | tf_op jit(solution)/shard_map/ppermute | solution.py:329
  287.7 26.7 %collective-permute-start.16 = (bf16[256,2048]{1,0:T(8,128)(2,1)S(1)}, bf16[256,2048]{1,0:T(8,128)(2,1)}, u32[]{:S(2)}, u32[]{:S(2)}) collective-permute-start(bf16[256,2048]{1,0:T(8,128)(2,1)S(1)} %get-tuple-element.69), channel_id=1, source_target_pairs={{0,8},{4,12},{8,16},{12,20},{16,24},{20,28},{24,0},{28,4},{1,9},{5... | collective-permute-start | bytes 3145736 | tf_op jit(solution)/shard_map/ppermute | solution.py:333
  287.7 27.1 %collective-permute-start.14 = (bf16[256,2048]{1,0:T(8,128)(2,1)S(1)}, bf16[256,2048]{1,0:T(8,128)(2,1)S(1)}, u32[]{:S(2)}, u32[]{:S(2)}) collective-permute-start(bf16[256,2048]{1,0:T(8,128)(2,1)S(1)} %get-tuple-element.69), channel_id=1, source_target_pairs={{0,4},{4,0},{8,12},{12,8},{16,20},{20,16},{24,28},{28,24},{1,5},{5... | collective-permute-start | bytes 3145736 | tf_op jit(solution)/shard_map/ppermute | solution.py:329
  314.3 31.6 %collective-permute-start.23 = (bf16[256,2048]{1,0:T(8,128)(2,1)}, bf16[256,2048]{1,0:T(8,128)(2,1)}, u32[]{:S(2)}, u32[]{:S(2)}) collective-permute-start(bf16[256,2048]{1,0:T(8,128)(2,1)} %collective-permute-done.16), channel_id=1, source_target_pairs={{0,4},{4,0},{8,12},{12,8},{16,20},{20,16},{24,28},{28,24},{1,5},{5... | collective-permute-start | bytes 3145736 | tf_op jit(solution)/shard_map/ppermute | solution.py:329
  314.3 44.3 %collective-permute-start.17 = (bf16[256,2048]{1,0:T(8,128)(2,1)}, bf16[256,2048]{1,0:T(8,128)(2,1)}, u32[]{:S(2)}, u32[]{:S(2)}) collective-permute-start(bf16[256,2048]{1,0:T(8,128)(2,1)} %collective-permute-done.16), channel_id=1, source_target_pairs={{0,8},{4,12},{8,16},{12,20},{16,24},{20,28},{24,0},{28,4},{1,9},{5... | collective-permute-start | bytes 3145736 | tf_op jit(solution)/shard_map/ppermute | solution.py:333
  339.4 189.6 %collective-permute-start.15 = (bf16[256,2048]{1,0:T(8,128)(2,1)}, bf16[256,2048]{1,0:T(8,128)(2,1)}, u32[]{:S(2)}, u32[]{:S(2)}) collective-permute-start(bf16[256,2048]{1,0:T(8,128)(2,1)} %split.285), channel_id=1, source_target_pairs={{0,4},{4,0},{8,12},{12,8},{16,20},{20,16},{24,28},{28,24},{1,5},{5... | collective-permute-start | bytes 3145736 | tf_op jit(solution)/shard_map/ppermute | solution.py:329
  357.8 7.6 collective-permute-start.24
  358.6 7.3 collective-permute-start.21
  362.5 14.4 %collective-permute-start.38 = (bf16[256,2048]{1,0:T(8,128)(2,1)S(1)}, bf16[256,2048]{1,0:T(8,128)(2,1)S(1)}, u32[]{:S(2)}, u32[]{:S(2)}) collective-permute-start(bf16[256,2048]{1,0:T(8,128)(2,1)S(1)} %split.278), channel_id=1, source_target_pairs={{0,4},{4,0},{8,12},{12,8},{16,20},{20,16},{24,28},{28,24},{1,5},{5... | collective-permute-start | bytes 3145736 | tf_op jit(solution)/shard_map/ppermute | solution.py:329
  363.0 28.0 %collective-permute-start.18 = (bf16[256,2048]{1,0:T(8,128)(2,1)}, bf16[256,2048]{1,0:T(8,128)(2,1)S(1)}, u32[]{:S(2)}, u32[]{:S(2)}) collective-permute-start(bf16[256,2048]{1,0:T(8,128)(2,1)} %collective-permute-done.17), channel_id=1, source_target_pairs={{0,8},{4,12},{8,16},{12,20},{16,24},{20,28},{24,0},{28,4},{1,9},{5... | collective-permute-start | bytes 3145736 | tf_op jit(solution)/shard_map/ppermute | solution.py:333
  365.7 47.8 %collective-permute-start.25 = (bf16[256,2048]{1,0:T(8,128)(2,1)S(1)}, bf16[256,2048]{1,0:T(8,128)(2,1)S(1)}, u32[]{:S(2)}, u32[]{:S(2)}) collective-permute-start(bf16[256,2048]{1,0:T(8,128)(2,1)S(1)} %fusion.41), channel_id=1, source_target_pairs={{0,8},{4,12},{8,16},{12,20},{16,24},{20,28},{24,0},{28,4},{1,9},{5... | collective-permute-start | bytes 3145736 | tf_op jit(solution)/shard_map/ppermute | solution.py:333
  376.8 36.7 %collective-permute-start.22 = (bf16[256,2048]{1,0:T(8,128)(2,1)S(1)}, bf16[256,2048]{1,0:T(8,128)(2,1)S(1)}, u32[]{:S(2)}, u32[]{:S(2)}) collective-permute-start(bf16[256,2048]{1,0:T(8,128)(2,1)S(1)} %split.283), channel_id=1, source_target_pairs={{0,4},{4,0},{8,12},{12,8},{16,20},{20,16},{24,28},{28,24},{1,5},{5... | collective-permute-start | bytes 3145736 | tf_op jit(solution)/shard_map/ppermute | solution.py:329
  377.2 58.7 %collective-permute-start.39 = (bf16[256,2048]{1,0:T(8,128)(2,1)S(1)}, bf16[256,2048]{1,0:T(8,128)(2,1)S(1)}, u32[]{:S(2)}, u32[]{:S(2)}) collective-permute-start(bf16[256,2048]{1,0:T(8,128)(2,1)S(1)} %fusion.35), channel_id=1, source_target_pairs={{0,8},{4,12},{8,16},{12,20},{16,24},{20,28},{24,0},{28,4},{1,9},{5... | collective-permute-start | bytes 3145736 | tf_op jit(solution)/shard_map/ppermute | solution.py:333
  391.1 23.5 %collective-permute-start.19 = (bf16[256,2048]{1,0:T(8,128)(2,1)S(1)}, bf16[256,2048]{1,0:T(8,128)(2,1)S(1)}, u32[]{:S(2)}, u32[]{:S(2)}) collective-permute-start(bf16[256,2048]{1,0:T(8,128)(2,1)S(1)} %collective-permute-done.18), channel_id=1, source_target_pairs={{0,4},{4,0},{8,12},{12,8},{16,20},{20,16},{24,28},{28,24},{1,5},{5... | collective-permute-start | bytes 3145736 | tf_op jit(solution)/shard_map/ppermute | solution.py:329
  413.5 22.5 %collective-permute-start.36 = (bf16[256,2048]{1,0:T(8,128)(2,1)S(1)}, bf16[256,2048]{1,0:T(8,128)(2,1)S(1)}, u32[]{:S(2)}, u32[]{:S(2)}) collective-permute-start(bf16[256,2048]{1,0:T(8,128)(2,1)S(1)} %split.279), channel_id=1, source_target_pairs={{0,4},{4,0},{8,12},{12,8},{16,20},{20,16},{24,28},{28,24},{1,5},{5... | collective-permute-start | bytes 3145736 | tf_op jit(solution)/shard_map/ppermute | solution.py:329
  414.1 44.4 %collective-permute-start.26 = (bf16[256,2048]{1,0:T(8,128)(2,1)S(1)}, bf16[256,2048]{1,0:T(8,128)(2,1)S(1)}, u32[]{:S(2)}, u32[]{:S(2)}) collective-permute-start(bf16[256,2048]{1,0:T(8,128)(2,1)S(1)} %fusion.43), channel_id=1, source_target_pairs={{0,8},{4,12},{8,16},{12,20},{16,24},{20,28},{24,0},{28,4},{1,9},{5... | collective-permute-start | bytes 3145736 | tf_op jit(solution)/shard_map/ppermute | solution.py:333
  425.5 33.0 %collective-permute-start.20 = (bf16[256,2048]{1,0:T(8,128)(2,1)S(1)}, bf16[256,2048]{1,0:T(8,128)(2,1)S(1)}, u32[]{:S(2)}, u32[]{:S(2)}) collective-permute-start(bf16[256,2048]{1,0:T(8,128)(2,1)S(1)} %split.284), channel_id=1, source_target_pairs={{0,4},{4,0},{8,12},{12,8},{16,20},{20,16},{24,28},{28,24},{1,5},{5... | collective-permute-start | bytes 3145736 | tf_op jit(solution)/shard_map/ppermute | solution.py:329
  436.5 44.4 %collective-permute-start.40 = (bf16[256,2048]{1,0:T(8,128)(2,1)S(1)}, bf16[256,2048]{1,0:T(8,128)(2,1)S(1)}, u32[]{:S(2)}, u32[]{:S(2)}) collective-permute-start(bf16[256,2048]{1,0:T(8,128)(2,1)S(1)} %fusion.37), channel_id=1, source_target_pairs={{0,8},{4,12},{8,16},{12,20},{16,24},{20,28},{24,0},{28,4},{1,9},{5... | collective-permute-start | bytes 3145736 | tf_op jit(solution)/shard_map/ppermute | solution.py:333
  440.5 40.5 %collective-permute-start.34 = (bf16[256,2048]{1,0:T(8,128)(2,1)S(1)}, bf16[256,2048]{1,0:T(8,128)(2,1)S(1)}, u32[]{:S(2)}, u32[]{:S(2)}) collective-permute-start(bf16[256,2048]{1,0:T(8,128)(2,1)S(1)} %split.280), channel_id=1, source_target_pairs={{0,4},{4,0},{8,12},{12,8},{16,20},{20,16},{24,28},{28,24},{1,5},{5... | collective-permute-start | bytes 3145736 | tf_op jit(solution)/shard_map/ppermute | solution.py:329
  458.5 32.6 %collective-permute-start.29 = (bf16[256,2048]{1,0:T(8,128)(2,1)}, bf16[256,2048]{1,0:T(8,128)(2,1)}, u32[]{:S(2)}, u32[]{:S(2)}) collective-permute-start(bf16[256,2048]{1,0:T(8,128)(2,1)} %split.281), channel_id=1, source_target_pairs={{0,4},{4,0},{8,12},{12,8},{16,20},{20,16},{24,28},{28,24},{1,5},{5... | collective-permute-start | bytes 3145736 | tf_op jit(solution)/shard_map/ppermute | solution.py:329
  460.0 69.0 %collective-permute-start.27 = (bf16[256,2048]{1,0:T(8,128)(2,1)}, bf16[256,2048]{1,0:T(8,128)(2,1)}, u32[]{:S(2)}, u32[]{:S(2)}) collective-permute-start(bf16[256,2048]{1,0:T(8,128)(2,1)} %fusion.45), channel_id=1, source_target_pairs={{0,8},{4,12},{8,16},{12,20},{16,24},{20,28},{24,0},{28,4},{1,9},{5... | collective-permute-start | bytes 3145736 | tf_op jit(solution)/shard_map/ppermute | solution.py:333
  482.4 42.7 %collective-permute-start.41 = (bf16[256,2048]{1,0:T(8,128)(2,1)}, bf16[256,2048]{1,0:T(8,128)(2,1)}, u32[]{:S(2)}, u32[]{:S(2)}) collective-permute-start(bf16[256,2048]{1,0:T(8,128)(2,1)} %fusion.39), channel_id=1, source_target_pairs={{0,8},{4,12},{8,16},{12,20},{16,24},{20,28},{24,0},{28,4},{1,9},{5... | collective-permute-start | bytes 3145736 | tf_op jit(solution)/shard_map/ppermute | solution.py:333
  491.0 283.7 %reduce-scatter.7.cloned.1.call-start = ((), (), s32[]{:S(2)}) async-start(), calls=%async_computation.9 | async-start | bytes 1638400 | tf_op jit(solution)/shard_map/reduce_scatter | solution.py:323
  536.4 26.1 %collective-permute-start.43 = (bf16[256,2048]{1,0:T(8,128)(2,1)S(1)}, bf16[256,2048]{1,0:T(8,128)(2,1)S(1)}, u32[]{:S(2)}, u32[]{:S(2)}) collective-permute-start(bf16[256,2048]{1,0:T(8,128)(2,1)S(1)} %get-tuple-element.71), channel_id=1, source_target_pairs={{0,8},{4,12},{8,16},{12,20},{16,24},{20,28},{24,0},{28,4},{1,9},{5... | collective-permute-start | bytes 3145736 | tf_op jit(solution)/shard_map/ppermute | solution.py:333
  538.9 48.9 %collective-permute-start.42 = (bf16[256,2048]{1,0:T(8,128)(2,1)S(1)}, bf16[256,2048]{1,0:T(8,128)(2,1)S(1)}, u32[]{:S(2)}, u32[]{:S(2)}) collective-permute-start(bf16[256,2048]{1,0:T(8,128)(2,1)S(1)} %get-tuple-element.71), channel_id=1, source_target_pairs={{0,4},{4,0},{8,12},{12,8},{16,20},{20,16},{24,28},{28,24},{1,5},{5... | collective-permute-start | bytes 3145736 | tf_op jit(solution)/shard_map/ppermute | solution.py:329
  562.5 25.2 %collective-permute-start.45 = (bf16[256,2048]{1,0:T(8,128)(2,1)S(1)}, bf16[256,2048]{1,0:T(8,128)(2,1)S(1)}, u32[]{:S(2)}, u32[]{:S(2)}) collective-permute-start(bf16[256,2048]{1,0:T(8,128)(2,1)S(1)} %collective-permute-done.43), channel_id=1, source_target_pairs={{0,8},{4,12},{8,16},{12,20},{16,24},{20,28},{24,0},{28,4},{1,9},{5... | collective-permute-start | bytes 3145736 | tf_op jit(solution)/shard_map/ppermute | solution.py:333
  565.5 24.6 %collective-permute-start.44 = (bf16[256,2048]{1,0:T(8,128)(2,1)S(1)}, bf16[256,2048]{1,0:T(8,128)(2,1)S(1)}, u32[]{:S(2)}, u32[]{:S(2)}) collective-permute-start(bf16[256,2048]{1,0:T(8,128)(2,1)S(1)} %collective-permute-done.43), channel_id=1, source_target_pairs={{0,4},{4,0},{8,12},{12,8},{16,20},{20,16},{24,28},{28,24},{1,5},{5... | collective-permute-start | bytes 3145736 | tf_op jit(solution)/shard_map/ppermute | solution.py:329
  587.8 24.3 %collective-permute-start.47 = (bf16[256,2048]{1,0:T(8,128)(2,1)S(1)}, bf16[256,2048]{1,0:T(8,128)(2,1)S(1)}, u32[]{:S(2)}, u32[]{:S(2)}) collective-permute-start(bf16[256,2048]{1,0:T(8,128)(2,1)S(1)} %collective-permute-done.45), channel_id=1, source_target_pairs={{0,8},{4,12},{8,16},{12,20},{16,24},{20,28},{24,0},{28,4},{1,9},{5... | collective-permute-start | bytes 3145736 | tf_op jit(solution)/shard_map/ppermute | solution.py:333
  590.0 24.3 %collective-permute-start.46 = (bf16[256,2048]{1,0:T(8,128)(2,1)S(1)}, bf16[256,2048]{1,0:T(8,128)(2,1)S(1)}, u32[]{:S(2)}, u32[]{:S(2)}) collective-permute-start(bf16[256,2048]{1,0:T(8,128)(2,1)S(1)} %collective-permute-done.45), channel_id=1, source_target_pairs={{0,4},{4,0},{8,12},{12,8},{16,20},{20,16},{24,28},{28,24},{1,5},{5... | collective-permute-start | bytes 3145736 | tf_op jit(solution)/shard_map/ppermute | solution.py:329
  620.4 203.1 %reduce-scatter.5.cloned.1.call-start = ((), (), s32[]{:S(2)}) async-start(), calls=%async_computation.8 | async-start | bytes 3276800 | tf_op jit(solution)/shard_map/reduce_scatter | solution.py:323
  660.1 165.7 %reduce-scatter.9.cloned.1.call-start = ((), (), s32[]{:S(2)}) async-start(), calls=%async_computation.10 | async-start | bytes 7864320 | tf_op jit(solution)/shard_map/reduce_scatter | solution.py:323
  683.9 145.2 %all-reduce.8.cloned.1.call-start = ((), (), s32[]{:S(2)}) async-start(), calls=%async_computation.12 | async-start | bytes 1310720 | tf_op jit(solution)/shard_map/psum | solution.py:487
  690.1 3.6 collective-permute-start.52
  693.6 3.7 collective-permute-start.51
  694.0 27.4 %collective-permute-start.53 = (bf16[256,2048]{1,0:T(8,128)(2,1)S(1)}, bf16[256,2048]{1,0:T(8,128)(2,1)S(1)}, u32[]{:S(2)}, u32[]{:S(2)}) collective-permute-start(bf16[256,2048]{1,0:T(8,128)(2,1)S(1)} %fusion.29), channel_id=1, source_target_pairs={{0,8},{4,12},{8,16},{12,20},{16,24},{20,28},{24,0},{28,4},{1,9},{5... | collective-permute-start | bytes 3145736 | tf_op jit(solution)/shard_map/ppermute | solution.py:333
  696.7 29.1 %collective-permute-start.50 = (bf16[256,2048]{1,0:T(8,128)(2,1)S(1)}, bf16[256,2048]{1,0:T(8,128)(2,1)S(1)}, u32[]{:S(2)}, u32[]{:S(2)}) collective-permute-start(bf16[256,2048]{1,0:T(8,128)(2,1)S(1)} %split.276), channel_id=1, source_target_pairs={{0,4},{4,0},{8,12},{12,8},{16,20},{20,16},{24,28},{28,24},{1,5},{5... | collective-permute-start | bytes 3145736 | tf_op jit(solution)/shard_map/ppermute | solution.py:329
  721.9 26.6 %collective-permute-start.54 = (bf16[256,2048]{1,0:T(8,128)(2,1)S(1)}, bf16[256,2048]{1,0:T(8,128)(2,1)S(1)}, u32[]{:S(2)}, u32[]{:S(2)}) collective-permute-start(bf16[256,2048]{1,0:T(8,128)(2,1)S(1)} %fusion.31), channel_id=1, source_target_pairs={{0,8},{4,12},{8,16},{12,20},{16,24},{20,28},{24,0},{28,4},{1,9},{5... | collective-permute-start | bytes 3145736 | tf_op jit(solution)/shard_map/ppermute | solution.py:333
  725.8 50.8 %collective-permute-start.49 = (bf16[256,2048]{1,0:T(8,128)(2,1)}, bf16[256,2048]{1,0:T(8,128)(2,1)}, u32[]{:S(2)}, u32[]{:S(2)}) collective-permute-start(bf16[256,2048]{1,0:T(8,128)(2,1)} %split.277), channel_id=1, source_target_pairs={{0,4},{4,0},{8,12},{12,8},{16,20},{20,16},{24,28},{28,24},{1,5},{5... | collective-permute-start | bytes 3145736 | tf_op jit(solution)/shard_map/ppermute | solution.py:329
  750.0 26.6 %collective-permute-start.55 = (bf16[256,2048]{1,0:T(8,128)(2,1)}, bf16[256,2048]{1,0:T(8,128)(2,1)}, u32[]{:S(2)}, u32[]{:S(2)}) collective-permute-start(bf16[256,2048]{1,0:T(8,128)(2,1)} %fusion.33), channel_id=1, source_target_pairs={{0,8},{4,12},{8,16},{12,20},{16,24},{20,28},{24,0},{28,4},{1,9},{5... | collective-permute-start | bytes 3145736 | tf_op jit(solution)/shard_map/ppermute | solution.py:333
  (133 other events, 1439.8 us)
Sparse Core Ops, SparseCore 0:
  9.9 42.2 all-gather.4
  53.9 28.6 all-gather.6
  84.5 70.1 all-gather.8
  240.0 44.8 all-gather.10
  491.1 44.9 reduce-scatter.10
  620.5 28.3 reduce-scatter.6
  660.2 38.9 reduce-scatter.4
  702.2 70.5 reduce-scatter.8
  776.4 47.4 all-reduce.7

commit v2 on v1

v2 whole, which is shorter than its diff:
```python
from functools import partial

import jax
import jax.numpy as jnp
from jax import lax
from jax.experimental import pallas as pl
from jax.experimental.pallas import tpu as pltpu
from jax.sharding import PartitionSpec as P

decay_scale = 8.0
norm_eps = 1e-06
gelu_in = 0.7978845608028654
gelu_cube = 0.044715
f32 = jnp.float32
bf16 = jnp.bfloat16
kernel_cost = pl.CostEstimate(flops=1, bytes_accessed=1, transcendentals=0)


def gelu_tanh(v):
    return jnp.tanh(gelu_in * (v + gelu_cube * v * v * v))


def gelu_pair(v):
    t = gelu_tanh(v)
    half = 0.5 * (1.0 + t)
    slope = half + 0.5 * v * (1.0 - t * t) * (gelu_in + (3.0 * gelu_in * gelu_cube) * v * v)
    return v * half, slope


def one_minus_exp(v, decay):
    series = 1.0 - v * (1.0 / 7.0)
    for order in (6.0, 5.0, 4.0, 3.0, 2.0):
        series = 1.0 - v * (1.0 / order) * series
    return jnp.where(v < 0.3, v * series, 1.0 - decay * decay)


def gate_tiles(channels, block_width, tile):
    tiles, offset = [], 0
    for start in range(0, channels, tile):
        stop = min(start + tile, channels)
        low = start // block_width * block_width // 128 * 128
        high = min(-(-((stop - 1) // block_width + 1) * block_width // 128) * 128, channels)
        tiles.append((start, stop, low, high, offset))
        offset += high - low
    return tiles


def split_rows(values):
    high = values.astype(bf16)
    return jnp.concatenate((high, (values - high.astype(f32)).astype(bf16)), axis=0)


def joined_dot(halves, weight):
    both = jnp.dot(halves, weight, preferred_element_type=f32)
    rows = both.shape[0] // 2
    return both[:rows] + both[rows:]


def tile_scan(decay, drive, backward):
    rows, channels = decay.shape
    a = decay.reshape(rows // 8, 8, channels)
    b = drive.reshape(rows // 8, 8, channels)
    row = lax.broadcasted_iota(jnp.int32, (1, 8, channels), 1)
    for step in (1, 2, 4):
        if backward:
            keep, shift = row < 8 - step, 8 - step
        else:
            keep, shift = row >= step, step
        a_moved = jnp.where(keep, pltpu.roll(a, shift, 1), 1.0)
        b_moved = jnp.where(keep, pltpu.roll(b, shift, 1), 0.0)
        b = b + a * b_moved
        a = a * a_moved
    return a, b


def mixer_forward_kernel(
    chips, block_width, place, lengths, *refs
):
    pre_refs, refs = refs[:chips], refs[chips:]
    conv_weight, conv_bias, gate_weight, gate_bias, rate_scale = refs[:5]
    mixed, conv_out, rate_out, in_out, states_out, final_state, conv_state = refs[5:12]
    pre_now, x_tail, carry = refs[12:]
    chunk = pl.program_id(0)
    seq_count, local_len, channels = pre_now.shape
    channels //= 2
    pick_block(chunk, place, chips, (pre_refs, pre_now))

    @pl.when(chunk == 0)
    def _():
        x_tail[...] = jnp.zeros_like(x_tail)
        carry[...] = jnp.zeros_like(carry)

    convs = []
    for seq in range(seq_count):
        x = pre_now[seq, :, channels:]
        extended = jnp.concatenate((x_tail[seq], x), axis=0)
        conv = conv_bias[...] + conv_weight[0:1] * x
        for lag in range(1, 4):
            conv = conv + conv_weight[lag : lag + 1] * extended[8 - lag : 8 - lag + local_len]
        x_tail[seq] = x[local_len - 8 :]
        convs.append(conv)
        for tap in range(3):
            position = lengths[seq] - 3 + tap

            @pl.when(position // local_len == chunk)
            def _(seq=seq, tap=tap, position=position):
                conv_state[seq, tap : tap + 1] = pre_now[
                    seq, pl.ds(lax.rem(position, local_len), 1), channels:
                ]

    conv_all = jnp.concatenate(convs, axis=0)
    parted = split_rows(conv_all)
    rate_parts, in_parts = [], []
    for start, stop, low, high, at in gate_tiles(channels, block_width, 128):
        both = joined_dot(parted[:, low:high], gate_weight[at : at + high - low])
        rate_parts.append(both[:, : stop - start])
        in_parts.append(both[:, 128 : 128 + stop - start])
    rate_all = jax.nn.sigmoid(jnp.concatenate(rate_parts, axis=1) + gate_bias[0:1])
    in_all = jax.nn.sigmoid(jnp.concatenate(in_parts, axis=1) + gate_bias[1:2])
    for seq in range(seq_count):
        rows = slice(seq * local_len, (seq + 1) * local_len)
        conv = convs[seq]
        rate_gate = rate_all[rows]
        in_gate = in_all[rows]
        step_log = rate_scale[...] * rate_gate
        decay = jnp.exp(-step_log)
        root = jnp.sqrt(one_minus_exp(2.0 * step_log, decay))
        position = chunk * local_len + lax.broadcasted_iota(jnp.int32, (local_len, 1), 0)
        live = position < lengths[seq]
        drive = jnp.where(live, root * in_gate * conv, 0.0)
        a, b = tile_scan(jnp.where(live, decay, 1.0), drive, False)
        last = carry[seq]
        gated, _ = gelu_pair(pre_now[seq, :, :channels])
        tiles = []
        for tile in range(local_len // 8):
            tiles.append(b[tile] + a[tile] * last)
            last = tiles[-1][7:8]
        states = jnp.concatenate(tiles, axis=0)
        states_out[0, 0, seq] = states
        mixed[0, 0, seq] = (gated * states).astype(bf16)
        carry[seq] = last
        final_state[seq : seq + 1] = last
        conv_out[0, 0, seq] = conv
        rate_out[0, 0, seq] = rate_gate
        in_out[0, 0, seq] = in_gate


def mixer_backward_kernel(
    chips, block_width, place, lengths, *refs
):
    pre_refs, back_refs, refs = refs[:chips], refs[chips : 2 * chips], refs[2 * chips :]
    conv_in, rate_in, in_in, states_in, conv_weight, gate_back, rate_scale = refs[:7]
    grads, sums, gate_sums = refs[7:10]
    pre_now, back_now, carry, grad_head = refs[10:]
    step = pl.program_id(0)
    chunk = pl.num_programs(0) - 1 - step
    seq_count, local_len, channels = back_now.shape
    pick_block(chunk, place, chips, (pre_refs, pre_now), (back_refs, back_now))

    @pl.when(step == 0)
    def _():
        carry[...] = jnp.zeros_like(carry)
        grad_head[...] = jnp.zeros_like(grad_head)
        sums[...] = jnp.zeros_like(sums)
        gate_sums[...] = jnp.zeros_like(gate_sums)

    rate_pre, in_pre, direct = [], [], []
    decay_sum = jnp.zeros((1, channels), f32)
    for seq in range(seq_count):
        position = chunk * local_len + lax.broadcasted_iota(jnp.int32, (local_len, 1), 0)
        live = position < lengths[seq]
        rate_gate = rate_in[0, 0, seq]
        in_gate = in_in[0, 0, seq]
        conv = conv_in[0, 0, seq]
        states = states_in[0, 0, seq]
        mixer_grad = back_now[seq]
        gated, slope = gelu_pair(pre_now[seq, :, :channels])
        step_log = rate_scale[...] * rate_gate
        decay_raw = jnp.exp(-step_log)
        decay = jnp.where(live, decay_raw, 1.0)
        grads[0, 0, seq, :, :channels] = (mixer_grad * states * slope).astype(bf16)
        source = mixer_grad * gated
        a, b = tile_scan(decay, decay * source, True)
        following = carry[seq]
        tiles = []
        for tile in reversed(range(local_len // 8)):
            passed = b[tile] + a[tile] * following
            tiles.append(jnp.concatenate((passed[1:], following), axis=0))
            following = passed[0:1]
        carry[seq] = following
        adjoint = source + jnp.concatenate(tiles[::-1], axis=0)
        adjoint = jnp.where(live, adjoint, 0.0)
        square = one_minus_exp(2.0 * step_log, decay_raw)
        inverse_root = lax.rsqrt(square)
        root = square * inverse_root
        gated_conv = in_gate * conv
        logd_grad = adjoint * (
            states - root * gated_conv - gated_conv * decay_raw * decay_raw * inverse_root
        )
        rate_part = logd_grad * rate_gate
        decay_sum = decay_sum + jnp.sum(rate_part, axis=0, keepdims=True)
        rate_pre.append(-rate_scale[...] * rate_part * (1.0 - rate_gate))
        through = adjoint * root
        in_pre.append(through * gated_conv * (1.0 - in_gate))
        direct.append(through * in_gate)
    rate_all = jnp.concatenate(rate_pre, axis=0)
    in_all = jnp.concatenate(in_pre, axis=0)
    conv_all = jnp.concatenate([conv_in[0, 0, seq] for seq in range(seq_count)], axis=0).astype(bf16)
    rate_b, in_b = rate_all.astype(bf16), in_all.astype(bf16)
    for start, stop, low, high, at in gate_tiles(channels, block_width, 128):
        both = jnp.concatenate((rate_b[:, start:stop], in_b[:, start:stop]), axis=1)
        part = lax.dot_general(
            conv_all[:, low:high], both, (((0,), (0,)), ((), ())), preferred_element_type=f32
        )
        if stop - start == 128:
            gate_sums[at : at + high - low] += part
        else:
            gate_sums[at : at + high - low, : stop - start] += part[:, : stop - start]
            gate_sums[at : at + high - low, 128 : 128 + stop - start] += part[:, stop - start :]
    rate_parted, in_parted = split_rows(rate_all), split_rows(in_all)
    parts = []
    for start, stop, low, high, at in gate_tiles(channels, block_width, 256):
        both = jnp.concatenate((rate_parted[:, low:high], in_parted[:, low:high]), axis=1)
        part = joined_dot(both, gate_back[2 * at : 2 * (at + high - low)])
        parts.append(part[:, : stop - start])
    conv_grad = jnp.concatenate(direct, axis=0) + jnp.concatenate(parts, axis=1)
    tap_sums = [jnp.zeros((1, channels), f32) for _ in range(4)]
    for seq in range(seq_count):
        part = conv_grad[seq * local_len : (seq + 1) * local_len]
        extended = jnp.concatenate((part, grad_head[seq]), axis=0)
        x = pre_now[seq, :, channels:]
        total = conv_weight[0:1] * part
        tap_sums[0] = tap_sums[0] + jnp.sum(part * x, axis=0, keepdims=True)
        for lag in range(1, 4):
            moved = extended[lag : lag + local_len]
            total = total + conv_weight[lag : lag + 1] * moved
            tap_sums[lag] = tap_sums[lag] + jnp.sum(moved * x, axis=0, keepdims=True)
        grads[0, 0, seq, :, channels:] = total.astype(bf16)
        grad_head[seq] = part[:8]
    sums[0:1] += jnp.sum(rate_all, axis=0, keepdims=True)
    sums[1:2] += jnp.sum(in_all, axis=0, keepdims=True)
    sums[2:3] += decay_sum
    sums[3:4] += jnp.sum(conv_grad, axis=0, keepdims=True)
    for lag in range(4):
        sums[4 + lag : 5 + lag] += tap_sums[lag]


def chunk_place(chunk, place, chips):
    return lax.rem(place[0] - chunk // 2 + chips, chips), lax.rem(chunk + place[1], 2)


def pick_block(chunk, place, chips, *pairs):
    chip, _ = chunk_place(chunk, place, chips)
    for hop in range(chips):

        @pl.when(chip == hop)
        def _(hop=hop):
            for refs, now in pairs:
                now[...] = refs[hop][0]


def mixer_specs(shape, chips, chunk_of):
    def hop_map(hop, step, place, lengths):
        first = 2 * lax.rem(place[0] - hop + chips, chips)
        return (jnp.where(chunk_of(step) <= first, place[1], 1 - place[1]), 0, 0, 0)

    def block_map(step, place, lengths):
        chip, core = chunk_place(chunk_of(step), place, chips)
        return (chip, core, 0, 0, 0)

    def hops(lanes):
        return [pl.BlockSpec((1, *shape[1:3], lanes), partial(hop_map, hop)) for hop in range(chips)]

    def block(lanes):
        return pl.BlockSpec((1, 1, *shape[1:3], lanes), block_map)

    return hops, block


def whole_spec(shape):
    return pl.BlockSpec(shape, lambda step, place, lengths: (0,) * len(shape))


def mixer_forward(
    pre_blocks, lengths, place, conv_weight, conv_bias, gate_weight, gate_bias, rate_scale, block_width
):
    chips = len(pre_blocks)
    _, seq_count, local_len, channels = pre_blocks[0].shape
    channels //= 2
    hops, block = mixer_specs(pre_blocks[0].shape, chips, lambda step: step)
    full = (chips, 2, seq_count, local_len, channels)
    params = (conv_weight, conv_bias, gate_weight, gate_bias, rate_scale)
    return pl.pallas_call(
        partial(mixer_forward_kernel, chips, block_width),
        grid_spec=pltpu.PrefetchScalarGridSpec(
            num_scalar_prefetch=2,
            grid=(2 * chips,),
            in_specs=hops(2 * channels) + [whole_spec(param.shape) for param in params],
            out_specs=[block(channels)] * 5
            + [whole_spec((seq_count, channels)), whole_spec((seq_count, 3, channels))],
            scratch_shapes=[
                pltpu.VMEM((seq_count, local_len, 2 * channels), f32),
                pltpu.VMEM((seq_count, 8, channels), f32),
                pltpu.VMEM((seq_count, 1, channels), f32),
            ],
        ),
        out_shape=[pltpu.HBM(full, bf16)]
        + [pltpu.HBM(full, f32)] * 4
        + [
            jax.ShapeDtypeStruct((seq_count, channels), f32),
            jax.ShapeDtypeStruct((seq_count, 3, channels), f32),
        ],
        compiler_params=pltpu.CompilerParams(vmem_limit_bytes=32 << 20),
        cost_estimate=kernel_cost,
        name="mixer_forward",
    )(place, lengths, *pre_blocks, *params)


def mixer_backward(
    pre_blocks, back_blocks, saved, lengths, place, conv_weight, gate_back, rate_scale, block_width
):
    chips = len(pre_blocks)
    _, seq_count, local_len, channels = pre_blocks[0].shape
    channels //= 2
    hops, block = mixer_specs(pre_blocks[0].shape, chips, lambda step: 2 * chips - 1 - step)
    full = (chips, 2, seq_count, local_len, channels)
    params = (conv_weight, gate_back, rate_scale)
    packed = gate_tiles(channels, block_width, 128)[-1]
    packed = packed[4] + packed[3] - packed[2]
    return pl.pallas_call(
        partial(mixer_backward_kernel, chips, block_width),
        grid_spec=pltpu.PrefetchScalarGridSpec(
            num_scalar_prefetch=2,
            grid=(2 * chips,),
            in_specs=hops(2 * channels)
            + hops(channels)
            + [block(channels)] * 4
            + [whole_spec(param.shape) for param in params],
            out_specs=[block(2 * channels), whole_spec((8, channels)), whole_spec((packed, 256))],
            scratch_shapes=[
                pltpu.VMEM((seq_count, local_len, 2 * channels), f32),
                pltpu.VMEM((seq_count, local_len, channels), f32),
                pltpu.VMEM((seq_count, 1, channels), f32),
                pltpu.VMEM((seq_count, 8, channels), f32),
            ],
        ),
        out_shape=[
            pltpu.HBM((*full[:-1], 2 * channels), bf16),
            jax.ShapeDtypeStruct((8, channels), f32),
            jax.ShapeDtypeStruct((packed, 256), f32),
        ],
        compiler_params=pltpu.CompilerParams(vmem_limit_bytes=32 << 20),
        cost_estimate=kernel_cost,
        name="mixer_backward",
    )(place, lengths, *pre_blocks, *back_blocks, *saved, *params)


def mlp_kernel(tiles, rows, back, own_in, other_in, own_down, other_down, *refs):
    hidden, gate_grads, up_grads, middle, out, middle_sum, out_sum = refs
    step = pl.program_id(0)

    @pl.when(step == 0)
    def _():
        middle_sum[...] = jnp.zeros_like(middle_sum)
        out_sum[...] = jnp.zeros_like(out_sum)

    def units(weight_in, weight_down):
        gated, slope = gelu_pair(dot(rows[...], weight_in[0]))
        up_pre = dot(rows[...], weight_in[1])
        hidden_grad = dot_nt(back[...], weight_down[...])
        hidden_b = (gated * up_pre).astype(bf16)
        gate_b = (hidden_grad * up_pre * slope).astype(bf16)
        up_b = (hidden_grad * gated).astype(bf16)
        hidden[...] = hidden_b
        gate_grads[...] = gate_b
        up_grads[...] = up_b
        out_sum[...] += dot(hidden_b, weight_down[...])
        middle_sum[...] += dot_nt(gate_b, weight_in[0]) + dot_nt(up_b, weight_in[1])

    @pl.when(step < tiles)
    def _():
        units(own_in, own_down)

    @pl.when(step >= tiles)
    def _():
        units(other_in, other_down)

    @pl.when(step == 2 * tiles - 1)
    def _():
        middle[...] = middle_sum[...]
        out[...] = out_sum[...]


def mlp_block(rows, back, own_in, other_in, own_down, other_down):
    count, width = rows.shape
    units = own_down.shape[0]
    tile = 256 if units % 256 == 0 else 128
    tiles = units // tile

    def own_tile(step):
        return jnp.minimum(step, tiles - 1)

    def other_tile(step):
        return jnp.maximum(step - tiles, 0)

    whole = pl.BlockSpec((count, width), lambda step: (0, 0))
    tiled = pl.BlockSpec((count, tile), lambda step: (0, step))
    return pl.pallas_call(
        partial(mlp_kernel, tiles),
        grid=(2 * tiles,),
        in_specs=[
            whole,
            whole,
            pl.BlockSpec((2, width, tile), lambda step: (0, 0, own_tile(step))),
            pl.BlockSpec((2, width, tile), lambda step: (0, 0, other_tile(step))),
            pl.BlockSpec((tile, width), lambda step: (own_tile(step), 0)),
            pl.BlockSpec((tile, width), lambda step: (other_tile(step), 0)),
        ],
        out_specs=[tiled] * 3 + [whole] * 2,
        out_shape=[pltpu.HBM((count, 2 * units), bf16)] * 3 + [pltpu.HBM((count, width), f32)] * 2,
        scratch_shapes=[pltpu.VMEM((count, width), f32)] * 2,
        compiler_params=pltpu.CompilerParams(vmem_limit_bytes=40 << 20),
        cost_estimate=kernel_cost,
        name="mlp_block",
    )(rows, back, own_in, other_in, own_down, other_down)


def weight_grad_kernel(count, filled, *refs):
    lefts, rights = refs[:count], refs[count : 2 * count]
    own, other = refs[2 * count + 2 * filled :]
    total = dot_tn(lefts[0][...], rights[0][...])
    for left, right in zip(lefts[1:], rights[1:]):
        total = total + dot_tn(left[...], right[...])
    kinds, half, _ = own.shape
    for kind in range(kinds):
        start = 2 * kind * half
        own[kind] = total[start : start + half]
        other[kind] = total[start + half : start + 2 * half].astype(bf16)


def weight_grad(lefts, rights, kinds, slots=1, slot=0, filled=()):
    count = len(rights)
    rows, width = rights[0].shape
    columns = lefts[0].shape[1]
    half, tile = columns // kinds // 2, min(512, width)

    joined = len(lefts) == 1

    def left_spec(at):
        block = at if joined else 0
        return pl.BlockSpec((rows, columns), lambda step: (block, 0))

    lefts = list(lefts) * (count if joined else 1)
    out_spec = pl.BlockSpec((kinds, half, tile), lambda step: (slot, 0, step))
    return pl.pallas_call(
        partial(weight_grad_kernel, count, len(filled) // 2),
        grid=(width // tile,),
        in_specs=[left_spec(at) for at in range(count)]
        + [pl.BlockSpec((rows, tile), lambda step: (0, step))] * count
        + [pl.BlockSpec(memory_space=pl.ANY)] * len(filled),
        out_specs=[out_spec] * 2,
        out_shape=[
            pltpu.HBM((slots * kinds, half, width), f32),
            pltpu.HBM((slots * kinds, half, width), bf16),
        ],
        input_output_aliases={2 * count + at: at for at in range(len(filled))},
        compiler_params=pltpu.CompilerParams(vmem_limit_bytes=40 << 20),
        cost_estimate=kernel_cost,
        name="weight_grad",
    )(*lefts, *rights, *filled)


def block_diagonal(weight):
    count, width, _ = weight.shape
    rows = [
        jnp.pad(weight[at], ((0, 0), (at * width, (count - 1 - at) * width))) for at in range(count)
    ]
    return jnp.concatenate(rows, axis=0)


def pack_gates(rate, into, block_width):
    def padded(values, width):
        return jnp.pad(values, ((0, 0), (0, width - values.shape[1])))

    channels = rate.shape[0]
    forward, back = [], []
    for start, stop, low, high, _ in gate_tiles(channels, block_width, 128):
        forward.append(
            jnp.concatenate(
                (padded(rate[low:high, start:stop], 128), padded(into[low:high, start:stop], 128)), axis=1
            )
        )
    for start, stop, low, high, _ in gate_tiles(channels, block_width, 256):
        back.append(padded(rate.T[low:high, start:stop], 256))
        back.append(padded(into.T[low:high, start:stop], 256))
    return jnp.concatenate(forward, axis=0), jnp.concatenate(back, axis=0)


def unpack_gates(packed, channels, block_width):
    tiles = gate_tiles(channels, block_width, 128)
    kinds = []
    for column in (0, 128):
        blocks = []
        for base in range(0, channels, block_width):
            pieces = []
            for start, stop, low, _, at in tiles:
                left, right = max(start, base), min(stop, base + block_width)
                if left < right:
                    row = at + base - low
                    pieces.append(
                        packed[row : row + block_width, column + left - start : column + right - start]
                    )
            blocks.append(jnp.concatenate(pieces, axis=1))
        kinds.append(jnp.stack(blocks))
    return jnp.stack(kinds)


def narrow_whole(weight, dim):
    return lax.all_gather(weight, "narrow", axis=dim, tiled=True)


def narrow_sum(grad, dim):
    return lax.psum_scatter(grad, "narrow", scatter_dimension=dim, tiled=True)


class DirectSum:
    def __init__(self, grad):
        self.size = lax.axis_size("narrow")
        self.grad, self.got = grad, {}

    def piece(self, flip):
        span = self.grad.shape[1] // self.size
        start = (lax.axis_index("narrow") ^ flip) * span
        return lax.dynamic_slice_in_dim(self.grad, start, span, axis=1)

    def send(self, flips):
        for flip in flips:
            pairs = [(at, at ^ flip) for at in range(self.size)]
            self.got[flip] = lax.ppermute(self.piece(flip), "narrow", pairs)

    def total(self):
        return plus(self.piece(0).astype(f32), *self.got.values())


def swap_cores(values, wide):
    return lax.ppermute(values, "wide", [(at, at ^ 1) for at in range(wide)])


def fence(*values):
    return lax.optimization_barrier(values)


class Chips:
    def __init__(self, wide, chip):
        self.chip, self.count = chip, wide // 2
        self.wide = wide

    def move(self, values, pairs):
        devices = [(2 * a + core, 2 * b + core) for a, b in pairs for core in range(2)]
        return lax.ppermute(values, "wide", devices)

    def ring(self, values):
        return self.move(values, [(at, (at + 1) % self.count) for at in range(self.count)])

    def gather_step(self, step, right, left):
        count = self.count
        to_right = [(at, at + 1) for at in range(step - 1, count - 1)]
        to_left = [(at, at - 1) for at in range(1, count - step + 1)]
        if 2 * step > count + 1:
            both = self.move(jnp.where(self.chip >= step - 1, right, left), to_right + to_left)
            return both, both
        return self.move(right, to_right), self.move(left, to_left)

    def gathered(self, hop, rights, lefts):
        return jnp.where(self.chip >= hop, rights[hop], lefts[self.count - hop])

    def sum_step(self, step, right, left):
        count = self.count
        to_right = [(at, at + 1) for at in range(step)]
        to_left = [(at, at - 1) for at in range(count - step, count)]
        if 2 * step < count - 1:
            both = self.move(jnp.where(self.chip < step, right, left), to_right + to_left)
            return both, both
        return self.move(right, to_right), self.move(left, to_left)


class Exchange:
    def __init__(self, line, rows):
        self.line, self.own = line, rows
        self.packed = line.count == 4
        if self.packed:
            self.odd = line.chip % 2 == 1
            self.edge = (line.chip == 0) | (line.chip == 3)
        self.ends, self.mids = [], []
        self.backs, self.moved = {0: (rows, rows)}, (0.0, 0.0)

    def pair(self, end, mid):
        self.ends.append(self.line.move(end, [(0, 1), (1, 0), (2, 3), (3, 2)]))
        self.mids.append(self.line.move(mid, [(1, 2), (2, 1)]))

    def step(self, number, parts):
        line, count = self.line, self.line.count
        if not self.packed:
            if number < count:
                self.backs[number] = line.gather_step(number, *self.backs[number - 1])
            if number > 1:
                sent = [
                    plus(parts[hop], self.moved[way]).astype(bf16)
                    for way, hop in enumerate((number - 1, count - number + 1))
                ]
                self.moved = line.sum_step(number - 1, *sent)
        elif number == 1:
            self.pair(self.own, self.own)
        elif number == 2:
            part = jnp.where(line.chip == 0, parts[1], parts[3]).astype(bf16)
            self.pair(jnp.where(self.edge, part, self.mids[0]), self.ends[0])
        elif number == 3:
            mid = plus(parts[2], self.ends[1]).astype(bf16)
            self.pair(jnp.where(self.edge, parts[2].astype(bf16), self.mids[1]), mid)
        else:
            end = plus(jnp.where(self.odd, parts[1], parts[3]), self.mids[2])
            mid = plus(jnp.where(line.chip == 1, parts[3], parts[1]), self.ends[2])
            self.pair(end.astype(bf16), mid.astype(bf16))

    def fence(self, *values):
        state = (self.ends, self.mids, self.backs, self.moved)
        state, values = fence(state, values)
        self.ends, self.mids, self.backs, self.moved = state
        return values

    def rows(self):
        if self.packed:
            far = jnp.where(self.edge, self.ends[2], self.mids[0])
            two = jnp.where(self.edge, self.ends[1], self.mids[1])
            near = self.ends[0]
            return [self.own, jnp.where(self.odd, near, far), two, jnp.where(self.odd, far, near)]
        rights, lefts = ({at: pair[way] for at, pair in self.backs.items()} for way in range(2))
        hops = range(1, self.line.count)
        return [self.own] + [self.line.gathered(hop, rights, lefts) for hop in hops]

    def total(self, part):
        if self.packed:
            return plus(part, self.ends[3], self.mids[3])
        return plus(part, *self.moved)


def plus(total, *moved):
    for values in moved:
        total = total + values.astype(f32)
    return total


def paired_sum(values, axis):
    size = lax.axis_size(axis)
    if size & (size - 1):
        return lax.psum(values, axis)
    bit = 1
    while bit < size:
        values = values + lax.ppermute(values, axis, [(at, at ^ bit) for at in range(size)])
        bit *= 2
    return values


def direct_sum(values, axis):
    size = lax.axis_size(axis)
    if size & (size - 1):
        return lax.psum(values, axis)
    terms = [values] + [
        lax.ppermute(values, axis, [(at, at ^ flip) for at in range(size)]) for flip in range(1, size)
    ]
    while len(terms) > 1:
        terms = [left + right for left, right in zip(terms[::2], terms[1::2])]
    return terms[0]


def norm_forward(values, gain):
    scale = lax.rsqrt(jnp.mean(values * values, axis=-1, keepdims=True) + norm_eps)
    return scale, (values * scale * gain).astype(bf16)


def norm_backward(values, scale, gain, grad):
    unit = values * scale
    scaled = grad * gain
    back = scale * (scaled - unit * jnp.mean(scaled * unit, axis=-1, keepdims=True))
    return back, jnp.sum(grad * unit, axis=0)


def dot(left, right):
    return jnp.dot(left, right, preferred_element_type=f32)


def dot_nt(left, right):
    return lax.dot_general(left, right, (((1,), (1,)), ((), ())), preferred_element_type=f32)


def dot_tn(left, right):
    return lax.dot_general(left, right, (((0,), (0,)), ((), ())), preferred_element_type=f32)


def body(
    tokens, lengths, cotangent, first_gain, proj_in, conv_weight, conv_bias, rate_weight, rate_bias,
    input_weight, input_bias, decay_param, proj_out, second_gain, mlp_in, mlp_down,
):
    seq_count, local_len, width = tokens.shape
    wide = lax.axis_size("wide")
    chips = wide // 2
    me = lax.axis_index("wide")
    chip, core = me // 2, me % 2
    place = jnp.stack((chip, core)).astype(jnp.int32)
    channels = proj_in.shape[2]
    block_width = rate_weight.shape[1]
    seq_half = seq_count // 2
    block_shape = (2, seq_half, local_len, 2 * channels)
    line = Chips(wide, chip)
    last = chips - 1

    def swap(values):
        return swap_cores(values, wide)

    def by_sequence(values):
        parts = values.reshape(2, seq_half * local_len, width)
        mine = jnp.where(core == 0, parts[0], parts[1])
        return jnp.concatenate((mine, swap(jnp.where(core == 0, parts[1], parts[0]))), axis=0)

    def both_orders(mine, other):
        return jnp.where(core == 0, jnp.stack((mine, other)), jnp.stack((other, mine)))

    def by_position(rows):
        own, other = jnp.split(rows, 2, axis=0)
        return both_orders(own, swap(other)).reshape(tokens.shape)

    def by_channel(values):
        mine, other = values[..., :channels], values[..., channels:]
        both = both_orders(mine, swap(other))
        return both.reshape(seq_count, *both.shape[2:])

    lengths = lax.dynamic_slice_in_dim(lengths, core * seq_half, seq_half)
    chunk = 2 * chip + (jnp.arange(2, dtype=jnp.int32) ^ core)
    positions = chunk[:, None] * local_len + jnp.arange(local_len, dtype=jnp.int32)
    mask = (positions[:, None, :] < lengths[None, :, None]).astype(f32).reshape(-1, 1)

    def both_cores(own, dim):
        return jnp.concatenate((own, swap(own)), axis=dim)

    own_in = narrow_whole(jnp.swapaxes(proj_in, 1, 2), 2)
    own_out = narrow_whole(proj_out, 1)
    own_mlp_in = narrow_whole(mlp_in, 1)
    own_down = narrow_whole(mlp_down, 1)
    tokens_f = by_sequence(tokens).astype(f32)
    scale_one, norm_in = norm_forward(tokens_f, first_gain)

    params = jnp.concatenate(
        (conv_weight, conv_bias[None], rate_bias[None], input_bias[None], decay_param[None]), axis=0
    )
    norm_in, params, cotangent = fence(norm_in, params, cotangent)
    rows_first = [norm_in]
    pre_blocks = []

    def project(rows):
        return dot_nt(rows, whole_in).reshape(2, seq_half, local_len, 4 * channels)

    for hop in range(1, chips):
        moved = line.ring(rows_first[-1])
        if hop == 1:
            out_grad = by_sequence(cotangent).astype(f32) * mask
            out_grad_b = out_grad.astype(bf16)
            params = both_cores(params, 1)
            gates = both_cores(jnp.stack((rate_weight, input_weight)), 1)
            gate_weight, gate_back = pack_gates(
                block_diagonal(gates[0]), block_diagonal(gates[1]), block_width
            )
            rate_scale = decay_scale * jax.nn.softplus(-params[7:8])
            moved, out_grad_b, gate_weight = fence(moved, out_grad_b, gate_weight)
        if hop == last - 1:
            moved, own_in = fence(moved, own_in)
        if hop == last:
            whole_in = both_cores(own_in, 1).reshape(-1, width)
            pre_blocks = [project(rows) for rows in rows_first]
            moved, out_grad_b, own_out, pre_blocks = fence(moved, out_grad_b, own_out, pre_blocks)
        rows_first.append(moved)

    lanes = Exchange(line, out_grad_b)
    lanes.step(1, None)
    whole_out = both_cores(own_out, 0)
    pre_blocks.append(project(rows_first[last]))
    mixed, conv, rate_gate, in_gate, states, final_state, conv_state = mixer_forward(
        pre_blocks, lengths, place, params[:4], params[4:5], gate_weight, params[5:7],
        rate_scale, block_width,
    )
    mixed_rows = mixed.reshape(chips, -1, 2 * channels)
    parts = {hop: dot(mixed_rows[hop], whole_out) for hop in (1, last)}
    parts, mixed_rows = lanes.fence(parts, mixed_rows)
    for step in range(2, chips + 1):
        lanes.step(step, parts)
        for hop in (step, chips - step):
            if hop < chips and hop not in parts:
                parts[hop] = dot(mixed_rows[hop], whole_out)
        if step == chips - 1:
            if 0 not in parts:
                parts[0] = dot(mixed_rows[0], whole_out)
            parts, own_mlp_in = lanes.fence(parts, own_mlp_in)
            other_mlp_in = swap(own_mlp_in)
        elif step < chips:
            (parts,) = lanes.fence(parts)
    rows_back = lanes.rows()
    parts, rows_back, own_down = lanes.fence(parts, rows_back, own_down)
    resid = tokens_f + lanes.total(parts[0])

    scale_two, norm_mid = norm_forward(resid, second_gain)
    norm_mid, own_down = fence(norm_mid, own_down)
    other_down = swap(own_down)
    rows_second = [norm_mid]
    hidden, gate_grads, up_grads, parts, outs = [], [], [], [], []
    sums = None
    for hop in range(chips):
        if hop < last:
            rows_second.append(line.ring(rows_second[hop]))
        if hop > 1:
            sums = line.ring(total_b)
        made = mlp_block(
            rows_second[hop], rows_back[hop], own_mlp_in, other_mlp_in, own_down, other_down
        )
        rows_second, made, sums = fence(rows_second, made, sums)
        for kept, value in zip((hidden, gate_grads, up_grads, parts, outs), made):
            kept.append(value)
        if hop:
            total = parts[hop] if sums is None else plus(parts[hop], sums)
            total_b = total.astype(bf16)
    sums = line.ring(total_b)
    grads_mlp = weight_grad(gate_grads, rows_second, 1, slots=2)
    grads_down = weight_grad(hidden, rows_back, 1)
    sums, grads_mlp, grads_down, up_grads = fence(sums, grads_mlp, grads_down, up_grads)
    mid_sum = plus(parts[0], sums)

    from_norm, gain_two = norm_backward(resid, scale_two, second_gain, mid_sum)
    resid_grad = out_grad + from_norm
    resid_grad_b = resid_grad.astype(bf16)
    resid_grad_b, up_grads, outs = fence(resid_grad_b, up_grads, outs)

    def shared(grads):
        own, other = grads
        return (own + swap(other).astype(f32)).astype(bf16).reshape(-1, width)

    def back_block(rows):
        return dot_nt(rows, whole_out).reshape(2, seq_half, local_len, 2 * channels)

    lanes = Exchange(line, resid_grad_b)
    lanes.step(1, None)
    grads_mlp = weight_grad(up_grads, rows_second, 1, slots=2, slot=1, filled=grads_mlp)
    grads_mlp, outs = lanes.fence(grads_mlp, outs)
    for step in range(2, chips + 1):
        lanes.step(step, outs)
        if step == 2:
            part_mlp_in = shared(grads_mlp)
            part_mlp_in, grads_down = lanes.fence(part_mlp_in, grads_down)
            grad_mlp_in = narrow_sum(part_mlp_in, 1)
        elif step == 3:
            part_down = shared(grads_down)
            back_blocks = [back_block(resid_grad_b)]
            part_down, back_blocks = lanes.fence(part_down, back_blocks)
            grad_mlp_down = narrow_sum(part_down, 1)
        elif step < chips:
            lanes.fence()
    rows_resid = lanes.rows()
    back_blocks += [back_block(rows) for rows in rows_resid[1:]]
    grads, small, gate_sums = mixer_backward(
        pre_blocks, back_blocks, (conv, rate_gate, in_gate, states),
        lengths, place, params[:4], gate_back, rate_scale, block_width,
    )
    grad_rows = grads.reshape(chips, -1, 4 * channels)
    sent = dot(grad_rows[1], whole_in).astype(bf16)
    sent, grads, small, gate_sums, mixed, grad_mlp_in = lanes.fence(
        sent, grads, small, gate_sums, mixed, grad_mlp_in
    )
    output = (resid + lanes.total(outs[0])).astype(bf16)

    grad_rows = grads.reshape(chips, -1, 4 * channels)
    count = rate_weight.shape[0]
    size = lax.axis_size("narrow")
    for hop in range(1, chips):
        moving = line.ring(sent)
        part = dot(grad_rows[(hop + 1) % chips], whole_in)
        if hop == 1:
            grads_in = weight_grad([grads.reshape(-1, 4 * channels)], rows_first, 2)
            part_in = shared(grads_in)
            gate_grads = unpack_gates(gate_sums, 2 * channels, block_width)
            mine = jnp.concatenate((small[:, :channels].reshape(-1), gate_grads[:, :count].reshape(-1)))
            other = jnp.concatenate((small[:, channels:].reshape(-1), gate_grads[:, count:].reshape(-1)))
            part_in, moving, part, mixed, mine, other, output = fence(
                part_in, moving, part, mixed, mine, other, output
            )
        elif hop == 2:
            sum_in = DirectSum(part_in)
            sum_in.send(range(1, size))
            grads_out = weight_grad([mixed.reshape(-1, 2 * channels)], rows_resid, 1)
            part_out = shared(grads_out)
            own_rows = own_in.reshape(-1, width).astype(f32)
            gain_one = jnp.sum(own_rows * part_in.astype(f32), axis=0) / first_gain
            flat = mine + swap(other)
            part_out, moving, part, flat, gain_one, sum_in.got, grad_mlp_down = fence(
                part_out, moving, part, flat, gain_one, sum_in.got, grad_mlp_down
            )
        elif hop == last:
            sum_out = DirectSum(part_out)
            sum_out.send(range(1, size))
            flat = paired_sum(flat, "narrow")
            gains = direct_sum(jnp.stack((gain_one, gain_two)), "wide")
            moving, gains, flat, sum_out.got = fence(moving, gains, flat, sum_out.got)
        sent = plus(part, moving).astype(bf16)
    in_sum = plus(part, moving)
    gains = direct_sum(gains, "narrow")
    grad_mlp_in, grad_mlp_down = grad_mlp_in.astype(f32), grad_mlp_down.astype(f32)
    grad_proj_in = sum_in.total().reshape(2, channels, -1)
    grad_proj_out = sum_out.total()
    from_norm, _ = norm_backward(tokens_f, scale_one, first_gain, in_sum)
    grad_tokens = (resid_grad + from_norm).astype(bf16)
    sums = flat[: 8 * channels].reshape(8, channels)
    grad_rate_weight, grad_input_weight = flat[8 * channels :].reshape(2, *rate_weight.shape)
    grad_mlp_in = grad_mlp_in.reshape(2, mlp_in.shape[2], -1)
    return (
        by_position(output),
        by_position(grad_tokens),
        by_channel(final_state),
        by_channel(conv_state),
        gains[0],
        jnp.swapaxes(grad_proj_in, 1, 2),
        sums[4:8],
        sums[3],
        grad_rate_weight,
        sums[0],
        grad_input_weight,
        sums[1],
        sums[2] * decay_scale * jax.nn.sigmoid(-decay_param),
        grad_proj_out,
        gains[1],
        jnp.swapaxes(grad_mlp_in, 1, 2),
        grad_mlp_down,
    )


def solution(mesh):
    return jax.shard_map(
        body,
        mesh=mesh,
        in_specs=(
            P("narrow", "wide", None),
            P("narrow"),
            P("narrow", "wide", None),
            P(),
            P(None, "narrow", "wide"),
            P(None, "wide"),
            P("wide"),
            P("wide", None, None),
            P("wide"),
            P("wide", None, None),
            P("wide"),
            P("wide"),
            P("wide", "narrow"),
            P(),
            P(None, "narrow", "wide"),
            P("wide", "narrow"),
        ),
        out_specs=(
            P("narrow", "wide", None),
            P("narrow", "wide", None),
            P("narrow", "wide"),
            P("narrow", None, "wide"),
            P(),
            P(None, "narrow", "wide"),
            P(None, "wide"),
            P("wide"),
            P("wide", None, None),
            P("wide"),
            P("wide", None, None),
            P("wide"),
            P("wide"),
            P("wide", "narrow"),
            P(),
            P(None, "narrow", "wide"),
            P("wide", "narrow"),
        ),
        check_vma=False,
    )
```

time: 848 us -> 708 us (0.83)
  waiting for transfers between devices: 424 us -> 298 us
  Pallas kernels: 40 us -> 146 us
  matrix products: 146 us -> 44 us
  blocking collectives: 57.2 us -> 0 us
  starting transfers between devices: 16.7 us -> 62.9 us
  local copies, waits for them, and re-layouts: 69.8 us -> 41.5 us
  other arithmetic: 68.7 us -> 90.7 us
    ppermute x24 -> x46, waiting for transfers between devices: 423 us -> 278 us  [the longest x28 211 us: move(): return lax.ppermute(values, 'wide', devices)]
    pallas_call x2 -> x11, Pallas kernels: 40 us -> 146 us  [the longest x4 69.5 us: mlp_block(): pl.pallas_call(partial(mlp_kernel, tiles), grid=(2 * tiles,), in_specs=[w...]
    psum x2 -> x0, blocking collectives: 57.2 us -> none  [the longest x1 39.4 us: body(): gains = lax.psum((gain_one, gain_two), ('wide', 'narrow'))]
    ppermute x24 -> x46, starting transfers between devices: 8.96 us -> 59 us  [the longest x28 40 us: move(): return lax.ppermute(values, 'wide', devices)]
    dot_general x24 -> x8, matrix products: 63.4 us -> 17.6 us  [dot_nt(): lax.dot_general(left, right, (((1,), (1,)), ((), ())), preferred_element_...]
    dot_general x6 -> x0, matrix products: 37.6 us -> none  [dot_tn(): lax.dot_general(left, right, (((0,), (0,)), ((), ())), preferred_element_...]
    unnamed x295 -> x249, local copies, waits for them, and re-layouts: 54.4 us -> 22.8 us
    convert_element_type x17 -> x18, other arithmetic: 19.4 us -> 46.6 us  [the longest x2 14.6 us: shared(): return (own + swap(other).astype(f32)).astype(bf16).reshape(-1, width)]
  transfers between devices with their start and end apart: 65 -> 69, of which waited for: 21 -> 26; matrix products, arithmetic and copies ran while one was open for 31% -> 22% of each run, Pallas kernels for 5% -> 21%
where the time goes in v2:
time: 708 us; the launch traced here: 699 us
  waiting for transfers between devices  298 us (42%)
  Pallas kernels  146 us (21%)
  other arithmetic  90.7 us (13%)
  starting transfers between devices  62.9 us (9%)
  matrix products  44 us (6%)
  local copies, waits for them, and re-layouts  41.5 us (6%)
  between operations  16.4 us (2%)
    ppermute x28, waiting for transfers between devices, move(): return lax.ppermute(values, 'wide', devices)  211 us
    pallas_call x4, Pallas kernels, mlp_block(): pl.pallas_call(partial(mlp_kernel, tiles), grid=(2 * tiles,), in_specs=[w...  69.5 us
    pallas_call x5, Pallas kernels, weight_grad(): pl.pallas_call(partial(weight_grad_kernel, count, len(filled) // 2), grid...  40.5 us
    ppermute x28, starting transfers between devices, move(): return lax.ppermute(values, 'wide', devices)  40 us
    dot_general x8, matrix products, dot(): return jnp.dot(left, right, preferred_element_type=f32)  26.4 us
    ppermute x6, waiting for transfers between devices, send(): self.got[flip] = lax.ppermute(self.piece(flip), 'narrow', pairs)  25.3 us
    ppermute x2, waiting for transfers between devices, paired_sum(): lax.ppermute(values, axis, [(at, at ^ bit) for at in range(size)])  23.2 us
    unnamed x249, local copies, waits for them, and re-layouts  22.8 us
  transfers between devices with their start and end apart: 69, of which 26 were waited for; matrix products, arithmetic and copies ran while one was open for 22% of the time, Pallas kernels for 21%

profile of v2, /device:TPU:0, one launch (start us, length us, event | category | flops | bytes accessed | tf_op | source)
XLA Modules:
  0.0 699.3 jit_solution(17420804264595041674)
XLA Ops:
  18.9 2.7 collective-permute-start.2
  23.1 24.3 %collective-permute-done.2.refs_5_ = bf16[256,2048]{1,0:T(8,128)(2,1)S(1)} collective-permute-done((bf16[256,2048]{1,0:T(8,128)(2,1)S(1)}, bf16[256,2048]{1,0:T(8,128)(2,1)S(1)}, u32[]{:S(2)}, u32[]{:S(2)}) %collective-permute-start.2) | collective-permute-done | bytes 1048608 | tf_op jit(solution)/shard_map/ppermute | solution.py:560
  48.4 26.8 %collective-permute-done.4.refs_6_ = bf16[256,2048]{1,0:T(8,128)(2,1)} collective-permute-done((bf16[256,2048]{1,0:T(8,128)(2,1)S(1)}, bf16[256,2048]{1,0:T(8,128)(2,1)}, u32[]{:S(2)}, u32[]{:S(2)}) %collective-permute-start.4) | collective-permute-done | bytes 1048608 | tf_op jit(solution)/shard_map/ppermute | solution.py:560
  77.9 2.6 collective-permute-done.6
  82.6 3.7 convolution_bitcast_fusion.1.refs_2_
  86.3 2.6 convolution_bitcast_fusion.2.refs_1_
  88.9 2.7 convolution_bitcast_fusion.3.refs_0_
  91.6 11.4 %collective-permute-done.5.refs_7_ = bf16[256,2048]{1,0:T(8,128)(2,1)} collective-permute-done((bf16[256,2048]{1,0:T(8,128)(2,1)}, bf16[256,2048]{1,0:T(8,128)(2,1)}, u32[]{:S(2)}, u32[]{:S(2)}) %collective-permute-start.5) | collective-permute-done | bytes 1048608 | tf_op jit(solution)/shard_map/ppermute | solution.py:560
  105.9 4.5 convolution_bitcast_fusion.refs_3_
  110.4 14.8 %mixer_forward.1 = (bf16[4,2,1,128,640]{4,3,2,1,0:T(8,128)(2,1)}, f32[4,2,1,128,640]{4,3,2,1,0:T(8,128)}, f32[4,2,1,128,640]{4,3,2,1,0:T(8,128)}, f32[4,2,1,128,...) custom-call(s32[2]{0:T(128)S(1)} %pad_add_fusion.place, ...), custom_call_target="tpu_custom_call" | custom-call | flops 1 | bytes 1 | tf_op jit(solution)/shard_map/mixer_forward/pallas_call | solution.py:293
  135.4 2.7 fusion.32
  138.2 20.3 %collective-permute-done.11 = bf16[256,2048]{1,0:T(8,128)(2,1)} collective-permute-done((bf16[256,2048]{1,0:T(8,128)(2,1)}, bf16[256,2048]{1,0:T(8,128)(2,1)}, u32[]{:S(2)}, u32[]{:S(2)}) %collective-permute-start.11) | collective-permute-done | bytes 1048608 | tf_op jit(solution)/shard_map/ppermute | solution.py:560
  158.5 2.5 add_convert_fusion.14
  162.2 3.5 collective-permute-start.13
  169.7 18.6 %collective-permute-done.13 = bf16[256,2048]{1,0:T(8,128)(2,1)} collective-permute-done((bf16[256,2048]{1,0:T(8,128)(2,1)}, bf16[256,2048]{1,0:T(8,128)(2,1)}, u32[]{:S(2)}, u32[]{:S(2)}) %collective-permute-start.13) | collective-permute-done | bytes 1048608 | tf_op jit(solution)/shard_map/ppermute | solution.py:560
  188.3 4.9 add_convert_fusion.12
  195.0 4.9 collective-permute-start.15
  201.3 2.7 broadcast_select_fusion.2
  204.0 19.8 %collective-permute-done.15 = bf16[256,2048]{1,0:T(8,128)(2,1)} collective-permute-done((bf16[256,2048]{1,0:T(8,128)(2,1)}, bf16[256,2048]{1,0:T(8,128)(2,1)}, u32[]{:S(2)}, u32[]{:S(2)}) %collective-permute-start.15) | collective-permute-done | bytes 1048608 | tf_op jit(solution)/shard_map/ppermute | solution.py:560
  223.8 3.1 multiply_reduce_fusion.2
  231.7 3.5 collective-permute-done.19.other_down
  235.2 17.4 %mlp_block.4 = (bf16[256,1536]{1,0:T(8,128)(2,1)}, bf16[256,1536]{1,0:T(8,128)(2,1)}, bf16[256,1536]{1,0:T(8,128)(2,1)}, f32[256,2048]{1,0:T(8,128)}, f32[256,2048]{1,0:T(8,128)}) custom-call(bf16[256,2048]{1,0:T(8,128)(2,1)S(1)} %multiply_convert_fusion.rows.refs_4_, bf16[256,2048]{1,0:T(8,128)(2,1)S(1)} %fusion.13.back.refs_4_, ...), custom_call_target="tpu_custom_call" | custom-call | flops 1 | bytes 1 | tf_op jit(solution)/shard_map/mlp_block/pallas_call | solution.py:408
  252.6 4.7 collective-permute-done.17.rows.refs_5_
  257.3 17.3 %mlp_block.5 = (bf16[256,1536]{1,0:T(8,128)(2,1)}, bf16[256,1536]{1,0:T(8,128)(2,1)}, bf16[256,1536]{1,0:T(8,128)(2,1)}, f32[256,2048]{1,0:T(8,128)}, f32[256,2048]{1,0:T(8,128)}) custom-call(bf16[256,2048]{1,0:T(8,128)(2,1)S(1)} %collective-permute-done.17.rows.refs_5_, bf16[256,2048]{1,0:T(8,128)(2,1)S(1)} %copy-done.4, ...), custom_call_target="tpu_custom_call" | custom-call | flops 1 | bytes 1 | tf_op jit(solution)/shard_map/mlp_block/pallas_call | solution.py:408
  274.6 9.3 %collective-permute-done.20.rows.refs_6_ = bf16[256,2048]{1,0:T(8,128)(2,1)S(1)} collective-permute-done((bf16[256,2048]{1,0:T(8,128)(2,1)S(1)}, bf16[256,2048]{1,0:T(8,128)(2,1)S(1)}, u32[]{:S(2)}, u32[]{:S(2)}) %collective-permute-start.20) | collective-permute-done | bytes 1048608 | tf_op jit(solution)/shard_map/ppermute | solution.py:560
  285.9 17.4 %mlp_block.6 = (bf16[256,1536]{1,0:T(8,128)(2,1)}, bf16[256,1536]{1,0:T(8,128)(2,1)}, bf16[256,1536]{1,0:T(8,128)(2,1)}, f32[256,2048]{1,0:T(8,128)}, f32[256,2048]{1,0:T(8,128)}) custom-call(bf16[256,2048]{1,0:T(8,128)(2,1)S(1)} %collective-permute-done.20.rows.refs_6_, bf16[256,2048]{1,0:T(8,128)(2,1)S(1)} %broadcast_select_fusion.6.back.refs_6_, ...), custom_call_target="tpu_custom_call" | custom-call | flops 1 | bytes 1 | tf_op jit(solution)/shard_map/mlp_block/pallas_call | solution.py:408
  303.4 10.2 %collective-permute-done.22 = bf16[256,2048]{1,0:T(8,128)(2,1)S(1)} collective-permute-done((bf16[256,2048]{1,0:T(8,128)(2,1)S(1)}, bf16[256,2048]{1,0:T(8,128)(2,1)S(1)}, u32[]{:S(2)}, u32[]{:S(2)}) %collective-permute-start.22) | collective-permute-done | bytes 1048608 | tf_op jit(solution)/shard_map/ppermute | solution.py:560
  313.6 20.3 %collective-permute-done.21.rows.refs_7_ = bf16[256,2048]{1,0:T(8,128)(2,1)S(1)} collective-permute-done((bf16[256,2048]{1,0:T(8,128)(2,1)S(1)}, bf16[256,2048]{1,0:T(8,128)(2,1)S(1)}, u32[]{:S(2)}, u32[]{:S(2)}) %collective-permute-start.21) | collective-permute-done | bytes 1048608 | tf_op jit(solution)/shard_map/ppermute | solution.py:560
  335.8 17.4 %mlp_block.7 = (bf16[256,1536]{1,0:T(8,128)(2,1)}, bf16[256,1536]{1,0:T(8,128)(2,1)}, bf16[256,1536]{1,0:T(8,128)(2,1)}, f32[256,2048]{1,0:T(8,128)}, f32[256,2048]{1,0:T(8,128)}) custom-call(bf16[256,2048]{1,0:T(8,128)(2,1)S(1)} %collective-permute-done.21.rows.refs_7_, bf16[256,2048]{1,0:T(8,128)(2,1)S(1)} %get-tuple-element.281.back.refs_7_, ...), custom_call_target="tpu_custom_call" | custom-call | flops 1 | bytes 1 | tf_op jit(solution)/shard_map/mlp_block/pallas_call | solution.py:408
  353.2 7.4 %collective-permute-done.23 = bf16[256,2048]{1,0:T(8,128)(2,1)S(1)} collective-permute-done((bf16[256,2048]{1,0:T(8,128)(2,1)S(1)}, bf16[256,2048]{1,0:T(8,128)(2,1)S(1)}, u32[]{:S(2)}, u32[]{:S(2)}) %collective-permute-start.23) | collective-permute-done | bytes 1048608 | tf_op jit(solution)/shard_map/ppermute | solution.py:560
  363.0 8.9 %weight_grad.6 = (f32[1,768,2048]{2,1,0:T(8,128)}, bf16[1,768,2048]{2,1,0:T(8,128)(2,1)}) custom-call(bf16[256,1536]{1,0:T(8,128)(2,1)S(1)} %copy-done.37, bf16[256,1536]{1,0:T(8,128)(2,1)S(1)} %copy-done.39, bf16[256,1536]{1,0:T(8,128)(2,1)S(1)} %copy-done.41, bf16[256,1536]{1,0:T(8,128)(2,1)S(1)} %copy-done.43, bf16[256,2048]{1,0:T(8,128)(2,1)S(1)} %fusion.13.back.refs_4_, ...), custom_call_target="tpu_custom_call" | custom-call | flops 1 | bytes 1 | tf_op jit(solution)/shard_map/weight_grad/pallas_call | solution.py:455
  372.0 9.1 %weight_grad.5 = (f32[2,768,2048]{2,1,0:T(8,128)}, bf16[2,768,2048]{2,1,0:T(8,128)(2,1)}) custom-call(bf16[256,1536]{1,0:T(8,128)(2,1)S(1)} %copy-done.36, bf16[256,1536]{1,0:T(8,128)(2,1)S(1)} %copy-done.38, bf16[256,1536]{1,0:T(8,128)(2,1)S(1)} %copy-done.40, bf16[256,1536]{1,0:T(8,128)(2,1)S(1)} %copy-done.42, ...), custom_call_target="tpu_custom_call" | custom-call | flops 1 | bytes 1 | tf_op jit(solution)/shard_map/weight_grad/pallas_call | solution.py:455
  381.0 5.7 collective-permute-done.24
  391.0 9.0 %weight_grad.7 = (f32[2,768,2048]{2,1,0:T(8,128)}, bf16[2,768,2048]{2,1,0:T(8,128)(2,1)}) custom-call(bf16[256,1536]{1,0:T(8,128)(2,1)S(1)} %copy-done.32, bf16[256,1536]{1,0:T(8,128)(2,1)S(1)} %copy-done.33, bf16[256,1536]{1,0:T(8,128)(2,1)S(1)} %copy-done.34, bf16[256,1536]{1,0:T(8,128)(2,1)S(1)} %copy-done.35, ...), custom_call_target="tpu_custom_call", output_to_operand_aliasing={{0}: (8, {}), {1}: (9, {})} | custom-call | flops 1 | bytes 1 | tf_op jit(solution)/shard_map/weight_grad/pallas_call | solution.py:455
  400.0 12.2 %collective-permute-done.25 = bf16[256,2048]{1,0:T(8,128)(2,1)} collective-permute-done((bf16[256,2048]{1,0:T(8,128)(2,1)S(1)}, bf16[256,2048]{1,0:T(8,128)(2,1)}, u32[]{:S(2)}, u32[]{:S(2)}) %collective-permute-start.25) | collective-permute-done | bytes 1048608 | tf_op jit(solution)/shard_map/ppermute | solution.py:560
  414.7 8.0 %collective-permute-done.29 = bf16[2,768,2048]{2,1,0:T(8,128)(2,1)} collective-permute-done((bf16[2,768,2048]{2,1,0:T(8,128)(2,1)}, bf16[2,768,2048]{2,1,0:T(8,128)(2,1)}, u32[]{:S(2)}, u32[]{:S(2)}) %collective-permute-start.29) | collective-permute-done | bytes 6291488 | tf_op jit(solution)/shard_map/ppermute | solution.py:546
  422.7 11.7 %add_convert_fusion = bf16[2,768,2048]{2,1,0:T(8,128)(2,1)} fusion(f32[2,768,2048]{2,1,0:T(8,128)} %get-tuple-element.337, bf16[2,768,2048]{2,1,0:T(8,128)(2,1)} %collective-permute-done.29), kind=kLoop, calls=%fused_computation | loop fusion | flops 9437184 | bytes 25165824 | tf_op jit(solution)/shard_map/convert_element_type | solution.py:842
  434.4 5.1 collective-permute-done.27
  445.8 3.1 collective-permute-done.58
  451.3 3.6 collective-permute-start.30
  458.9 6.0 fusion.1
  464.9 13.8 %collective-permute-done.30 = bf16[256,2048]{1,0:T(8,128)(2,1)} collective-permute-done((bf16[256,2048]{1,0:T(8,128)(2,1)}, bf16[256,2048]{1,0:T(8,128)(2,1)}, u32[]{:S(2)}, u32[]{:S(2)}) %collective-permute-start.30) | collective-permute-done | bytes 1048608 | tf_op jit(solution)/shard_map/ppermute | solution.py:560
  478.7 5.0 add_convert_fusion.7
  485.5 5.9 collective-permute-start.33
  499.7 20.8 %mixer_backward.1 = (bf16[4,2,1,128,1280]{4,3,2,1,0:T(8,128)(2,1)}, f32[8,640]{1,0:T(8,128)S(1)}, f32[1664,256]{1,0:T(8,128)S(1)}) custom-call(s32[2]{0:T(128)S(1)} %pad_add_fusion.place, s32[1]{0:T(128)} %dynamic_slice.27.lengths, f32[2,1,128,1280]{3,2,1,0:T(8,128)S(1)} %copy-done.10, f32[2,1,128,1280]{3,2,1,0:T(8,128)S(1)} %copy-done.8, ...), custom_call_target="tpu_custom_call" | custom-call | flops 1 | bytes 1 | tf_op jit(solution)/shard_map/mixer_backward/pallas_call | solution.py:330
  522.9 5.2 convolution_convert_fusion
  530.5 2.7 reshape.316
  536.3 8.8 %weight_grad.8 = (f32[2,320,2048]{2,1,0:T(8,128)}, bf16[2,320,2048]{2,1,0:T(8,128)(2,1)}) custom-call(bf16[1024,1280]{1,0:T(8,128)(2,1)S(1)} %bitcast.149, bf16[1024,1280]{1,0:T(8,128)(2,1)S(1)} %bitcast.150, bf16[1024,1280]{1,0:T(8,128)(2,1)S(1)} %bitcast.151, bf16[1024,1280]{1,0:T(8,128)(2,1)S(1)} %bitcast.152, bf16[256,2048]{1,0:T(8,128)(2,1)S(1)} %copy-done.14, ...), custom_call_target="tpu_custom_call" | custom-call | flops 1 | bytes 1 | tf_op jit(solution)/shard_map/weight_grad/pallas_call | solution.py:455
  545.9 5.5 fusion.82
  553.5 3.7 copy.43
  557.1 2.8 add_convert_fusion.6
  560.0 4.2 fusion.81
  564.4 2.9 add_convert_fusion.2
  567.7 4.7 weight_grad.9
  574.3 2.7 add_convert_fusion.5
  580.7 2.4 collective-permute-start.43
  587.0 12.6 %collective-permute-done.43 = bf16[640,512]{1,0:T(8,128)(2,1)} collective-permute-done((bf16[640,512]{1,0:T(8,128)(2,1)}, bf16[640,512]{1,0:T(8,128)(2,1)}, u32[]{:S(2)}, u32[]{:S(2)}) %collective-permute-start.43) | collective-permute-done | bytes 655392 | tf_op jit(solution)/shard_map/ppermute | solution.py:539
  599.6 12.7 %collective-permute-done.42 = bf16[640,512]{1,0:T(8,128)(2,1)} collective-permute-done((bf16[640,512]{1,0:T(8,128)(2,1)}, bf16[640,512]{1,0:T(8,128)(2,1)}, u32[]{:S(2)}, u32[]{:S(2)}) %collective-permute-start.42) | collective-permute-done | bytes 655392 | tf_op jit(solution)/shard_map/ppermute | solution.py:539
  616.0 3.2 collective-permute-start.44
  621.6 2.9 convert_add_fusion.2
  624.5 18.8 %collective-permute-done.50 = f32[2,2048]{1,0:T(2,128)S(1)} collective-permute-done((f32[2,2048]{1,0:T(2,128)S(1)}, f32[2,2048]{1,0:T(2,128)S(1)}, u32[]{:S(2)}, u32[]{:S(2)}) %collective-permute-start.50) | collective-permute-done | bytes 16416 | tf_op jit(solution)/shard_map/ppermute | solution.py:669
  644.7 2.9 collective-permute-start.51
  653.1 23.2 %collective-permute-done.53 = f32[104960]{0:T(1024)S(1)} collective-permute-done((f32[104960]{0:T(1024)S(1)}, f32[104960]{0:T(1024)S(1)}, u32[]{:S(2)}, u32[]{:S(2)}) %collective-permute-start.53) | collective-permute-done | bytes 419872 | tf_op jit(solution)/shard_map/ppermute | solution.py:659
  679.9 4.4 fusion.7
  (487 shorter events, 124.3 us)
Async XLA Ops:
  7.2 68.0 %all-gather.5.cloned.1.call-start = ((), (), s32[]{:S(2)}) async-start(), calls=%async_computation.2 | async-start | bytes 3276800 | tf_op jit(solution)/shard_map/all_gather | solution.py:519
  7.9 83.7 %all-gather.7.cloned.1.call-start = ((), (), s32[]{:S(2)}) async-start(), calls=%async_computation.3 | async-start | bytes 1638400 | tf_op jit(solution)/shard_map/all_gather | solution.py:519
  8.7 161.0 %all-gather.9.cloned.1.call-start = ((), (), s32[]{:S(2)}) async-start(), calls=%async_computation.4 | async-start | bytes 7864320 | tf_op jit(solution)/shard_map/all_gather | solution.py:519
  13.1 190.9 %all-gather.11.cloned.1.call-start = ((), (), s32[]{:S(2)}) async-start(), calls=%async_computation.5 | async-start | bytes 3932160 | tf_op jit(solution)/shard_map/all_gather | solution.py:519
  18.4 4.5 collective-permute-start.1
  18.9 28.5 %collective-permute-start.2 = (bf16[256,2048]{1,0:T(8,128)(2,1)S(1)}, bf16[256,2048]{1,0:T(8,128)(2,1)S(1)}, u32[]{:S(2)}, u32[]{:S(2)}) collective-permute-start(bf16[256,2048]{1,0:T(8,128)(2,1)S(1)} %fusion.6.refs_4_), channel_id=1, source_target_pairs={{0,8},{4,12},{8,16},{12,20},{16,24},{20,28},{24,0},{28,4},{1,9},{5... | collective-permute-start | bytes 3145736 | tf_op jit(solution)/shard_map/ppermute | solution.py:560
  48.4 26.8 %collective-permute-start.4 = (bf16[256,2048]{1,0:T(8,128)(2,1)S(1)}, bf16[256,2048]{1,0:T(8,128)(2,1)}, u32[]{:S(2)}, u32[]{:S(2)}) collective-permute-start(bf16[256,2048]{1,0:T(8,128)(2,1)S(1)} %collective-permute-done.2.refs_5_), channel_id=1, source_target_pairs={{0,8},{4,12},{8,16},{12,20},{16,24},{20,28},{24,0},{28,4},{1,9},{5... | collective-permute-start | bytes 3145736 | tf_op jit(solution)/shard_map/ppermute | solution.py:560
  75.2 5.3 collective-permute-start.6
  75.3 27.8 %collective-permute-start.9 = (f32[8,320]{1,0:T(8,128)S(1)}, f32[8,320]{1,0:T(8,128)S(1)}, u32[]{:S(2)}, u32[]{:S(2)}) collective-permute-start(f32[8,320]{1,0:T(8,128)S(1)} %concatenate.113), channel_id=1, source_target_pairs={{0,4},{4,0},{8,12},{12,8},{16,20},{20,16},{24,28},{28,24},{1,5},{5... | collective-permute-start | bytes 30728 | tf_op jit(solution)/shard_map/ppermute | solution.py:546
  75.8 27.2 %collective-permute-start.5 = (bf16[256,2048]{1,0:T(8,128)(2,1)}, bf16[256,2048]{1,0:T(8,128)(2,1)}, u32[]{:S(2)}, u32[]{:S(2)}) collective-permute-start(bf16[256,2048]{1,0:T(8,128)(2,1)} %collective-permute-done.4.refs_6_), channel_id=1, source_target_pairs={{0,8},{4,12},{8,16},{12,20},{16,24},{20,28},{24,0},{28,4},{1,9},{5... | collective-permute-start | bytes 3145736 | tf_op jit(solution)/shard_map/ppermute | solution.py:560
  103.0 23.6 %collective-permute-start.10 = (bf16[320,2048]{1,0:T(8,128)(2,1)}, bf16[320,2048]{1,0:T(8,128)(2,1)}, u32[]{:S(2)}, u32[]{:S(2)}) collective-permute-start(bf16[320,2048]{1,0:T(8,128)(2,1)} %all-gather.7.cloned.1.call-done), channel_id=1, source_target_pairs={{0,4},{4,0},{8,12},{12,8},{16,20},{20,16},{24,28},{28,24},{1,5},{5... | collective-permute-start | bytes 3932168 | tf_op jit(solution)/shard_map/ppermute | solution.py:546
  104.8 25.8 %collective-permute-start.8 = (bf16[256,2048]{1,0:T(8,128)(2,1)S(1)}, bf16[256,2048]{1,0:T(8,128)(2,1)S(1)}, u32[]{:S(2)}, u32[]{:S(2)}) collective-permute-start(bf16[256,2048]{1,0:T(8,128)(2,1)S(1)} %fusion.13.back.refs_4_), channel_id=1, source_target_pairs={{8,16},{12,20},{16,8},{20,12},{9,17},{13,21},{17,9},{21,13},{10,18... | collective-permute-start | bytes 3145736 | tf_op jit(solution)/shard_map/ppermute | solution.py:560
  105.8 25.7 %collective-permute-start.7 = (bf16[256,2048]{1,0:T(8,128)(2,1)S(1)}, bf16[256,2048]{1,0:T(8,128)(2,1)}, u32[]{:S(2)}, u32[]{:S(2)}) collective-permute-start(bf16[256,2048]{1,0:T(8,128)(2,1)S(1)} %fusion.13.back.refs_4_), channel_id=1, source_target_pairs={{0,8},{4,12},{8,0},{12,4},{16,24},{20,28},{24,16},{28,20},{1,9},{5... | collective-permute-start | bytes 3145736 | tf_op jit(solution)/shard_map/ppermute | solution.py:560
  133.0 25.5 %collective-permute-start.11 = (bf16[256,2048]{1,0:T(8,128)(2,1)}, bf16[256,2048]{1,0:T(8,128)(2,1)}, u32[]{:S(2)}, u32[]{:S(2)}) collective-permute-start(bf16[256,2048]{1,0:T(8,128)(2,1)} %fusion.15), channel_id=1, source_target_pairs={{0,8},{4,12},{8,0},{12,4},{16,24},{20,28},{24,16},{28,20},{1,9},{5... | collective-permute-start | bytes 3145736 | tf_op jit(solution)/shard_map/ppermute | solution.py:560
  134.6 23.9 %collective-permute-start.12 = (bf16[256,2048]{1,0:T(8,128)(2,1)}, bf16[256,2048]{1,0:T(8,128)(2,1)S(1)}, u32[]{:S(2)}, u32[]{:S(2)}) collective-permute-start(bf16[256,2048]{1,0:T(8,128)(2,1)} %collective-permute-done.7), channel_id=1, source_target_pairs={{8,16},{12,20},{16,8},{20,12},{9,17},{13,21},{17,9},{21,13},{10,18... | collective-permute-start | bytes 3145736 | tf_op jit(solution)/shard_map/ppermute | solution.py:560
  135.4 392.7 %reduce-scatter.3.cloned.1.call-start = ((), (), s32[]{:S(2)}) async-start(), calls=%async_computation.6 | async-start | bytes 7864320 | tf_op jit(solution)/shard_map/reduce_scatter | solution.py:523
  162.2 26.1 %collective-permute-start.13 = (bf16[256,2048]{1,0:T(8,128)(2,1)}, bf16[256,2048]{1,0:T(8,128)(2,1)}, u32[]{:S(2)}, u32[]{:S(2)}) collective-permute-start(bf16[256,2048]{1,0:T(8,128)(2,1)} %convert_select_fusion.1), channel_id=1, source_target_pairs={{0,8},{4,12},{8,0},{12,4},{16,24},{20,28},{24,16},{28,20},{1,9},{5... | collective-permute-start | bytes 3145736 | tf_op jit(solution)/shard_map/ppermute | solution.py:560
  165.7 22.6 %collective-permute-start.14 = (bf16[256,2048]{1,0:T(8,128)(2,1)}, bf16[256,2048]{1,0:T(8,128)(2,1)}, u32[]{:S(2)}, u32[]{:S(2)}) collective-permute-start(bf16[256,2048]{1,0:T(8,128)(2,1)} %add_convert_fusion.14), channel_id=1, source_target_pairs={{8,16},{12,20},{16,8},{20,12},{9,17},{13,21},{17,9},{21,13},{10,18... | collective-permute-start | bytes 3145736 | tf_op jit(solution)/shard_map/ppermute | solution.py:560
  188.3 46.9 %collective-permute-start.18 = (bf16[2,2048,768]{2,1,0:T(8,128)(2,1)}, bf16[2,2048,768]{2,1,0:T(8,128)(2,1)}, u32[]{:S(2)}, u32[]{:S(2)}) collective-permute-start(bf16[2,2048,768]{2,1,0:T(8,128)(2,1)} %all-gather.9.cloned.1.call-done.own_in), channel_id=1, source_target_pairs={{0,4},{4,0},{8,12},{12,8},{16,20},{20,16},{24,28},{28,24},{1,5},{5... | collective-permute-start | bytes 18874376 | tf_op jit(solution)/shard_map/ppermute | solution.py:546
  193.2 10.8 %collective-permute-start.16 = (bf16[256,2048]{1,0:T(8,128)(2,1)}, bf16[256,2048]{1,0:T(8,128)(2,1)}, u32[]{:S(2)}, u32[]{:S(2)}) collective-permute-start(bf16[256,2048]{1,0:T(8,128)(2,1)} %get-tuple-element.443), channel_id=1, source_target_pairs={{8,16},{12,20},{16,8},{20,12},{9,17},{13,21},{17,9},{21,13},{10,18... | collective-permute-start | bytes 3145736 | tf_op jit(solution)/shard_map/ppermute | solution.py:560
  195.0 28.8 %collective-permute-start.15 = (bf16[256,2048]{1,0:T(8,128)(2,1)}, bf16[256,2048]{1,0:T(8,128)(2,1)}, u32[]{:S(2)}, u32[]{:S(2)}) collective-permute-start(bf16[256,2048]{1,0:T(8,128)(2,1)} %get-tuple-element.444), channel_id=1, source_target_pairs={{0,8},{4,12},{8,0},{12,4},{16,24},{20,28},{24,16},{28,20},{1,9},{5... | collective-permute-start | bytes 3145736 | tf_op jit(solution)/shard_map/ppermute | solution.py:560
  229.5 5.7 collective-permute-start.19
  229.5 27.8 %collective-permute-start.17 = (bf16[256,2048]{1,0:T(8,128)(2,1)S(1)}, bf16[256,2048]{1,0:T(8,128)(2,1)S(1)}, u32[]{:S(2)}, u32[]{:S(2)}) collective-permute-start(bf16[256,2048]{1,0:T(8,128)(2,1)S(1)} %multiply_convert_fusion.rows.refs_4_), channel_id=1, source_target_pairs={{0,8},{4,12},{8,16},{12,20},{16,24},{20,28},{24,0},{28,4},{1,9},{5... | collective-permute-start | bytes 3145736 | tf_op jit(solution)/shard_map/ppermute | solution.py:560
  257.3 26.6 %collective-permute-start.20 = (bf16[256,2048]{1,0:T(8,128)(2,1)S(1)}, bf16[256,2048]{1,0:T(8,128)(2,1)S(1)}, u32[]{:S(2)}, u32[]{:S(2)}) collective-permute-start(bf16[256,2048]{1,0:T(8,128)(2,1)S(1)} %collective-permute-done.17.rows.refs_5_), channel_id=1, source_target_pairs={{0,8},{4,12},{8,16},{12,20},{16,24},{20,28},{24,0},{28,4},{1,9},{5... | collective-permute-start | bytes 3145736 | tf_op jit(solution)/shard_map/ppermute | solution.py:560
  285.6 27.9 %collective-permute-start.22 = (bf16[256,2048]{1,0:T(8,128)(2,1)S(1)}, bf16[256,2048]{1,0:T(8,128)(2,1)S(1)}, u32[]{:S(2)}, u32[]{:S(2)}) collective-permute-start(bf16[256,2048]{1,0:T(8,128)(2,1)S(1)} %convert_element_type.225), channel_id=1, source_target_pairs={{0,8},{4,12},{8,16},{12,20},{16,24},{20,28},{24,0},{28,4},{1,9},{5... | collective-permute-start | bytes 3145736 | tf_op jit(solution)/shard_map/ppermute | solution.py:560
  285.7 48.2 %collective-permute-start.21 = (bf16[256,2048]{1,0:T(8,128)(2,1)S(1)}, bf16[256,2048]{1,0:T(8,128)(2,1)S(1)}, u32[]{:S(2)}, u32[]{:S(2)}) collective-permute-start(bf16[256,2048]{1,0:T(8,128)(2,1)S(1)} %collective-permute-done.20.rows.refs_6_), channel_id=1, source_target_pairs={{0,8},{4,12},{8,16},{12,20},{16,24},{20,28},{24,0},{28,4},{1,9},{5... | collective-permute-start | bytes 3145736 | tf_op jit(solution)/shard_map/ppermute | solution.py:560
  335.7 24.8 %collective-permute-start.23 = (bf16[256,2048]{1,0:T(8,128)(2,1)S(1)}, bf16[256,2048]{1,0:T(8,128)(2,1)S(1)}, u32[]{:S(2)}, u32[]{:S(2)}) collective-permute-start(bf16[256,2048]{1,0:T(8,128)(2,1)S(1)} %add_convert_fusion.11), channel_id=1, source_target_pairs={{0,8},{4,12},{8,16},{12,20},{16,24},{20,28},{24,0},{28,4},{1,9},{5... | collective-permute-start | bytes 3145736 | tf_op jit(solution)/shard_map/ppermute | solution.py:560
  362.6 24.1 %collective-permute-start.24 = (bf16[256,2048]{1,0:T(8,128)(2,1)S(1)}, bf16[256,2048]{1,0:T(8,128)(2,1)S(1)}, u32[]{:S(2)}, u32[]{:S(2)}) collective-permute-start(bf16[256,2048]{1,0:T(8,128)(2,1)S(1)} %add_convert_fusion.10), channel_id=1, source_target_pairs={{0,8},{4,12},{8,16},{12,20},{16,24},{20,28},{24,0},{28,4},{1,9},{5... | collective-permute-start | bytes 3145736 | tf_op jit(solution)/shard_map/ppermute | solution.py:560
  390.1 10.0 %collective-permute-start.26 = (bf16[256,2048]{1,0:T(8,128)(2,1)S(1)}, bf16[256,2048]{1,0:T(8,128)(2,1)S(1)}, u32[]{:S(2)}, u32[]{:S(2)}) collective-permute-start(bf16[256,2048]{1,0:T(8,128)(2,1)S(1)} %get-tuple-element.320.refs_4_), channel_id=1, source_target_pairs={{8,16},{12,20},{16,8},{20,12},{9,17},{13,21},{17,9},{21,13},{10,18... | collective-permute-start | bytes 3145736 | tf_op jit(solution)/shard_map/ppermute | solution.py:560
  390.9 21.3 %collective-permute-start.25 = (bf16[256,2048]{1,0:T(8,128)(2,1)S(1)}, bf16[256,2048]{1,0:T(8,128)(2,1)}, u32[]{:S(2)}, u32[]{:S(2)}) collective-permute-start(bf16[256,2048]{1,0:T(8,128)(2,1)S(1)} %get-tuple-element.320.refs_4_), channel_id=1, source_target_pairs={{0,8},{4,12},{8,0},{12,4},{16,24},{20,28},{24,16},{28,20},{1,9},{5... | collective-permute-start | bytes 3145736 | tf_op jit(solution)/shard_map/ppermute | solution.py:560
  412.2 10.5 %collective-permute-start.29 = (bf16[2,768,2048]{2,1,0:T(8,128)(2,1)}, bf16[2,768,2048]{2,1,0:T(8,128)(2,1)}, u32[]{:S(2)}, u32[]{:S(2)}) collective-permute-start(bf16[2,768,2048]{2,1,0:T(8,128)(2,1)} %get-tuple-element.338), channel_id=1, source_target_pairs={{0,4},{4,0},{8,12},{12,8},{16,20},{20,16},{24,28},{28,24},{1,5},{5... | collective-permute-start | bytes 18874376 | tf_op jit(solution)/shard_map/ppermute | solution.py:546
  413.7 25.8 %collective-permute-start.27 = (bf16[256,2048]{1,0:T(8,128)(2,1)}, bf16[256,2048]{1,0:T(8,128)(2,1)S(1)}, u32[]{:S(2)}, u32[]{:S(2)}) collective-permute-start(bf16[256,2048]{1,0:T(8,128)(2,1)} %fusion.16), channel_id=1, source_target_pairs={{0,8},{4,12},{8,0},{12,4},{16,24},{20,28},{24,16},{28,20},{1,9},{5... | collective-permute-start | bytes 3145736 | tf_op jit(solution)/shard_map/ppermute | solution.py:560
  414.0 25.5 %collective-permute-start.28 = (bf16[256,2048]{1,0:T(8,128)(2,1)}, bf16[256,2048]{1,0:T(8,128)(2,1)S(1)}, u32[]{:S(2)}, u32[]{:S(2)}) collective-permute-start(bf16[256,2048]{1,0:T(8,128)(2,1)} %collective-permute-done.25), channel_id=1, source_target_pairs={{8,16},{12,20},{16,8},{20,12},{9,17},{13,21},{17,9},{21,13},{10,18... | collective-permute-start | bytes 3145736 | tf_op jit(solution)/shard_map/ppermute | solution.py:560
  440.9 146.1 %reduce-scatter.5.cloned.1.call-start = ((), (), s32[]{:S(2)}) async-start(), calls=%async_computation.7 | async-start | bytes 3932160 | tf_op jit(solution)/shard_map/reduce_scatter | solution.py:523
  443.2 15.7 %collective-permute-start.32 = (bf16[1,768,2048]{2,1,0:T(8,128)(2,1)}, bf16[1,768,2048]{2,1,0:T(8,128)(2,1)S(1)}, u32[]{:S(2)}, u32[]{:S(2)}) collective-permute-start(bf16[1,768,2048]{2,1,0:T(8,128)(2,1)} %get-tuple-element.347), channel_id=1, source_target_pairs={{0,4},{4,0},{8,12},{12,8},{16,20},{20,16},{24,28},{28,24},{1,5},{5... | collective-permute-start | bytes 9437192 | tf_op jit(solution)/shard_map/ppermute | solution.py:546
  451.3 27.4 %collective-permute-start.30 = (bf16[256,2048]{1,0:T(8,128)(2,1)}, bf16[256,2048]{1,0:T(8,128)(2,1)}, u32[]{:S(2)}, u32[]{:S(2)}) collective-permute-start(bf16[256,2048]{1,0:T(8,128)(2,1)} %convert_select_fusion), channel_id=1, source_target_pairs={{0,8},{4,12},{8,0},{12,4},{16,24},{20,28},{24,16},{28,20},{1,9},{5... | collective-permute-start | bytes 3145736 | tf_op jit(solution)/shard_map/ppermute | solution.py:560
  456.2 22.5 %collective-permute-start.31 = (bf16[256,2048]{1,0:T(8,128)(2,1)}, bf16[256,2048]{1,0:T(8,128)(2,1)}, u32[]{:S(2)}, u32[]{:S(2)}) collective-permute-start(bf16[256,2048]{1,0:T(8,128)(2,1)} %add_convert_fusion.9), channel_id=1, source_target_pairs={{8,16},{12,20},{16,8},{20,12},{9,17},{13,21},{17,9},{21,13},{10,18... | collective-permute-start | bytes 3145736 | tf_op jit(solution)/shard_map/ppermute | solution.py:560
  483.8 44.3 %collective-permute-start.34 = (bf16[256,2048]{1,0:T(8,128)(2,1)}, bf16[256,2048]{1,0:T(8,128)(2,1)}, u32[]{:S(2)}, u32[]{:S(2)}) collective-permute-start(bf16[256,2048]{1,0:T(8,128)(2,1)} %get-tuple-element.441), channel_id=1, source_target_pairs={{8,16},{12,20},{16,8},{20,12},{9,17},{13,21},{17,9},{21,13},{10,18... | collective-permute-start | bytes 3145736 | tf_op jit(solution)/shard_map/ppermute | solution.py:560
  485.5 42.6 %collective-permute-start.33 = (bf16[256,2048]{1,0:T(8,128)(2,1)}, bf16[256,2048]{1,0:T(8,128)(2,1)}, u32[]{:S(2)}, u32[]{:S(2)}) collective-permute-start(bf16[256,2048]{1,0:T(8,128)(2,1)} %get-tuple-element.442), channel_id=1, source_target_pairs={{0,8},{4,12},{8,0},{12,4},{16,24},{20,28},{24,16},{28,20},{1,9},{5... | collective-permute-start | bytes 3145736 | tf_op jit(solution)/shard_map/ppermute | solution.py:560
  534.5 32.8 %collective-permute-start.36 = (bf16[256,2048]{1,0:T(8,128)(2,1)}, bf16[256,2048]{1,0:T(8,128)(2,1)}, u32[]{:S(2)}, u32[]{:S(2)}) collective-permute-start(bf16[256,2048]{1,0:T(8,128)(2,1)} %convolution_convert_fusion), channel_id=1, source_target_pairs={{0,8},{4,12},{8,16},{12,20},{16,24},{20,28},{24,0},{28,4},{1,9},{5... | collective-permute-start | bytes 3145736 | tf_op jit(solution)/shard_map/ppermute | solution.py:560
  545.1 19.2 %collective-permute-start.35 = (bf16[2,320,2048]{2,1,0:T(8,128)(2,1)}, bf16[2,320,2048]{2,1,0:T(8,128)(2,1)}, u32[]{:S(2)}, u32[]{:S(2)}) collective-permute-start(bf16[2,320,2048]{2,1,0:T(8,128)(2,1)} %get-tuple-element.365), channel_id=1, source_target_pairs={{0,4},{4,0},{8,12},{12,8},{16,20},{20,16},{24,28},{28,24},{1,5},{5... | collective-permute-start | bytes 7864328 | tf_op jit(solution)/shard_map/ppermute | solution.py:546
  572.5 10.6 %collective-permute-start.40 = (f32[104960]{0:T(1024)S(1)}, f32[104960]{0:T(1024)S(1)}, u32[]{:S(2)}, u32[]{:S(2)}) collective-permute-start(f32[104960]{0:T(1024)S(1)} %copy-done.103), channel_id=1, source_target_pairs={{0,4},{4,0},{8,12},{12,8},{16,20},{20,16},{24,28},{28,24},{1,5},{5... | collective-permute-start | bytes 1259528 | tf_op jit(solution)/shard_map/ppermute | solution.py:546
  573.1 10.4 %collective-permute-start.37 = (bf16[128,2048]{1,0:T(8,128)(2,1)S(1)}, bf16[128,2048]{1,0:T(8,128)(2,1)S(1)}, u32[]{:S(2)}, u32[]{:S(2)}) collective-permute-start(bf16[128,2048]{1,0:T(8,128)(2,1)S(1)} %get-tuple-element.481), channel_id=1, source_target_pairs={{0,4},{4,0},{8,12},{12,8},{16,20},{20,16},{24,28},{28,24},{1,5},{5... | collective-permute-start | bytes 1572872 | tf_op jit(solution)/shard_map/ppermute | solution.py:546
  573.8 11.6 %collective-permute-start.38 = (bf16[1,320,2048]{2,1,0:T(8,128)(2,1)S(1)}, bf16[1,320,2048]{2,1,0:T(8,128)(2,1)S(1)}, u32[]{:S(2)}, u32[]{:S(2)}) collective-permute-start(bf16[1,320,2048]{2,1,0:T(8,128)(2,1)S(1)} %copy-done.115), channel_id=1, source_target_pairs={{0,4},{4,0},{8,12},{12,8},{16,20},{20,16},{24,28},{28,24},{1,5},{5... | collective-permute-start | bytes 3932168 | tf_op jit(solution)/shard_map/ppermute | solution.py:546
  577.0 35.2 %collective-permute-start.39 = (bf16[256,2048]{1,0:T(8,128)(2,1)}, bf16[256,2048]{1,0:T(8,128)(2,1)}, u32[]{:S(2)}, u32[]{:S(2)}) collective-permute-start(bf16[256,2048]{1,0:T(8,128)(2,1)} %add_convert_fusion.5), channel_id=1, source_target_pairs={{0,8},{4,12},{8,16},{12,20},{16,24},{20,28},{24,0},{28,4},{1,9},{5... | collective-permute-start | bytes 3145736 | tf_op jit(solution)/shard_map/ppermute | solution.py:560
  580.7 18.9 %collective-permute-start.43 = (bf16[640,512]{1,0:T(8,128)(2,1)}, bf16[640,512]{1,0:T(8,128)(2,1)}, u32[]{:S(2)}, u32[]{:S(2)}) collective-permute-start(bf16[640,512]{1,0:T(8,128)(2,1)} %get-tuple-element.449), channel_id=1, source_target_pairs={{0,3},{1,2},{2,1},{3,0},{4,7},{5,6},{6,5},{7,4},{8,11},{9,10},{10,... | collective-permute-start | bytes 1966088 | tf_op jit(solution)/shard_map/ppermute | solution.py:539
  583.1 29.1 %collective-permute-start.42 = (bf16[640,512]{1,0:T(8,128)(2,1)}, bf16[640,512]{1,0:T(8,128)(2,1)}, u32[]{:S(2)}, u32[]{:S(2)}) collective-permute-start(bf16[640,512]{1,0:T(8,128)(2,1)} %get-tuple-element.450), channel_id=1, source_target_pairs={{0,2},{1,3},{2,0},{3,1},{4,6},{5,7},{6,4},{7,5},{8,10},{9,11},{10,... | collective-permute-start | bytes 1966088 | tf_op jit(solution)/shard_map/ppermute | solution.py:539
  583.5 28.8 %collective-permute-start.41 = (bf16[640,512]{1,0:T(8,128)(2,1)}, bf16[640,512]{1,0:T(8,128)(2,1)}, u32[]{:S(2)}, u32[]{:S(2)}) collective-permute-start(bf16[640,512]{1,0:T(8,128)(2,1)} %get-tuple-element.451), channel_id=1, source_target_pairs={{0,1},{1,0},{2,3},{3,2},{4,5},{5,4},{6,7},{7,6},{8,9},{9,8},{10,11... | collective-permute-start | bytes 1966088 | tf_op jit(solution)/shard_map/ppermute | solution.py:539
  612.3 35.3 %collective-permute-start.52 = (f32[104960]{0:T(1024)S(1)}, f32[104960]{0:T(1024)S(1)}, u32[]{:S(2)}, u32[]{:S(2)}) collective-permute-start(f32[104960]{0:T(1024)S(1)} %add.265), channel_id=1, source_target_pairs={{0,1},{1,0},{2,3},{3,2},{4,5},{5,4},{6,7},{7,6},{8,9},{9,8},{10,11... | collective-permute-start | bytes 1259528 | tf_op jit(solution)/shard_map/ppermute | solution.py:659
  616.0 60.4 %collective-permute-start.44 = (bf16[256,2048]{1,0:T(8,128)(2,1)S(1)}, bf16[256,2048]{1,0:T(8,128)(2,1)S(1)}, u32[]{:S(2)}, u32[]{:S(2)}) collective-permute-start(bf16[256,2048]{1,0:T(8,128)(2,1)S(1)} %add_convert_fusion.4), channel_id=1, source_target_pairs={{0,8},{4,12},{8,16},{12,20},{16,24},{20,28},{24,0},{28,4},{1,9},{5... | collective-permute-start | bytes 3145736 | tf_op jit(solution)/shard_map/ppermute | solution.py:560
  619.2 24.1 %collective-permute-start.50 = (f32[2,2048]{1,0:T(2,128)S(1)}, f32[2,2048]{1,0:T(2,128)S(1)}, u32[]{:S(2)}, u32[]{:S(2)}) collective-permute-start(f32[2,2048]{1,0:T(2,128)S(1)} %pad_maximum_fusion.10), channel_id=1, source_target_pairs={{0,24},{4,28},{8,16},{12,20},{16,8},{20,12},{24,0},{28,4},{1,25},{... | collective-permute-start | bytes 49160 | tf_op jit(solution)/shard_map/ppermute | solution.py:669
  620.2 24.0 %collective-permute-start.49 = (f32[2,2048]{1,0:T(2,128)S(1)}, f32[2,2048]{1,0:T(2,128)S(1)}, u32[]{:S(2)}, u32[]{:S(2)}) collective-permute-start(f32[2,2048]{1,0:T(2,128)S(1)} %pad_maximum_fusion.10), channel_id=1, source_target_pairs={{0,20},{4,16},{8,28},{12,24},{16,4},{20,0},{24,12},{28,8},{1,21},{... | collective-permute-start | bytes 49160 | tf_op jit(solution)/shard_map/ppermute | solution.py:669
  620.2 24.5 %collective-permute-start.48 = (f32[2,2048]{1,0:T(2,128)S(1)}, f32[2,2048]{1,0:T(2,128)S(1)}, u32[]{:S(2)}, u32[]{:S(2)}) collective-permute-start(f32[2,2048]{1,0:T(2,128)S(1)} %pad_maximum_fusion.10), channel_id=1, source_target_pairs={{0,16},{4,20},{8,24},{12,28},{16,0},{20,4},{24,8},{28,12},{1,17},{... | collective-permute-start | bytes 49160 | tf_op jit(solution)/shard_map/ppermute | solution.py:669
  643.3 5.8 collective-permute-start.47
  644.2 6.5 collective-permute-start.46
  644.7 6.8 collective-permute-start.51
  647.5 5.2 collective-permute-start.45
  649.1 27.2 %collective-permute-start.56 = (bf16[320,512]{1,0:T(8,128)(2,1)S(1)}, bf16[320,512]{1,0:T(8,128)(2,1)S(1)}, u32[]{:S(2)}, u32[]{:S(2)}) collective-permute-start(bf16[320,512]{1,0:T(8,128)(2,1)S(1)} %get-tuple-element.471), channel_id=1, source_target_pairs={{0,3},{1,2},{2,1},{3,0},{4,7},{5,6},{6,5},{7,4},{8,11},{9,10},{10,... | collective-permute-start | bytes 983048 | tf_op jit(solution)/shard_map/ppermute | solution.py:539
  650.7 25.6 %collective-permute-start.55 = (bf16[320,512]{1,0:T(8,128)(2,1)S(1)}, bf16[320,512]{1,0:T(8,128)(2,1)S(1)}, u32[]{:S(2)}, u32[]{:S(2)}) collective-permute-start(bf16[320,512]{1,0:T(8,128)(2,1)S(1)} %get-tuple-element.472), channel_id=1, source_target_pairs={{0,2},{1,3},{2,0},{3,1},{4,6},{5,7},{6,4},{7,5},{8,10},{9,11},{10,... | collective-permute-start | bytes 983048 | tf_op jit(solution)/shard_map/ppermute | solution.py:539
  651.5 24.9 %collective-permute-start.54 = (bf16[320,512]{1,0:T(8,128)(2,1)S(1)}, bf16[320,512]{1,0:T(8,128)(2,1)S(1)}, u32[]{:S(2)}, u32[]{:S(2)}) collective-permute-start(bf16[320,512]{1,0:T(8,128)(2,1)S(1)} %get-tuple-element.473), channel_id=1, source_target_pairs={{0,1},{1,0},{2,3},{3,2},{4,5},{5,4},{6,7},{7,6},{8,9},{9,8},{10,11... | collective-permute-start | bytes 983048 | tf_op jit(solution)/shard_map/ppermute | solution.py:539
  652.7 23.6 %collective-permute-start.53 = (f32[104960]{0:T(1024)S(1)}, f32[104960]{0:T(1024)S(1)}, u32[]{:S(2)}, u32[]{:S(2)}) collective-permute-start(f32[104960]{0:T(1024)S(1)} %add.277), channel_id=1, source_target_pairs={{0,2},{1,3},{2,0},{3,1},{4,6},{5,7},{6,4},{7,5},{8,10},{9,11},{10,... | collective-permute-start | bytes 1259528 | tf_op jit(solution)/shard_map/ppermute | solution.py:659
  676.4 12.8 %collective-permute-start.62 = (f32[2,2048]{1,0:T(2,128)S(1)}, f32[2,2048]{1,0:T(2,128)S(1)}, u32[]{:S(2)}, u32[]{:S(2)}) collective-permute-start(f32[2,2048]{1,0:T(2,128)S(1)} %add_add_fusion.1), channel_id=1, source_target_pairs={{0,3},{1,2},{2,1},{3,0},{4,7},{5,6},{6,5},{7,4},{8,11},{9,10},{10,... | collective-permute-start | bytes 49160 | tf_op jit(solution)/shard_map/ppermute | solution.py:669
  677.9 11.3 %collective-permute-start.61 = (f32[2,2048]{1,0:T(2,128)S(1)}, f32[2,2048]{1,0:T(2,128)S(1)}, u32[]{:S(2)}, u32[]{:S(2)}) collective-permute-start(f32[2,2048]{1,0:T(2,128)S(1)} %add_add_fusion.1), channel_id=1, source_target_pairs={{0,2},{1,3},{2,0},{3,1},{4,6},{5,7},{6,4},{7,5},{8,10},{9,11},{10,... | collective-permute-start | bytes 49160 | tf_op jit(solution)/shard_map/ppermute | solution.py:669
  678.5 10.7 %collective-permute-start.60 = (f32[2,2048]{1,0:T(2,128)S(1)}, f32[2,2048]{1,0:T(2,128)S(1)}, u32[]{:S(2)}, u32[]{:S(2)}) collective-permute-start(f32[2,2048]{1,0:T(2,128)S(1)} %add_add_fusion.1), channel_id=1, source_target_pairs={{0,1},{1,0},{2,3},{3,2},{4,5},{5,4},{6,7},{7,6},{8,9},{9,8},{10,11... | collective-permute-start | bytes 49160 | tf_op jit(solution)/shard_map/ppermute | solution.py:669
  (124 other events, 1137.7 us)
Sparse Core Ops, SparseCore 0:
  9.9 42.1 all-gather.4
  53.9 28.6 all-gather.6
  84.5 70.1 all-gather.8
  156.3 43.8 all-gather.10
  441.0 70.9 reduce-scatter.2
  523.0 44.8 reduce-scatter.4

commit v3 on v2

--- a/solution.py
+++ b/solution.py
@@ -83,7 +83,7 @@
     chunk = pl.program_id(0)
     seq_count, local_len, channels = pre_now.shape
     channels //= 2
-    pick_block(chunk, place, chips, (pre_refs, pre_now))
+    pick_block(chunk, place, chips, pre_refs, pre_now)
 
     @pl.when(chunk == 0)
     def _():
@@ -146,16 +146,17 @@
 
 
 def mixer_backward_kernel(
-    chips, block_width, place, lengths, *refs
+    chips, block_width, crossed, place, lengths, *refs
 ):
     pre_refs, back_refs, refs = refs[:chips], refs[chips : 2 * chips], refs[2 * chips :]
     conv_in, rate_in, in_in, states_in, conv_weight, gate_back, rate_scale = refs[:7]
-    grads, sums, gate_sums = refs[7:10]
-    pre_now, back_now, carry, grad_head = refs[10:]
+    grads, sums, gate_grads = refs[7:10]
+    pre_now, back_now, carry, grad_head, gate_sums = refs[10:]
     step = pl.program_id(0)
     chunk = pl.num_programs(0) - 1 - step
     seq_count, local_len, channels = back_now.shape
-    pick_block(chunk, place, chips, (pre_refs, pre_now), (back_refs, back_now))
+    pick_block(chunk, place, chips, pre_refs, pre_now)
+    pick_block(chunk, place, chips, back_refs, back_now, crossed)
 
     @pl.when(step == 0)
     def _():
@@ -244,32 +245,46 @@
     for lag in range(4):
         sums[4 + lag : 5 + lag] += tap_sums[lag]
 
+    @pl.when(chunk == 0)
+    def _():
+        tiles = gate_tiles(channels, block_width, 128)
+        for kind, column in enumerate((0, 128)):
+            for base in range(0, channels, block_width):
+                pieces = []
+                for start, stop, low, _, at in tiles:
+                    left, right = max(start, base), min(stop, base + block_width)
+                    if left < right:
+                        row = at + base - low
+                        span = gate_sums[row : row + block_width, column : column + 128]
+                        pieces.append(span[:, left - start : right - start])
+                gate_grads[base // block_width, kind] = jnp.concatenate(pieces, axis=1)
+
 
 def chunk_place(chunk, place, chips):
     return lax.rem(place[0] - chunk // 2 + chips, chips), lax.rem(chunk + place[1], 2)
 
 
-def pick_block(chunk, place, chips, *pairs):
-    chip, _ = chunk_place(chunk, place, chips)
+def pick_block(chunk, place, chips, refs, now, crossed=False):
+    slot = (chunk // 2) ^ place[0] if crossed else chunk_place(chunk, place, chips)[0]
     for hop in range(chips):
 
-        @pl.when(chip == hop)
+        @pl.when(slot == hop)
         def _(hop=hop):
-            for refs, now in pairs:
-                now[...] = refs[hop][0]
+            now[...] = refs[hop][0]
 
 
 def mixer_specs(shape, chips, chunk_of):
-    def hop_map(hop, step, place, lengths):
-        first = 2 * lax.rem(place[0] - hop + chips, chips)
+    def hop_map(hop, crossed, step, place, lengths):
+        first = 2 * (place[0] ^ hop if crossed else lax.rem(place[0] - hop + chips, chips))
         return (jnp.where(chunk_of(step) <= first, place[1], 1 - place[1]), 0, 0, 0)
 
     def block_map(step, place, lengths):
         chip, core = chunk_place(chunk_of(step), place, chips)
         return (chip, core, 0, 0, 0)
 
-    def hops(lanes):
-        return [pl.BlockSpec((1, *shape[1:3], lanes), partial(hop_map, hop)) for hop in range(chips)]
+    def hops(lanes, crossed=False):
+        block = (1, *shape[1:3], lanes)
+        return [pl.BlockSpec(block, partial(hop_map, hop, crossed)) for hop in range(chips)]
 
     def block(lanes):
         return pl.BlockSpec((1, 1, *shape[1:3], lanes), block_map)
@@ -317,7 +332,7 @@
 
 
 def mixer_backward(
-    pre_blocks, back_blocks, saved, lengths, place, conv_weight, gate_back, rate_scale, block_width
+    pre_blocks, back_blocks, crossed, saved, lengths, place, conv_weight, gate_back, rate_scale, block_width
 ):
     chips = len(pre_blocks)
     _, seq_count, local_len, channels = pre_blocks[0].shape
@@ -327,27 +342,29 @@
     params = (conv_weight, gate_back, rate_scale)
     packed = gate_tiles(channels, block_width, 128)[-1]
     packed = packed[4] + packed[3] - packed[2]
+    gate_shape = (channels // block_width, 2, block_width, block_width)
     return pl.pallas_call(
-        partial(mixer_backward_kernel, chips, block_width),
+        partial(mixer_backward_kernel, chips, block_width, crossed),
         grid_spec=pltpu.PrefetchScalarGridSpec(
             num_scalar_prefetch=2,
             grid=(2 * chips,),
             in_specs=hops(2 * channels)
-            + hops(channels)
+            + hops(channels, crossed)
             + [block(channels)] * 4
             + [whole_spec(param.shape) for param in params],
-            out_specs=[block(2 * channels), whole_spec((8, channels)), whole_spec((packed, 256))],
+            out_specs=[block(2 * channels), whole_spec((8, channels)), whole_spec(gate_shape)],
             scratch_shapes=[
                 pltpu.VMEM((seq_count, local_len, 2 * channels), f32),
                 pltpu.VMEM((seq_count, local_len, channels), f32),
                 pltpu.VMEM((seq_count, 1, channels), f32),
                 pltpu.VMEM((seq_count, 8, channels), f32),
+                pltpu.VMEM((packed, 256), f32),
             ],
         ),
         out_shape=[
             pltpu.HBM((*full[:-1], 2 * channels), bf16),
             jax.ShapeDtypeStruct((8, channels), f32),
-            jax.ShapeDtypeStruct((packed, 256), f32),
+            jax.ShapeDtypeStruct(gate_shape, f32),
         ],
         compiler_params=pltpu.CompilerParams(vmem_limit_bytes=32 << 20),
         cost_estimate=kernel_cost,
@@ -388,7 +405,7 @@
     @pl.when(step == 2 * tiles - 1)
     def _():
         middle[...] = middle_sum[...]
-        out[...] = out_sum[...]
+        out[...] = out_sum[...].astype(bf16)
 
 
 def mlp_block(rows, back, own_in, other_in, own_down, other_down):
@@ -417,7 +434,8 @@
             pl.BlockSpec((tile, width), lambda step: (other_tile(step), 0)),
         ],
         out_specs=[tiled] * 3 + [whole] * 2,
-        out_shape=[pltpu.HBM((count, 2 * units), bf16)] * 3 + [pltpu.HBM((count, width), f32)] * 2,
+        out_shape=[pltpu.HBM((count, 2 * units), bf16)] * 3
+        + [pltpu.HBM((count, width), f32), pltpu.HBM((count, width), bf16)],
         scratch_shapes=[pltpu.VMEM((count, width), f32)] * 2,
         compiler_params=pltpu.CompilerParams(vmem_limit_bytes=40 << 20),
         cost_estimate=kernel_cost,
@@ -425,25 +443,27 @@
     )(rows, back, own_in, other_in, own_down, other_down)
 
 
-def weight_grad_kernel(count, filled, *refs):
+def weight_grad_kernel(count, kinds, weighted, *refs):
     lefts, rights = refs[:count], refs[count : 2 * count]
-    own, other = refs[2 * count + 2 * filled :]
+    outs = refs[2 * count + weighted :]
     total = dot_tn(lefts[0][...], rights[0][...])
     for left, right in zip(lefts[1:], rights[1:]):
         total = total + dot_tn(left[...], right[...])
-    kinds, half, _ = own.shape
+    half = outs[0].shape[0]
     for kind in range(kinds):
         start = 2 * kind * half
-        own[kind] = total[start : start + half]
-        other[kind] = total[start + half : start + 2 * half].astype(bf16)
-
-
-def weight_grad(lefts, rights, kinds, slots=1, slot=0, filled=()):
+        outs[kind][...] = total[start : start + half]
+        outs[kinds + kind][...] = total[start + half : start + 2 * half].astype(bf16)
+    if weighted:
+        weight = refs[2 * count][...]
+        outs[2 * kinds][...] = jnp.sum(total * weight.astype(f32), axis=0, keepdims=True)
+
+
+def weight_grad(lefts, rights, kinds, weight=None):
     count = len(rights)
     rows, width = rights[0].shape
     columns = lefts[0].shape[1]
     half, tile = columns // kinds // 2, min(512, width)
-
     joined = len(lefts) == 1
 
     def left_spec(at):
@@ -451,23 +471,75 @@
         return pl.BlockSpec((rows, columns), lambda step: (block, 0))
 
     lefts = list(lefts) * (count if joined else 1)
-    out_spec = pl.BlockSpec((kinds, half, tile), lambda step: (slot, 0, step))
-    return pl.pallas_call(
-        partial(weight_grad_kernel, count, len(filled) // 2),
+    weights = [] if weight is None else [weight]
+    made = pl.pallas_call(
+        partial(weight_grad_kernel, count, kinds, len(weights)),
         grid=(width // tile,),
         in_specs=[left_spec(at) for at in range(count)]
         + [pl.BlockSpec((rows, tile), lambda step: (0, step))] * count
-        + [pl.BlockSpec(memory_space=pl.ANY)] * len(filled),
-        out_specs=[out_spec] * 2,
-        out_shape=[
-            pltpu.HBM((slots * kinds, half, width), f32),
-            pltpu.HBM((slots * kinds, half, width), bf16),
-        ],
-        input_output_aliases={2 * count + at: at for at in range(len(filled))},
+        + [pl.BlockSpec((columns, tile), lambda step: (0, step))] * len(weights),
+        out_specs=[pl.BlockSpec((half, tile), lambda step: (0, step))] * (2 * kinds)
+        + [pl.BlockSpec((1, tile), lambda step: (0, step))] * len(weights),
+        out_shape=[pltpu.HBM((half, width), f32)] * kinds
+        + [pltpu.HBM((half, width), bf16)] * kinds
+        + [jax.ShapeDtypeStruct((1, width), f32)] * len(weights),
         compiler_params=pltpu.CompilerParams(vmem_limit_bytes=40 << 20),
         cost_estimate=kernel_cost,
         name="weight_grad",
-    )(*lefts, *rights, *filled)
+    )(*lefts, *rights, *weights)
+    return list(zip(made[:kinds], made[kinds : 2 * kinds])), made[2 * kinds :]
+
+
+def row_dot_kernel(rows, weight, out):
+    out[...] = dot(rows[...], weight[...]).astype(out.dtype)
+
+
+def row_dot(rows, weight, block, count, kind=f32):
+    depth, width = weight.shape
+    size, tile = rows.shape[0] // count, min(512, width)
+    return pl.pallas_call(
+        row_dot_kernel,
+        grid=(width // tile,),
+        in_specs=[
+            pl.BlockSpec((size, depth), lambda step: (block, 0)),
+            pl.BlockSpec((depth, tile), lambda step: (0, step)),
+        ],
+        out_specs=pl.BlockSpec((size, tile), lambda step: (0, step)),
+        out_shape=pltpu.HBM((size, width), kind),
+        compiler_params=pltpu.CompilerParams(vmem_limit_bytes=32 << 20),
+        cost_estimate=kernel_cost,
+        name="row_dot",
+    )(rows, weight)
+
+
+def join_kernel(count, tiles, *refs):
+    out = refs[2 * count]
+    for at in range(count):
+
+        @pl.when(pl.program_id(0) // tiles == at)
+        def _(at=at):
+            out[...] = (refs[2 * at][...] + refs[2 * at + 1][...].astype(f32)).astype(bf16)
+
+
+def join(*pairs):
+    count = len(pairs)
+    rows, width = pairs[0][0].shape
+    tile = 128 if rows % 128 == 0 else rows // 2
+    tiles = rows // tile
+
+    def spec(at):
+        return pl.BlockSpec((tile, width), lambda step: (jnp.clip(step - at * tiles, 0, tiles - 1), 0))
+
+    return pl.pallas_call(
+        partial(join_kernel, count, tiles),
+        grid=(count * tiles,),
+        in_specs=[spec(at) for at in range(count) for _ in range(2)],
+        out_specs=pl.BlockSpec((tile, width), lambda step: (step, 0)),
+        out_shape=pltpu.HBM((count * rows, width), bf16),
+        compiler_params=pltpu.CompilerParams(vmem_limit_bytes=40 << 20),
+        cost_estimate=kernel_cost,
+        name="join",
+    )(*[value for pair in pairs for value in pair])
 
 
 def block_diagonal(weight):
@@ -496,25 +568,6 @@
     return jnp.concatenate(forward, axis=0), jnp.concatenate(back, axis=0)
 
 
-def unpack_gates(packed, channels, block_width):
-    tiles = gate_tiles(channels, block_width, 128)
-    kinds = []
-    for column in (0, 128):
-        blocks = []
-        for base in range(0, channels, block_width):
-            pieces = []
-            for start, stop, low, _, at in tiles:
-                left, right = max(start, base), min(stop, base + block_width)
-                if left < right:
-                    row = at + base - low
-                    pieces.append(
-                        packed[row : row + block_width, column + left - start : column + right - start]
-                    )
-            blocks.append(jnp.concatenate(pieces, axis=1))
-        kinds.append(jnp.stack(blocks))
-    return jnp.stack(kinds)
-
-
 def narrow_whole(weight, dim):
     return lax.all_gather(weight, "narrow", axis=dim, tiled=True)
 
@@ -524,9 +577,12 @@
 
 
 class DirectSum:
-    def __init__(self, grad):
+    def __init__(self, grad, got=()):
         self.size = lax.axis_size("narrow")
-        self.grad, self.got = grad, {}
+        self.grad, self.got = grad, list(got)
+
+    def state(self):
+        return self.grad, self.got
 
     def piece(self, flip):
         span = self.grad.shape[1] // self.size
@@ -536,10 +592,10 @@
     def send(self, flips):
         for flip in flips:
             pairs = [(at, at ^ flip) for at in range(self.size)]
-            self.got[flip] = lax.ppermute(self.piece(flip), "narrow", pairs)
+            self.got.append(lax.ppermute(self.piece(flip), "narrow", pairs))
 
     def total(self):
-        return plus(self.piece(0).astype(f32), *self.got.values())
+        return plus(self.piece(0), *self.got)
 
 
 def swap_cores(values, wide):
@@ -551,8 +607,8 @@
 
 
 class Chips:
-    def __init__(self, wide, chip):
-        self.chip, self.count = chip, wide // 2
+    def __init__(self, wide, place):
+        self.place, self.chip, self.count = place, place[0], wide // 2
         self.wide = wide
 
     def move(self, values, pairs):
@@ -584,6 +640,39 @@
         return self.move(right, to_right), self.move(left, to_left)
 
 
+def advance_kernel(place, end_part, end_moved, mid_part, mid_moved, end, mid, *, inner):
+    added = end_part[...].astype(f32) + end_moved[...].astype(f32)
+    mid[...] = (mid_part[...].astype(f32) + mid_moved[...].astype(f32)).astype(bf16)
+    if inner:
+        edge = (place[0] == 0) | (place[0] == 3)
+
+        @pl.when(edge)
+        def _():
+            end[...] = end_part[...].astype(bf16)
+
+        @pl.when(jnp.logical_not(edge))
+        def _():
+            end[...] = end_moved[...]
+    else:
+        end[...] = added.astype(bf16)
+
+
+def advance(place, end_part, end_moved, mid_part, mid_moved, inner):
+    rows, width = end_moved.shape
+    tile = min(64, rows)
+    spec = pl.BlockSpec((tile, width), lambda step, place: (step, 0))
+    return pl.pallas_call(
+        partial(advance_kernel, inner=inner),
+        grid_spec=pltpu.PrefetchScalarGridSpec(
+            num_scalar_prefetch=1, grid=(rows // tile,), in_specs=[spec] * 4, out_specs=[spec] * 2
+        ),
+        out_shape=[pltpu.HBM((rows, width), bf16)] * 2,
+        compiler_params=pltpu.CompilerParams(vmem_limit_bytes=32 << 20),
+        cost_estimate=kernel_cost,
+        name="advance",
+    )(place, end_part, end_moved, mid_part, mid_moved)
+
+
 class Exchange:
     def __init__(self, line, rows):
         self.line, self.own = line, rows
@@ -591,7 +680,7 @@
         if self.packed:
             self.odd = line.chip % 2 == 1
             self.edge = (line.chip == 0) | (line.chip == 3)
-        self.ends, self.mids = [], []
+        self.ends, self.mids, self.chosen = [], [], ()
         self.backs, self.moved = {0: (rows, rows)}, (0.0, 0.0)
 
     def pair(self, end, mid):
@@ -615,24 +704,34 @@
             part = jnp.where(line.chip == 0, parts[1], parts[3]).astype(bf16)
             self.pair(jnp.where(self.edge, part, self.mids[0]), self.ends[0])
         elif number == 3:
-            mid = plus(parts[2], self.ends[1]).astype(bf16)
-            self.pair(jnp.where(self.edge, parts[2].astype(bf16), self.mids[1]), mid)
+            self.pair(*advance(line.place, parts[2], self.mids[1], parts[2], self.ends[1], True))
+            self.chosen = (
+                jnp.where(self.odd, parts[1], parts[3]),
+                jnp.where(line.chip == 1, parts[3], parts[1]),
+            )
         else:
-            end = plus(jnp.where(self.odd, parts[1], parts[3]), self.mids[2])
-            mid = plus(jnp.where(line.chip == 1, parts[3], parts[1]), self.ends[2])
-            self.pair(end.astype(bf16), mid.astype(bf16))
+            self.pair(
+                *advance(line.place, self.chosen[0], self.mids[2], self.chosen[1], self.ends[2], False)
+            )
 
     def fence(self, *values):
-        state = (self.ends, self.mids, self.backs, self.moved)
+        state = (self.ends, self.mids, self.chosen, self.backs, self.moved)
         state, values = fence(state, values)
-        self.ends, self.mids, self.backs, self.moved = state
+        self.ends, self.mids, self.chosen, self.backs, self.moved = state
         return values
+
+    def arrived(self, number):
+        if self.packed:
+            if number == 1:
+                return self.ends[0]
+            if number == 2:
+                return jnp.where(self.edge, self.ends[1], self.mids[1])
+            return jnp.where(self.edge, self.ends[2], self.mids[0])
+        return self.rows()[number] if number < self.line.count else None
 
     def rows(self):
         if self.packed:
-            far = jnp.where(self.edge, self.ends[2], self.mids[0])
-            two = jnp.where(self.edge, self.ends[1], self.mids[1])
-            near = self.ends[0]
+            near, two, far = (self.arrived(number) for number in (1, 2, 3))
             return [self.own, jnp.where(self.odd, near, far), two, jnp.where(self.odd, far, near)]
         rights, lefts = ({at: pair[way] for at, pair in self.backs.items()} for way in range(2))
         hops = range(1, self.line.count)
@@ -645,28 +744,22 @@
 
 
 def plus(total, *moved):
+    total = total.astype(f32)
     for values in moved:
-        total = total + values.astype(f32)
+        total = total + (values.astype(f32) if isinstance(values, jax.Array) else values)
     return total
 
 
-def paired_sum(values, axis):
+def paired_step(values, axis, bit):
     size = lax.axis_size(axis)
-    if size & (size - 1):
-        return lax.psum(values, axis)
-    bit = 1
-    while bit < size:
-        values = values + lax.ppermute(values, axis, [(at, at ^ bit) for at in range(size)])
-        bit *= 2
-    return values
-
-
-def direct_sum(values, axis):
+    return values + lax.ppermute(values, axis, [(at, at ^ bit) for at in range(size)])
+
+
+def direct_sum(values, axis, stride=1):
     size = lax.axis_size(axis)
-    if size & (size - 1):
-        return lax.psum(values, axis)
     terms = [values] + [
-        lax.ppermute(values, axis, [(at, at ^ flip) for at in range(size)]) for flip in range(1, size)
+        lax.ppermute(values, axis, [(at, at ^ flip) for at in range(size)])
+        for flip in range(stride, size, stride)
     ]
     while len(terms) > 1:
         terms = [left + right for left, right in zip(terms[::2], terms[1::2])]
@@ -711,7 +804,7 @@
     block_width = rate_weight.shape[1]
     seq_half = seq_count // 2
     block_shape = (2, seq_half, local_len, 2 * channels)
-    line = Chips(wide, chip)
+    line = Chips(wide, place)
     last = chips - 1
 
     def swap(values):
@@ -753,12 +846,11 @@
         (conv_weight, conv_bias[None], rate_bias[None], input_bias[None], decay_param[None]), axis=0
     )
     norm_in, params, cotangent = fence(norm_in, params, cotangent)
-    rows_first = [norm_in]
-    pre_blocks = []
 
     def project(rows):
         return dot_nt(rows, whole_in).reshape(2, seq_half, local_len, 4 * channels)
 
+    rows_first = [norm_in]
     for hop in range(1, chips):
         moved = line.ring(rows_first[-1])
         if hop == 1:
@@ -789,13 +881,18 @@
     )
     mixed_rows = mixed.reshape(chips, -1, 2 * channels)
     parts = {hop: dot(mixed_rows[hop], whole_out) for hop in (1, last)}
-    parts, mixed_rows = lanes.fence(parts, mixed_rows)
+    parts, mixed_rows, final_state, conv_state = lanes.fence(
+        parts, mixed_rows, final_state, conv_state
+    )
     for step in range(2, chips + 1):
         lanes.step(step, parts)
         for hop in (step, chips - step):
             if hop < chips and hop not in parts:
                 parts[hop] = dot(mixed_rows[hop], whole_out)
-        if step == chips - 1:
+        if step == 2:
+            final_state, conv_state = by_channel(final_state), by_channel(conv_state)
+            parts, final_state, conv_state = lanes.fence(parts, final_state, conv_state)
+        elif step == chips - 1:
             if 0 not in parts:
                 parts[0] = dot(mixed_rows[0], whole_out)
             parts, own_mlp_in = lanes.fence(parts, own_mlp_in)
@@ -827,9 +924,9 @@
             total = parts[hop] if sums is None else plus(parts[hop], sums)
             total_b = total.astype(bf16)
     sums = line.ring(total_b)
-    grads_mlp = weight_grad(gate_grads, rows_second, 1, slots=2)
-    grads_down = weight_grad(hidden, rows_back, 1)
-    sums, grads_mlp, grads_down, up_grads = fence(sums, grads_mlp, grads_down, up_grads)
+    [grads_gate], _ = weight_grad(gate_grads, rows_second, 1)
+    [grads_down], _ = weight_grad(hidden, rows_back, 1)
+    sums, grads_gate, grads_down, up_grads = fence(sums, grads_gate, grads_down, up_grads)
     mid_sum = plus(parts[0], sums)
 
     from_norm, gain_two = norm_backward(resid, scale_two, second_gain, mid_sum)
@@ -837,100 +934,114 @@
     resid_grad_b = resid_grad.astype(bf16)
     resid_grad_b, up_grads, outs = fence(resid_grad_b, up_grads, outs)
 
-    def shared(grads):
-        own, other = grads
-        return (own + swap(other).astype(f32)).astype(bf16).reshape(-1, width)
-
     def back_block(rows):
         return dot_nt(rows, whole_out).reshape(2, seq_half, local_len, 2 * channels)
 
     lanes = Exchange(line, resid_grad_b)
     lanes.step(1, None)
-    grads_mlp = weight_grad(up_grads, rows_second, 1, slots=2, slot=1, filled=grads_mlp)
-    grads_mlp, outs = lanes.fence(grads_mlp, outs)
+    [grads_up], _ = weight_grad(up_grads, rows_second, 1)
+    from_down = swap(grads_down[1])
+    grads_up, from_down, outs = lanes.fence(grads_up, from_down, outs)
+    back_blocks = [back_block(resid_grad_b)]
     for step in range(2, chips + 1):
         lanes.step(step, outs)
         if step == 2:
-            part_mlp_in = shared(grads_mlp)
-            part_mlp_in, grads_down = lanes.fence(part_mlp_in, grads_down)
+            part_down = join((grads_down[0], from_down))
+            from_gate, from_up = swap(grads_gate[1]), swap(grads_up[1])
+            part_down, from_gate, from_up = lanes.fence(part_down, from_gate, from_up)
+            grad_mlp_down = narrow_sum(part_down, 1)
+        elif step == 3:
+            part_mlp_in = join((grads_gate[0], from_gate), (grads_up[0], from_up))
+            if lanes.packed:
+                back_blocks += [back_block(lanes.arrived(at)) for at in (1, 2)]
+            part_mlp_in, back_blocks = lanes.fence(part_mlp_in, back_blocks)
             grad_mlp_in = narrow_sum(part_mlp_in, 1)
-        elif step == 3:
-            part_down = shared(grads_down)
-            back_blocks = [back_block(resid_grad_b)]
-            part_down, back_blocks = lanes.fence(part_down, back_blocks)
-            grad_mlp_down = narrow_sum(part_down, 1)
         elif step < chips:
             lanes.fence()
-    rows_resid = lanes.rows()
-    back_blocks += [back_block(rows) for rows in rows_resid[1:]]
-    grads, small, gate_sums = mixer_backward(
-        pre_blocks, back_blocks, (conv, rate_gate, in_gate, states),
+    if lanes.packed:
+        back_blocks.append(back_block(lanes.arrived(3)))
+    else:
+        back_blocks += [back_block(rows) for rows in lanes.rows()[1:]]
+    grads, small, gate_grads = mixer_backward(
+        pre_blocks, back_blocks, lanes.packed, (conv, rate_gate, in_gate, states),
         lengths, place, params[:4], gate_back, rate_scale, block_width,
     )
-    grad_rows = grads.reshape(chips, -1, 4 * channels)
-    sent = dot(grad_rows[1], whole_in).astype(bf16)
-    sent, grads, small, gate_sums, mixed, grad_mlp_in = lanes.fence(
-        sent, grads, small, gate_sums, mixed, grad_mlp_in
+    grad_rows = grads.reshape(-1, 4 * channels)
+    part = row_dot(grad_rows, whole_in, 1, chips, bf16)
+    part, grad_rows, small, gate_grads, mixed, grad_mlp_down = lanes.fence(
+        part, grad_rows, small, gate_grads, mixed, grad_mlp_down
     )
-    output = (resid + lanes.total(outs[0])).astype(bf16)
-
-    grad_rows = grads.reshape(chips, -1, 4 * channels)
+
+    size = lax.axis_size("narrow")
+    split = size // 2 + 1
     count = rate_weight.shape[0]
-    size = lax.axis_size("narrow")
+
+    def gate_rows(gates, sums):
+        return jnp.concatenate((gates.reshape(-1, block_width), sums.reshape(-1, block_width)), axis=0)
+
+    gate_mine = gate_rows(gate_grads[:count], small[:, :channels])
+    gate_other = gate_rows(gate_grads[count:], small[:, channels:])
+    sent = part
     for hop in range(1, chips):
         moving = line.ring(sent)
-        part = dot(grad_rows[(hop + 1) % chips], whole_in)
+        part = row_dot(grad_rows, whole_in, (hop + 1) % chips, chips)
         if hop == 1:
-            grads_in = weight_grad([grads.reshape(-1, 4 * channels)], rows_first, 2)
-            part_in = shared(grads_in)
-            gate_grads = unpack_gates(gate_sums, 2 * channels, block_width)
-            mine = jnp.concatenate((small[:, :channels].reshape(-1), gate_grads[:, :count].reshape(-1)))
-            other = jnp.concatenate((small[:, channels:].reshape(-1), gate_grads[:, count:].reshape(-1)))
-            part_in, moving, part, mixed, mine, other, output = fence(
-                part_in, moving, part, mixed, mine, other, output
+            grads_in, [gain_one] = weight_grad([grad_rows], rows_first, 2, weight=whole_in)
+            [grads_out], _ = weight_grad([mixed.reshape(-1, 2 * channels)], lanes.rows(), 1)
+            gate_sum = (gate_mine + swap(gate_other.astype(bf16)).astype(f32)).astype(bf16)
+            grads_in, grads_out, gain_one, moving, part, gate_sum, resid = fence(
+                grads_in, grads_out, gain_one, moving, part, gate_sum, resid
             )
         elif hop == 2:
-            sum_in = DirectSum(part_in)
-            sum_in.send(range(1, size))
-            grads_out = weight_grad([mixed.reshape(-1, 2 * channels)], rows_resid, 1)
-            part_out = shared(grads_out)
-            own_rows = own_in.reshape(-1, width).astype(f32)
-            gain_one = jnp.sum(own_rows * part_in.astype(f32), axis=0) / first_gain
-            flat = mine + swap(other)
-            part_out, moving, part, flat, gain_one, sum_in.got, grad_mlp_down = fence(
-                part_out, moving, part, flat, gain_one, sum_in.got, grad_mlp_down
+            parts = join(*[(own, swap(other)) for own, other in (*grads_in, grads_out)])
+            gains = jnp.concatenate((gain_one / first_gain, gain_two[None]), axis=0)
+            gains = direct_sum(gains, "narrow")
+            gate_sum = paired_step(gate_sum, "narrow", 1)
+            parts, moving, part, grad_mlp_in, gains, gate_sum, resid = fence(
+                parts, moving, part, grad_mlp_in, gains, gate_sum, resid
             )
         elif hop == last:
-            sum_out = DirectSum(part_out)
-            sum_out.send(range(1, size))
-            flat = paired_sum(flat, "narrow")
-            gains = direct_sum(jnp.stack((gain_one, gain_two)), "wide")
-            moving, gains, flat, sum_out.got = fence(moving, gains, flat, sum_out.got)
+            sum_proj = DirectSum(parts)
+            sum_proj.send(range(1, split))
+            output = by_position((resid + lanes.total(outs[0])).astype(bf16))
+            bit = 2
+            while bit < size:
+                gate_sum = paired_step(gate_sum, "narrow", bit)
+                bit *= 2
+            moving, sum_proj.got, parts, gains, gate_sum, output = fence(
+                moving, sum_proj.got, parts, gains, gate_sum, output
+            )
         sent = plus(part, moving).astype(bf16)
     in_sum = plus(part, moving)
-    gains = direct_sum(gains, "narrow")
-    grad_mlp_in, grad_mlp_down = grad_mlp_in.astype(f32), grad_mlp_down.astype(f32)
-    grad_proj_in = sum_in.total().reshape(2, channels, -1)
-    grad_proj_out = sum_out.total()
+    sum_proj.grad = parts
+    sum_proj.send(range(split, size))
+    gains = gains + swap(gains)
+    gains = direct_sum(gains, "wide", 2)
     from_norm, _ = norm_backward(tokens_f, scale_one, first_gain, in_sum)
     grad_tokens = (resid_grad + from_norm).astype(bf16)
-    sums = flat[: 8 * channels].reshape(8, channels)
-    grad_rate_weight, grad_input_weight = flat[8 * channels :].reshape(2, *rate_weight.shape)
+    grad_tokens, gains = fence(grad_tokens, gains)
+    grad_proj = sum_proj.total()
+    gate_sum = gate_sum.astype(f32)
+    gate_grads = gate_sum[: count * 2 * block_width].reshape(count, 2, block_width, block_width)
+    small = gate_sum[count * 2 * block_width :].reshape(8, channels)
+    grad_mlp_in, grad_mlp_down = grad_mlp_in.astype(f32), grad_mlp_down.astype(f32)
+    grad_proj_in = grad_proj[: 2 * channels].reshape(2, channels, -1)
+    grad_proj_out = grad_proj[2 * channels :]
     grad_mlp_in = grad_mlp_in.reshape(2, mlp_in.shape[2], -1)
     return (
-        by_position(output),
+        output,
         by_position(grad_tokens),
-        by_channel(final_state),
-        by_channel(conv_state),
+        final_state,
+        conv_state,
         gains[0],
         jnp.swapaxes(grad_proj_in, 1, 2),
-        sums[4:8],
-        sums[3],
-        grad_rate_weight,
-        sums[0],
-        grad_input_weight,
-        sums[1],
-        sums[2] * decay_scale * jax.nn.sigmoid(-decay_param),
+        small[4:8],
+        small[3],
+        gate_grads[:, 0],
+        small[0],
+        gate_grads[:, 1],
+        small[1],
+        small[2] * decay_scale * jax.nn.sigmoid(-decay_param),
         grad_proj_out,
         gains[1],
         jnp.swapaxes(grad_mlp_in, 1, 2),

time: 708 us -> 665 us (0.939)
  waiting for transfers between devices: 298 us -> 243 us
  Pallas kernels: 146 us -> 194 us
  other arithmetic: 90.7 us -> 54.1 us
  local copies, waits for them, and re-layouts: 41.5 us -> 54.8 us
  matrix products: 44 us -> 32.1 us
    pallas_call x6 -> x17, Pallas kernels: 61.3 us -> 111 us  [the longest x5 40.9 us: weight_grad(): pl.pallas_call(partial(weight_grad_kernel, count, kinds, len(weights)), g...]
    ppermute x8 -> x5, waiting for transfers between devices: 48.5 us -> 19.8 us  [the longest x2 17.8 us: paired_step(): lax.ppermute(values, axis, [(at, at ^ bit) for at in range(size)])]
    convert_element_type x7 -> x3, other arithmetic: 31.1 us -> 3.73 us  [the longest x1 1.88 us: body(): output = by_position((resid + lanes.total(outs[0])).astype(bf16))]
    dot_general x8 -> x4, matrix products: 26.4 us -> 7.34 us  [dot(): return jnp.dot(left, right, preferred_element_type=f32)]
    ppermute x17 -> x20, waiting for transfers between devices: 18.5 us -> 4.24 us  [swap_cores(): return lax.ppermute(values, 'wide', [(at, at ^ 1) for at in range(wide)])]
    unnamed x249 -> x259, local copies, waits for them, and re-layouts: 22.8 us -> 33.3 us
    ppermute x10 -> x6, waiting for transfers between devices: 18.9 us -> 8.84 us  [direct_sum(): lax.ppermute(values, axis, [(at, at ^ flip) for at in range(size)])]
    reshape x2 -> x0, other arithmetic: 7.52 us -> none  [shared(): return (own + swap(other).astype(f32)).astype(bf16).reshape(-1, width)]
  transfers between devices with their start and end apart: 69 -> 65, of which waited for: 26 -> 25; matrix products, arithmetic and copies ran while one was open for 22% -> 15% of each run, Pallas kernels for 21% -> 30%
where the time goes in v3:
time: 665 us; the launch traced here: 656 us
  waiting for transfers between devices  243 us (37%)
  Pallas kernels  194 us (29%)
  starting transfers between devices  61.6 us (9%)
  local copies, waits for them, and re-layouts  54.8 us (8%)
  other arithmetic  54.1 us (8%)
  matrix products  32.1 us (5%)
  between operations  16.1 us (2%)
    ppermute x28, waiting for transfers between devices, move(): return lax.ppermute(values, 'wide', devices)  208 us
    pallas_call x4, Pallas kernels, mlp_block(): pl.pallas_call(partial(mlp_kernel, tiles), grid=(2 * tiles,), in_specs=[w...  68 us
    ppermute x28, starting transfers between devices, move(): return lax.ppermute(values, 'wide', devices)  44.3 us
    pallas_call x5, Pallas kernels, weight_grad(): pl.pallas_call(partial(weight_grad_kernel, count, kinds, len(weights)), g...  40.9 us
    unnamed x259, local copies, waits for them, and re-layouts  33.3 us
    dot_general x8, matrix products, dot_nt(): lax.dot_general(left, right, (((1,), (1,)), ((), ())), preferred_element_...  24.7 us
    pallas_call x1, Pallas kernels, mixer_backward(): pl.pallas_call(partial(mixer_backward_kernel, chips, block_width, crossed...  21.4 us
    pallas_call x3, Pallas kernels, join(): pl.pallas_call(partial(join_kernel, count, tiles), grid=(count * tiles,),...  21.1 us
  transfers between devices with their start and end apart: 65, of which 25 were waited for; matrix products, arithmetic and copies ran while one was open for 15% of the time, Pallas kernels for 30%

profile of v3, /device:TPU:0, one launch (start us, length us, event | category | flops | bytes accessed | tf_op | source)
XLA Modules:
  0.0 656.3 jit_solution(16155196352881784122)
XLA Ops:
  16.1 2.6 collective-permute-start.2
  20.3 24.3 %collective-permute-done.2.refs_5_ = bf16[256,2048]{1,0:T(8,128)(2,1)S(1)} collective-permute-done((bf16[256,2048]{1,0:T(8,128)(2,1)S(1)}, bf16[256,2048]{1,0:T(8,128)(2,1)S(1)}, u32[]{:S(2)}, u32[]{:S(2)}) %collective-permute-start.2) | collective-permute-done | bytes 1048608 | tf_op jit(solution)/shard_map/ppermute | solution.py:616
  44.6 26.8 %collective-permute-done.4.refs_6_ = bf16[256,2048]{1,0:T(8,128)(2,1)} collective-permute-done((bf16[256,2048]{1,0:T(8,128)(2,1)S(1)}, bf16[256,2048]{1,0:T(8,128)(2,1)}, u32[]{:S(2)}, u32[]{:S(2)}) %collective-permute-start.4) | collective-permute-done | bytes 1048608 | tf_op jit(solution)/shard_map/ppermute | solution.py:616
  74.2 2.5 collective-permute-done.6
  78.8 3.7 convolution_bitcast_fusion.1.refs_2_
  82.4 2.6 convolution_bitcast_fusion.2.refs_1_
  85.1 2.7 convolution_bitcast_fusion.3.refs_0_
  87.8 11.5 %collective-permute-done.5.refs_7_ = bf16[256,2048]{1,0:T(8,128)(2,1)} collective-permute-done((bf16[256,2048]{1,0:T(8,128)(2,1)}, bf16[256,2048]{1,0:T(8,128)(2,1)}, u32[]{:S(2)}, u32[]{:S(2)}) %collective-permute-start.5) | collective-permute-done | bytes 1048608 | tf_op jit(solution)/shard_map/ppermute | solution.py:616
  102.4 4.5 convolution_bitcast_fusion.refs_3_
  107.0 14.8 %mixer_forward.1 = (bf16[4,2,1,128,640]{4,3,2,1,0:T(8,128)(2,1)}, f32[4,2,1,128,640]{4,3,2,1,0:T(8,128)}, f32[4,2,1,128,640]{4,3,2,1,0:T(8,128)}, f32[4,2,1,128,...) custom-call(s32[2]{0:T(128)S(1)} %pad_add_fusion.place, ...), custom_call_target="tpu_custom_call" | custom-call | flops 1 | bytes 1 | tf_op jit(solution)/shard_map/mixer_forward/pallas_call | solution.py:308
  128.3 3.4 collective-permute-start.11
  134.7 20.3 %collective-permute-done.11.mid_moved = bf16[256,2048]{1,0:T(8,128)(2,1)S(1)} collective-permute-done((bf16[256,2048]{1,0:T(8,128)(2,1)S(1)}, bf16[256,2048]{1,0:T(8,128)(2,1)S(1)}, u32[]{:S(2)}, u32[]{:S(2)}) %collective-permute-start.11) | collective-permute-done | bytes 1048608 | tf_op jit(solution)/shard_map/ppermute | solution.py:616
  155.1 2.5 advance.4
  157.6 4.0 collective-permute-start.15
  163.2 4.4 fusion.31
  170.0 14.6 %collective-permute-done.15.mid_moved = bf16[256,2048]{1,0:T(8,128)(2,1)} collective-permute-done((bf16[256,2048]{1,0:T(8,128)(2,1)}, bf16[256,2048]{1,0:T(8,128)(2,1)}, u32[]{:S(2)}, u32[]{:S(2)}) %collective-permute-start.15) | collective-permute-done | bytes 1048608 | tf_op jit(solution)/shard_map/ppermute | solution.py:616
  187.8 4.4 advance.5
  192.2 3.7 collective-permute-start.17
  197.7 2.5 broadcast_select_fusion.5
  200.3 19.8 %collective-permute-done.17 = bf16[256,2048]{1,0:T(8,128)(2,1)} collective-permute-done((bf16[256,2048]{1,0:T(8,128)(2,1)}, bf16[256,2048]{1,0:T(8,128)(2,1)}, u32[]{:S(2)}, u32[]{:S(2)}) %collective-permute-start.17) | collective-permute-done | bytes 1048608 | tf_op jit(solution)/shard_map/ppermute | solution.py:616
  220.0 3.1 multiply_reduce_fusion.2
  225.8 3.9 collective-permute-start.19
  231.4 17.1 %mlp_block.4 = (bf16[256,1536]{1,0:T(8,128)(2,1)}, bf16[256,1536]{1,0:T(8,128)(2,1)}, bf16[256,1536]{1,0:T(8,128)(2,1)}, f32[256,2048]{1,0:T(8,128)}, bf16[256,2048]{1,0:T(8,128)(2,1)}) custom-call(bf16[256,2048]{1,0:T(8,128)(2,1)S(1)} %multiply_convert_fusion.rows.refs_4_, bf16[256,2048]{1,0:T(8,128)(2,1)S(1)} %fusion.10.back.refs_4_, ...), custom_call_target="tpu_custom_call" | custom-call | flops 1 | bytes 1 | tf_op jit(solution)/shard_map/mlp_block/pallas_call | solution.py:425
  248.5 4.8 collective-permute-done.19.rows.refs_5_
  255.3 16.8 %mlp_block.5 = (bf16[256,1536]{1,0:T(8,128)(2,1)}, bf16[256,1536]{1,0:T(8,128)(2,1)}, bf16[256,1536]{1,0:T(8,128)(2,1)}, f32[256,2048]{1,0:T(8,128)}, bf16[256,2048]{1,0:T(8,128)(2,1)}) custom-call(bf16[256,2048]{1,0:T(8,128)(2,1)S(1)} %collective-permute-done.19.rows.refs_5_, bf16[256,2048]{1,0:T(8,128)(2,1)S(1)} %copy-done.10, ...), custom_call_target="tpu_custom_call" | custom-call | flops 1 | bytes 1 | tf_op jit(solution)/shard_map/mlp_block/pallas_call | solution.py:425
  272.1 7.8 %collective-permute-done.22.rows.refs_6_ = bf16[256,2048]{1,0:T(8,128)(2,1)S(1)} collective-permute-done((bf16[256,2048]{1,0:T(8,128)(2,1)S(1)}, bf16[256,2048]{1,0:T(8,128)(2,1)S(1)}, u32[]{:S(2)}, u32[]{:S(2)}) %collective-permute-start.22) | collective-permute-done | bytes 1048608 | tf_op jit(solution)/shard_map/ppermute | solution.py:616
  283.4 17.0 %mlp_block.6 = (bf16[256,1536]{1,0:T(8,128)(2,1)}, bf16[256,1536]{1,0:T(8,128)(2,1)}, bf16[256,1536]{1,0:T(8,128)(2,1)}, f32[256,2048]{1,0:T(8,128)}, bf16[256,2048]{1,0:T(8,128)(2,1)}) custom-call(bf16[256,2048]{1,0:T(8,128)(2,1)S(1)} %collective-permute-done.22.rows.refs_6_, bf16[256,2048]{1,0:T(8,128)(2,1)S(1)} %broadcast_select_fusion.10.back.refs_6_, ...), custom_call_target="tpu_custom_call" | custom-call | flops 1 | bytes 1 | tf_op jit(solution)/shard_map/mlp_block/pallas_call | solution.py:425
  300.4 9.1 %collective-permute-done.24 = bf16[256,2048]{1,0:T(8,128)(2,1)S(1)} collective-permute-done((bf16[256,2048]{1,0:T(8,128)(2,1)S(1)}, bf16[256,2048]{1,0:T(8,128)(2,1)S(1)}, u32[]{:S(2)}, u32[]{:S(2)}) %collective-permute-start.24) | collective-permute-done | bytes 1048608 | tf_op jit(solution)/shard_map/ppermute | solution.py:616
  309.6 20.3 %collective-permute-done.23.rows.refs_7_ = bf16[256,2048]{1,0:T(8,128)(2,1)S(1)} collective-permute-done((bf16[256,2048]{1,0:T(8,128)(2,1)S(1)}, bf16[256,2048]{1,0:T(8,128)(2,1)S(1)}, u32[]{:S(2)}, u32[]{:S(2)}) %collective-permute-start.23) | collective-permute-done | bytes 1048608 | tf_op jit(solution)/shard_map/ppermute | solution.py:616
  331.8 17.1 %mlp_block.7 = (bf16[256,1536]{1,0:T(8,128)(2,1)}, bf16[256,1536]{1,0:T(8,128)(2,1)}, bf16[256,1536]{1,0:T(8,128)(2,1)}, f32[256,2048]{1,0:T(8,128)}, bf16[256,2048]{1,0:T(8,128)(2,1)}) custom-call(bf16[256,2048]{1,0:T(8,128)(2,1)S(1)} %collective-permute-done.23.rows.refs_7_, bf16[256,2048]{1,0:T(8,128)(2,1)S(1)} %get-tuple-element.319.back.refs_7_, ...), custom_call_target="tpu_custom_call" | custom-call | flops 1 | bytes 1 | tf_op jit(solution)/shard_map/mlp_block/pallas_call | solution.py:425
  348.8 7.7 %collective-permute-done.25 = bf16[256,2048]{1,0:T(8,128)(2,1)S(1)} collective-permute-done((bf16[256,2048]{1,0:T(8,128)(2,1)S(1)}, bf16[256,2048]{1,0:T(8,128)(2,1)S(1)}, u32[]{:S(2)}, u32[]{:S(2)}) %collective-permute-start.25) | collective-permute-done | bytes 1048608 | tf_op jit(solution)/shard_map/ppermute | solution.py:616
  359.0 9.0 %weight_grad.6 = (f32[768,2048]{1,0:T(8,128)}, bf16[768,2048]{1,0:T(8,128)(2,1)}) custom-call(bf16[256,1536]{1,0:T(8,128)(2,1)S(1)} %copy-done.47, bf16[256,1536]{1,0:T(8,128)(2,1)S(1)} %copy-done.50, bf16[256,1536]{1,0:T(8,128)(2,1)S(1)} %copy-done.52, bf16[256,1536]{1,0:T(8,128)(2,1)S(1)} %copy-done.54, bf16[256,2048]{1,0:T(8,128)(2,1)S(1)} %fusion.10.back.refs_4_, ...), custom_call_target="tpu_custom_call" | custom-call | flops 1 | bytes 1 | tf_op jit(solution)/shard_map/weight_grad/pallas_call | solution.py:475
  368.1 8.9 %weight_grad.5 = (f32[768,2048]{1,0:T(8,128)}, bf16[768,2048]{1,0:T(8,128)(2,1)}) custom-call(bf16[256,1536]{1,0:T(8,128)(2,1)S(1)} %copy-done.46, bf16[256,1536]{1,0:T(8,128)(2,1)S(1)} %copy-done.49, bf16[256,1536]{1,0:T(8,128)(2,1)S(1)} %copy-done.51, bf16[256,1536]{1,0:T(8,128)(2,1)S(1)} %copy-done.53, ...), custom_call_target="tpu_custom_call" | custom-call | flops 1 | bytes 1 | tf_op jit(solution)/shard_map/weight_grad/pallas_call | solution.py:475
  377.0 5.8 collective-permute-done.26
  387.3 9.0 %weight_grad.7 = (f32[768,2048]{1,0:T(8,128)}, bf16[768,2048]{1,0:T(8,128)(2,1)}) custom-call(bf16[256,1536]{1,0:T(8,128)(2,1)S(1)} %copy-done.43, bf16[256,1536]{1,0:T(8,128)(2,1)S(1)} %copy-done.44, bf16[256,1536]{1,0:T(8,128)(2,1)S(1)} %copy-done.45, bf16[256,1536]{1,0:T(8,128)(2,1)S(1)} %copy-done.48, ...), custom_call_target="tpu_custom_call" | custom-call | flops 1 | bytes 1 | tf_op jit(solution)/shard_map/weight_grad/pallas_call | solution.py:475
  396.3 15.2 %collective-permute-done.27 = bf16[256,2048]{1,0:T(8,128)(2,1)} collective-permute-done((bf16[256,2048]{1,0:T(8,128)(2,1)S(1)}, bf16[256,2048]{1,0:T(8,128)(2,1)}, u32[]{:S(2)}, u32[]{:S(2)}) %collective-permute-start.27) | collective-permute-done | bytes 1048608 | tf_op jit(solution)/shard_map/ppermute | solution.py:616
  413.5 3.5 collective-permute-start.30
  417.8 2.9 join.3
  420.7 20.2 %collective-permute-done.30.mid_moved = bf16[256,2048]{1,0:T(8,128)(2,1)S(1)} collective-permute-done((bf16[256,2048]{1,0:T(8,128)(2,1)}, bf16[256,2048]{1,0:T(8,128)(2,1)S(1)}, u32[]{:S(2)}, u32[]{:S(2)}) %collective-permute-start.30) | collective-permute-done | bytes 1048608 | tf_op jit(solution)/shard_map/ppermute | solution.py:616
  442.9 2.5 advance.6
  445.4 3.3 collective-permute-start.34
  452.8 3.0 copy-done.13
  455.8 11.8 %join.4 = bf16[1536,2048]{1,0:T(8,128)(2,1)} custom-call(f32[768,2048]{1,0:T(8,128)S(1)} %copy-done.13, bf16[768,2048]{1,0:T(8,128)(2,1)} %collective-permute-done.32.refs_1_, f32[768,2048]{1,0:T(8,128)} %get-tuple-element.387.refs_2_, bf16[768,2048]{1,0:T(8,128)(2,1)} %collective-permute-done.33.refs_3_), custom_call_target="tpu_custom_call" | custom-call | flops 1 | bytes 1 | tf_op jit(solution)/shard_map/join/pallas_call | solution.py:533
  467.6 4.1 fusion.73
  478.1 4.7 advance.7
  486.5 3.2 fusion.12
  490.3 21.4 %mixer_backward.1 = (bf16[4,2,1,128,1280]{4,3,2,1,0:T(8,128)(2,1)}, f32[8,640]{1,0:T(8,128)S(1)}, f32[4,2,160,160]{3,2,1,0:T(8,128)S(1)}) custom-call(s32[2]{0:T(128)S(1)} %pad_add_fusion.place, s32[1]{0:T(128)} %dynamic_slice.15.lengths, f32[2,1,128,1280]{3,2,1,0:T(8,128)S(1)} %copy-done.19, f32[2,1,128,1280]{3,2,1,0:T(8,128)S(1)} %copy-done.17, ...), custom_call_target="tpu_custom_call" | custom-call | flops 1 | bytes 1 | tf_op jit(solution)/shard_map/mixer_backward/pallas_call | solution.py:346
  514.0 3.3 row_dot.4
  524.1 2.6 copy-done.3
  526.6 3.5 row_dot.5
  530.2 2.5 copy-done.4
  532.7 9.1 %weight_grad.8 = (f32[320,2048]{1,0:T(8,128)}, f32[320,2048]{1,0:T(8,128)}, bf16[320,2048]{1,0:T(8,128)(2,1)}, bf16[320,2048]{1,0:T(8,128)(2,1)}, f32[1,2048]{1,0:T(1,128)S(1)}) custom-call(bf16[1024,1280]{1,0:T(8,128)(2,1)S(1)} %bitcast.114, bf16[1024,1280]{1,0:T(8,128)(2,1)S(1)} %bitcast.115, bf16[1024,1280]{1,0:T(8,128)(2,1)S(1)} %bitcast.116, ...), custom_call_target="tpu_custom_call" | custom-call | flops 1 | bytes 1 | tf_op jit(solution)/shard_map/weight_grad/pallas_call | solution.py:475
  541.8 4.8 weight_grad.9
  549.0 3.1 add_convert_fusion.2
  563.8 2.5 copy-done.5
  566.3 3.5 row_dot.6
  570.4 7.2 %collective-permute-done.47 = bf16[656,160]{1,0:T(8,128)(2,1)S(1)} collective-permute-done((bf16[656,160]{1,0:T(8,128)(2,1)S(1)}, bf16[656,160]{1,0:T(8,128)(2,1)S(1)}, u32[]{:S(2)}, u32[]{:S(2)}) %collective-permute-start.47) | collective-permute-done | bytes 209952 | tf_op jit(solution)/shard_map/ppermute | solution.py:755
  577.8 6.4 join.5
  584.2 3.1 constant_dynamic-slice_fusion.1
  589.2 2.8 add_convert_fusion.1
  596.8 2.5 copy-done.6
  599.3 3.5 row_dot.7
  606.9 10.6 %collective-permute-done.51 = bf16[656,160]{1,0:T(8,128)(2,1)} collective-permute-done((bf16[656,160]{1,0:T(8,128)(2,1)S(1)}, bf16[656,160]{1,0:T(8,128)(2,1)}, u32[]{:S(2)}, u32[]{:S(2)}) %collective-permute-start.51) | collective-permute-done | bytes 209952 | tf_op jit(solution)/shard_map/ppermute | solution.py:755
  634.5 3.2 collective-permute-done.56
  (478 shorter events, 137.1 us)
Async XLA Ops:
  7.2 64.2 %all-gather.5.cloned.1.call-start = ((), (), s32[]{:S(2)}) async-start(), calls=%async_computation.2 | async-start | bytes 3276800 | tf_op jit(solution)/shard_map/all_gather | solution.py:572
  7.9 79.9 %all-gather.7.cloned.1.call-start = ((), (), s32[]{:S(2)}) async-start(), calls=%async_computation.3 | async-start | bytes 1638400 | tf_op jit(solution)/shard_map/all_gather | solution.py:572
  8.7 161.3 %all-gather.9.cloned.1.call-start = ((), (), s32[]{:S(2)}) async-start(), calls=%async_computation.4 | async-start | bytes 7864320 | tf_op jit(solution)/shard_map/all_gather | solution.py:572
  9.5 190.8 %all-gather.11.cloned.1.call-start = ((), (), s32[]{:S(2)}) async-start(), calls=%async_computation.5 | async-start | bytes 3932160 | tf_op jit(solution)/shard_map/all_gather | solution.py:572
  10.4 3.7 collective-permute-start
  11.2 1.9 collective-permute-start.3
  15.6 4.4 collective-permute-start.1
  16.1 28.4 %collective-permute-start.2 = (bf16[256,2048]{1,0:T(8,128)(2,1)S(1)}, bf16[256,2048]{1,0:T(8,128)(2,1)S(1)}, u32[]{:S(2)}, u32[]{:S(2)}) collective-permute-start(bf16[256,2048]{1,0:T(8,128)(2,1)S(1)} %fusion.3.refs_4_), channel_id=1, source_target_pairs={{0,8},{4,12},{8,16},{12,20},{16,24},{20,28},{24,0},{28,4},{1,9},{5... | collective-permute-start | bytes 3145736 | tf_op jit(solution)/shard_map/ppermute | solution.py:616
  44.6 26.8 %collective-permute-start.4 = (bf16[256,2048]{1,0:T(8,128)(2,1)S(1)}, bf16[256,2048]{1,0:T(8,128)(2,1)}, u32[]{:S(2)}, u32[]{:S(2)}) collective-permute-start(bf16[256,2048]{1,0:T(8,128)(2,1)S(1)} %collective-permute-done.2.refs_5_), channel_id=1, source_target_pairs={{0,8},{4,12},{8,16},{12,20},{16,24},{20,28},{24,0},{28,4},{1,9},{5... | collective-permute-start | bytes 3145736 | tf_op jit(solution)/shard_map/ppermute | solution.py:616
  71.4 5.3 collective-permute-start.6
  71.4 446.8 %reduce-scatter.3.cloned.1.call-start = ((), (), s32[]{:S(2)}) async-start(), calls=%async_computation.6 | async-start | bytes 3932160 | tf_op jit(solution)/shard_map/reduce_scatter | solution.py:576
  71.6 27.8 %collective-permute-start.9 = (f32[8,320]{1,0:T(8,128)S(1)}, f32[8,320]{1,0:T(8,128)S(1)}, u32[]{:S(2)}, u32[]{:S(2)}) collective-permute-start(f32[8,320]{1,0:T(8,128)S(1)} %concatenate.93), channel_id=1, source_target_pairs={{0,4},{4,0},{8,12},{12,8},{16,20},{20,16},{24,28},{28,24},{1,5},{5... | collective-permute-start | bytes 30728 | tf_op jit(solution)/shard_map/ppermute | solution.py:602
  72.1 27.2 %collective-permute-start.5 = (bf16[256,2048]{1,0:T(8,128)(2,1)}, bf16[256,2048]{1,0:T(8,128)(2,1)}, u32[]{:S(2)}, u32[]{:S(2)}) collective-permute-start(bf16[256,2048]{1,0:T(8,128)(2,1)} %collective-permute-done.4.refs_6_), channel_id=1, source_target_pairs={{0,8},{4,12},{8,16},{12,20},{16,24},{20,28},{24,0},{28,4},{1,9},{5... | collective-permute-start | bytes 3145736 | tf_op jit(solution)/shard_map/ppermute | solution.py:616
  99.3 23.9 %collective-permute-start.10 = (bf16[320,2048]{1,0:T(8,128)(2,1)}, bf16[320,2048]{1,0:T(8,128)(2,1)}, u32[]{:S(2)}, u32[]{:S(2)}) collective-permute-start(bf16[320,2048]{1,0:T(8,128)(2,1)} %all-gather.7.cloned.1.call-done), channel_id=1, source_target_pairs={{0,4},{4,0},{8,12},{12,8},{16,20},{20,16},{24,28},{28,24},{1,5},{5... | collective-permute-start | bytes 3932168 | tf_op jit(solution)/shard_map/ppermute | solution.py:602
  101.1 25.6 %collective-permute-start.7 = (bf16[256,2048]{1,0:T(8,128)(2,1)S(1)}, bf16[256,2048]{1,0:T(8,128)(2,1)S(1)}, u32[]{:S(2)}, u32[]{:S(2)}) collective-permute-start(bf16[256,2048]{1,0:T(8,128)(2,1)S(1)} %fusion.10.back.refs_4_), channel_id=1, source_target_pairs={{0,8},{4,12},{8,0},{12,4},{16,24},{20,28},{24,16},{28,20},{1,9},{5... | collective-permute-start | bytes 3145736 | tf_op jit(solution)/shard_map/ppermute | solution.py:616
  101.2 25.6 %collective-permute-start.8 = (bf16[256,2048]{1,0:T(8,128)(2,1)S(1)}, bf16[256,2048]{1,0:T(8,128)(2,1)S(1)}, u32[]{:S(2)}, u32[]{:S(2)}) collective-permute-start(bf16[256,2048]{1,0:T(8,128)(2,1)S(1)} %fusion.10.back.refs_4_), channel_id=1, source_target_pairs={{8,16},{12,20},{16,8},{20,12},{9,17},{13,21},{17,9},{21,13},{10,18... | collective-permute-start | bytes 3145736 | tf_op jit(solution)/shard_map/ppermute | solution.py:616
  128.3 26.8 %collective-permute-start.11 = (bf16[256,2048]{1,0:T(8,128)(2,1)S(1)}, bf16[256,2048]{1,0:T(8,128)(2,1)S(1)}, u32[]{:S(2)}, u32[]{:S(2)}) collective-permute-start(bf16[256,2048]{1,0:T(8,128)(2,1)S(1)} %fusion.11), channel_id=1, source_target_pairs={{0,8},{4,12},{8,0},{12,4},{16,24},{20,28},{24,16},{28,20},{1,9},{5... | collective-permute-start | bytes 3145736 | tf_op jit(solution)/shard_map/ppermute | solution.py:616
  131.7 23.3 %collective-permute-start.12 = (bf16[256,2048]{1,0:T(8,128)(2,1)S(1)}, bf16[256,2048]{1,0:T(8,128)(2,1)S(1)}, u32[]{:S(2)}, u32[]{:S(2)}) collective-permute-start(bf16[256,2048]{1,0:T(8,128)(2,1)S(1)} %collective-permute-done.7), channel_id=1, source_target_pairs={{8,16},{12,20},{16,8},{20,12},{9,17},{13,21},{17,9},{21,13},{10,18... | collective-permute-start | bytes 3145736 | tf_op jit(solution)/shard_map/ppermute | solution.py:616
  132.5 2.2 collective-permute-start.14
  157.6 27.0 %collective-permute-start.15 = (bf16[256,2048]{1,0:T(8,128)(2,1)}, bf16[256,2048]{1,0:T(8,128)(2,1)}, u32[]{:S(2)}, u32[]{:S(2)}) collective-permute-start(bf16[256,2048]{1,0:T(8,128)(2,1)} %get-tuple-element.267), channel_id=1, source_target_pairs={{0,8},{4,12},{8,0},{12,4},{16,24},{20,28},{24,16},{28,20},{1,9},{5... | collective-permute-start | bytes 3145736 | tf_op jit(solution)/shard_map/ppermute | solution.py:616
  161.5 23.1 %collective-permute-start.16 = (bf16[256,2048]{1,0:T(8,128)(2,1)}, bf16[256,2048]{1,0:T(8,128)(2,1)}, u32[]{:S(2)}, u32[]{:S(2)}) collective-permute-start(bf16[256,2048]{1,0:T(8,128)(2,1)} %get-tuple-element.269), channel_id=1, source_target_pairs={{8,16},{12,20},{16,8},{20,12},{9,17},{13,21},{17,9},{21,13},{10,18... | collective-permute-start | bytes 3145736 | tf_op jit(solution)/shard_map/ppermute | solution.py:616
  184.6 46.8 %collective-permute-start.20 = (bf16[2,2048,768]{2,1,0:T(8,128)(2,1)}, bf16[2,2048,768]{2,1,0:T(8,128)(2,1)}, u32[]{:S(2)}, u32[]{:S(2)}) collective-permute-start(bf16[2,2048,768]{2,1,0:T(8,128)(2,1)} %all-gather.9.cloned.1.call-done.own_in), channel_id=1, source_target_pairs={{0,4},{4,0},{8,12},{12,8},{16,20},{20,16},{24,28},{28,24},{1,5},{5... | collective-permute-start | bytes 18874376 | tf_op jit(solution)/shard_map/ppermute | solution.py:602
  192.2 27.8 %collective-permute-start.17 = (bf16[256,2048]{1,0:T(8,128)(2,1)}, bf16[256,2048]{1,0:T(8,128)(2,1)}, u32[]{:S(2)}, u32[]{:S(2)}) collective-permute-start(bf16[256,2048]{1,0:T(8,128)(2,1)} %get-tuple-element.278), channel_id=1, source_target_pairs={{0,8},{4,12},{8,0},{12,4},{16,24},{20,28},{24,16},{28,20},{1,9},{5... | collective-permute-start | bytes 3145736 | tf_op jit(solution)/shard_map/ppermute | solution.py:616
  195.9 24.2 %collective-permute-start.18 = (bf16[256,2048]{1,0:T(8,128)(2,1)}, bf16[256,2048]{1,0:T(8,128)(2,1)}, u32[]{:S(2)}, u32[]{:S(2)}) collective-permute-start(bf16[256,2048]{1,0:T(8,128)(2,1)} %get-tuple-element.281), channel_id=1, source_target_pairs={{8,16},{12,20},{16,8},{20,12},{9,17},{13,21},{17,9},{21,13},{10,18... | collective-permute-start | bytes 3145736 | tf_op jit(solution)/shard_map/ppermute | solution.py:616
  225.8 5.7 collective-permute-start.21
  225.8 27.5 %collective-permute-start.19 = (bf16[256,2048]{1,0:T(8,128)(2,1)S(1)}, bf16[256,2048]{1,0:T(8,128)(2,1)S(1)}, u32[]{:S(2)}, u32[]{:S(2)}) collective-permute-start(bf16[256,2048]{1,0:T(8,128)(2,1)S(1)} %multiply_convert_fusion.rows.refs_4_), channel_id=1, source_target_pairs={{0,8},{4,12},{8,16},{12,20},{16,24},{20,28},{24,0},{28,4},{1,9},{5... | collective-permute-start | bytes 3145736 | tf_op jit(solution)/shard_map/ppermute | solution.py:616
  253.3 26.6 %collective-permute-start.22 = (bf16[256,2048]{1,0:T(8,128)(2,1)S(1)}, bf16[256,2048]{1,0:T(8,128)(2,1)S(1)}, u32[]{:S(2)}, u32[]{:S(2)}) collective-permute-start(bf16[256,2048]{1,0:T(8,128)(2,1)S(1)} %collective-permute-done.19.rows.refs_5_), channel_id=1, source_target_pairs={{0,8},{4,12},{8,16},{12,20},{16,24},{20,28},{24,0},{28,4},{1,9},{5... | collective-permute-start | bytes 3145736 | tf_op jit(solution)/shard_map/ppermute | solution.py:616
  281.6 27.9 %collective-permute-start.24 = (bf16[256,2048]{1,0:T(8,128)(2,1)S(1)}, bf16[256,2048]{1,0:T(8,128)(2,1)S(1)}, u32[]{:S(2)}, u32[]{:S(2)}) collective-permute-start(bf16[256,2048]{1,0:T(8,128)(2,1)S(1)} %convert_element_type.138), channel_id=1, source_target_pairs={{0,8},{4,12},{8,16},{12,20},{16,24},{20,28},{24,0},{28,4},{1,9},{5... | collective-permute-start | bytes 3145736 | tf_op jit(solution)/shard_map/ppermute | solution.py:616
  281.9 48.0 %collective-permute-start.23 = (bf16[256,2048]{1,0:T(8,128)(2,1)S(1)}, bf16[256,2048]{1,0:T(8,128)(2,1)S(1)}, u32[]{:S(2)}, u32[]{:S(2)}) collective-permute-start(bf16[256,2048]{1,0:T(8,128)(2,1)S(1)} %collective-permute-done.22.rows.refs_6_), channel_id=1, source_target_pairs={{0,8},{4,12},{8,16},{12,20},{16,24},{20,28},{24,0},{28,4},{1,9},{5... | collective-permute-start | bytes 3145736 | tf_op jit(solution)/shard_map/ppermute | solution.py:616
  331.7 24.8 %collective-permute-start.25 = (bf16[256,2048]{1,0:T(8,128)(2,1)S(1)}, bf16[256,2048]{1,0:T(8,128)(2,1)S(1)}, u32[]{:S(2)}, u32[]{:S(2)}) collective-permute-start(bf16[256,2048]{1,0:T(8,128)(2,1)S(1)} %add_convert_fusion.4), channel_id=1, source_target_pairs={{0,8},{4,12},{8,16},{12,20},{16,24},{20,28},{24,0},{28,4},{1,9},{5... | collective-permute-start | bytes 3145736 | tf_op jit(solution)/shard_map/ppermute | solution.py:616
  358.6 24.2 %collective-permute-start.26 = (bf16[256,2048]{1,0:T(8,128)(2,1)S(1)}, bf16[256,2048]{1,0:T(8,128)(2,1)S(1)}, u32[]{:S(2)}, u32[]{:S(2)}) collective-permute-start(bf16[256,2048]{1,0:T(8,128)(2,1)S(1)} %add_convert_fusion.3), channel_id=1, source_target_pairs={{0,8},{4,12},{8,16},{12,20},{16,24},{20,28},{24,0},{28,4},{1,9},{5... | collective-permute-start | bytes 3145736 | tf_op jit(solution)/shard_map/ppermute | solution.py:616
  382.8 28.7 %collective-permute-start.29 = (bf16[768,2048]{1,0:T(8,128)(2,1)}, bf16[768,2048]{1,0:T(8,128)(2,1)S(1)}, u32[]{:S(2)}, u32[]{:S(2)}) collective-permute-start(bf16[768,2048]{1,0:T(8,128)(2,1)} %get-tuple-element.365), channel_id=1, source_target_pairs={{0,4},{4,0},{8,12},{12,8},{16,20},{20,16},{24,28},{28,24},{1,5},{5... | collective-permute-start | bytes 9437192 | tf_op jit(solution)/shard_map/ppermute | solution.py:602
  386.2 25.3 %collective-permute-start.27 = (bf16[256,2048]{1,0:T(8,128)(2,1)S(1)}, bf16[256,2048]{1,0:T(8,128)(2,1)}, u32[]{:S(2)}, u32[]{:S(2)}) collective-permute-start(bf16[256,2048]{1,0:T(8,128)(2,1)S(1)} %get-tuple-element.358.refs_4_), channel_id=1, source_target_pairs={{0,8},{4,12},{8,0},{12,4},{16,24},{20,28},{24,16},{28,20},{1,9},{5... | collective-permute-start | bytes 3145736 | tf_op jit(solution)/shard_map/ppermute | solution.py:616
  386.3 25.2 %collective-permute-start.28 = (bf16[256,2048]{1,0:T(8,128)(2,1)S(1)}, bf16[256,2048]{1,0:T(8,128)(2,1)S(1)}, u32[]{:S(2)}, u32[]{:S(2)}) collective-permute-start(bf16[256,2048]{1,0:T(8,128)(2,1)S(1)} %get-tuple-element.358.refs_4_), channel_id=1, source_target_pairs={{8,16},{12,20},{16,8},{20,12},{9,17},{13,21},{17,9},{21,13},{10,18... | collective-permute-start | bytes 3145736 | tf_op jit(solution)/shard_map/ppermute | solution.py:616
  387.1 33.6 %collective-permute-start.32 = (bf16[768,2048]{1,0:T(8,128)(2,1)}, bf16[768,2048]{1,0:T(8,128)(2,1)}, u32[]{:S(2)}, u32[]{:S(2)}) collective-permute-start(bf16[768,2048]{1,0:T(8,128)(2,1)} %get-tuple-element.376), channel_id=1, source_target_pairs={{0,4},{4,0},{8,12},{12,8},{16,20},{20,16},{24,28},{28,24},{1,5},{5... | collective-permute-start | bytes 9437192 | tf_op jit(solution)/shard_map/ppermute | solution.py:602
  411.5 29.4 %collective-permute-start.33 = (bf16[768,2048]{1,0:T(8,128)(2,1)}, bf16[768,2048]{1,0:T(8,128)(2,1)}, u32[]{:S(2)}, u32[]{:S(2)}) collective-permute-start(bf16[768,2048]{1,0:T(8,128)(2,1)} %get-tuple-element.377), channel_id=1, source_target_pairs={{0,4},{4,0},{8,12},{12,8},{16,20},{20,16},{24,28},{28,24},{1,5},{5... | collective-permute-start | bytes 9437192 | tf_op jit(solution)/shard_map/ppermute | solution.py:602
  413.5 27.4 %collective-permute-start.30 = (bf16[256,2048]{1,0:T(8,128)(2,1)}, bf16[256,2048]{1,0:T(8,128)(2,1)S(1)}, u32[]{:S(2)}, u32[]{:S(2)}) collective-permute-start(bf16[256,2048]{1,0:T(8,128)(2,1)} %get-tuple-element.528), channel_id=1, source_target_pairs={{0,8},{4,12},{8,0},{12,4},{16,24},{20,28},{24,16},{28,20},{1,9},{5... | collective-permute-start | bytes 3145736 | tf_op jit(solution)/shard_map/ppermute | solution.py:616
  417.1 23.9 %collective-permute-start.31 = (bf16[256,2048]{1,0:T(8,128)(2,1)}, bf16[256,2048]{1,0:T(8,128)(2,1)S(1)}, u32[]{:S(2)}, u32[]{:S(2)}) collective-permute-start(bf16[256,2048]{1,0:T(8,128)(2,1)} %collective-permute-done.27), channel_id=1, source_target_pairs={{8,16},{12,20},{16,8},{20,12},{9,17},{13,21},{17,9},{21,13},{10,18... | collective-permute-start | bytes 3145736 | tf_op jit(solution)/shard_map/ppermute | solution.py:616
  441.0 143.2 %reduce-scatter.5.cloned.1.call-start = ((), (), s32[]{:S(2)}) async-start(), calls=%async_computation.7 | async-start | bytes 7864320 | tf_op jit(solution)/shard_map/reduce_scatter | solution.py:576
  445.4 28.2 %collective-permute-start.34 = (bf16[256,2048]{1,0:T(8,128)(2,1)}, bf16[256,2048]{1,0:T(8,128)(2,1)}, u32[]{:S(2)}, u32[]{:S(2)}) collective-permute-start(bf16[256,2048]{1,0:T(8,128)(2,1)} %get-tuple-element.382), channel_id=1, source_target_pairs={{0,8},{4,12},{8,0},{12,4},{16,24},{20,28},{24,16},{28,20},{1,9},{5... | collective-permute-start | bytes 3145736 | tf_op jit(solution)/shard_map/ppermute | solution.py:616
  448.7 24.9 %collective-permute-start.35 = (bf16[256,2048]{1,0:T(8,128)(2,1)}, bf16[256,2048]{1,0:T(8,128)(2,1)}, u32[]{:S(2)}, u32[]{:S(2)}) collective-permute-start(bf16[256,2048]{1,0:T(8,128)(2,1)} %get-tuple-element.384), channel_id=1, source_target_pairs={{8,16},{12,20},{16,8},{20,12},{9,17},{13,21},{17,9},{21,13},{10,18... | collective-permute-start | bytes 3145736 | tf_op jit(solution)/shard_map/ppermute | solution.py:616
  482.8 34.5 %collective-permute-start.36 = (bf16[256,2048]{1,0:T(8,128)(2,1)}, bf16[256,2048]{1,0:T(8,128)(2,1)S(1)}, u32[]{:S(2)}, u32[]{:S(2)}) collective-permute-start(bf16[256,2048]{1,0:T(8,128)(2,1)} %get-tuple-element.395), channel_id=1, source_target_pairs={{0,8},{4,12},{8,0},{12,4},{16,24},{20,28},{24,16},{28,20},{1,9},{5... | collective-permute-start | bytes 3145736 | tf_op jit(solution)/shard_map/ppermute | solution.py:616
  484.7 33.6 %collective-permute-start.37 = (bf16[256,2048]{1,0:T(8,128)(2,1)}, bf16[256,2048]{1,0:T(8,128)(2,1)}, u32[]{:S(2)}, u32[]{:S(2)}) collective-permute-start(bf16[256,2048]{1,0:T(8,128)(2,1)} %get-tuple-element.398), channel_id=1, source_target_pairs={{8,16},{12,20},{16,8},{20,12},{9,17},{13,21},{17,9},{21,13},{10,18... | collective-permute-start | bytes 3145736 | tf_op jit(solution)/shard_map/ppermute | solution.py:616
  518.3 30.2 %collective-permute-start.38 = (bf16[256,2048]{1,0:T(8,128)(2,1)}, bf16[256,2048]{1,0:T(8,128)(2,1)}, u32[]{:S(2)}, u32[]{:S(2)}) collective-permute-start(bf16[256,2048]{1,0:T(8,128)(2,1)} %row_dot.4), channel_id=1, source_target_pairs={{0,8},{4,12},{8,16},{12,20},{16,24},{20,28},{24,0},{28,4},{1,9},{5... | collective-permute-start | bytes 3145736 | tf_op jit(solution)/shard_map/ppermute | solution.py:616
  521.4 25.4 %collective-permute-start.39 = (bf16[656,160]{1,0:T(8,128)(2,1)}, bf16[656,160]{1,0:T(8,128)(2,1)}, u32[]{:S(2)}, u32[]{:S(2)}) collective-permute-start(bf16[656,160]{1,0:T(8,128)(2,1)} %pad_maximum_fusion.4), channel_id=1, source_target_pairs={{0,4},{4,0},{8,12},{12,8},{16,20},{20,16},{24,28},{28,24},{1,5},{5... | collective-permute-start | bytes 629768 | tf_op jit(solution)/shard_map/ppermute | solution.py:602
  548.5 29.2 %collective-permute-start.40 = (bf16[320,2048]{1,0:T(8,128)(2,1)}, bf16[320,2048]{1,0:T(8,128)(2,1)}, u32[]{:S(2)}, u32[]{:S(2)}) collective-permute-start(bf16[320,2048]{1,0:T(8,128)(2,1)} %get-tuple-element.428), channel_id=1, source_target_pairs={{0,4},{4,0},{8,12},{12,8},{16,20},{20,16},{24,28},{28,24},{1,5},{5... | collective-permute-start | bytes 3932168 | tf_op jit(solution)/shard_map/ppermute | solution.py:602
  548.5 29.2 %collective-permute-start.41 = (bf16[320,2048]{1,0:T(8,128)(2,1)}, bf16[320,2048]{1,0:T(8,128)(2,1)}, u32[]{:S(2)}, u32[]{:S(2)}) collective-permute-start(bf16[320,2048]{1,0:T(8,128)(2,1)} %get-tuple-element.430), channel_id=1, source_target_pairs={{0,4},{4,0},{8,12},{12,8},{16,20},{20,16},{24,28},{28,24},{1,5},{5... | collective-permute-start | bytes 3932168 | tf_op jit(solution)/shard_map/ppermute | solution.py:602
  549.0 28.7 %collective-permute-start.42 = (bf16[320,2048]{1,0:T(8,128)(2,1)}, bf16[320,2048]{1,0:T(8,128)(2,1)}, u32[]{:S(2)}, u32[]{:S(2)}) collective-permute-start(bf16[320,2048]{1,0:T(8,128)(2,1)} %get-tuple-element.432), channel_id=1, source_target_pairs={{0,4},{4,0},{8,12},{12,8},{16,20},{20,16},{24,28},{28,24},{1,5},{5... | collective-permute-start | bytes 3932168 | tf_op jit(solution)/shard_map/ppermute | solution.py:602
  552.2 32.0 %collective-permute-start.43 = (bf16[256,2048]{1,0:T(8,128)(2,1)}, bf16[256,2048]{1,0:T(8,128)(2,1)}, u32[]{:S(2)}, u32[]{:S(2)}) collective-permute-start(bf16[256,2048]{1,0:T(8,128)(2,1)} %add_convert_fusion.2), channel_id=1, source_target_pairs={{0,8},{4,12},{8,16},{12,20},{16,24},{20,28},{24,0},{28,4},{1,9},{5... | collective-permute-start | bytes 3145736 | tf_op jit(solution)/shard_map/ppermute | solution.py:616
  553.9 3.8 collective-permute-start.44
  557.7 3.7 collective-permute-start.45
  561.5 8.3 %collective-permute-start.46 = (f32[2,2048]{1,0:T(2,128)S(1)}, f32[2,2048]{1,0:T(2,128)S(1)}, u32[]{:S(2)}, u32[]{:S(2)}) collective-permute-start(f32[2,2048]{1,0:T(2,128)S(1)} %pad_maximum_fusion.8), channel_id=1, source_target_pairs={{0,3},{1,2},{2,1},{3,0},{4,7},{5,6},{6,5},{7,4},{8,11},{9,10},{10,... | collective-permute-start | bytes 49160 | tf_op jit(solution)/shard_map/ppermute | solution.py:761
  569.8 7.9 %collective-permute-start.47 = (bf16[656,160]{1,0:T(8,128)(2,1)S(1)}, bf16[656,160]{1,0:T(8,128)(2,1)S(1)}, u32[]{:S(2)}, u32[]{:S(2)}) collective-permute-start(bf16[656,160]{1,0:T(8,128)(2,1)S(1)} %copy-done.96), channel_id=1, source_target_pairs={{0,1},{1,0},{2,3},{3,2},{4,5},{5,4},{6,7},{7,6},{8,9},{9,8},{10,11... | collective-permute-start | bytes 629768 | tf_op jit(solution)/shard_map/ppermute | solution.py:755
  587.3 33.6 %collective-permute-start.49 = (bf16[960,512]{1,0:T(8,128)(2,1)}, bf16[960,512]{1,0:T(8,128)(2,1)}, u32[]{:S(2)}, u32[]{:S(2)}) collective-permute-start(bf16[960,512]{1,0:T(8,128)(2,1)} %get-tuple-element.521), channel_id=1, source_target_pairs={{0,1},{1,0},{2,3},{3,2},{4,5},{5,4},{6,7},{7,6},{8,9},{9,8},{10,11... | collective-permute-start | bytes 2949128 | tf_op jit(solution)/shard_map/ppermute | solution.py:595
  588.6 32.3 %collective-permute-start.50 = (bf16[960,512]{1,0:T(8,128)(2,1)}, bf16[960,512]{1,0:T(8,128)(2,1)}, u32[]{:S(2)}, u32[]{:S(2)}) collective-permute-start(bf16[960,512]{1,0:T(8,128)(2,1)} %get-tuple-element.520), channel_id=1, source_target_pairs={{0,2},{1,3},{2,0},{3,1},{4,6},{5,7},{6,4},{7,5},{8,10},{9,11},{10,... | collective-permute-start | bytes 2949128 | tf_op jit(solution)/shard_map/ppermute | solution.py:595
  592.0 28.9 %collective-permute-start.48 = (bf16[256,2048]{1,0:T(8,128)(2,1)}, bf16[256,2048]{1,0:T(8,128)(2,1)}, u32[]{:S(2)}, u32[]{:S(2)}) collective-permute-start(bf16[256,2048]{1,0:T(8,128)(2,1)} %add_convert_fusion.1), channel_id=1, source_target_pairs={{0,8},{4,12},{8,16},{12,20},{16,24},{20,28},{24,0},{28,4},{1,9},{5... | collective-permute-start | bytes 3145736 | tf_op jit(solution)/shard_map/ppermute | solution.py:616
  595.1 23.4 %collective-permute-start.52 = (bf16[128,2048]{1,0:T(8,128)(2,1)}, bf16[128,2048]{1,0:T(8,128)(2,1)}, u32[]{:S(2)}, u32[]{:S(2)}) collective-permute-start(bf16[128,2048]{1,0:T(8,128)(2,1)} %get-tuple-element.534), channel_id=1, source_target_pairs={{0,4},{4,0},{8,12},{12,8},{16,20},{20,16},{24,28},{28,24},{1,5},{5... | collective-permute-start | bytes 1572872 | tf_op jit(solution)/shard_map/ppermute | solution.py:602
  595.1 22.3 %collective-permute-start.51 = (bf16[656,160]{1,0:T(8,128)(2,1)S(1)}, bf16[656,160]{1,0:T(8,128)(2,1)}, u32[]{:S(2)}, u32[]{:S(2)}) collective-permute-start(bf16[656,160]{1,0:T(8,128)(2,1)S(1)} %add.204), channel_id=1, source_target_pairs={{0,2},{1,3},{2,0},{3,1},{4,6},{5,7},{6,4},{7,5},{8,10},{9,11},{10,... | collective-permute-start | bytes 629768 | tf_op jit(solution)/shard_map/ppermute | solution.py:755
  623.4 21.5 %collective-permute-start.58 = (bf16[960,512]{1,0:T(8,128)(2,1)}, bf16[960,512]{1,0:T(8,128)(2,1)S(1)}, u32[]{:S(2)}, u32[]{:S(2)}) collective-permute-start(bf16[960,512]{1,0:T(8,128)(2,1)} %constant_dynamic-slice_fusion), channel_id=1, source_target_pairs={{0,3},{1,2},{2,1},{3,0},{4,7},{5,6},{6,5},{7,4},{8,11},{9,10},{10,... | collective-permute-start | bytes 2949128 | tf_op jit(solution)/shard_map/ppermute | solution.py:595
  624.2 4.7 collective-permute-start.53
  628.9 4.5 collective-permute-start.54
  629.8 4.7 collective-permute-start.55
  632.1 5.5 collective-permute-start.56
  637.8 4.0 collective-permute-start.57
  (125 other events, 1180.9 us)
Sparse Core Ops, SparseCore 0:
  9.9 42.1 all-gather.4
  53.9 28.7 all-gather.6
  84.5 70.1 all-gather.8
  156.4 43.8 all-gather.10
  441.1 45.0 reduce-scatter.2
  489.0 70.1 reduce-scatter.4

commit v4 on v3

--- a/solution.py
+++ b/solution.py
@@ -14,6 +14,7 @@
 f32 = jnp.float32
 bf16 = jnp.bfloat16
 kernel_cost = pl.CostEstimate(flops=1, bytes_accessed=1, transcendentals=0)
+chain_cost = pl.CostEstimate(flops=1, bytes_accessed=1 << 26, transcendentals=0)
 
 
 def gelu_tanh(v):
@@ -78,8 +79,8 @@
 ):
     pre_refs, refs = refs[:chips], refs[chips:]
     conv_weight, conv_bias, gate_weight, gate_bias, rate_scale = refs[:5]
-    mixed, conv_out, rate_out, in_out, states_out, final_state, conv_state = refs[5:12]
-    pre_now, x_tail, carry = refs[12:]
+    mixed, *saved = refs[5:15]
+    final_state, conv_state, pre_now, x_tail, carry = refs[15:]
     chunk = pl.program_id(0)
     seq_count, local_len, channels = pre_now.shape
     channels //= 2
@@ -124,38 +125,53 @@
         in_gate = in_all[rows]
         step_log = rate_scale[...] * rate_gate
         decay = jnp.exp(-step_log)
-        root = jnp.sqrt(one_minus_exp(2.0 * step_log, decay))
+        square = jnp.maximum(one_minus_exp(2.0 * step_log, decay), 1e-36)
+        inverse_root = lax.rsqrt(square)
+        root = square * inverse_root
         position = chunk * local_len + lax.broadcasted_iota(jnp.int32, (local_len, 1), 0)
         live = position < lengths[seq]
-        drive = jnp.where(live, root * in_gate * conv, 0.0)
-        a, b = tile_scan(jnp.where(live, decay, 1.0), drive, False)
+        gated_conv = in_gate * conv
+        driven = root * gated_conv
+        kept_decay = jnp.where(live, decay, 1.0)
+        a, b = tile_scan(kept_decay, jnp.where(live, driven, 0.0), False)
         last = carry[seq]
-        gated, _ = gelu_pair(pre_now[seq, :, :channels])
         tiles = []
         for tile in range(local_len // 8):
             tiles.append(b[tile] + a[tile] * last)
             last = tiles[-1][7:8]
         states = jnp.concatenate(tiles, axis=0)
-        states_out[0, 0, seq] = states
-        mixed[0, 0, seq] = (gated * states).astype(bf16)
         carry[seq] = last
         final_state[seq : seq + 1] = last
-        conv_out[0, 0, seq] = conv
-        rate_out[0, 0, seq] = rate_gate
-        in_out[0, 0, seq] = in_gate
+        gated, slope = gelu_pair(pre_now[seq, :, :channels])
+        mixed[0, 0, seq] = (gated * states).astype(bf16)
+        rate_factor = (states - driven - gated_conv * decay * decay * inverse_root) * rate_gate
+        for out, value in zip(
+            saved,
+            (
+                gated,
+                slope * states,
+                kept_decay,
+                rate_factor,
+                -rate_scale[...] * rate_factor * (1.0 - rate_gate),
+                driven * (1.0 - in_gate),
+                root * in_gate,
+                pre_now[seq, :, channels:],
+                conv.astype(bf16),
+            ),
+        ):
+            out[0, 0, seq] = value
 
 
 def mixer_backward_kernel(
     chips, block_width, crossed, place, lengths, *refs
 ):
-    pre_refs, back_refs, refs = refs[:chips], refs[chips : 2 * chips], refs[2 * chips :]
-    conv_in, rate_in, in_in, states_in, conv_weight, gate_back, rate_scale = refs[:7]
-    grads, sums, gate_grads = refs[7:10]
-    pre_now, back_now, carry, grad_head, gate_sums = refs[10:]
+    back_refs, refs = refs[:chips], refs[chips:]
+    gated_in, y_in, decay_in, rate_in, rate_pre_in, in_pre_in, direct_in, x_in, conv_in = refs[:9]
+    conv_weight, gate_back, grads, sums, gate_grads = refs[9:14]
+    back_now, carry, grad_head, gate_sums = refs[14:]
     step = pl.program_id(0)
     chunk = pl.num_programs(0) - 1 - step
     seq_count, local_len, channels = back_now.shape
-    pick_block(chunk, place, chips, pre_refs, pre_now)
     pick_block(chunk, place, chips, back_refs, back_now, crossed)
 
     @pl.when(step == 0)
@@ -170,17 +186,10 @@
     for seq in range(seq_count):
         position = chunk * local_len + lax.broadcasted_iota(jnp.int32, (local_len, 1), 0)
         live = position < lengths[seq]
-        rate_gate = rate_in[0, 0, seq]
-        in_gate = in_in[0, 0, seq]
-        conv = conv_in[0, 0, seq]
-        states = states_in[0, 0, seq]
         mixer_grad = back_now[seq]
-        gated, slope = gelu_pair(pre_now[seq, :, :channels])
-        step_log = rate_scale[...] * rate_gate
-        decay_raw = jnp.exp(-step_log)
-        decay = jnp.where(live, decay_raw, 1.0)
-        grads[0, 0, seq, :, :channels] = (mixer_grad * states * slope).astype(bf16)
-        source = mixer_grad * gated
+        grads[0, 0, seq, :, :channels] = (mixer_grad * y_in[0, 0, seq]).astype(bf16)
+        source = mixer_grad * gated_in[0, 0, seq]
+        decay = decay_in[0, 0, seq]
         a, b = tile_scan(decay, decay * source, True)
         following = carry[seq]
         tiles = []
@@ -191,22 +200,13 @@
         carry[seq] = following
         adjoint = source + jnp.concatenate(tiles[::-1], axis=0)
         adjoint = jnp.where(live, adjoint, 0.0)
-        square = one_minus_exp(2.0 * step_log, decay_raw)
-        inverse_root = lax.rsqrt(square)
-        root = square * inverse_root
-        gated_conv = in_gate * conv
-        logd_grad = adjoint * (
-            states - root * gated_conv - gated_conv * decay_raw * decay_raw * inverse_root
-        )
-        rate_part = logd_grad * rate_gate
-        decay_sum = decay_sum + jnp.sum(rate_part, axis=0, keepdims=True)
-        rate_pre.append(-rate_scale[...] * rate_part * (1.0 - rate_gate))
-        through = adjoint * root
-        in_pre.append(through * gated_conv * (1.0 - in_gate))
-        direct.append(through * in_gate)
+        decay_sum = decay_sum + jnp.sum(adjoint * rate_in[0, 0, seq], axis=0, keepdims=True)
+        rate_pre.append(adjoint * rate_pre_in[0, 0, seq])
+        in_pre.append(adjoint * in_pre_in[0, 0, seq])
+        direct.append(adjoint * direct_in[0, 0, seq])
     rate_all = jnp.concatenate(rate_pre, axis=0)
     in_all = jnp.concatenate(in_pre, axis=0)
-    conv_all = jnp.concatenate([conv_in[0, 0, seq] for seq in range(seq_count)], axis=0).astype(bf16)
+    conv_all = jnp.concatenate([conv_in[0, 0, seq] for seq in range(seq_count)], axis=0)
     rate_b, in_b = rate_all.astype(bf16), in_all.astype(bf16)
     for start, stop, low, high, at in gate_tiles(channels, block_width, 128):
         both = jnp.concatenate((rate_b[:, start:stop], in_b[:, start:stop]), axis=1)
@@ -218,18 +218,16 @@
         else:
             gate_sums[at : at + high - low, : stop - start] += part[:, : stop - start]
             gate_sums[at : at + high - low, 128 : 128 + stop - start] += part[:, stop - start :]
-    rate_parted, in_parted = split_rows(rate_all), split_rows(in_all)
     parts = []
     for start, stop, low, high, at in gate_tiles(channels, block_width, 256):
-        both = jnp.concatenate((rate_parted[:, low:high], in_parted[:, low:high]), axis=1)
-        part = joined_dot(both, gate_back[2 * at : 2 * (at + high - low)])
-        parts.append(part[:, : stop - start])
+        both = jnp.concatenate((rate_b[:, low:high], in_b[:, low:high]), axis=1)
+        parts.append(dot(both, gate_back[2 * at : 2 * (at + high - low)])[:, : stop - start])
     conv_grad = jnp.concatenate(direct, axis=0) + jnp.concatenate(parts, axis=1)
     tap_sums = [jnp.zeros((1, channels), f32) for _ in range(4)]
     for seq in range(seq_count):
         part = conv_grad[seq * local_len : (seq + 1) * local_len]
         extended = jnp.concatenate((part, grad_head[seq]), axis=0)
-        x = pre_now[seq, :, channels:]
+        x = x_in[0, 0, seq]
         total = conv_weight[0:1] * part
         tap_sums[0] = tap_sums[0] + jnp.sum(part * x, axis=0, keepdims=True)
         for lag in range(1, 4):
@@ -311,7 +309,7 @@
             num_scalar_prefetch=2,
             grid=(2 * chips,),
             in_specs=hops(2 * channels) + [whole_spec(param.shape) for param in params],
-            out_specs=[block(channels)] * 5
+            out_specs=[block(channels)] * 10
             + [whole_spec((seq_count, channels)), whole_spec((seq_count, 3, channels))],
             scratch_shapes=[
                 pltpu.VMEM((seq_count, local_len, 2 * channels), f32),
@@ -320,7 +318,8 @@
             ],
         ),
         out_shape=[pltpu.HBM(full, bf16)]
-        + [pltpu.HBM(full, f32)] * 4
+        + [pltpu.HBM(full, f32)] * 8
+        + [pltpu.HBM(full, bf16)]
         + [
             jax.ShapeDtypeStruct((seq_count, channels), f32),
             jax.ShapeDtypeStruct((seq_count, 3, channels), f32),
@@ -332,14 +331,13 @@
 
 
 def mixer_backward(
-    pre_blocks, back_blocks, crossed, saved, lengths, place, conv_weight, gate_back, rate_scale, block_width
+    back_blocks, crossed, saved, lengths, place, conv_weight, gate_back, block_width
 ):
-    chips = len(pre_blocks)
-    _, seq_count, local_len, channels = pre_blocks[0].shape
-    channels //= 2
-    hops, block = mixer_specs(pre_blocks[0].shape, chips, lambda step: 2 * chips - 1 - step)
+    chips = len(back_blocks)
+    _, seq_count, local_len, channels = back_blocks[0].shape
+    hops, block = mixer_specs(back_blocks[0].shape, chips, lambda step: 2 * chips - 1 - step)
     full = (chips, 2, seq_count, local_len, channels)
-    params = (conv_weight, gate_back, rate_scale)
+    params = (conv_weight, gate_back)
     packed = gate_tiles(channels, block_width, 128)[-1]
     packed = packed[4] + packed[3] - packed[2]
     gate_shape = (channels // block_width, 2, block_width, block_width)
@@ -348,13 +346,11 @@
         grid_spec=pltpu.PrefetchScalarGridSpec(
             num_scalar_prefetch=2,
             grid=(2 * chips,),
-            in_specs=hops(2 * channels)
-            + hops(channels, crossed)
-            + [block(channels)] * 4
+            in_specs=hops(channels, crossed)
+            + [block(channels)] * 9
             + [whole_spec(param.shape) for param in params],
             out_specs=[block(2 * channels), whole_spec((8, channels)), whole_spec(gate_shape)],
             scratch_shapes=[
-                pltpu.VMEM((seq_count, local_len, 2 * channels), f32),
                 pltpu.VMEM((seq_count, local_len, channels), f32),
                 pltpu.VMEM((seq_count, 1, channels), f32),
                 pltpu.VMEM((seq_count, 8, channels), f32),
@@ -369,7 +365,7 @@
         compiler_params=pltpu.CompilerParams(vmem_limit_bytes=32 << 20),
         cost_estimate=kernel_cost,
         name="mixer_backward",
-    )(place, lengths, *pre_blocks, *back_blocks, *saved, *params)
+    )(place, lengths, *back_blocks, *saved, *params)
 
 
 def mlp_kernel(tiles, rows, back, own_in, other_in, own_down, other_down, *refs):
@@ -437,7 +433,7 @@
         out_shape=[pltpu.HBM((count, 2 * units), bf16)] * 3
         + [pltpu.HBM((count, width), f32), pltpu.HBM((count, width), bf16)],
         scratch_shapes=[pltpu.VMEM((count, width), f32)] * 2,
-        compiler_params=pltpu.CompilerParams(vmem_limit_bytes=40 << 20),
+        compiler_params=pltpu.CompilerParams(vmem_limit_bytes=36 << 20),
         cost_estimate=kernel_cost,
         name="mlp_block",
     )(rows, back, own_in, other_in, own_down, other_down)
@@ -483,18 +479,21 @@
         out_shape=[pltpu.HBM((half, width), f32)] * kinds
         + [pltpu.HBM((half, width), bf16)] * kinds
         + [jax.ShapeDtypeStruct((1, width), f32)] * len(weights),
-        compiler_params=pltpu.CompilerParams(vmem_limit_bytes=40 << 20),
+        compiler_params=pltpu.CompilerParams(vmem_limit_bytes=28 << 20),
         cost_estimate=kernel_cost,
         name="weight_grad",
     )(*lefts, *rights, *weights)
     return list(zip(made[:kinds], made[kinds : 2 * kinds])), made[2 * kinds :]
 
 
-def row_dot_kernel(rows, weight, out):
-    out[...] = dot(rows[...], weight[...]).astype(out.dtype)
-
-
-def row_dot(rows, weight, block, count, kind=f32):
+def row_dot_kernel(rows, weight, *refs):
+    total = dot(rows[...], weight[...])
+    if len(refs) > 1:
+        total = total + refs[0][...].astype(f32)
+    refs[-1][...] = total.astype(refs[-1].dtype)
+
+
+def row_dot(rows, weight, block, count, kind=f32, moving=()):
     depth, width = weight.shape
     size, tile = rows.shape[0] // count, min(512, width)
     return pl.pallas_call(
@@ -503,17 +502,18 @@
         in_specs=[
             pl.BlockSpec((size, depth), lambda step: (block, 0)),
             pl.BlockSpec((depth, tile), lambda step: (0, step)),
-        ],
+        ]
+        + [pl.BlockSpec((size, tile), lambda step: (0, step))] * len(moving),
         out_specs=pl.BlockSpec((size, tile), lambda step: (0, step)),
         out_shape=pltpu.HBM((size, width), kind),
-        compiler_params=pltpu.CompilerParams(vmem_limit_bytes=32 << 20),
-        cost_estimate=kernel_cost,
+        compiler_params=pltpu.CompilerParams(vmem_limit_bytes=10 << 20),
+        cost_estimate=chain_cost if moving else kernel_cost,
         name="row_dot",
-    )(rows, weight)
+    )(rows, weight, *moving)
 
 
 def join_kernel(count, tiles, *refs):
-    out = refs[2 * count]
+    out = refs[-1]
     for at in range(count):
 
         @pl.when(pl.program_id(0) // tiles == at)
@@ -521,10 +521,10 @@
             out[...] = (refs[2 * at][...] + refs[2 * at + 1][...].astype(f32)).astype(bf16)
 
 
-def join(*pairs):
+def join(*pairs, slots=1, slot=0, filled=(), tile=128):
     count = len(pairs)
     rows, width = pairs[0][0].shape
-    tile = 128 if rows % 128 == 0 else rows // 2
+    tile = tile if rows % tile == 0 else rows // 2
     tiles = rows // tile
 
     def spec(at):
@@ -533,13 +533,15 @@
     return pl.pallas_call(
         partial(join_kernel, count, tiles),
         grid=(count * tiles,),
-        in_specs=[spec(at) for at in range(count) for _ in range(2)],
-        out_specs=pl.BlockSpec((tile, width), lambda step: (step, 0)),
-        out_shape=pltpu.HBM((count * rows, width), bf16),
-        compiler_params=pltpu.CompilerParams(vmem_limit_bytes=40 << 20),
+        in_specs=[spec(at) for at in range(count) for _ in range(2)]
+        + [pl.BlockSpec(memory_space=pl.ANY)] * len(filled),
+        out_specs=pl.BlockSpec((tile, width), lambda step: (slot * count * tiles + step, 0)),
+        out_shape=pltpu.HBM((slots * count * rows, width), bf16),
+        input_output_aliases={2 * count: 0} if filled else {},
+        compiler_params=pltpu.CompilerParams(vmem_limit_bytes=16 << 20),
         cost_estimate=kernel_cost,
         name="join",
-    )(*[value for pair in pairs for value in pair])
+    )(*[value for pair in pairs for value in pair], *filled)
 
 
 def block_diagonal(weight):
@@ -577,12 +579,9 @@
 
 
 class DirectSum:
-    def __init__(self, grad, got=()):
+    def __init__(self, grad):
         self.size = lax.axis_size("narrow")
-        self.grad, self.got = grad, list(got)
-
-    def state(self):
-        return self.grad, self.got
+        self.grad, self.got = grad, []
 
     def piece(self, flip):
         span = self.grad.shape[1] // self.size
@@ -667,7 +666,7 @@
             num_scalar_prefetch=1, grid=(rows // tile,), in_specs=[spec] * 4, out_specs=[spec] * 2
         ),
         out_shape=[pltpu.HBM((rows, width), bf16)] * 2,
-        compiler_params=pltpu.CompilerParams(vmem_limit_bytes=32 << 20),
+        compiler_params=pltpu.CompilerParams(vmem_limit_bytes=8 << 20),
         cost_estimate=kernel_cost,
         name="advance",
     )(place, end_part, end_moved, mid_part, mid_moved)
@@ -687,32 +686,32 @@
         self.ends.append(self.line.move(end, [(0, 1), (1, 0), (2, 3), (3, 2)]))
         self.mids.append(self.line.move(mid, [(1, 2), (2, 1)]))
 
-    def step(self, number, parts):
+    def first(self, choose):
+        if self.packed:
+            self.chosen = (choose(self.line.chip == 0, 1, 3),)
+
+    def step(self, number, choose):
         line, count = self.line, self.line.count
         if not self.packed:
             if number < count:
                 self.backs[number] = line.gather_step(number, *self.backs[number - 1])
             if number > 1:
                 sent = [
-                    plus(parts[hop], self.moved[way]).astype(bf16)
+                    plus(choose(True, hop, hop), self.moved[way]).astype(bf16)
                     for way, hop in enumerate((number - 1, count - number + 1))
                 ]
                 self.moved = line.sum_step(number - 1, *sent)
         elif number == 1:
             self.pair(self.own, self.own)
         elif number == 2:
-            part = jnp.where(line.chip == 0, parts[1], parts[3]).astype(bf16)
-            self.pair(jnp.where(self.edge, part, self.mids[0]), self.ends[0])
+            self.pair(jnp.where(self.edge, self.chosen[0], self.mids[0]), self.ends[0])
+            self.chosen = (choose(self.odd, 1, 3), choose(line.chip == 1, 3, 1), choose(True, 2, 2))
         elif number == 3:
-            self.pair(*advance(line.place, parts[2], self.mids[1], parts[2], self.ends[1], True))
-            self.chosen = (
-                jnp.where(self.odd, parts[1], parts[3]),
-                jnp.where(line.chip == 1, parts[3], parts[1]),
-            )
+            end, mid, two = self.chosen
+            self.pair(*advance(line.place, two, self.mids[1], two, self.ends[1], True))
         else:
-            self.pair(
-                *advance(line.place, self.chosen[0], self.mids[2], self.chosen[1], self.ends[2], False)
-            )
+            end, mid, _ = self.chosen
+            self.pair(*advance(line.place, end, self.mids[2], mid, self.ends[2], False))
 
     def fence(self, *values):
         state = (self.ends, self.mids, self.chosen, self.backs, self.moved)
@@ -875,33 +874,36 @@
     lanes.step(1, None)
     whole_out = both_cores(own_out, 0)
     pre_blocks.append(project(rows_first[last]))
-    mixed, conv, rate_gate, in_gate, states, final_state, conv_state = mixer_forward(
+    mixed, *saved, final_state, conv_state = mixer_forward(
         pre_blocks, lengths, place, params[:4], params[4:5], gate_weight, params[5:7],
         rate_scale, block_width,
     )
+
+    def mixed_part(flag, left, right):
+        rows = mixed_rows[left]
+        if left != right:
+            rows = jnp.where(flag, rows, mixed_rows[right])
+        return dot(rows, whole_out).astype(bf16)
+
     mixed_rows = mixed.reshape(chips, -1, 2 * channels)
-    parts = {hop: dot(mixed_rows[hop], whole_out) for hop in (1, last)}
-    parts, mixed_rows, final_state, conv_state = lanes.fence(
-        parts, mixed_rows, final_state, conv_state
-    )
+    lanes.first(mixed_part)
+    mixed_rows, final_state, conv_state = lanes.fence(mixed_rows, final_state, conv_state)
     for step in range(2, chips + 1):
-        lanes.step(step, parts)
-        for hop in (step, chips - step):
-            if hop < chips and hop not in parts:
-                parts[hop] = dot(mixed_rows[hop], whole_out)
+        lanes.step(step, mixed_part)
         if step == 2:
+            own_part = dot(mixed_rows[0], whole_out)
             final_state, conv_state = by_channel(final_state), by_channel(conv_state)
-            parts, final_state, conv_state = lanes.fence(parts, final_state, conv_state)
+            own_part, mixed_rows, final_state, conv_state = lanes.fence(
+                own_part, mixed_rows, final_state, conv_state
+            )
         elif step == chips - 1:
-            if 0 not in parts:
-                parts[0] = dot(mixed_rows[0], whole_out)
-            parts, own_mlp_in = lanes.fence(parts, own_mlp_in)
+            own_part, own_mlp_in = lanes.fence(own_part, own_mlp_in)
             other_mlp_in = swap(own_mlp_in)
         elif step < chips:
-            (parts,) = lanes.fence(parts)
+            (own_part,) = lanes.fence(own_part)
     rows_back = lanes.rows()
-    parts, rows_back, own_down = lanes.fence(parts, rows_back, own_down)
-    resid = tokens_f + lanes.total(parts[0])
+    own_part, rows_back, own_down = lanes.fence(own_part, rows_back, own_down)
+    resid = tokens_f + lanes.total(own_part)
 
     scale_two, norm_mid = norm_forward(resid, second_gain)
     norm_mid, own_down = fence(norm_mid, own_down)
@@ -937,21 +939,26 @@
     def back_block(rows):
         return dot_nt(rows, whole_out).reshape(2, seq_half, local_len, 2 * channels)
 
+    def out_part(flag, left, right):
+        return outs[left] if left == right else jnp.where(flag, outs[left], outs[right])
+
     lanes = Exchange(line, resid_grad_b)
     lanes.step(1, None)
+    lanes.first(out_part)
     [grads_up], _ = weight_grad(up_grads, rows_second, 1)
-    from_down = swap(grads_down[1])
-    grads_up, from_down, outs = lanes.fence(grads_up, from_down, outs)
+    from_down, from_gate = swap(grads_down[1]), swap(grads_gate[1])
+    grads_up, from_down, from_gate, outs = lanes.fence(grads_up, from_down, from_gate, outs)
     back_blocks = [back_block(resid_grad_b)]
     for step in range(2, chips + 1):
-        lanes.step(step, outs)
+        lanes.step(step, out_part)
         if step == 2:
             part_down = join((grads_down[0], from_down))
-            from_gate, from_up = swap(grads_gate[1]), swap(grads_up[1])
-            part_down, from_gate, from_up = lanes.fence(part_down, from_gate, from_up)
+            part_mlp_in = join((grads_gate[0], from_gate), slots=2)
+            from_up = swap(grads_up[1])
+            part_down, part_mlp_in, from_up, outs = lanes.fence(part_down, part_mlp_in, from_up, outs)
             grad_mlp_down = narrow_sum(part_down, 1)
         elif step == 3:
-            part_mlp_in = join((grads_gate[0], from_gate), (grads_up[0], from_up))
+            part_mlp_in = join((grads_up[0], from_up), slots=2, slot=1, filled=(part_mlp_in,))
             if lanes.packed:
                 back_blocks += [back_block(lanes.arrived(at)) for at in (1, 2)]
             part_mlp_in, back_blocks = lanes.fence(part_mlp_in, back_blocks)
@@ -963,8 +970,7 @@
     else:
         back_blocks += [back_block(rows) for rows in lanes.rows()[1:]]
     grads, small, gate_grads = mixer_backward(
-        pre_blocks, back_blocks, lanes.packed, (conv, rate_gate, in_gate, states),
-        lengths, place, params[:4], gate_back, rate_scale, block_width,
+        back_blocks, lanes.packed, saved, lengths, place, params[:4], gate_back, block_width
     )
     grad_rows = grads.reshape(-1, 4 * channels)
     part = row_dot(grad_rows, whole_in, 1, chips, bf16)
@@ -981,45 +987,45 @@
 
     gate_mine = gate_rows(gate_grads[:count], small[:, :channels])
     gate_other = gate_rows(gate_grads[count:], small[:, channels:])
-    sent = part
-    for hop in range(1, chips):
+    moving = line.ring(part)
+    grads_in, [gain_one] = weight_grad([grad_rows], rows_first, 2, weight=whole_in)
+    [grads_out], _ = weight_grad([mixed.reshape(-1, 2 * channels)], lanes.rows(), 1)
+    gate_sum = (gate_mine + swap(gate_other.astype(bf16)).astype(f32)).astype(bf16)
+    gate_sum = paired_step(gate_sum, "narrow", 1)
+    grads_in, grads_out, gain_one, moving, gate_sum, resid, grad_rows = fence(
+        grads_in, grads_out, gain_one, moving, gate_sum, resid, grad_rows
+    )
+    for hop in range(2, chips):
+        sent = row_dot(grad_rows, whole_in, hop, chips, bf16, (moving,))
+        if hop == 2:
+            sent, grads_in, grads_out, gain_one = fence(sent, grads_in, grads_out, gain_one)
         moving = line.ring(sent)
-        part = row_dot(grad_rows, whole_in, (hop + 1) % chips, chips)
-        if hop == 1:
-            grads_in, [gain_one] = weight_grad([grad_rows], rows_first, 2, weight=whole_in)
-            [grads_out], _ = weight_grad([mixed.reshape(-1, 2 * channels)], lanes.rows(), 1)
-            gate_sum = (gate_mine + swap(gate_other.astype(bf16)).astype(f32)).astype(bf16)
-            grads_in, grads_out, gain_one, moving, part, gate_sum, resid = fence(
-                grads_in, grads_out, gain_one, moving, part, gate_sum, resid
-            )
-        elif hop == 2:
-            parts = join(*[(own, swap(other)) for own, other in (*grads_in, grads_out)])
-            gains = jnp.concatenate((gain_one / first_gain, gain_two[None]), axis=0)
-            gains = direct_sum(gains, "narrow")
-            gate_sum = paired_step(gate_sum, "narrow", 1)
-            parts, moving, part, grad_mlp_in, gains, gate_sum, resid = fence(
-                parts, moving, part, grad_mlp_in, gains, gate_sum, resid
-            )
-        elif hop == last:
-            sum_proj = DirectSum(parts)
-            sum_proj.send(range(1, split))
-            output = by_position((resid + lanes.total(outs[0])).astype(bf16))
-            bit = 2
-            while bit < size:
-                gate_sum = paired_step(gate_sum, "narrow", bit)
-                bit *= 2
-            moving, sum_proj.got, parts, gains, gate_sum, output = fence(
-                moving, sum_proj.got, parts, gains, gate_sum, output
-            )
-        sent = plus(part, moving).astype(bf16)
-    in_sum = plus(part, moving)
+    part = row_dot(grad_rows, whole_in, 0, chips)
+    parts = join(*[(own, swap(other)) for own, other in (*grads_in, grads_out)])
+    gains = jnp.concatenate((gain_one / first_gain, gain_two[None]), axis=0)
+    parts, gate_sum, gains = fence(parts, gate_sum, gains)
+    gains, parts = fence(direct_sum(gains, "narrow"), parts)
+    sum_proj = DirectSum(parts)
+    sum_proj.send(range(1, split))
+    part, parts, grad_mlp_in, gate_sum, resid, gains, sum_proj.got = fence(
+        part, parts, grad_mlp_in, gate_sum, resid, gains, sum_proj.got
+    )
     sum_proj.grad = parts
     sum_proj.send(range(split, size))
+    output = by_position((resid + lanes.total(outs[0])).astype(bf16))
     gains = gains + swap(gains)
-    gains = direct_sum(gains, "wide", 2)
+    moving, output, gains, sum_proj.got, gate_sum = fence(
+        moving, output, gains, sum_proj.got, gate_sum
+    )
+    bit = 2
+    while bit < size:
+        gate_sum = paired_step(gate_sum, "narrow", bit)
+        bit *= 2
+    in_sum = plus(part, moving)
     from_norm, _ = norm_backward(tokens_f, scale_one, first_gain, in_sum)
     grad_tokens = (resid_grad + from_norm).astype(bf16)
-    grad_tokens, gains = fence(grad_tokens, gains)
+    grad_tokens, gains, sum_proj.got = fence(grad_tokens, gains, sum_proj.got)
+    gains = direct_sum(gains, "wide", 2)
     grad_proj = sum_proj.total()
     gate_sum = gate_sum.astype(f32)
     gate_grads = gate_sum[: count * 2 * block_width].reshape(count, 2, block_width, block_width)

time: 665 us -> 660 us (level)
  waiting for transfers between devices: 243 us -> 260 us
  other arithmetic: 54.1 us -> 41.8 us
  Pallas kernels: 194 us -> 185 us
    ppermute x28, waiting for transfers between devices: 208 us -> 238 us  [move(): return lax.ppermute(values, 'wide', devices)]
    ppermute x2, waiting for transfers between devices: 17.8 us -> 1.39 us  [paired_step(): lax.ppermute(values, axis, [(at, at ^ bit) for at in range(size)])]
    pallas_call x3 -> x4, Pallas kernels: 21.1 us -> 14.4 us  [join(): pl.pallas_call(partial(join_kernel, count, tiles), grid=(count * tiles,),...]
    unnamed x259 -> x247, local copies, waits for them, and re-layouts: 33.3 us -> 28.5 us
  transfers between devices with their start and end apart: 65 -> 65, of which waited for: 25 -> 30; matrix products, arithmetic and copies ran while one was open for 15% -> 14% of each run, Pallas kernels for 30% -> 28%
where the time goes in v4:
time: 660 us; the launch traced here: 652 us
  waiting for transfers between devices  260 us (39%)
  Pallas kernels  185 us (28%)
  starting transfers between devices  62.5 us (9%)
  local copies, waits for them, and re-layouts  52.8 us (8%)
  other arithmetic  41.8 us (6%)
  matrix products  32.7 us (5%)
  between operations  16.6 us (3%)
    ppermute x28, waiting for transfers between devices, move(): return lax.ppermute(values, 'wide', devices)  238 us
    pallas_call x4, Pallas kernels, mlp_block(): pl.pallas_call(partial(mlp_kernel, tiles), grid=(2 * tiles,), in_specs=[w...  65.8 us
    ppermute x28, starting transfers between devices, move(): return lax.ppermute(values, 'wide', devices)  43.9 us
    pallas_call x5, Pallas kernels, weight_grad(): pl.pallas_call(partial(weight_grad_kernel, count, kinds, len(weights)), g...  40.7 us
    unnamed x247, local copies, waits for them, and re-layouts  28.5 us
    dot_general x8, matrix products, dot_nt(): lax.dot_general(left, right, (((1,), (1,)), ((), ())), preferred_element_...  24.4 us
    pallas_call x1, Pallas kernels, mixer_forward(): pl.pallas_call(partial(mixer_forward_kernel, chips, block_width), grid_sp...  17.5 us
    pallas_call x4, Pallas kernels, row_dot(): pl.pallas_call(row_dot_kernel, grid=(width // tile,), in_specs=[pl.BlockS...  17.4 us
  transfers between devices with their start and end apart: 65, of which 30 were waited for; matrix products, arithmetic and copies ran while one was open for 14% of the time, Pallas kernels for 28%

profile of v4, /device:TPU:0, one launch (start us, length us, event | category | flops | bytes accessed | tf_op | source)
XLA Modules:
  0.0 651.6 jit_solution(5496946669024198601)
XLA Ops:
  17.0 2.6 collective-permute-start.2
  21.2 24.3 %collective-permute-done.2.refs_5_ = bf16[256,2048]{1,0:T(8,128)(2,1)S(1)} collective-permute-done((bf16[256,2048]{1,0:T(8,128)(2,1)S(1)}, bf16[256,2048]{1,0:T(8,128)(2,1)S(1)}, u32[]{:S(2)}, u32[]{:S(2)}) %collective-permute-start.2) | collective-permute-done | bytes 1048608 | tf_op jit(solution)/shard_map/ppermute | solution.py:615
  46.4 26.8 %collective-permute-done.4.refs_6_ = bf16[256,2048]{1,0:T(8,128)(2,1)} collective-permute-done((bf16[256,2048]{1,0:T(8,128)(2,1)S(1)}, bf16[256,2048]{1,0:T(8,128)(2,1)}, u32[]{:S(2)}, u32[]{:S(2)}) %collective-permute-start.4) | collective-permute-done | bytes 1048608 | tf_op jit(solution)/shard_map/ppermute | solution.py:615
  80.6 3.7 convolution_bitcast_fusion.1.refs_2_
  84.3 2.6 convolution_bitcast_fusion.2.refs_1_
  86.9 2.6 convolution_bitcast_fusion.3.refs_0_
  89.5 11.7 %collective-permute-done.5.refs_7_ = bf16[256,2048]{1,0:T(8,128)(2,1)} collective-permute-done((bf16[256,2048]{1,0:T(8,128)(2,1)}, bf16[256,2048]{1,0:T(8,128)(2,1)}, u32[]{:S(2)}, u32[]{:S(2)}) %collective-permute-start.5) | collective-permute-done | bytes 1048608 | tf_op jit(solution)/shard_map/ppermute | solution.py:615
  104.1 4.5 convolution_bitcast_fusion.refs_3_
  108.6 17.5 %mixer_forward.1 = (bf16[4,2,1,128,640]{4,3,2,1,0:T(8,128)(2,1)}, f32[4,2,1,128,640]{4,3,2,1,0:T(8,128)}, f32[4,2,1,128,640]{4,3,2,1,0:T(8,128)}, f32[4,2,1,128,...) custom-call(s32[2]{0:T(128)S(1)} %pad_add_fusion.place, ...), custom_call_target="tpu_custom_call" | custom-call | flops 1 | bytes 1 | tf_op jit(solution)/shard_map/mixer_forward/pallas_call | solution.py:306
  130.6 3.2 collective-permute-start.11
  142.5 15.0 %collective-permute-done.11.mid_moved = bf16[256,2048]{1,0:T(8,128)(2,1)S(1)} collective-permute-done((bf16[256,2048]{1,0:T(8,128)(2,1)S(1)}, bf16[256,2048]{1,0:T(8,128)(2,1)S(1)}, u32[]{:S(2)}, u32[]{:S(2)}) %collective-permute-start.11) | collective-permute-done | bytes 1048608 | tf_op jit(solution)/shard_map/ppermute | solution.py:615
  160.0 3.8 collective-permute-start.15
  165.4 21.4 %collective-permute-done.15.mid_moved = bf16[256,2048]{1,0:T(8,128)(2,1)S(1)} collective-permute-done((bf16[256,2048]{1,0:T(8,128)(2,1)}, bf16[256,2048]{1,0:T(8,128)(2,1)S(1)}, u32[]{:S(2)}, u32[]{:S(2)}) %collective-permute-start.15) | collective-permute-done | bytes 1048608 | tf_op jit(solution)/shard_map/ppermute | solution.py:615
  189.6 4.2 advance.5
  193.8 3.4 collective-permute-start.17
  200.5 20.9 %collective-permute-done.17 = bf16[256,2048]{1,0:T(8,128)(2,1)} collective-permute-done((bf16[256,2048]{1,0:T(8,128)(2,1)}, bf16[256,2048]{1,0:T(8,128)(2,1)}, u32[]{:S(2)}, u32[]{:S(2)}) %collective-permute-start.17) | collective-permute-done | bytes 1048608 | tf_op jit(solution)/shard_map/ppermute | solution.py:615
  221.4 3.2 multiply_reduce_fusion.2
  227.3 4.3 collective-permute-start.19
  233.0 16.5 %mlp_block.4 = (bf16[256,1536]{1,0:T(8,128)(2,1)}, bf16[256,1536]{1,0:T(8,128)(2,1)}, bf16[256,1536]{1,0:T(8,128)(2,1)}, f32[256,2048]{1,0:T(8,128)}, bf16[256,2048]{1,0:T(8,128)(2,1)}) custom-call(bf16[256,2048]{1,0:T(8,128)(2,1)S(1)} %multiply_convert_fusion.rows.refs_4_, bf16[256,2048]{1,0:T(8,128)(2,1)S(1)} %copy-done.9, ...), custom_call_target="tpu_custom_call" | custom-call | flops 1 | bytes 1 | tf_op jit(solution)/shard_map/mlp_block/pallas_call | solution.py:421
  249.5 5.6 collective-permute-done.19.rows.refs_5_
  257.2 16.4 %mlp_block.5 = (bf16[256,1536]{1,0:T(8,128)(2,1)}, bf16[256,1536]{1,0:T(8,128)(2,1)}, bf16[256,1536]{1,0:T(8,128)(2,1)}, f32[256,2048]{1,0:T(8,128)}, bf16[256,2048]{1,0:T(8,128)(2,1)}) custom-call(bf16[256,2048]{1,0:T(8,128)(2,1)S(1)} %collective-permute-done.19.rows.refs_5_, bf16[256,2048]{1,0:T(8,128)(2,1)S(1)} %copy-done.11, ...), custom_call_target="tpu_custom_call" | custom-call | flops 1 | bytes 1 | tf_op jit(solution)/shard_map/mlp_block/pallas_call | solution.py:421
  273.6 8.1 %collective-permute-done.22.rows.refs_6_ = bf16[256,2048]{1,0:T(8,128)(2,1)S(1)} collective-permute-done((bf16[256,2048]{1,0:T(8,128)(2,1)S(1)}, bf16[256,2048]{1,0:T(8,128)(2,1)S(1)}, u32[]{:S(2)}, u32[]{:S(2)}) %collective-permute-start.22) | collective-permute-done | bytes 1048608 | tf_op jit(solution)/shard_map/ppermute | solution.py:615
  285.3 16.4 %mlp_block.6 = (bf16[256,1536]{1,0:T(8,128)(2,1)}, bf16[256,1536]{1,0:T(8,128)(2,1)}, bf16[256,1536]{1,0:T(8,128)(2,1)}, f32[256,2048]{1,0:T(8,128)}, bf16[256,2048]{1,0:T(8,128)(2,1)}) custom-call(bf16[256,2048]{1,0:T(8,128)(2,1)S(1)} %collective-permute-done.22.rows.refs_6_, bf16[256,2048]{1,0:T(8,128)(2,1)S(1)} %broadcast_select_fusion.10.back.refs_6_, ...), custom_call_target="tpu_custom_call" | custom-call | flops 1 | bytes 1 | tf_op jit(solution)/shard_map/mlp_block/pallas_call | solution.py:421
  301.8 9.6 %collective-permute-done.24 = bf16[256,2048]{1,0:T(8,128)(2,1)S(1)} collective-permute-done((bf16[256,2048]{1,0:T(8,128)(2,1)S(1)}, bf16[256,2048]{1,0:T(8,128)(2,1)S(1)}, u32[]{:S(2)}, u32[]{:S(2)}) %collective-permute-start.24) | collective-permute-done | bytes 1048608 | tf_op jit(solution)/shard_map/ppermute | solution.py:615
  311.3 20.3 %collective-permute-done.23.rows.refs_7_ = bf16[256,2048]{1,0:T(8,128)(2,1)S(1)} collective-permute-done((bf16[256,2048]{1,0:T(8,128)(2,1)S(1)}, bf16[256,2048]{1,0:T(8,128)(2,1)S(1)}, u32[]{:S(2)}, u32[]{:S(2)}) %collective-permute-start.23) | collective-permute-done | bytes 1048608 | tf_op jit(solution)/shard_map/ppermute | solution.py:615
  333.6 16.4 %mlp_block.7 = (bf16[256,1536]{1,0:T(8,128)(2,1)}, bf16[256,1536]{1,0:T(8,128)(2,1)}, bf16[256,1536]{1,0:T(8,128)(2,1)}, f32[256,2048]{1,0:T(8,128)}, bf16[256,2048]{1,0:T(8,128)(2,1)}) custom-call(bf16[256,2048]{1,0:T(8,128)(2,1)S(1)} %collective-permute-done.23.rows.refs_7_, bf16[256,2048]{1,0:T(8,128)(2,1)S(1)} %copy-done.10, ...), custom_call_target="tpu_custom_call" | custom-call | flops 1 | bytes 1 | tf_op jit(solution)/shard_map/mlp_block/pallas_call | solution.py:421
  350.1 8.3 %collective-permute-done.25 = bf16[256,2048]{1,0:T(8,128)(2,1)S(1)} collective-permute-done((bf16[256,2048]{1,0:T(8,128)(2,1)S(1)}, bf16[256,2048]{1,0:T(8,128)(2,1)S(1)}, u32[]{:S(2)}, u32[]{:S(2)}) %collective-permute-start.25) | collective-permute-done | bytes 1048608 | tf_op jit(solution)/shard_map/ppermute | solution.py:615
  360.9 8.9 %weight_grad.6 = (f32[768,2048]{1,0:T(8,128)}, bf16[768,2048]{1,0:T(8,128)(2,1)}) custom-call(bf16[256,1536]{1,0:T(8,128)(2,1)S(1)} %copy-done.45, bf16[256,1536]{1,0:T(8,128)(2,1)S(1)} %copy-done.48, bf16[256,1536]{1,0:T(8,128)(2,1)S(1)} %copy-done.50, bf16[256,1536]{1,0:T(8,128)(2,1)S(1)} %copy-done.52, bf16[256,2048]{1,0:T(8,128)(2,1)S(1)} %copy-done.9, ...), custom_call_target="tpu_custom_call" | custom-call | flops 1 | bytes 1 | tf_op jit(solution)/shard_map/weight_grad/pallas_call | solution.py:471
  369.8 9.0 %weight_grad.5 = (f32[768,2048]{1,0:T(8,128)}, bf16[768,2048]{1,0:T(8,128)(2,1)}) custom-call(bf16[256,1536]{1,0:T(8,128)(2,1)S(1)} %copy-done.44, bf16[256,1536]{1,0:T(8,128)(2,1)S(1)} %copy-done.47, bf16[256,1536]{1,0:T(8,128)(2,1)S(1)} %copy-done.49, bf16[256,1536]{1,0:T(8,128)(2,1)S(1)} %copy-done.51, ...), custom_call_target="tpu_custom_call" | custom-call | flops 1 | bytes 1 | tf_op jit(solution)/shard_map/weight_grad/pallas_call | solution.py:471
  378.8 5.8 collective-permute-done.26
  389.0 8.9 %weight_grad.7 = (f32[768,2048]{1,0:T(8,128)}, bf16[768,2048]{1,0:T(8,128)(2,1)}) custom-call(bf16[256,1536]{1,0:T(8,128)(2,1)S(1)} %copy-done.41, bf16[256,1536]{1,0:T(8,128)(2,1)S(1)} %copy-done.42, bf16[256,1536]{1,0:T(8,128)(2,1)S(1)} %copy-done.43, bf16[256,1536]{1,0:T(8,128)(2,1)S(1)} %copy-done.46, ...), custom_call_target="tpu_custom_call" | custom-call | flops 1 | bytes 1 | tf_op jit(solution)/shard_map/weight_grad/pallas_call | solution.py:471
  398.1 15.3 %collective-permute-done.27 = bf16[256,2048]{1,0:T(8,128)(2,1)} collective-permute-done((bf16[256,2048]{1,0:T(8,128)(2,1)S(1)}, bf16[256,2048]{1,0:T(8,128)(2,1)}, u32[]{:S(2)}, u32[]{:S(2)}) %collective-permute-start.27) | collective-permute-done | bytes 1048608 | tf_op jit(solution)/shard_map/ppermute | solution.py:615
  415.5 3.5 collective-permute-start.31
  419.7 2.9 join.5.refs_2_
  422.7 2.9 join.4
  425.5 3.0 broadcast_select_fusion
  428.6 13.6 %collective-permute-done.31.mid_moved = bf16[256,2048]{1,0:T(8,128)(2,1)S(1)} collective-permute-done((bf16[256,2048]{1,0:T(8,128)(2,1)}, bf16[256,2048]{1,0:T(8,128)(2,1)S(1)}, u32[]{:S(2)}, u32[]{:S(2)}) %collective-permute-start.31) | collective-permute-done | bytes 1048608 | tf_op jit(solution)/shard_map/ppermute | solution.py:615
  446.6 3.5 collective-permute-start.34
  453.9 3.0 copy-done.12
  456.9 5.4 join.6
  462.3 4.0 fusion.77
  468.3 4.2 collective-permute-done.34.mid_moved
  477.1 4.6 advance.7
  481.7 3.7 collective-permute-start.36
  487.2 3.2 fusion.11
  493.2 15.9 %mixer_backward.1 = (bf16[4,2,1,128,1280]{4,3,2,1,0:T(8,128)(2,1)}, f32[8,640]{1,0:T(8,128)S(1)}, f32[4,2,160,160]{3,2,1,0:T(8,128)S(1)}) custom-call(s32[2]{0:T(128)S(1)} %pad_add_fusion.place, s32[1]{0:T(128)} %dynamic_slice.15.lengths, f32[2,1,128,640]{3,2,1,0:T(8,128)S(1)} %bitcast.154, f32[2,1,128,640]{3,2,1,0:T(8,128)S(1)} %bitcast.155, ...), custom_call_target="tpu_custom_call" | custom-call | flops 1 | bytes 1 | tf_op jit(solution)/shard_map/mixer_backward/pallas_call | solution.py:344
  511.3 3.3 row_dot.4
  525.8 9.1 %weight_grad.8 = (f32[320,2048]{1,0:T(8,128)}, f32[320,2048]{1,0:T(8,128)}, bf16[320,2048]{1,0:T(8,128)(2,1)}, bf16[320,2048]{1,0:T(8,128)(2,1)}, f32[1,2048]{1,0:T(1,128)S(1)}) custom-call(bf16[1024,1280]{1,0:T(8,128)(2,1)S(1)} %bitcast.118, bf16[1024,1280]{1,0:T(8,128)(2,1)S(1)} %bitcast.119, bf16[1024,1280]{1,0:T(8,128)(2,1)S(1)} %bitcast.120, ...), custom_call_target="tpu_custom_call" | custom-call | flops 1 | bytes 1 | tf_op jit(solution)/shard_map/weight_grad/pallas_call | solution.py:471
  535.0 4.8 weight_grad.9
  539.9 5.1 collective-permute-done.38.refs_0_
  545.1 5.9 row_dot.5
  554.0 3.7 collective-permute-done.44.refs_3_
  558.0 3.2 join.7
  568.9 2.9 constant_dynamic-slice_fusion.1
  575.3 3.6 row_dot.7
  578.9 12.2 %collective-permute-done.41.refs_0_ = bf16[256,2048]{1,0:T(8,128)(2,1)} collective-permute-done((bf16[256,2048]{1,0:T(8,128)(2,1)}, bf16[256,2048]{1,0:T(8,128)(2,1)}, u32[]{:S(2)}, u32[]{:S(2)}) %collective-permute-start.41) | collective-permute-done | bytes 1048608 | tf_op jit(solution)/shard_map/ppermute | solution.py:615
  591.1 4.5 row_dot.6
  598.0 2.5 collective-permute-start.53
  600.5 2.8 add_convert_fusion
  606.7 3.2 copy.55
  611.0 10.1 %collective-permute-done.42 = bf16[256,2048]{1,0:T(8,128)(2,1)S(1)} collective-permute-done((bf16[256,2048]{1,0:T(8,128)(2,1)}, bf16[256,2048]{1,0:T(8,128)(2,1)S(1)}, u32[]{:S(2)}, u32[]{:S(2)}) %collective-permute-start.42) | collective-permute-done | bytes 1048608 | tf_op jit(solution)/shard_map/ppermute | solution.py:615
  622.6 2.6 convert_add_fusion.2
  627.3 4.0 collective-permute-start.56
  633.4 3.3 collective-permute-done.57
  (468 shorter events, 133.5 us)
Async XLA Ops:
  7.2 66.1 %all-gather.5.cloned.1.call-start = ((), (), s32[]{:S(2)}) async-start(), calls=%async_computation.2 | async-start | bytes 3276800 | tf_op jit(solution)/shard_map/all_gather | solution.py:574
  7.9 81.6 %all-gather.7.cloned.1.call-start = ((), (), s32[]{:S(2)}) async-start(), calls=%async_computation.3 | async-start | bytes 1638400 | tf_op jit(solution)/shard_map/all_gather | solution.py:574
  8.7 156.7 %all-gather.9.cloned.1.call-start = ((), (), s32[]{:S(2)}) async-start(), calls=%async_computation.4 | async-start | bytes 7864320 | tf_op jit(solution)/shard_map/all_gather | solution.py:574
  9.5 191.0 %all-gather.11.cloned.1.call-start = ((), (), s32[]{:S(2)}) async-start(), calls=%async_computation.5 | async-start | bytes 3932160 | tf_op jit(solution)/shard_map/all_gather | solution.py:574
  9.7 5.3 collective-permute-start
  16.5 4.4 collective-permute-start.1
  17.0 28.4 %collective-permute-start.2 = (bf16[256,2048]{1,0:T(8,128)(2,1)S(1)}, bf16[256,2048]{1,0:T(8,128)(2,1)S(1)}, u32[]{:S(2)}, u32[]{:S(2)}) collective-permute-start(bf16[256,2048]{1,0:T(8,128)(2,1)S(1)} %fusion.3.refs_4_), channel_id=1, source_target_pairs={{0,8},{4,12},{8,16},{12,20},{16,24},{20,28},{24,0},{28,4},{1,9},{5... | collective-permute-start | bytes 3145736 | tf_op jit(solution)/shard_map/ppermute | solution.py:615
  46.4 26.8 %collective-permute-start.4 = (bf16[256,2048]{1,0:T(8,128)(2,1)S(1)}, bf16[256,2048]{1,0:T(8,128)(2,1)}, u32[]{:S(2)}, u32[]{:S(2)}) collective-permute-start(bf16[256,2048]{1,0:T(8,128)(2,1)S(1)} %collective-permute-done.2.refs_5_), channel_id=1, source_target_pairs={{0,8},{4,12},{8,16},{12,20},{16,24},{20,28},{24,0},{28,4},{1,9},{5... | collective-permute-start | bytes 3145736 | tf_op jit(solution)/shard_map/ppermute | solution.py:615
  73.3 5.3 collective-permute-start.6
  73.3 442.3 %reduce-scatter.3.cloned.1.call-start = ((), (), s32[]{:S(2)}) async-start(), calls=%async_computation.6 | async-start | bytes 3932160 | tf_op jit(solution)/shard_map/reduce_scatter | solution.py:578
  73.4 27.8 %collective-permute-start.9 = (f32[8,320]{1,0:T(8,128)S(1)}, f32[8,320]{1,0:T(8,128)S(1)}, u32[]{:S(2)}, u32[]{:S(2)}) collective-permute-start(f32[8,320]{1,0:T(8,128)S(1)} %concatenate.93), channel_id=1, source_target_pairs={{0,4},{4,0},{8,12},{12,8},{16,20},{20,16},{24,28},{28,24},{1,5},{5... | collective-permute-start | bytes 30728 | tf_op jit(solution)/shard_map/ppermute | solution.py:601
  74.0 27.2 %collective-permute-start.5 = (bf16[256,2048]{1,0:T(8,128)(2,1)}, bf16[256,2048]{1,0:T(8,128)(2,1)}, u32[]{:S(2)}, u32[]{:S(2)}) collective-permute-start(bf16[256,2048]{1,0:T(8,128)(2,1)} %collective-permute-done.4.refs_6_), channel_id=1, source_target_pairs={{0,8},{4,12},{8,16},{12,20},{16,24},{20,28},{24,0},{28,4},{1,9},{5... | collective-permute-start | bytes 3145736 | tf_op jit(solution)/shard_map/ppermute | solution.py:615
  101.2 26.1 %collective-permute-start.10 = (bf16[320,2048]{1,0:T(8,128)(2,1)}, bf16[320,2048]{1,0:T(8,128)(2,1)}, u32[]{:S(2)}, u32[]{:S(2)}) collective-permute-start(bf16[320,2048]{1,0:T(8,128)(2,1)} %all-gather.7.cloned.1.call-done), channel_id=1, source_target_pairs={{0,4},{4,0},{8,12},{12,8},{16,20},{20,16},{24,28},{28,24},{1,5},{5... | collective-permute-start | bytes 3932168 | tf_op jit(solution)/shard_map/ppermute | solution.py:601
  103.0 26.8 %collective-permute-start.7 = (bf16[256,2048]{1,0:T(8,128)(2,1)S(1)}, bf16[256,2048]{1,0:T(8,128)(2,1)S(1)}, u32[]{:S(2)}, u32[]{:S(2)}) collective-permute-start(bf16[256,2048]{1,0:T(8,128)(2,1)S(1)} %fusion.10.back.refs_4_), channel_id=1, source_target_pairs={{0,8},{4,12},{8,0},{12,4},{16,24},{20,28},{24,16},{28,20},{1,9},{5... | collective-permute-start | bytes 3145736 | tf_op jit(solution)/shard_map/ppermute | solution.py:615
  103.1 26.7 %collective-permute-start.8 = (bf16[256,2048]{1,0:T(8,128)(2,1)S(1)}, bf16[256,2048]{1,0:T(8,128)(2,1)S(1)}, u32[]{:S(2)}, u32[]{:S(2)}) collective-permute-start(bf16[256,2048]{1,0:T(8,128)(2,1)S(1)} %fusion.10.back.refs_4_), channel_id=1, source_target_pairs={{8,16},{12,20},{16,8},{20,12},{9,17},{13,21},{17,9},{21,13},{10,18... | collective-permute-start | bytes 3145736 | tf_op jit(solution)/shard_map/ppermute | solution.py:615
  129.9 12.6 %collective-permute-start.14 = (f32[1,3,320]{2,1,0:T(4,128)S(1)}, f32[1,3,320]{2,1,0:T(4,128)S(1)}, u32[]{:S(2)}, u32[]{:S(2)}) collective-permute-start(f32[1,3,320]{2,1,0:T(4,128)S(1)} %get-tuple-element.609), channel_id=1, source_target_pairs={{0,4},{4,0},{8,12},{12,8},{16,20},{20,16},{24,28},{28,24},{1,5},{5... | collective-permute-start | bytes 11528 | tf_op jit(solution)/shard_map/ppermute | solution.py:601
  130.5 11.4 %collective-permute-start.13 = (f32[1,320]{1,0:T(1,128)S(1)}, f32[1,320]{1,0:T(1,128)S(1)}, u32[]{:S(2)}, u32[]{:S(2)}) collective-permute-start(f32[1,320]{1,0:T(1,128)S(1)} %get-tuple-element.611), channel_id=1, source_target_pairs={{0,4},{4,0},{8,12},{12,8},{16,20},{20,16},{24,28},{28,24},{1,5},{5... | collective-permute-start | bytes 3848 | tf_op jit(solution)/shard_map/ppermute | solution.py:601
  130.6 26.8 %collective-permute-start.11 = (bf16[256,2048]{1,0:T(8,128)(2,1)S(1)}, bf16[256,2048]{1,0:T(8,128)(2,1)S(1)}, u32[]{:S(2)}, u32[]{:S(2)}) collective-permute-start(bf16[256,2048]{1,0:T(8,128)(2,1)S(1)} %broadcast_select_fusion.12), channel_id=1, source_target_pairs={{0,8},{4,12},{8,0},{12,4},{16,24},{20,28},{24,16},{28,20},{1,9},{5... | collective-permute-start | bytes 3145736 | tf_op jit(solution)/shard_map/ppermute | solution.py:615
  133.9 23.6 %collective-permute-start.12 = (bf16[256,2048]{1,0:T(8,128)(2,1)S(1)}, bf16[256,2048]{1,0:T(8,128)(2,1)S(1)}, u32[]{:S(2)}, u32[]{:S(2)}) collective-permute-start(bf16[256,2048]{1,0:T(8,128)(2,1)S(1)} %collective-permute-done.7), channel_id=1, source_target_pairs={{8,16},{12,20},{16,8},{20,12},{9,17},{13,21},{17,9},{21,13},{10,18... | collective-permute-start | bytes 3145736 | tf_op jit(solution)/shard_map/ppermute | solution.py:615
  160.0 26.8 %collective-permute-start.15 = (bf16[256,2048]{1,0:T(8,128)(2,1)}, bf16[256,2048]{1,0:T(8,128)(2,1)S(1)}, u32[]{:S(2)}, u32[]{:S(2)}) collective-permute-start(bf16[256,2048]{1,0:T(8,128)(2,1)} %get-tuple-element.294), channel_id=1, source_target_pairs={{0,8},{4,12},{8,0},{12,4},{16,24},{20,28},{24,16},{28,20},{1,9},{5... | collective-permute-start | bytes 3145736 | tf_op jit(solution)/shard_map/ppermute | solution.py:615
  163.8 23.0 %collective-permute-start.16 = (bf16[256,2048]{1,0:T(8,128)(2,1)}, bf16[256,2048]{1,0:T(8,128)(2,1)}, u32[]{:S(2)}, u32[]{:S(2)}) collective-permute-start(bf16[256,2048]{1,0:T(8,128)(2,1)} %get-tuple-element.296), channel_id=1, source_target_pairs={{8,16},{12,20},{16,8},{20,12},{9,17},{13,21},{17,9},{21,13},{10,18... | collective-permute-start | bytes 3145736 | tf_op jit(solution)/shard_map/ppermute | solution.py:615
  186.8 46.2 %collective-permute-start.20 = (bf16[2,2048,768]{2,1,0:T(8,128)(2,1)}, bf16[2,2048,768]{2,1,0:T(8,128)(2,1)}, u32[]{:S(2)}, u32[]{:S(2)}) collective-permute-start(bf16[2,2048,768]{2,1,0:T(8,128)(2,1)} %all-gather.9.cloned.1.call-done.own_in), channel_id=1, source_target_pairs={{0,4},{4,0},{8,12},{12,8},{16,20},{20,16},{24,28},{28,24},{1,5},{5... | collective-permute-start | bytes 18874376 | tf_op jit(solution)/shard_map/ppermute | solution.py:601
  193.8 27.6 %collective-permute-start.17 = (bf16[256,2048]{1,0:T(8,128)(2,1)}, bf16[256,2048]{1,0:T(8,128)(2,1)}, u32[]{:S(2)}, u32[]{:S(2)}) collective-permute-start(bf16[256,2048]{1,0:T(8,128)(2,1)} %get-tuple-element.306), channel_id=1, source_target_pairs={{0,8},{4,12},{8,0},{12,4},{16,24},{20,28},{24,16},{28,20},{1,9},{5... | collective-permute-start | bytes 3145736 | tf_op jit(solution)/shard_map/ppermute | solution.py:615
  197.2 24.2 %collective-permute-start.18 = (bf16[256,2048]{1,0:T(8,128)(2,1)}, bf16[256,2048]{1,0:T(8,128)(2,1)}, u32[]{:S(2)}, u32[]{:S(2)}) collective-permute-start(bf16[256,2048]{1,0:T(8,128)(2,1)} %get-tuple-element.309), channel_id=1, source_target_pairs={{8,16},{12,20},{16,8},{20,12},{9,17},{13,21},{17,9},{21,13},{10,18... | collective-permute-start | bytes 3145736 | tf_op jit(solution)/shard_map/ppermute | solution.py:615
  227.3 5.7 collective-permute-start.21
  227.3 27.8 %collective-permute-start.19 = (bf16[256,2048]{1,0:T(8,128)(2,1)S(1)}, bf16[256,2048]{1,0:T(8,128)(2,1)S(1)}, u32[]{:S(2)}, u32[]{:S(2)}) collective-permute-start(bf16[256,2048]{1,0:T(8,128)(2,1)S(1)} %multiply_convert_fusion.rows.refs_4_), channel_id=1, source_target_pairs={{0,8},{4,12},{8,16},{12,20},{16,24},{20,28},{24,0},{28,4},{1,9},{5... | collective-permute-start | bytes 3145736 | tf_op jit(solution)/shard_map/ppermute | solution.py:615
  255.1 26.6 %collective-permute-start.22 = (bf16[256,2048]{1,0:T(8,128)(2,1)S(1)}, bf16[256,2048]{1,0:T(8,128)(2,1)S(1)}, u32[]{:S(2)}, u32[]{:S(2)}) collective-permute-start(bf16[256,2048]{1,0:T(8,128)(2,1)S(1)} %collective-permute-done.19.rows.refs_5_), channel_id=1, source_target_pairs={{0,8},{4,12},{8,16},{12,20},{16,24},{20,28},{24,0},{28,4},{1,9},{5... | collective-permute-start | bytes 3145736 | tf_op jit(solution)/shard_map/ppermute | solution.py:615
  283.4 27.9 %collective-permute-start.24 = (bf16[256,2048]{1,0:T(8,128)(2,1)S(1)}, bf16[256,2048]{1,0:T(8,128)(2,1)S(1)}, u32[]{:S(2)}, u32[]{:S(2)}) collective-permute-start(bf16[256,2048]{1,0:T(8,128)(2,1)S(1)} %convert_element_type.138), channel_id=1, source_target_pairs={{0,8},{4,12},{8,16},{12,20},{16,24},{20,28},{24,0},{28,4},{1,9},{5... | collective-permute-start | bytes 3145736 | tf_op jit(solution)/shard_map/ppermute | solution.py:615
  283.7 47.9 %collective-permute-start.23 = (bf16[256,2048]{1,0:T(8,128)(2,1)S(1)}, bf16[256,2048]{1,0:T(8,128)(2,1)S(1)}, u32[]{:S(2)}, u32[]{:S(2)}) collective-permute-start(bf16[256,2048]{1,0:T(8,128)(2,1)S(1)} %collective-permute-done.22.rows.refs_6_), channel_id=1, source_target_pairs={{0,8},{4,12},{8,16},{12,20},{16,24},{20,28},{24,0},{28,4},{1,9},{5... | collective-permute-start | bytes 3145736 | tf_op jit(solution)/shard_map/ppermute | solution.py:615
  333.6 24.8 %collective-permute-start.25 = (bf16[256,2048]{1,0:T(8,128)(2,1)S(1)}, bf16[256,2048]{1,0:T(8,128)(2,1)S(1)}, u32[]{:S(2)}, u32[]{:S(2)}) collective-permute-start(bf16[256,2048]{1,0:T(8,128)(2,1)S(1)} %add_convert_fusion.2), channel_id=1, source_target_pairs={{0,8},{4,12},{8,16},{12,20},{16,24},{20,28},{24,0},{28,4},{1,9},{5... | collective-permute-start | bytes 3145736 | tf_op jit(solution)/shard_map/ppermute | solution.py:615
  360.5 24.1 %collective-permute-start.26 = (bf16[256,2048]{1,0:T(8,128)(2,1)S(1)}, bf16[256,2048]{1,0:T(8,128)(2,1)S(1)}, u32[]{:S(2)}, u32[]{:S(2)}) collective-permute-start(bf16[256,2048]{1,0:T(8,128)(2,1)S(1)} %add_convert_fusion.1), channel_id=1, source_target_pairs={{0,8},{4,12},{8,16},{12,20},{16,24},{20,28},{24,0},{28,4},{1,9},{5... | collective-permute-start | bytes 3145736 | tf_op jit(solution)/shard_map/ppermute | solution.py:615
  384.6 28.8 %collective-permute-start.29 = (bf16[768,2048]{1,0:T(8,128)(2,1)S(1)}, bf16[768,2048]{1,0:T(8,128)(2,1)S(1)}, u32[]{:S(2)}, u32[]{:S(2)}) collective-permute-start(bf16[768,2048]{1,0:T(8,128)(2,1)S(1)} %copy-done.104), channel_id=1, source_target_pairs={{0,4},{4,0},{8,12},{12,8},{16,20},{20,16},{24,28},{28,24},{1,5},{5... | collective-permute-start | bytes 9437192 | tf_op jit(solution)/shard_map/ppermute | solution.py:601
  384.6 28.7 %collective-permute-start.30 = (bf16[768,2048]{1,0:T(8,128)(2,1)}, bf16[768,2048]{1,0:T(8,128)(2,1)S(1)}, u32[]{:S(2)}, u32[]{:S(2)}) collective-permute-start(bf16[768,2048]{1,0:T(8,128)(2,1)} %get-tuple-element.396), channel_id=1, source_target_pairs={{0,4},{4,0},{8,12},{12,8},{16,20},{20,16},{24,28},{28,24},{1,5},{5... | collective-permute-start | bytes 9437192 | tf_op jit(solution)/shard_map/ppermute | solution.py:601
  388.0 25.3 %collective-permute-start.27 = (bf16[256,2048]{1,0:T(8,128)(2,1)S(1)}, bf16[256,2048]{1,0:T(8,128)(2,1)}, u32[]{:S(2)}, u32[]{:S(2)}) collective-permute-start(bf16[256,2048]{1,0:T(8,128)(2,1)S(1)} %get-tuple-element.386.refs_4_), channel_id=1, source_target_pairs={{0,8},{4,12},{8,0},{12,4},{16,24},{20,28},{24,16},{28,20},{1,9},{5... | collective-permute-start | bytes 3145736 | tf_op jit(solution)/shard_map/ppermute | solution.py:615
  388.1 25.2 %collective-permute-start.28 = (bf16[256,2048]{1,0:T(8,128)(2,1)S(1)}, bf16[256,2048]{1,0:T(8,128)(2,1)S(1)}, u32[]{:S(2)}, u32[]{:S(2)}) collective-permute-start(bf16[256,2048]{1,0:T(8,128)(2,1)S(1)} %get-tuple-element.386.refs_4_), channel_id=1, source_target_pairs={{8,16},{12,20},{16,8},{20,12},{9,17},{13,21},{17,9},{21,13},{10,18... | collective-permute-start | bytes 3145736 | tf_op jit(solution)/shard_map/ppermute | solution.py:615
  413.4 28.8 %collective-permute-start.33 = (bf16[768,2048]{1,0:T(8,128)(2,1)}, bf16[768,2048]{1,0:T(8,128)(2,1)}, u32[]{:S(2)}, u32[]{:S(2)}) collective-permute-start(bf16[768,2048]{1,0:T(8,128)(2,1)} %get-tuple-element.409), channel_id=1, source_target_pairs={{0,4},{4,0},{8,12},{12,8},{16,20},{20,16},{24,28},{28,24},{1,5},{5... | collective-permute-start | bytes 9437192 | tf_op jit(solution)/shard_map/ppermute | solution.py:601
  415.5 26.7 %collective-permute-start.31 = (bf16[256,2048]{1,0:T(8,128)(2,1)}, bf16[256,2048]{1,0:T(8,128)(2,1)S(1)}, u32[]{:S(2)}, u32[]{:S(2)}) collective-permute-start(bf16[256,2048]{1,0:T(8,128)(2,1)} %broadcast_select_fusion.9), channel_id=1, source_target_pairs={{0,8},{4,12},{8,0},{12,4},{16,24},{20,28},{24,16},{28,20},{1,9},{5... | collective-permute-start | bytes 3145736 | tf_op jit(solution)/shard_map/ppermute | solution.py:615
  419.0 23.1 %collective-permute-start.32 = (bf16[256,2048]{1,0:T(8,128)(2,1)}, bf16[256,2048]{1,0:T(8,128)(2,1)S(1)}, u32[]{:S(2)}, u32[]{:S(2)}) collective-permute-start(bf16[256,2048]{1,0:T(8,128)(2,1)} %collective-permute-done.27), channel_id=1, source_target_pairs={{8,16},{12,20},{16,8},{20,12},{9,17},{13,21},{17,9},{21,13},{10,18... | collective-permute-start | bytes 3145736 | tf_op jit(solution)/shard_map/ppermute | solution.py:615
  442.2 153.5 %reduce-scatter.5.cloned.1.call-start = ((), (), s32[]{:S(2)}) async-start(), calls=%async_computation.7 | async-start | bytes 7864320 | tf_op jit(solution)/shard_map/reduce_scatter | solution.py:578
  446.6 25.9 %collective-permute-start.34 = (bf16[256,2048]{1,0:T(8,128)(2,1)}, bf16[256,2048]{1,0:T(8,128)(2,1)}, u32[]{:S(2)}, u32[]{:S(2)}) collective-permute-start(bf16[256,2048]{1,0:T(8,128)(2,1)} %get-tuple-element.415), channel_id=1, source_target_pairs={{0,8},{4,12},{8,0},{12,4},{16,24},{20,28},{24,16},{28,20},{1,9},{5... | collective-permute-start | bytes 3145736 | tf_op jit(solution)/shard_map/ppermute | solution.py:615
  450.1 22.3 %collective-permute-start.35 = (bf16[256,2048]{1,0:T(8,128)(2,1)}, bf16[256,2048]{1,0:T(8,128)(2,1)}, u32[]{:S(2)}, u32[]{:S(2)}) collective-permute-start(bf16[256,2048]{1,0:T(8,128)(2,1)} %get-tuple-element.417), channel_id=1, source_target_pairs={{8,16},{12,20},{16,8},{20,12},{9,17},{13,21},{17,9},{21,13},{10,18... | collective-permute-start | bytes 3145736 | tf_op jit(solution)/shard_map/ppermute | solution.py:615
  481.7 33.0 %collective-permute-start.36 = (bf16[256,2048]{1,0:T(8,128)(2,1)}, bf16[256,2048]{1,0:T(8,128)(2,1)S(1)}, u32[]{:S(2)}, u32[]{:S(2)}) collective-permute-start(bf16[256,2048]{1,0:T(8,128)(2,1)} %get-tuple-element.429), channel_id=1, source_target_pairs={{0,8},{4,12},{8,0},{12,4},{16,24},{20,28},{24,16},{28,20},{1,9},{5... | collective-permute-start | bytes 3145736 | tf_op jit(solution)/shard_map/ppermute | solution.py:615
  485.4 30.3 %collective-permute-start.37 = (bf16[256,2048]{1,0:T(8,128)(2,1)}, bf16[256,2048]{1,0:T(8,128)(2,1)}, u32[]{:S(2)}, u32[]{:S(2)}) collective-permute-start(bf16[256,2048]{1,0:T(8,128)(2,1)} %get-tuple-element.432), channel_id=1, source_target_pairs={{8,16},{12,20},{16,8},{20,12},{9,17},{13,21},{17,9},{21,13},{10,18... | collective-permute-start | bytes 3145736 | tf_op jit(solution)/shard_map/ppermute | solution.py:615
  517.0 2.5 collective-permute-start.39
  517.1 28.0 %collective-permute-start.38 = (bf16[256,2048]{1,0:T(8,128)(2,1)}, bf16[256,2048]{1,0:T(8,128)(2,1)}, u32[]{:S(2)}, u32[]{:S(2)}) collective-permute-start(bf16[256,2048]{1,0:T(8,128)(2,1)} %row_dot.4), channel_id=1, source_target_pairs={{0,8},{4,12},{8,16},{12,20},{16,24},{20,28},{24,0},{28,4},{1,9},{5... | collective-permute-start | bytes 3145736 | tf_op jit(solution)/shard_map/ppermute | solution.py:615
  519.6 20.2 %collective-permute-start.40 = (bf16[656,160]{1,0:T(8,128)(2,1)S(1)}, bf16[656,160]{1,0:T(8,128)(2,1)S(1)}, u32[]{:S(2)}, u32[]{:S(2)}) collective-permute-start(bf16[656,160]{1,0:T(8,128)(2,1)S(1)} %fusion.17), channel_id=1, source_target_pairs={{0,1},{1,0},{2,3},{3,2},{4,5},{5,4},{6,7},{7,6},{8,9},{9,8},{10,11... | collective-permute-start | bytes 629768 | tf_op jit(solution)/shard_map/ppermute | solution.py:754
  551.0 3.0 collective-permute-start.43
  551.0 6.8 %collective-permute-start.44 = (bf16[320,2048]{1,0:T(8,128)(2,1)S(1)}, bf16[320,2048]{1,0:T(8,128)(2,1)S(1)}, u32[]{:S(2)}, u32[]{:S(2)}) collective-permute-start(bf16[320,2048]{1,0:T(8,128)(2,1)S(1)} %copy-done.105), channel_id=1, source_target_pairs={{0,4},{4,0},{8,12},{12,8},{16,20},{20,16},{24,28},{28,24},{1,5},{5... | collective-permute-start | bytes 3932168 | tf_op jit(solution)/shard_map/ppermute | solution.py:601
  551.5 6.5 collective-permute-start.45
  561.2 4.1 collective-permute-start.46
  562.8 3.7 collective-permute-start.47
  564.3 4.6 collective-permute-start.48
  564.7 26.5 %collective-permute-start.41 = (bf16[256,2048]{1,0:T(8,128)(2,1)}, bf16[256,2048]{1,0:T(8,128)(2,1)}, u32[]{:S(2)}, u32[]{:S(2)}) collective-permute-start(bf16[256,2048]{1,0:T(8,128)(2,1)} %row_dot.5), channel_id=1, source_target_pairs={{0,8},{4,12},{8,16},{12,20},{16,24},{20,28},{24,0},{28,4},{1,9},{5... | collective-permute-start | bytes 3145736 | tf_op jit(solution)/shard_map/ppermute | solution.py:615
  571.8 23.8 %collective-permute-start.49 = (bf16[960,512]{1,0:T(8,128)(2,1)}, bf16[960,512]{1,0:T(8,128)(2,1)}, u32[]{:S(2)}, u32[]{:S(2)}) collective-permute-start(bf16[960,512]{1,0:T(8,128)(2,1)} %get-tuple-element.575), channel_id=1, source_target_pairs={{0,1},{1,0},{2,3},{3,2},{4,5},{5,4},{6,7},{7,6},{8,9},{9,8},{10,11... | collective-permute-start | bytes 2949128 | tf_op jit(solution)/shard_map/ppermute | solution.py:594
  572.4 23.3 %collective-permute-start.50 = (bf16[960,512]{1,0:T(8,128)(2,1)}, bf16[960,512]{1,0:T(8,128)(2,1)}, u32[]{:S(2)}, u32[]{:S(2)}) collective-permute-start(bf16[960,512]{1,0:T(8,128)(2,1)} %get-tuple-element.574), channel_id=1, source_target_pairs={{0,2},{1,3},{2,0},{3,1},{4,6},{5,7},{6,4},{7,5},{8,10},{9,11},{10,... | collective-permute-start | bytes 2949128 | tf_op jit(solution)/shard_map/ppermute | solution.py:594
  595.7 25.4 %collective-permute-start.42 = (bf16[256,2048]{1,0:T(8,128)(2,1)}, bf16[256,2048]{1,0:T(8,128)(2,1)S(1)}, u32[]{:S(2)}, u32[]{:S(2)}) collective-permute-start(bf16[256,2048]{1,0:T(8,128)(2,1)} %row_dot.6), channel_id=1, source_target_pairs={{0,8},{4,12},{8,16},{12,20},{16,24},{20,28},{24,0},{28,4},{1,9},{5... | collective-permute-start | bytes 3145736 | tf_op jit(solution)/shard_map/ppermute | solution.py:615
  598.0 23.2 %collective-permute-start.53 = (bf16[960,512]{1,0:T(8,128)(2,1)}, bf16[960,512]{1,0:T(8,128)(2,1)}, u32[]{:S(2)}, u32[]{:S(2)}) collective-permute-start(bf16[960,512]{1,0:T(8,128)(2,1)} %constant_dynamic-slice_fusion), channel_id=1, source_target_pairs={{0,3},{1,2},{2,1},{3,0},{4,7},{5,6},{6,5},{7,4},{8,11},{9,10},{10,... | collective-permute-start | bytes 2949128 | tf_op jit(solution)/shard_map/ppermute | solution.py:594
  604.2 5.7 collective-permute-start.51
  604.2 5.6 collective-permute-start.52
  627.2 6.2 collective-permute-start.55
  627.3 6.2 collective-permute-start.56
  631.2 5.5 collective-permute-start.57
  631.6 7.2 %collective-permute-start.58 = (bf16[656,160]{1,0:T(8,128)(2,1)S(1)}, bf16[656,160]{1,0:T(8,128)(2,1)S(1)}, u32[]{:S(2)}, u32[]{:S(2)}) collective-permute-start(bf16[656,160]{1,0:T(8,128)(2,1)S(1)} %add.194), channel_id=1, source_target_pairs={{0,2},{1,3},{2,0},{3,1},{4,6},{5,7},{6,4},{7,5},{8,10},{9,11},{10,... | collective-permute-start | bytes 629768 | tf_op jit(solution)/shard_map/ppermute | solution.py:754
  633.3 9.8 %collective-permute-start.54 = (bf16[128,2048]{1,0:T(8,128)(2,1)S(1)}, bf16[128,2048]{1,0:T(8,128)(2,1)S(1)}, u32[]{:S(2)}, u32[]{:S(2)}) collective-permute-start(bf16[128,2048]{1,0:T(8,128)(2,1)S(1)} %get-tuple-element.583), channel_id=1, source_target_pairs={{0,4},{4,0},{8,12},{12,8},{16,20},{20,16},{24,28},{28,24},{1,5},{5... | collective-permute-start | bytes 1572872 | tf_op jit(solution)/shard_map/ppermute | solution.py:601
  (119 other events, 1305.7 us)
Sparse Core Ops, SparseCore 0:
  9.9 42.1 all-gather.4
  53.9 28.6 all-gather.6
  84.5 70.1 all-gather.8
  156.3 43.8 all-gather.10
  442.3 45.3 reduce-scatter.2
  490.5 77.3 reduce-scatter.4

commit v5 on v4

--- a/solution.py
+++ b/solution.py
@@ -14,7 +14,7 @@
 f32 = jnp.float32
 bf16 = jnp.bfloat16
 kernel_cost = pl.CostEstimate(flops=1, bytes_accessed=1, transcendentals=0)
-chain_cost = pl.CostEstimate(flops=1, bytes_accessed=1 << 26, transcendentals=0)
+chain_cost = pl.CostEstimate(flops=1 << 35, bytes_accessed=1 << 27, transcendentals=0)
 
 
 def gelu_tanh(v):
@@ -1004,7 +1004,7 @@
     parts = join(*[(own, swap(other)) for own, other in (*grads_in, grads_out)])
     gains = jnp.concatenate((gain_one / first_gain, gain_two[None]), axis=0)
     parts, gate_sum, gains = fence(parts, gate_sum, gains)
-    gains, parts = fence(direct_sum(gains, "narrow"), parts)
+    gains = direct_sum(gains, "narrow")
     sum_proj = DirectSum(parts)
     sum_proj.send(range(1, split))
     part, parts, grad_mlp_in, gate_sum, resid, gains, sum_proj.got = fence(

time: 660 us -> 671 us (1.017)
    ppermute x3, waiting for transfers between devices: 0.15 us -> 28.7 us  [send(): self.got.append(lax.ppermute(self.piece(flip), 'narrow', pairs))]
    ppermute x28, waiting for transfers between devices: 238 us -> 224 us  [move(): return lax.ppermute(values, 'wide', devices)]
    ppermute x6, waiting for transfers between devices: 7.59 us -> 0.65 us  [direct_sum(): lax.ppermute(values, axis, [(at, at ^ flip) for at in range(size)])]
    unnamed x247 -> x253, local copies, waits for them, and re-layouts: 28.5 us -> 32.7 us
  transfers between devices with their start and end apart: 65 -> 65, of which waited for: 30 -> 26; matrix products, arithmetic and copies ran while one was open for 14% -> 14% of each run, Pallas kernels for 28% -> 28%
where the time goes in v5:
time: 671 us; the launch traced here: 662 us
  waiting for transfers between devices  264 us (39%)
  Pallas kernels  187 us (28%)
  starting transfers between devices  62.5 us (9%)
  local copies, waits for them, and re-layouts  55.6 us (8%)
  other arithmetic  42.7 us (6%)
  matrix products  32.7 us (5%)
  between operations  16.7 us (2%)
    ppermute x28, waiting for transfers between devices, move(): return lax.ppermute(values, 'wide', devices)  224 us
    pallas_call x4, Pallas kernels, mlp_block(): pl.pallas_call(partial(mlp_kernel, tiles), grid=(2 * tiles,), in_specs=[w...  65.8 us
    ppermute x28, starting transfers between devices, move(): return lax.ppermute(values, 'wide', devices)  43.6 us
    pallas_call x5, Pallas kernels, weight_grad(): pl.pallas_call(partial(weight_grad_kernel, count, kinds, len(weights)), g...  40.7 us
    unnamed x253, local copies, waits for them, and re-layouts  32.7 us
    ppermute x3, waiting for transfers between devices, send(): self.got.append(lax.ppermute(self.piece(flip), 'narrow', pairs))  28.7 us
    dot_general x8, matrix products, dot_nt(): lax.dot_general(left, right, (((1,), (1,)), ((), ())), preferred_element_...  24.5 us
    pallas_call x4, Pallas kernels, join(): pl.pallas_call(partial(join_kernel, count, tiles), grid=(count * tiles,),...  17.7 us
  transfers between devices with their start and end apart: 65, of which 26 were waited for; matrix products, arithmetic and copies ran while one was open for 14% of the time, Pallas kernels for 28%

profile of v5, /device:TPU:0, one launch (start us, length us, event | category | flops | bytes accessed | tf_op | source)
XLA Modules:
  0.0 661.8 jit_solution(11451242043730734443)
XLA Ops:
  17.0 2.6 collective-permute-start.2
  21.2 24.3 %collective-permute-done.2.refs_5_ = bf16[256,2048]{1,0:T(8,128)(2,1)S(1)} collective-permute-done((bf16[256,2048]{1,0:T(8,128)(2,1)S(1)}, bf16[256,2048]{1,0:T(8,128)(2,1)S(1)}, u32[]{:S(2)}, u32[]{:S(2)}) %collective-permute-start.2) | collective-permute-done | bytes 1048608 | tf_op jit(solution)/shard_map/ppermute | solution.py:615
  46.5 26.8 %collective-permute-done.4.refs_6_ = bf16[256,2048]{1,0:T(8,128)(2,1)} collective-permute-done((bf16[256,2048]{1,0:T(8,128)(2,1)S(1)}, bf16[256,2048]{1,0:T(8,128)(2,1)}, u32[]{:S(2)}, u32[]{:S(2)}) %collective-permute-start.4) | collective-permute-done | bytes 1048608 | tf_op jit(solution)/shard_map/ppermute | solution.py:615
  80.6 3.7 convolution_bitcast_fusion.1.refs_2_
  84.3 2.6 convolution_bitcast_fusion.2.refs_1_
  86.9 2.6 convolution_bitcast_fusion.3.refs_0_
  89.6 11.7 %collective-permute-done.5.refs_7_ = bf16[256,2048]{1,0:T(8,128)(2,1)} collective-permute-done((bf16[256,2048]{1,0:T(8,128)(2,1)}, bf16[256,2048]{1,0:T(8,128)(2,1)}, u32[]{:S(2)}, u32[]{:S(2)}) %collective-permute-start.5) | collective-permute-done | bytes 1048608 | tf_op jit(solution)/shard_map/ppermute | solution.py:615
  104.1 4.5 convolution_bitcast_fusion.refs_3_
  108.6 17.5 %mixer_forward.1 = (bf16[4,2,1,128,640]{4,3,2,1,0:T(8,128)(2,1)}, f32[4,2,1,128,640]{4,3,2,1,0:T(8,128)}, f32[4,2,1,128,640]{4,3,2,1,0:T(8,128)}, f32[4,2,1,128,...) custom-call(s32[2]{0:T(128)S(1)} %pad_add_fusion.place, ...), custom_call_target="tpu_custom_call" | custom-call | flops 1 | bytes 1 | tf_op jit(solution)/shard_map/mixer_forward/pallas_call | solution.py:306
  130.6 3.2 collective-permute-start.11
  143.1 14.4 %collective-permute-done.11.mid_moved = bf16[256,2048]{1,0:T(8,128)(2,1)S(1)} collective-permute-done((bf16[256,2048]{1,0:T(8,128)(2,1)S(1)}, bf16[256,2048]{1,0:T(8,128)(2,1)S(1)}, u32[]{:S(2)}, u32[]{:S(2)}) %collective-permute-start.11) | collective-permute-done | bytes 1048608 | tf_op jit(solution)/shard_map/ppermute | solution.py:615
  160.0 3.8 collective-permute-start.15
  165.5 21.4 %collective-permute-done.15.mid_moved = bf16[256,2048]{1,0:T(8,128)(2,1)S(1)} collective-permute-done((bf16[256,2048]{1,0:T(8,128)(2,1)}, bf16[256,2048]{1,0:T(8,128)(2,1)S(1)}, u32[]{:S(2)}, u32[]{:S(2)}) %collective-permute-start.15) | collective-permute-done | bytes 1048608 | tf_op jit(solution)/shard_map/ppermute | solution.py:615
  189.7 4.2 advance.5
  193.9 3.4 collective-permute-start.17
  200.6 20.9 %collective-permute-done.17 = bf16[256,2048]{1,0:T(8,128)(2,1)} collective-permute-done((bf16[256,2048]{1,0:T(8,128)(2,1)}, bf16[256,2048]{1,0:T(8,128)(2,1)}, u32[]{:S(2)}, u32[]{:S(2)}) %collective-permute-start.17) | collective-permute-done | bytes 1048608 | tf_op jit(solution)/shard_map/ppermute | solution.py:615
  221.4 3.2 multiply_reduce_fusion.2
  227.3 4.3 collective-permute-start.19
  233.0 16.5 %mlp_block.4 = (bf16[256,1536]{1,0:T(8,128)(2,1)}, bf16[256,1536]{1,0:T(8,128)(2,1)}, bf16[256,1536]{1,0:T(8,128)(2,1)}, f32[256,2048]{1,0:T(8,128)}, bf16[256,2048]{1,0:T(8,128)(2,1)}) custom-call(bf16[256,2048]{1,0:T(8,128)(2,1)S(1)} %multiply_convert_fusion.rows.refs_4_, bf16[256,2048]{1,0:T(8,128)(2,1)S(1)} %copy-done.10, ...), custom_call_target="tpu_custom_call" | custom-call | flops 1 | bytes 1 | tf_op jit(solution)/shard_map/mlp_block/pallas_call | solution.py:421
  249.5 5.6 collective-permute-done.19.rows.refs_5_
  257.2 16.4 %mlp_block.5 = (bf16[256,1536]{1,0:T(8,128)(2,1)}, bf16[256,1536]{1,0:T(8,128)(2,1)}, bf16[256,1536]{1,0:T(8,128)(2,1)}, f32[256,2048]{1,0:T(8,128)}, bf16[256,2048]{1,0:T(8,128)(2,1)}) custom-call(bf16[256,2048]{1,0:T(8,128)(2,1)S(1)} %collective-permute-done.19.rows.refs_5_, bf16[256,2048]{1,0:T(8,128)(2,1)S(1)} %copy-done.12, ...), custom_call_target="tpu_custom_call" | custom-call | flops 1 | bytes 1 | tf_op jit(solution)/shard_map/mlp_block/pallas_call | solution.py:421
  273.6 8.0 %collective-permute-done.22.rows.refs_6_ = bf16[256,2048]{1,0:T(8,128)(2,1)S(1)} collective-permute-done((bf16[256,2048]{1,0:T(8,128)(2,1)S(1)}, bf16[256,2048]{1,0:T(8,128)(2,1)S(1)}, u32[]{:S(2)}, u32[]{:S(2)}) %collective-permute-start.22) | collective-permute-done | bytes 1048608 | tf_op jit(solution)/shard_map/ppermute | solution.py:615
  285.4 16.4 %mlp_block.6 = (bf16[256,1536]{1,0:T(8,128)(2,1)}, bf16[256,1536]{1,0:T(8,128)(2,1)}, bf16[256,1536]{1,0:T(8,128)(2,1)}, f32[256,2048]{1,0:T(8,128)}, bf16[256,2048]{1,0:T(8,128)(2,1)}) custom-call(bf16[256,2048]{1,0:T(8,128)(2,1)S(1)} %collective-permute-done.22.rows.refs_6_, bf16[256,2048]{1,0:T(8,128)(2,1)S(1)} %broadcast_select_fusion.10.back.refs_6_, ...), custom_call_target="tpu_custom_call" | custom-call | flops 1 | bytes 1 | tf_op jit(solution)/shard_map/mlp_block/pallas_call | solution.py:421
  301.8 9.6 %collective-permute-done.24 = bf16[256,2048]{1,0:T(8,128)(2,1)S(1)} collective-permute-done((bf16[256,2048]{1,0:T(8,128)(2,1)S(1)}, bf16[256,2048]{1,0:T(8,128)(2,1)S(1)}, u32[]{:S(2)}, u32[]{:S(2)}) %collective-permute-start.24) | collective-permute-done | bytes 1048608 | tf_op jit(solution)/shard_map/ppermute | solution.py:615
  311.4 20.3 %collective-permute-done.23.rows.refs_7_ = bf16[256,2048]{1,0:T(8,128)(2,1)S(1)} collective-permute-done((bf16[256,2048]{1,0:T(8,128)(2,1)S(1)}, bf16[256,2048]{1,0:T(8,128)(2,1)S(1)}, u32[]{:S(2)}, u32[]{:S(2)}) %collective-permute-start.23) | collective-permute-done | bytes 1048608 | tf_op jit(solution)/shard_map/ppermute | solution.py:615
  333.7 16.4 %mlp_block.7 = (bf16[256,1536]{1,0:T(8,128)(2,1)}, bf16[256,1536]{1,0:T(8,128)(2,1)}, bf16[256,1536]{1,0:T(8,128)(2,1)}, f32[256,2048]{1,0:T(8,128)}, bf16[256,2048]{1,0:T(8,128)(2,1)}) custom-call(bf16[256,2048]{1,0:T(8,128)(2,1)S(1)} %collective-permute-done.23.rows.refs_7_, bf16[256,2048]{1,0:T(8,128)(2,1)S(1)} %copy-done.11, ...), custom_call_target="tpu_custom_call" | custom-call | flops 1 | bytes 1 | tf_op jit(solution)/shard_map/mlp_block/pallas_call | solution.py:421
  350.1 8.3 %collective-permute-done.25 = bf16[256,2048]{1,0:T(8,128)(2,1)S(1)} collective-permute-done((bf16[256,2048]{1,0:T(8,128)(2,1)S(1)}, bf16[256,2048]{1,0:T(8,128)(2,1)S(1)}, u32[]{:S(2)}, u32[]{:S(2)}) %collective-permute-start.25) | collective-permute-done | bytes 1048608 | tf_op jit(solution)/shard_map/ppermute | solution.py:615
  360.9 8.9 %weight_grad.6 = (f32[768,2048]{1,0:T(8,128)}, bf16[768,2048]{1,0:T(8,128)(2,1)}) custom-call(bf16[256,1536]{1,0:T(8,128)(2,1)S(1)} %copy-done.46, bf16[256,1536]{1,0:T(8,128)(2,1)S(1)} %copy-done.49, bf16[256,1536]{1,0:T(8,128)(2,1)S(1)} %copy-done.51, bf16[256,1536]{1,0:T(8,128)(2,1)S(1)} %copy-done.53, bf16[256,2048]{1,0:T(8,128)(2,1)S(1)} %copy-done.10, ...), custom_call_target="tpu_custom_call" | custom-call | flops 1 | bytes 1 | tf_op jit(solution)/shard_map/weight_grad/pallas_call | solution.py:471
  369.9 9.0 %weight_grad.5 = (f32[768,2048]{1,0:T(8,128)}, bf16[768,2048]{1,0:T(8,128)(2,1)}) custom-call(bf16[256,1536]{1,0:T(8,128)(2,1)S(1)} %copy-done.45, bf16[256,1536]{1,0:T(8,128)(2,1)S(1)} %copy-done.48, bf16[256,1536]{1,0:T(8,128)(2,1)S(1)} %copy-done.50, bf16[256,1536]{1,0:T(8,128)(2,1)S(1)} %copy-done.52, ...), custom_call_target="tpu_custom_call" | custom-call | flops 1 | bytes 1 | tf_op jit(solution)/shard_map/weight_grad/pallas_call | solution.py:471
  378.8 5.8 collective-permute-done.26
  389.0 8.9 %weight_grad.7 = (f32[768,2048]{1,0:T(8,128)}, bf16[768,2048]{1,0:T(8,128)(2,1)}) custom-call(bf16[256,1536]{1,0:T(8,128)(2,1)S(1)} %copy-done.42, bf16[256,1536]{1,0:T(8,128)(2,1)S(1)} %copy-done.43, bf16[256,1536]{1,0:T(8,128)(2,1)S(1)} %copy-done.44, bf16[256,1536]{1,0:T(8,128)(2,1)S(1)} %copy-done.47, ...), custom_call_target="tpu_custom_call" | custom-call | flops 1 | bytes 1 | tf_op jit(solution)/shard_map/weight_grad/pallas_call | solution.py:471
  398.1 15.3 %collective-permute-done.27 = bf16[256,2048]{1,0:T(8,128)(2,1)} collective-permute-done((bf16[256,2048]{1,0:T(8,128)(2,1)S(1)}, bf16[256,2048]{1,0:T(8,128)(2,1)}, u32[]{:S(2)}, u32[]{:S(2)}) %collective-permute-start.27) | collective-permute-done | bytes 1048608 | tf_op jit(solution)/shard_map/ppermute | solution.py:615
  414.6 3.5 collective-permute-start.31
  418.8 2.9 join.5.refs_2_
  421.8 2.9 join.4
  424.7 3.0 broadcast_select_fusion
  427.7 14.4 %collective-permute-done.31.mid_moved = bf16[256,2048]{1,0:T(8,128)(2,1)S(1)} collective-permute-done((bf16[256,2048]{1,0:T(8,128)(2,1)}, bf16[256,2048]{1,0:T(8,128)(2,1)S(1)}, u32[]{:S(2)}, u32[]{:S(2)}) %collective-permute-start.31) | collective-permute-done | bytes 1048608 | tf_op jit(solution)/shard_map/ppermute | solution.py:615
  446.6 3.5 collective-permute-start.34
  453.9 3.0 copy-done.13
  456.9 5.5 join.6
  462.4 4.1 fusion.77
  468.3 5.1 collective-permute-done.34.mid_moved
  478.1 4.7 advance.7
  482.8 3.5 collective-permute-start.36
  488.1 3.2 fusion.11
  494.1 15.9 %mixer_backward.1 = (bf16[4,2,1,128,1280]{4,3,2,1,0:T(8,128)(2,1)}, f32[8,640]{1,0:T(8,128)S(1)}, f32[4,2,160,160]{3,2,1,0:T(8,128)S(1)}) custom-call(s32[2]{0:T(128)S(1)} %pad_add_fusion.place, s32[1]{0:T(128)} %dynamic_slice.15.lengths, f32[2,1,128,640]{3,2,1,0:T(8,128)S(1)} %bitcast.154, f32[2,1,128,640]{3,2,1,0:T(8,128)S(1)} %bitcast.155, ...), custom_call_target="tpu_custom_call" | custom-call | flops 1 | bytes 1 | tf_op jit(solution)/shard_map/mixer_backward/pallas_call | solution.py:344
  512.1 3.3 row_dot.4
  526.2 9.1 %weight_grad.8 = (f32[320,2048]{1,0:T(8,128)}, f32[320,2048]{1,0:T(8,128)}, bf16[320,2048]{1,0:T(8,128)(2,1)}, bf16[320,2048]{1,0:T(8,128)(2,1)}, f32[1,2048]{1,0:T(1,128)S(1)}) custom-call(bf16[1024,1280]{1,0:T(8,128)(2,1)S(1)} %bitcast.120, bf16[1024,1280]{1,0:T(8,128)(2,1)S(1)} %bitcast.121, bf16[1024,1280]{1,0:T(8,128)(2,1)S(1)} %bitcast.122, ...), custom_call_target="tpu_custom_call" | custom-call | flops 1 | bytes 1 | tf_op jit(solution)/shard_map/weight_grad/pallas_call | solution.py:471
  535.3 4.7 weight_grad.9
  540.2 5.4 collective-permute-done.38.refs_0_
  545.6 3.5 copy-done.4
  549.1 4.5 row_dot.5
  557.0 3.5 row_dot.7
  562.7 6.4 join.7
  575.3 6.8 %collective-permute-done.41.refs_0_ = bf16[256,2048]{1,0:T(8,128)(2,1)} collective-permute-done((bf16[256,2048]{1,0:T(8,128)(2,1)}, bf16[256,2048]{1,0:T(8,128)(2,1)}, u32[]{:S(2)}, u32[]{:S(2)}) %collective-permute-start.41) | collective-permute-done | bytes 1048608 | tf_op jit(solution)/shard_map/ppermute | solution.py:615
  583.2 4.5 row_dot.6
  587.8 9.6 %collective-permute-done.49 = bf16[960,512]{1,0:T(8,128)(2,1)} collective-permute-done((bf16[960,512]{1,0:T(8,128)(2,1)S(1)}, bf16[960,512]{1,0:T(8,128)(2,1)}, u32[]{:S(2)}, u32[]{:S(2)}) %collective-permute-start.49) | collective-permute-done | bytes 983072 | tf_op jit(solution)/shard_map/ppermute | solution.py:594
  597.4 8.2 %collective-permute-done.50 = bf16[960,512]{1,0:T(8,128)(2,1)} collective-permute-done((bf16[960,512]{1,0:T(8,128)(2,1)S(1)}, bf16[960,512]{1,0:T(8,128)(2,1)}, u32[]{:S(2)}, u32[]{:S(2)}) %collective-permute-start.50) | collective-permute-done | bytes 983072 | tf_op jit(solution)/shard_map/ppermute | solution.py:594
  610.1 2.8 add_convert_fusion
  616.2 3.2 copy.55
  620.6 10.9 %collective-permute-done.53 = bf16[960,512]{1,0:T(8,128)(2,1)} collective-permute-done((bf16[960,512]{1,0:T(8,128)(2,1)}, bf16[960,512]{1,0:T(8,128)(2,1)}, u32[]{:S(2)}, u32[]{:S(2)}) %collective-permute-start.53) | collective-permute-done | bytes 983072 | tf_op jit(solution)/shard_map/ppermute | solution.py:594
  632.8 2.6 convert_add_fusion.2
  637.6 4.3 collective-permute-start.57
  644.4 4.6 collective-permute-done.58
  (474 shorter events, 131.4 us)
Async XLA Ops:
  7.2 66.1 %all-gather.5.cloned.1.call-start = ((), (), s32[]{:S(2)}) async-start(), calls=%async_computation.2 | async-start | bytes 3276800 | tf_op jit(solution)/shard_map/all_gather | solution.py:574
  7.9 81.6 %all-gather.7.cloned.1.call-start = ((), (), s32[]{:S(2)}) async-start(), calls=%async_computation.3 | async-start | bytes 1638400 | tf_op jit(solution)/shard_map/all_gather | solution.py:574
  8.7 156.7 %all-gather.9.cloned.1.call-start = ((), (), s32[]{:S(2)}) async-start(), calls=%async_computation.4 | async-start | bytes 7864320 | tf_op jit(solution)/shard_map/all_gather | solution.py:574
  9.5 191.1 %all-gather.11.cloned.1.call-start = ((), (), s32[]{:S(2)}) async-start(), calls=%async_computation.5 | async-start | bytes 3932160 | tf_op jit(solution)/shard_map/all_gather | solution.py:574
  9.7 5.3 collective-permute-start
  16.5 4.4 collective-permute-start.1
  17.0 28.4 %collective-permute-start.2 = (bf16[256,2048]{1,0:T(8,128)(2,1)S(1)}, bf16[256,2048]{1,0:T(8,128)(2,1)S(1)}, u32[]{:S(2)}, u32[]{:S(2)}) collective-permute-start(bf16[256,2048]{1,0:T(8,128)(2,1)S(1)} %fusion.3.refs_4_), channel_id=1, source_target_pairs={{0,8},{4,12},{8,16},{12,20},{16,24},{20,28},{24,0},{28,4},{1,9},{5... | collective-permute-start | bytes 3145736 | tf_op jit(solution)/shard_map/ppermute | solution.py:615
  46.4 26.8 %collective-permute-start.4 = (bf16[256,2048]{1,0:T(8,128)(2,1)S(1)}, bf16[256,2048]{1,0:T(8,128)(2,1)}, u32[]{:S(2)}, u32[]{:S(2)}) collective-permute-start(bf16[256,2048]{1,0:T(8,128)(2,1)S(1)} %collective-permute-done.2.refs_5_), channel_id=1, source_target_pairs={{0,8},{4,12},{8,16},{12,20},{16,24},{20,28},{24,0},{28,4},{1,9},{5... | collective-permute-start | bytes 3145736 | tf_op jit(solution)/shard_map/ppermute | solution.py:615
  73.3 5.3 collective-permute-start.6
  73.3 443.2 %reduce-scatter.3.cloned.1.call-start = ((), (), s32[]{:S(2)}) async-start(), calls=%async_computation.6 | async-start | bytes 3932160 | tf_op jit(solution)/shard_map/reduce_scatter | solution.py:578
  73.5 27.8 %collective-permute-start.9 = (f32[8,320]{1,0:T(8,128)S(1)}, f32[8,320]{1,0:T(8,128)S(1)}, u32[]{:S(2)}, u32[]{:S(2)}) collective-permute-start(f32[8,320]{1,0:T(8,128)S(1)} %concatenate.93), channel_id=1, source_target_pairs={{0,4},{4,0},{8,12},{12,8},{16,20},{20,16},{24,28},{28,24},{1,5},{5... | collective-permute-start | bytes 30728 | tf_op jit(solution)/shard_map/ppermute | solution.py:601
  74.0 27.2 %collective-permute-start.5 = (bf16[256,2048]{1,0:T(8,128)(2,1)}, bf16[256,2048]{1,0:T(8,128)(2,1)}, u32[]{:S(2)}, u32[]{:S(2)}) collective-permute-start(bf16[256,2048]{1,0:T(8,128)(2,1)} %collective-permute-done.4.refs_6_), channel_id=1, source_target_pairs={{0,8},{4,12},{8,16},{12,20},{16,24},{20,28},{24,0},{28,4},{1,9},{5... | collective-permute-start | bytes 3145736 | tf_op jit(solution)/shard_map/ppermute | solution.py:615
  101.2 26.1 %collective-permute-start.10 = (bf16[320,2048]{1,0:T(8,128)(2,1)}, bf16[320,2048]{1,0:T(8,128)(2,1)}, u32[]{:S(2)}, u32[]{:S(2)}) collective-permute-start(bf16[320,2048]{1,0:T(8,128)(2,1)} %all-gather.7.cloned.1.call-done), channel_id=1, source_target_pairs={{0,4},{4,0},{8,12},{12,8},{16,20},{20,16},{24,28},{28,24},{1,5},{5... | collective-permute-start | bytes 3932168 | tf_op jit(solution)/shard_map/ppermute | solution.py:601
  103.0 26.8 %collective-permute-start.7 = (bf16[256,2048]{1,0:T(8,128)(2,1)S(1)}, bf16[256,2048]{1,0:T(8,128)(2,1)S(1)}, u32[]{:S(2)}, u32[]{:S(2)}) collective-permute-start(bf16[256,2048]{1,0:T(8,128)(2,1)S(1)} %fusion.10.back.refs_4_), channel_id=1, source_target_pairs={{0,8},{4,12},{8,0},{12,4},{16,24},{20,28},{24,16},{28,20},{1,9},{5... | collective-permute-start | bytes 3145736 | tf_op jit(solution)/shard_map/ppermute | solution.py:615
  103.1 26.7 %collective-permute-start.8 = (bf16[256,2048]{1,0:T(8,128)(2,1)S(1)}, bf16[256,2048]{1,0:T(8,128)(2,1)S(1)}, u32[]{:S(2)}, u32[]{:S(2)}) collective-permute-start(bf16[256,2048]{1,0:T(8,128)(2,1)S(1)} %fusion.10.back.refs_4_), channel_id=1, source_target_pairs={{8,16},{12,20},{16,8},{20,12},{9,17},{13,21},{17,9},{21,13},{10,18... | collective-permute-start | bytes 3145736 | tf_op jit(solution)/shard_map/ppermute | solution.py:615
  129.9 12.6 %collective-permute-start.14 = (f32[1,3,320]{2,1,0:T(4,128)S(1)}, f32[1,3,320]{2,1,0:T(4,128)S(1)}, u32[]{:S(2)}, u32[]{:S(2)}) collective-permute-start(f32[1,3,320]{2,1,0:T(4,128)S(1)} %get-tuple-element.605), channel_id=1, source_target_pairs={{0,4},{4,0},{8,12},{12,8},{16,20},{20,16},{24,28},{28,24},{1,5},{5... | collective-permute-start | bytes 11528 | tf_op jit(solution)/shard_map/ppermute | solution.py:601
  130.5 11.4 %collective-permute-start.13 = (f32[1,320]{1,0:T(1,128)S(1)}, f32[1,320]{1,0:T(1,128)S(1)}, u32[]{:S(2)}, u32[]{:S(2)}) collective-permute-start(f32[1,320]{1,0:T(1,128)S(1)} %get-tuple-element.607), channel_id=1, source_target_pairs={{0,4},{4,0},{8,12},{12,8},{16,20},{20,16},{24,28},{28,24},{1,5},{5... | collective-permute-start | bytes 3848 | tf_op jit(solution)/shard_map/ppermute | solution.py:601
  130.6 26.8 %collective-permute-start.11 = (bf16[256,2048]{1,0:T(8,128)(2,1)S(1)}, bf16[256,2048]{1,0:T(8,128)(2,1)S(1)}, u32[]{:S(2)}, u32[]{:S(2)}) collective-permute-start(bf16[256,2048]{1,0:T(8,128)(2,1)S(1)} %broadcast_select_fusion.12), channel_id=1, source_target_pairs={{0,8},{4,12},{8,0},{12,4},{16,24},{20,28},{24,16},{28,20},{1,9},{5... | collective-permute-start | bytes 3145736 | tf_op jit(solution)/shard_map/ppermute | solution.py:615
  133.9 23.6 %collective-permute-start.12 = (bf16[256,2048]{1,0:T(8,128)(2,1)S(1)}, bf16[256,2048]{1,0:T(8,128)(2,1)S(1)}, u32[]{:S(2)}, u32[]{:S(2)}) collective-permute-start(bf16[256,2048]{1,0:T(8,128)(2,1)S(1)} %collective-permute-done.7), channel_id=1, source_target_pairs={{8,16},{12,20},{16,8},{20,12},{9,17},{13,21},{17,9},{21,13},{10,18... | collective-permute-start | bytes 3145736 | tf_op jit(solution)/shard_map/ppermute | solution.py:615
  160.0 26.8 %collective-permute-start.15 = (bf16[256,2048]{1,0:T(8,128)(2,1)}, bf16[256,2048]{1,0:T(8,128)(2,1)S(1)}, u32[]{:S(2)}, u32[]{:S(2)}) collective-permute-start(bf16[256,2048]{1,0:T(8,128)(2,1)} %get-tuple-element.292), channel_id=1, source_target_pairs={{0,8},{4,12},{8,0},{12,4},{16,24},{20,28},{24,16},{28,20},{1,9},{5... | collective-permute-start | bytes 3145736 | tf_op jit(solution)/shard_map/ppermute | solution.py:615
  163.8 23.0 %collective-permute-start.16 = (bf16[256,2048]{1,0:T(8,128)(2,1)}, bf16[256,2048]{1,0:T(8,128)(2,1)}, u32[]{:S(2)}, u32[]{:S(2)}) collective-permute-start(bf16[256,2048]{1,0:T(8,128)(2,1)} %get-tuple-element.294), channel_id=1, source_target_pairs={{8,16},{12,20},{16,8},{20,12},{9,17},{13,21},{17,9},{21,13},{10,18... | collective-permute-start | bytes 3145736 | tf_op jit(solution)/shard_map/ppermute | solution.py:615
  186.8 46.2 %collective-permute-start.20 = (bf16[2,2048,768]{2,1,0:T(8,128)(2,1)}, bf16[2,2048,768]{2,1,0:T(8,128)(2,1)}, u32[]{:S(2)}, u32[]{:S(2)}) collective-permute-start(bf16[2,2048,768]{2,1,0:T(8,128)(2,1)} %all-gather.9.cloned.1.call-done.own_in), channel_id=1, source_target_pairs={{0,4},{4,0},{8,12},{12,8},{16,20},{20,16},{24,28},{28,24},{1,5},{5... | collective-permute-start | bytes 18874376 | tf_op jit(solution)/shard_map/ppermute | solution.py:601
  193.9 27.6 %collective-permute-start.17 = (bf16[256,2048]{1,0:T(8,128)(2,1)}, bf16[256,2048]{1,0:T(8,128)(2,1)}, u32[]{:S(2)}, u32[]{:S(2)}) collective-permute-start(bf16[256,2048]{1,0:T(8,128)(2,1)} %get-tuple-element.304), channel_id=1, source_target_pairs={{0,8},{4,12},{8,0},{12,4},{16,24},{20,28},{24,16},{28,20},{1,9},{5... | collective-permute-start | bytes 3145736 | tf_op jit(solution)/shard_map/ppermute | solution.py:615
  197.3 24.2 %collective-permute-start.18 = (bf16[256,2048]{1,0:T(8,128)(2,1)}, bf16[256,2048]{1,0:T(8,128)(2,1)}, u32[]{:S(2)}, u32[]{:S(2)}) collective-permute-start(bf16[256,2048]{1,0:T(8,128)(2,1)} %get-tuple-element.307), channel_id=1, source_target_pairs={{8,16},{12,20},{16,8},{20,12},{9,17},{13,21},{17,9},{21,13},{10,18... | collective-permute-start | bytes 3145736 | tf_op jit(solution)/shard_map/ppermute | solution.py:615
  227.3 5.7 collective-permute-start.21
  227.3 27.8 %collective-permute-start.19 = (bf16[256,2048]{1,0:T(8,128)(2,1)S(1)}, bf16[256,2048]{1,0:T(8,128)(2,1)S(1)}, u32[]{:S(2)}, u32[]{:S(2)}) collective-permute-start(bf16[256,2048]{1,0:T(8,128)(2,1)S(1)} %multiply_convert_fusion.rows.refs_4_), channel_id=1, source_target_pairs={{0,8},{4,12},{8,16},{12,20},{16,24},{20,28},{24,0},{28,4},{1,9},{5... | collective-permute-start | bytes 3145736 | tf_op jit(solution)/shard_map/ppermute | solution.py:615
  255.1 26.6 %collective-permute-start.22 = (bf16[256,2048]{1,0:T(8,128)(2,1)S(1)}, bf16[256,2048]{1,0:T(8,128)(2,1)S(1)}, u32[]{:S(2)}, u32[]{:S(2)}) collective-permute-start(bf16[256,2048]{1,0:T(8,128)(2,1)S(1)} %collective-permute-done.19.rows.refs_5_), channel_id=1, source_target_pairs={{0,8},{4,12},{8,16},{12,20},{16,24},{20,28},{24,0},{28,4},{1,9},{5... | collective-permute-start | bytes 3145736 | tf_op jit(solution)/shard_map/ppermute | solution.py:615
  283.4 27.9 %collective-permute-start.24 = (bf16[256,2048]{1,0:T(8,128)(2,1)S(1)}, bf16[256,2048]{1,0:T(8,128)(2,1)S(1)}, u32[]{:S(2)}, u32[]{:S(2)}) collective-permute-start(bf16[256,2048]{1,0:T(8,128)(2,1)S(1)} %convert_element_type.138), channel_id=1, source_target_pairs={{0,8},{4,12},{8,16},{12,20},{16,24},{20,28},{24,0},{28,4},{1,9},{5... | collective-permute-start | bytes 3145736 | tf_op jit(solution)/shard_map/ppermute | solution.py:615
  283.8 47.9 %collective-permute-start.23 = (bf16[256,2048]{1,0:T(8,128)(2,1)S(1)}, bf16[256,2048]{1,0:T(8,128)(2,1)S(1)}, u32[]{:S(2)}, u32[]{:S(2)}) collective-permute-start(bf16[256,2048]{1,0:T(8,128)(2,1)S(1)} %collective-permute-done.22.rows.refs_6_), channel_id=1, source_target_pairs={{0,8},{4,12},{8,16},{12,20},{16,24},{20,28},{24,0},{28,4},{1,9},{5... | collective-permute-start | bytes 3145736 | tf_op jit(solution)/shard_map/ppermute | solution.py:615
  333.6 24.8 %collective-permute-start.25 = (bf16[256,2048]{1,0:T(8,128)(2,1)S(1)}, bf16[256,2048]{1,0:T(8,128)(2,1)S(1)}, u32[]{:S(2)}, u32[]{:S(2)}) collective-permute-start(bf16[256,2048]{1,0:T(8,128)(2,1)S(1)} %add_convert_fusion.2), channel_id=1, source_target_pairs={{0,8},{4,12},{8,16},{12,20},{16,24},{20,28},{24,0},{28,4},{1,9},{5... | collective-permute-start | bytes 3145736 | tf_op jit(solution)/shard_map/ppermute | solution.py:615
  360.5 24.1 %collective-permute-start.26 = (bf16[256,2048]{1,0:T(8,128)(2,1)S(1)}, bf16[256,2048]{1,0:T(8,128)(2,1)S(1)}, u32[]{:S(2)}, u32[]{:S(2)}) collective-permute-start(bf16[256,2048]{1,0:T(8,128)(2,1)S(1)} %add_convert_fusion.1), channel_id=1, source_target_pairs={{0,8},{4,12},{8,16},{12,20},{16,24},{20,28},{24,0},{28,4},{1,9},{5... | collective-permute-start | bytes 3145736 | tf_op jit(solution)/shard_map/ppermute | solution.py:615
  384.6 28.7 %collective-permute-start.29 = (bf16[768,2048]{1,0:T(8,128)(2,1)S(1)}, bf16[768,2048]{1,0:T(8,128)(2,1)S(1)}, u32[]{:S(2)}, u32[]{:S(2)}) collective-permute-start(bf16[768,2048]{1,0:T(8,128)(2,1)S(1)} %copy-done.109), channel_id=1, source_target_pairs={{0,4},{4,0},{8,12},{12,8},{16,20},{20,16},{24,28},{28,24},{1,5},{5... | collective-permute-start | bytes 9437192 | tf_op jit(solution)/shard_map/ppermute | solution.py:601
  384.6 28.7 %collective-permute-start.30 = (bf16[768,2048]{1,0:T(8,128)(2,1)}, bf16[768,2048]{1,0:T(8,128)(2,1)S(1)}, u32[]{:S(2)}, u32[]{:S(2)}) collective-permute-start(bf16[768,2048]{1,0:T(8,128)(2,1)} %get-tuple-element.394), channel_id=1, source_target_pairs={{0,4},{4,0},{8,12},{12,8},{16,20},{20,16},{24,28},{28,24},{1,5},{5... | collective-permute-start | bytes 9437192 | tf_op jit(solution)/shard_map/ppermute | solution.py:601
  388.1 25.3 %collective-permute-start.27 = (bf16[256,2048]{1,0:T(8,128)(2,1)S(1)}, bf16[256,2048]{1,0:T(8,128)(2,1)}, u32[]{:S(2)}, u32[]{:S(2)}) collective-permute-start(bf16[256,2048]{1,0:T(8,128)(2,1)S(1)} %get-tuple-element.384.refs_4_), channel_id=1, source_target_pairs={{0,8},{4,12},{8,0},{12,4},{16,24},{20,28},{24,16},{28,20},{1,9},{5... | collective-permute-start | bytes 3145736 | tf_op jit(solution)/shard_map/ppermute | solution.py:615
  388.1 25.2 %collective-permute-start.28 = (bf16[256,2048]{1,0:T(8,128)(2,1)S(1)}, bf16[256,2048]{1,0:T(8,128)(2,1)S(1)}, u32[]{:S(2)}, u32[]{:S(2)}) collective-permute-start(bf16[256,2048]{1,0:T(8,128)(2,1)S(1)} %get-tuple-element.384.refs_4_), channel_id=1, source_target_pairs={{8,16},{12,20},{16,8},{20,12},{9,17},{13,21},{17,9},{21,13},{10,18... | collective-permute-start | bytes 3145736 | tf_op jit(solution)/shard_map/ppermute | solution.py:615
  413.4 28.7 %collective-permute-start.33 = (bf16[768,2048]{1,0:T(8,128)(2,1)}, bf16[768,2048]{1,0:T(8,128)(2,1)}, u32[]{:S(2)}, u32[]{:S(2)}) collective-permute-start(bf16[768,2048]{1,0:T(8,128)(2,1)} %get-tuple-element.407), channel_id=1, source_target_pairs={{0,4},{4,0},{8,12},{12,8},{16,20},{20,16},{24,28},{28,24},{1,5},{5... | collective-permute-start | bytes 9437192 | tf_op jit(solution)/shard_map/ppermute | solution.py:601
  414.6 27.5 %collective-permute-start.31 = (bf16[256,2048]{1,0:T(8,128)(2,1)}, bf16[256,2048]{1,0:T(8,128)(2,1)S(1)}, u32[]{:S(2)}, u32[]{:S(2)}) collective-permute-start(bf16[256,2048]{1,0:T(8,128)(2,1)} %broadcast_select_fusion.9), channel_id=1, source_target_pairs={{0,8},{4,12},{8,0},{12,4},{16,24},{20,28},{24,16},{28,20},{1,9},{5... | collective-permute-start | bytes 3145736 | tf_op jit(solution)/shard_map/ppermute | solution.py:615
  418.1 24.0 %collective-permute-start.32 = (bf16[256,2048]{1,0:T(8,128)(2,1)}, bf16[256,2048]{1,0:T(8,128)(2,1)S(1)}, u32[]{:S(2)}, u32[]{:S(2)}) collective-permute-start(bf16[256,2048]{1,0:T(8,128)(2,1)} %collective-permute-done.27), channel_id=1, source_target_pairs={{8,16},{12,20},{16,8},{20,12},{9,17},{13,21},{17,9},{21,13},{10,18... | collective-permute-start | bytes 3145736 | tf_op jit(solution)/shard_map/ppermute | solution.py:615
  442.2 163.4 %reduce-scatter.5.cloned.1.call-start = ((), (), s32[]{:S(2)}) async-start(), calls=%async_computation.7 | async-start | bytes 7864320 | tf_op jit(solution)/shard_map/reduce_scatter | solution.py:578
  446.6 26.9 %collective-permute-start.34 = (bf16[256,2048]{1,0:T(8,128)(2,1)}, bf16[256,2048]{1,0:T(8,128)(2,1)}, u32[]{:S(2)}, u32[]{:S(2)}) collective-permute-start(bf16[256,2048]{1,0:T(8,128)(2,1)} %get-tuple-element.413), channel_id=1, source_target_pairs={{0,8},{4,12},{8,0},{12,4},{16,24},{20,28},{24,16},{28,20},{1,9},{5... | collective-permute-start | bytes 3145736 | tf_op jit(solution)/shard_map/ppermute | solution.py:615
  450.1 23.3 %collective-permute-start.35 = (bf16[256,2048]{1,0:T(8,128)(2,1)}, bf16[256,2048]{1,0:T(8,128)(2,1)}, u32[]{:S(2)}, u32[]{:S(2)}) collective-permute-start(bf16[256,2048]{1,0:T(8,128)(2,1)} %get-tuple-element.415), channel_id=1, source_target_pairs={{8,16},{12,20},{16,8},{20,12},{9,17},{13,21},{17,9},{21,13},{10,18... | collective-permute-start | bytes 3145736 | tf_op jit(solution)/shard_map/ppermute | solution.py:615
  482.8 32.7 %collective-permute-start.36 = (bf16[256,2048]{1,0:T(8,128)(2,1)}, bf16[256,2048]{1,0:T(8,128)(2,1)S(1)}, u32[]{:S(2)}, u32[]{:S(2)}) collective-permute-start(bf16[256,2048]{1,0:T(8,128)(2,1)} %get-tuple-element.427), channel_id=1, source_target_pairs={{0,8},{4,12},{8,0},{12,4},{16,24},{20,28},{24,16},{28,20},{1,9},{5... | collective-permute-start | bytes 3145736 | tf_op jit(solution)/shard_map/ppermute | solution.py:615
  486.3 30.2 %collective-permute-start.37 = (bf16[256,2048]{1,0:T(8,128)(2,1)}, bf16[256,2048]{1,0:T(8,128)(2,1)}, u32[]{:S(2)}, u32[]{:S(2)}) collective-permute-start(bf16[256,2048]{1,0:T(8,128)(2,1)} %get-tuple-element.430), channel_id=1, source_target_pairs={{8,16},{12,20},{16,8},{20,12},{9,17},{13,21},{17,9},{21,13},{10,18... | collective-permute-start | bytes 3145736 | tf_op jit(solution)/shard_map/ppermute | solution.py:615
  517.8 2.1 collective-permute-start.39
  517.9 27.7 %collective-permute-start.38 = (bf16[256,2048]{1,0:T(8,128)(2,1)}, bf16[256,2048]{1,0:T(8,128)(2,1)}, u32[]{:S(2)}, u32[]{:S(2)}) collective-permute-start(bf16[256,2048]{1,0:T(8,128)(2,1)} %row_dot.4), channel_id=1, source_target_pairs={{0,8},{4,12},{8,16},{12,20},{16,24},{20,28},{24,0},{28,4},{1,9},{5... | collective-permute-start | bytes 3145736 | tf_op jit(solution)/shard_map/ppermute | solution.py:615
  520.0 20.1 %collective-permute-start.40 = (bf16[656,160]{1,0:T(8,128)(2,1)S(1)}, bf16[656,160]{1,0:T(8,128)(2,1)S(1)}, u32[]{:S(2)}, u32[]{:S(2)}) collective-permute-start(bf16[656,160]{1,0:T(8,128)(2,1)S(1)} %fusion.17), channel_id=1, source_target_pairs={{0,1},{1,0},{2,3},{3,2},{4,5},{5,4},{6,7},{7,6},{8,9},{9,8},{10,11... | collective-permute-start | bytes 629768 | tf_op jit(solution)/shard_map/ppermute | solution.py:754
  553.6 7.0 %collective-permute-start.43 = (bf16[320,2048]{1,0:T(8,128)(2,1)}, bf16[320,2048]{1,0:T(8,128)(2,1)}, u32[]{:S(2)}, u32[]{:S(2)}) collective-permute-start(bf16[320,2048]{1,0:T(8,128)(2,1)} %get-tuple-element.475), channel_id=1, source_target_pairs={{0,4},{4,0},{8,12},{12,8},{16,20},{20,16},{24,28},{28,24},{1,5},{5... | collective-permute-start | bytes 3932168 | tf_op jit(solution)/shard_map/ppermute | solution.py:601
  553.6 7.0 %collective-permute-start.44 = (bf16[320,2048]{1,0:T(8,128)(2,1)}, bf16[320,2048]{1,0:T(8,128)(2,1)}, u32[]{:S(2)}, u32[]{:S(2)}) collective-permute-start(bf16[320,2048]{1,0:T(8,128)(2,1)} %get-tuple-element.477), channel_id=1, source_target_pairs={{0,4},{4,0},{8,12},{12,8},{16,20},{20,16},{24,28},{28,24},{1,5},{5... | collective-permute-start | bytes 3932168 | tf_op jit(solution)/shard_map/ppermute | solution.py:601
  554.1 6.6 collective-permute-start.45
  554.1 28.0 %collective-permute-start.41 = (bf16[256,2048]{1,0:T(8,128)(2,1)}, bf16[256,2048]{1,0:T(8,128)(2,1)}, u32[]{:S(2)}, u32[]{:S(2)}) collective-permute-start(bf16[256,2048]{1,0:T(8,128)(2,1)} %row_dot.5), channel_id=1, source_target_pairs={{0,8},{4,12},{8,16},{12,20},{16,24},{20,28},{24,0},{28,4},{1,9},{5... | collective-permute-start | bytes 3145736 | tf_op jit(solution)/shard_map/ppermute | solution.py:615
  569.1 18.6 %collective-permute-start.46 = (f32[2,2048]{1,0:T(2,128)S(1)}, f32[2,2048]{1,0:T(2,128)S(1)}, u32[]{:S(2)}, u32[]{:S(2)}) collective-permute-start(f32[2,2048]{1,0:T(2,128)S(1)} %pad_maximum_fusion.8), channel_id=1, source_target_pairs={{0,1},{1,0},{2,3},{3,2},{4,5},{5,4},{6,7},{7,6},{8,9},{9,8},{10,11... | collective-permute-start | bytes 49160 | tf_op jit(solution)/shard_map/ppermute | solution.py:760
  570.1 17.6 %collective-permute-start.47 = (f32[2,2048]{1,0:T(2,128)S(1)}, f32[2,2048]{1,0:T(2,128)S(1)}, u32[]{:S(2)}, u32[]{:S(2)}) collective-permute-start(f32[2,2048]{1,0:T(2,128)S(1)} %pad_maximum_fusion.8), channel_id=1, source_target_pairs={{0,2},{1,3},{2,0},{3,1},{4,6},{5,7},{6,4},{7,5},{8,10},{9,11},{10,... | collective-permute-start | bytes 49160 | tf_op jit(solution)/shard_map/ppermute | solution.py:760
  571.8 15.9 %collective-permute-start.48 = (f32[2,2048]{1,0:T(2,128)S(1)}, f32[2,2048]{1,0:T(2,128)S(1)}, u32[]{:S(2)}, u32[]{:S(2)}) collective-permute-start(f32[2,2048]{1,0:T(2,128)S(1)} %pad_maximum_fusion.8), channel_id=1, source_target_pairs={{0,3},{1,2},{2,1},{3,0},{4,7},{5,6},{6,5},{7,4},{8,11},{9,10},{10,... | collective-permute-start | bytes 49160 | tf_op jit(solution)/shard_map/ppermute | solution.py:760
  574.2 23.2 %collective-permute-start.49 = (bf16[960,512]{1,0:T(8,128)(2,1)S(1)}, bf16[960,512]{1,0:T(8,128)(2,1)}, u32[]{:S(2)}, u32[]{:S(2)}) collective-permute-start(bf16[960,512]{1,0:T(8,128)(2,1)S(1)} %get-tuple-element.571), channel_id=1, source_target_pairs={{0,1},{1,0},{2,3},{3,2},{4,5},{5,4},{6,7},{7,6},{8,9},{9,8},{10,11... | collective-permute-start | bytes 2949128 | tf_op jit(solution)/shard_map/ppermute | solution.py:594
  582.1 23.5 %collective-permute-start.50 = (bf16[960,512]{1,0:T(8,128)(2,1)S(1)}, bf16[960,512]{1,0:T(8,128)(2,1)}, u32[]{:S(2)}, u32[]{:S(2)}) collective-permute-start(bf16[960,512]{1,0:T(8,128)(2,1)S(1)} %get-tuple-element.570), channel_id=1, source_target_pairs={{0,2},{1,3},{2,0},{3,1},{4,6},{5,7},{6,4},{7,5},{8,10},{9,11},{10,... | collective-permute-start | bytes 2949128 | tf_op jit(solution)/shard_map/ppermute | solution.py:594
  587.7 32.8 %collective-permute-start.42 = (bf16[256,2048]{1,0:T(8,128)(2,1)}, bf16[256,2048]{1,0:T(8,128)(2,1)S(1)}, u32[]{:S(2)}, u32[]{:S(2)}) collective-permute-start(bf16[256,2048]{1,0:T(8,128)(2,1)} %row_dot.6), channel_id=1, source_target_pairs={{0,8},{4,12},{8,16},{12,20},{16,24},{20,28},{24,0},{28,4},{1,9},{5... | collective-permute-start | bytes 3145736 | tf_op jit(solution)/shard_map/ppermute | solution.py:615
  607.8 23.7 %collective-permute-start.53 = (bf16[960,512]{1,0:T(8,128)(2,1)}, bf16[960,512]{1,0:T(8,128)(2,1)}, u32[]{:S(2)}, u32[]{:S(2)}) collective-permute-start(bf16[960,512]{1,0:T(8,128)(2,1)} %constant_dynamic-slice_fusion), channel_id=1, source_target_pairs={{0,3},{1,2},{2,1},{3,0},{4,7},{5,6},{6,5},{7,4},{8,11},{9,10},{10,... | collective-permute-start | bytes 2949128 | tf_op jit(solution)/shard_map/ppermute | solution.py:594
  613.7 5.7 collective-permute-start.51
  613.7 5.6 collective-permute-start.52
  637.5 5.6 collective-permute-start.55
  637.5 5.6 collective-permute-start.56
  637.6 6.2 collective-permute-start.57
  641.9 7.2 %collective-permute-start.58 = (bf16[656,160]{1,0:T(8,128)(2,1)S(1)}, bf16[656,160]{1,0:T(8,128)(2,1)S(1)}, u32[]{:S(2)}, u32[]{:S(2)}) collective-permute-start(bf16[656,160]{1,0:T(8,128)(2,1)S(1)} %add.194), channel_id=1, source_target_pairs={{0,2},{1,3},{2,0},{3,1},{4,6},{5,7},{6,4},{7,5},{8,10},{9,11},{10,... | collective-permute-start | bytes 629768 | tf_op jit(solution)/shard_map/ppermute | solution.py:754
  643.0 10.4 %collective-permute-start.54 = (bf16[128,2048]{1,0:T(8,128)(2,1)S(1)}, bf16[128,2048]{1,0:T(8,128)(2,1)S(1)}, u32[]{:S(2)}, u32[]{:S(2)}) collective-permute-start(bf16[128,2048]{1,0:T(8,128)(2,1)S(1)} %get-tuple-element.579), channel_id=1, source_target_pairs={{0,4},{4,0},{8,12},{12,8},{16,20},{20,16},{24,28},{28,24},{1,5},{5... | collective-permute-start | bytes 1572872 | tf_op jit(solution)/shard_map/ppermute | solution.py:601
  (122 other events, 1334.4 us)
Sparse Core Ops, SparseCore 0:
  9.9 42.1 all-gather.4
  53.9 28.6 all-gather.6
  84.5 70.1 all-gather.8
  156.3 43.8 all-gather.10
  442.3 45.3 reduce-scatter.2
  490.5 77.2 reduce-scatter.4

commit v6 on v5

--- a/solution.py
+++ b/solution.py
@@ -14,7 +14,7 @@
 f32 = jnp.float32
 bf16 = jnp.bfloat16
 kernel_cost = pl.CostEstimate(flops=1, bytes_accessed=1, transcendentals=0)
-chain_cost = pl.CostEstimate(flops=1 << 35, bytes_accessed=1 << 27, transcendentals=0)
+chain_cost = pl.CostEstimate(flops=1, bytes_accessed=1 << 26, transcendentals=0)
 
 
 def gelu_tanh(v):

time: 671 us -> 662 us (0.987)
  waiting for transfers between devices: 264 us -> 254 us
    ppermute x3, waiting for transfers between devices: 28.7 us -> 0.87 us  [send(): self.got.append(lax.ppermute(self.piece(flip), 'narrow', pairs))]
    ppermute x6, waiting for transfers between devices: 0.65 us -> 8.87 us  [direct_sum(): lax.ppermute(values, axis, [(at, at ^ flip) for at in range(size)])]
    unnamed x253 -> x243, local copies, waits for them, and re-layouts: 32.7 us -> 33.7 us
  transfers between devices with their start and end apart: 65 -> 65, of which waited for: 26 -> 29; matrix products, arithmetic and copies ran while one was open for 14% -> 14% of each run, Pallas kernels for 28% -> 29%
where the time goes in v6:
time: 662 us; the launch traced here: 653 us
  waiting for transfers between devices  254 us (38%)
  Pallas kernels  187 us (28%)
  starting transfers between devices  63.3 us (10%)
  local copies, waits for them, and re-layouts  58 us (9%)
  other arithmetic  41.8 us (6%)
  matrix products  32.7 us (5%)
  between operations  16.6 us (3%)
    ppermute x28, waiting for transfers between devices, move(): return lax.ppermute(values, 'wide', devices)  229 us
    pallas_call x4, Pallas kernels, mlp_block(): pl.pallas_call(partial(mlp_kernel, tiles), grid=(2 * tiles,), in_specs=[w...  65.7 us
    ppermute x28, starting transfers between devices, move(): return lax.ppermute(values, 'wide', devices)  43.9 us
    pallas_call x5, Pallas kernels, weight_grad(): pl.pallas_call(partial(weight_grad_kernel, count, kinds, len(weights)), g...  40.7 us
    unnamed x243, local copies, waits for them, and re-layouts  33.7 us
    dot_general x8, matrix products, dot_nt(): lax.dot_general(left, right, (((1,), (1,)), ((), ())), preferred_element_...  24.5 us
    pallas_call x4, Pallas kernels, join(): pl.pallas_call(partial(join_kernel, count, tiles), grid=(count * tiles,),...  17.5 us
    pallas_call x1, Pallas kernels, mixer_forward(): pl.pallas_call(partial(mixer_forward_kernel, chips, block_width), grid_sp...  17.5 us
  transfers between devices with their start and end apart: 65, of which 29 were waited for; matrix products, arithmetic and copies ran while one was open for 14% of the time, Pallas kernels for 29%

profile of v6, /device:TPU:0, one launch (start us, length us, event | category | flops | bytes accessed | tf_op | source)
XLA Modules:
  0.0 653.2 jit_solution(14192309476424047500)
XLA Ops:
  17.0 2.6 collective-permute-start.2
  21.2 24.3 %collective-permute-done.2.refs_5_ = bf16[256,2048]{1,0:T(8,128)(2,1)S(1)} collective-permute-done((bf16[256,2048]{1,0:T(8,128)(2,1)S(1)}, bf16[256,2048]{1,0:T(8,128)(2,1)S(1)}, u32[]{:S(2)}, u32[]{:S(2)}) %collective-permute-start.2) | collective-permute-done | bytes 1048608 | tf_op jit(solution)/shard_map/ppermute | solution.py:615
  46.4 26.8 %collective-permute-done.4.refs_6_ = bf16[256,2048]{1,0:T(8,128)(2,1)} collective-permute-done((bf16[256,2048]{1,0:T(8,128)(2,1)S(1)}, bf16[256,2048]{1,0:T(8,128)(2,1)}, u32[]{:S(2)}, u32[]{:S(2)}) %collective-permute-start.4) | collective-permute-done | bytes 1048608 | tf_op jit(solution)/shard_map/ppermute | solution.py:615
  80.6 3.7 convolution_bitcast_fusion.1.refs_2_
  84.3 2.6 convolution_bitcast_fusion.2.refs_1_
  86.9 2.6 convolution_bitcast_fusion.3.refs_0_
  89.5 11.7 %collective-permute-done.5.refs_7_ = bf16[256,2048]{1,0:T(8,128)(2,1)} collective-permute-done((bf16[256,2048]{1,0:T(8,128)(2,1)}, bf16[256,2048]{1,0:T(8,128)(2,1)}, u32[]{:S(2)}, u32[]{:S(2)}) %collective-permute-start.5) | collective-permute-done | bytes 1048608 | tf_op jit(solution)/shard_map/ppermute | solution.py:615
  104.1 4.5 convolution_bitcast_fusion.refs_3_
  108.6 17.5 %mixer_forward.1 = (bf16[4,2,1,128,640]{4,3,2,1,0:T(8,128)(2,1)}, f32[4,2,1,128,640]{4,3,2,1,0:T(8,128)}, f32[4,2,1,128,640]{4,3,2,1,0:T(8,128)}, f32[4,2,1,128,...) custom-call(s32[2]{0:T(128)S(1)} %pad_add_fusion.place, ...), custom_call_target="tpu_custom_call" | custom-call | flops 1 | bytes 1 | tf_op jit(solution)/shard_map/mixer_forward/pallas_call | solution.py:306
  130.6 3.2 collective-permute-start.11
  142.5 15.0 %collective-permute-done.11.mid_moved = bf16[256,2048]{1,0:T(8,128)(2,1)S(1)} collective-permute-done((bf16[256,2048]{1,0:T(8,128)(2,1)S(1)}, bf16[256,2048]{1,0:T(8,128)(2,1)S(1)}, u32[]{:S(2)}, u32[]{:S(2)}) %collective-permute-start.11) | collective-permute-done | bytes 1048608 | tf_op jit(solution)/shard_map/ppermute | solution.py:615
  157.4 2.5 advance.4
  160.0 3.8 collective-permute-start.15
  165.4 21.4 %collective-permute-done.15.mid_moved = bf16[256,2048]{1,0:T(8,128)(2,1)S(1)} collective-permute-done((bf16[256,2048]{1,0:T(8,128)(2,1)}, bf16[256,2048]{1,0:T(8,128)(2,1)S(1)}, u32[]{:S(2)}, u32[]{:S(2)}) %collective-permute-start.15) | collective-permute-done | bytes 1048608 | tf_op jit(solution)/shard_map/ppermute | solution.py:615
  189.7 4.2 advance.5
  193.9 3.4 collective-permute-start.17
  200.6 20.9 %collective-permute-done.17 = bf16[256,2048]{1,0:T(8,128)(2,1)} collective-permute-done((bf16[256,2048]{1,0:T(8,128)(2,1)}, bf16[256,2048]{1,0:T(8,128)(2,1)}, u32[]{:S(2)}, u32[]{:S(2)}) %collective-permute-start.17) | collective-permute-done | bytes 1048608 | tf_op jit(solution)/shard_map/ppermute | solution.py:615
  221.4 3.2 multiply_reduce_fusion.2
  227.3 4.3 collective-permute-start.19
  233.0 16.5 %mlp_block.4 = (bf16[256,1536]{1,0:T(8,128)(2,1)}, bf16[256,1536]{1,0:T(8,128)(2,1)}, bf16[256,1536]{1,0:T(8,128)(2,1)}, f32[256,2048]{1,0:T(8,128)}, bf16[256,2048]{1,0:T(8,128)(2,1)}) custom-call(bf16[256,2048]{1,0:T(8,128)(2,1)S(1)} %multiply_convert_fusion.rows.refs_4_, bf16[256,2048]{1,0:T(8,128)(2,1)S(1)} %copy-done.9, ...), custom_call_target="tpu_custom_call" | custom-call | flops 1 | bytes 1 | tf_op jit(solution)/shard_map/mlp_block/pallas_call | solution.py:421
  249.5 5.6 collective-permute-done.19.rows.refs_5_
  257.2 16.4 %mlp_block.5 = (bf16[256,1536]{1,0:T(8,128)(2,1)}, bf16[256,1536]{1,0:T(8,128)(2,1)}, bf16[256,1536]{1,0:T(8,128)(2,1)}, f32[256,2048]{1,0:T(8,128)}, bf16[256,2048]{1,0:T(8,128)(2,1)}) custom-call(bf16[256,2048]{1,0:T(8,128)(2,1)S(1)} %collective-permute-done.19.rows.refs_5_, bf16[256,2048]{1,0:T(8,128)(2,1)S(1)} %copy-done.11, ...), custom_call_target="tpu_custom_call" | custom-call | flops 1 | bytes 1 | tf_op jit(solution)/shard_map/mlp_block/pallas_call | solution.py:421
  273.6 8.1 %collective-permute-done.22.rows.refs_6_ = bf16[256,2048]{1,0:T(8,128)(2,1)S(1)} collective-permute-done((bf16[256,2048]{1,0:T(8,128)(2,1)S(1)}, bf16[256,2048]{1,0:T(8,128)(2,1)S(1)}, u32[]{:S(2)}, u32[]{:S(2)}) %collective-permute-start.22) | collective-permute-done | bytes 1048608 | tf_op jit(solution)/shard_map/ppermute | solution.py:615
  285.4 16.4 %mlp_block.6 = (bf16[256,1536]{1,0:T(8,128)(2,1)}, bf16[256,1536]{1,0:T(8,128)(2,1)}, bf16[256,1536]{1,0:T(8,128)(2,1)}, f32[256,2048]{1,0:T(8,128)}, bf16[256,2048]{1,0:T(8,128)(2,1)}) custom-call(bf16[256,2048]{1,0:T(8,128)(2,1)S(1)} %collective-permute-done.22.rows.refs_6_, bf16[256,2048]{1,0:T(8,128)(2,1)S(1)} %broadcast_select_fusion.10.back.refs_6_, ...), custom_call_target="tpu_custom_call" | custom-call | flops 1 | bytes 1 | tf_op jit(solution)/shard_map/mlp_block/pallas_call | solution.py:421
  301.8 9.6 %collective-permute-done.24 = bf16[256,2048]{1,0:T(8,128)(2,1)S(1)} collective-permute-done((bf16[256,2048]{1,0:T(8,128)(2,1)S(1)}, bf16[256,2048]{1,0:T(8,128)(2,1)S(1)}, u32[]{:S(2)}, u32[]{:S(2)}) %collective-permute-start.24) | collective-permute-done | bytes 1048608 | tf_op jit(solution)/shard_map/ppermute | solution.py:615
  311.4 20.3 %collective-permute-done.23.rows.refs_7_ = bf16[256,2048]{1,0:T(8,128)(2,1)S(1)} collective-permute-done((bf16[256,2048]{1,0:T(8,128)(2,1)S(1)}, bf16[256,2048]{1,0:T(8,128)(2,1)S(1)}, u32[]{:S(2)}, u32[]{:S(2)}) %collective-permute-start.23) | collective-permute-done | bytes 1048608 | tf_op jit(solution)/shard_map/ppermute | solution.py:615
  333.7 16.5 %mlp_block.7 = (bf16[256,1536]{1,0:T(8,128)(2,1)}, bf16[256,1536]{1,0:T(8,128)(2,1)}, bf16[256,1536]{1,0:T(8,128)(2,1)}, f32[256,2048]{1,0:T(8,128)}, bf16[256,2048]{1,0:T(8,128)(2,1)}) custom-call(bf16[256,2048]{1,0:T(8,128)(2,1)S(1)} %collective-permute-done.23.rows.refs_7_, bf16[256,2048]{1,0:T(8,128)(2,1)S(1)} %copy-done.10, ...), custom_call_target="tpu_custom_call" | custom-call | flops 1 | bytes 1 | tf_op jit(solution)/shard_map/mlp_block/pallas_call | solution.py:421
  350.1 8.3 %collective-permute-done.25 = bf16[256,2048]{1,0:T(8,128)(2,1)S(1)} collective-permute-done((bf16[256,2048]{1,0:T(8,128)(2,1)S(1)}, bf16[256,2048]{1,0:T(8,128)(2,1)S(1)}, u32[]{:S(2)}, u32[]{:S(2)}) %collective-permute-start.25) | collective-permute-done | bytes 1048608 | tf_op jit(solution)/shard_map/ppermute | solution.py:615
  360.9 8.9 %weight_grad.6 = (f32[768,2048]{1,0:T(8,128)}, bf16[768,2048]{1,0:T(8,128)(2,1)}) custom-call(bf16[256,1536]{1,0:T(8,128)(2,1)S(1)} %copy-done.45, bf16[256,1536]{1,0:T(8,128)(2,1)S(1)} %copy-done.48, bf16[256,1536]{1,0:T(8,128)(2,1)S(1)} %copy-done.50, bf16[256,1536]{1,0:T(8,128)(2,1)S(1)} %copy-done.52, bf16[256,2048]{1,0:T(8,128)(2,1)S(1)} %copy-done.9, ...), custom_call_target="tpu_custom_call" | custom-call | flops 1 | bytes 1 | tf_op jit(solution)/shard_map/weight_grad/pallas_call | solution.py:471
  369.9 9.0 %weight_grad.5 = (f32[768,2048]{1,0:T(8,128)}, bf16[768,2048]{1,0:T(8,128)(2,1)}) custom-call(bf16[256,1536]{1,0:T(8,128)(2,1)S(1)} %copy-done.44, bf16[256,1536]{1,0:T(8,128)(2,1)S(1)} %copy-done.47, bf16[256,1536]{1,0:T(8,128)(2,1)S(1)} %copy-done.49, bf16[256,1536]{1,0:T(8,128)(2,1)S(1)} %copy-done.51, ...), custom_call_target="tpu_custom_call" | custom-call | flops 1 | bytes 1 | tf_op jit(solution)/shard_map/weight_grad/pallas_call | solution.py:471
  378.8 5.8 collective-permute-done.26
  389.1 8.9 %weight_grad.7 = (f32[768,2048]{1,0:T(8,128)}, bf16[768,2048]{1,0:T(8,128)(2,1)}) custom-call(bf16[256,1536]{1,0:T(8,128)(2,1)S(1)} %copy-done.41, bf16[256,1536]{1,0:T(8,128)(2,1)S(1)} %copy-done.42, bf16[256,1536]{1,0:T(8,128)(2,1)S(1)} %copy-done.43, bf16[256,1536]{1,0:T(8,128)(2,1)S(1)} %copy-done.46, ...), custom_call_target="tpu_custom_call" | custom-call | flops 1 | bytes 1 | tf_op jit(solution)/shard_map/weight_grad/pallas_call | solution.py:471
  398.1 15.3 %collective-permute-done.27 = bf16[256,2048]{1,0:T(8,128)(2,1)} collective-permute-done((bf16[256,2048]{1,0:T(8,128)(2,1)S(1)}, bf16[256,2048]{1,0:T(8,128)(2,1)}, u32[]{:S(2)}, u32[]{:S(2)}) %collective-permute-start.27) | collective-permute-done | bytes 1048608 | tf_op jit(solution)/shard_map/ppermute | solution.py:615
  415.5 3.5 collective-permute-start.31
  419.8 2.9 join.5.refs_2_
  422.7 2.9 join.4
  425.5 3.0 broadcast_select_fusion
  428.6 13.6 %collective-permute-done.31.mid_moved = bf16[256,2048]{1,0:T(8,128)(2,1)S(1)} collective-permute-done((bf16[256,2048]{1,0:T(8,128)(2,1)}, bf16[256,2048]{1,0:T(8,128)(2,1)S(1)}, u32[]{:S(2)}, u32[]{:S(2)}) %collective-permute-start.31) | collective-permute-done | bytes 1048608 | tf_op jit(solution)/shard_map/ppermute | solution.py:615
  446.6 3.5 collective-permute-start.34
  453.9 3.0 copy-done.12
  456.9 5.4 join.6
  462.3 4.1 fusion.77
  468.3 4.2 collective-permute-done.34.mid_moved
  477.1 4.6 advance.7
  481.7 3.7 collective-permute-start.36
  487.2 3.3 fusion.11
  493.2 15.9 %mixer_backward.1 = (bf16[4,2,1,128,1280]{4,3,2,1,0:T(8,128)(2,1)}, f32[8,640]{1,0:T(8,128)S(1)}, f32[4,2,160,160]{3,2,1,0:T(8,128)S(1)}) custom-call(s32[2]{0:T(128)S(1)} %pad_add_fusion.place, s32[1]{0:T(128)} %dynamic_slice.15.lengths, f32[2,1,128,640]{3,2,1,0:T(8,128)S(1)} %bitcast.154, f32[2,1,128,640]{3,2,1,0:T(8,128)S(1)} %bitcast.155, ...), custom_call_target="tpu_custom_call" | custom-call | flops 1 | bytes 1 | tf_op jit(solution)/shard_map/mixer_backward/pallas_call | solution.py:344
  511.4 3.3 row_dot.4
  525.6 9.1 %weight_grad.8 = (f32[320,2048]{1,0:T(8,128)}, f32[320,2048]{1,0:T(8,128)}, bf16[320,2048]{1,0:T(8,128)(2,1)}, bf16[320,2048]{1,0:T(8,128)(2,1)}, f32[1,2048]{1,0:T(1,128)S(1)}) custom-call(bf16[1024,1280]{1,0:T(8,128)(2,1)S(1)} %bitcast.118, bf16[1024,1280]{1,0:T(8,128)(2,1)S(1)} %bitcast.119, bf16[1024,1280]{1,0:T(8,128)(2,1)S(1)} %bitcast.120, ...), custom_call_target="tpu_custom_call" | custom-call | flops 1 | bytes 1 | tf_op jit(solution)/shard_map/weight_grad/pallas_call | solution.py:471
  534.7 4.7 weight_grad.9
  539.6 5.2 collective-permute-done.38.refs_0_
  544.8 4.6 row_dot.5
  561.9 6.3 join.7
  568.2 2.9 constant_dynamic-slice_fusion.1
  575.2 2.7 collective-permute-done.41.refs_0_
  582.7 3.5 row_dot.7
  586.2 4.5 row_dot.6
  590.8 4.9 collective-permute-done.46
  600.7 2.8 add_convert_fusion
  606.9 3.2 copy.55
  611.2 10.8 %collective-permute-done.42 = bf16[256,2048]{1,0:T(8,128)(2,1)S(1)} collective-permute-done((bf16[256,2048]{1,0:T(8,128)(2,1)}, bf16[256,2048]{1,0:T(8,128)(2,1)S(1)}, u32[]{:S(2)}, u32[]{:S(2)}) %collective-permute-start.42) | collective-permute-done | bytes 1048608 | tf_op jit(solution)/shard_map/ppermute | solution.py:615
  624.2 2.6 convert_add_fusion.2
  628.9 3.3 collective-permute-start.56
  635.0 2.7 collective-permute-done.57
  (464 shorter events, 142.1 us)
Async XLA Ops:
  7.2 66.1 %all-gather.5.cloned.1.call-start = ((), (), s32[]{:S(2)}) async-start(), calls=%async_computation.2 | async-start | bytes 3276800 | tf_op jit(solution)/shard_map/all_gather | solution.py:574
  7.9 81.6 %all-gather.7.cloned.1.call-start = ((), (), s32[]{:S(2)}) async-start(), calls=%async_computation.3 | async-start | bytes 1638400 | tf_op jit(solution)/shard_map/all_gather | solution.py:574
  8.7 156.7 %all-gather.9.cloned.1.call-start = ((), (), s32[]{:S(2)}) async-start(), calls=%async_computation.4 | async-start | bytes 7864320 | tf_op jit(solution)/shard_map/all_gather | solution.py:574
  9.5 191.1 %all-gather.11.cloned.1.call-start = ((), (), s32[]{:S(2)}) async-start(), calls=%async_computation.5 | async-start | bytes 3932160 | tf_op jit(solution)/shard_map/all_gather | solution.py:574
  9.7 5.3 collective-permute-start
  16.5 4.4 collective-permute-start.1
  17.0 28.4 %collective-permute-start.2 = (bf16[256,2048]{1,0:T(8,128)(2,1)S(1)}, bf16[256,2048]{1,0:T(8,128)(2,1)S(1)}, u32[]{:S(2)}, u32[]{:S(2)}) collective-permute-start(bf16[256,2048]{1,0:T(8,128)(2,1)S(1)} %fusion.3.refs_4_), channel_id=1, source_target_pairs={{0,8},{4,12},{8,16},{12,20},{16,24},{20,28},{24,0},{28,4},{1,9},{5... | collective-permute-start | bytes 3145736 | tf_op jit(solution)/shard_map/ppermute | solution.py:615
  46.4 26.8 %collective-permute-start.4 = (bf16[256,2048]{1,0:T(8,128)(2,1)S(1)}, bf16[256,2048]{1,0:T(8,128)(2,1)}, u32[]{:S(2)}, u32[]{:S(2)}) collective-permute-start(bf16[256,2048]{1,0:T(8,128)(2,1)S(1)} %collective-permute-done.2.refs_5_), channel_id=1, source_target_pairs={{0,8},{4,12},{8,16},{12,20},{16,24},{20,28},{24,0},{28,4},{1,9},{5... | collective-permute-start | bytes 3145736 | tf_op jit(solution)/shard_map/ppermute | solution.py:615
  73.3 5.3 collective-permute-start.6
  73.3 442.4 %reduce-scatter.3.cloned.1.call-start = ((), (), s32[]{:S(2)}) async-start(), calls=%async_computation.6 | async-start | bytes 3932160 | tf_op jit(solution)/shard_map/reduce_scatter | solution.py:578
  73.4 27.8 %collective-permute-start.9 = (f32[8,320]{1,0:T(8,128)S(1)}, f32[8,320]{1,0:T(8,128)S(1)}, u32[]{:S(2)}, u32[]{:S(2)}) collective-permute-start(f32[8,320]{1,0:T(8,128)S(1)} %concatenate.93), channel_id=1, source_target_pairs={{0,4},{4,0},{8,12},{12,8},{16,20},{20,16},{24,28},{28,24},{1,5},{5... | collective-permute-start | bytes 30728 | tf_op jit(solution)/shard_map/ppermute | solution.py:601
  74.0 27.2 %collective-permute-start.5 = (bf16[256,2048]{1,0:T(8,128)(2,1)}, bf16[256,2048]{1,0:T(8,128)(2,1)}, u32[]{:S(2)}, u32[]{:S(2)}) collective-permute-start(bf16[256,2048]{1,0:T(8,128)(2,1)} %collective-permute-done.4.refs_6_), channel_id=1, source_target_pairs={{0,8},{4,12},{8,16},{12,20},{16,24},{20,28},{24,0},{28,4},{1,9},{5... | collective-permute-start | bytes 3145736 | tf_op jit(solution)/shard_map/ppermute | solution.py:615
  101.2 26.1 %collective-permute-start.10 = (bf16[320,2048]{1,0:T(8,128)(2,1)}, bf16[320,2048]{1,0:T(8,128)(2,1)}, u32[]{:S(2)}, u32[]{:S(2)}) collective-permute-start(bf16[320,2048]{1,0:T(8,128)(2,1)} %all-gather.7.cloned.1.call-done), channel_id=1, source_target_pairs={{0,4},{4,0},{8,12},{12,8},{16,20},{20,16},{24,28},{28,24},{1,5},{5... | collective-permute-start | bytes 3932168 | tf_op jit(solution)/shard_map/ppermute | solution.py:601
  103.0 26.8 %collective-permute-start.7 = (bf16[256,2048]{1,0:T(8,128)(2,1)S(1)}, bf16[256,2048]{1,0:T(8,128)(2,1)S(1)}, u32[]{:S(2)}, u32[]{:S(2)}) collective-permute-start(bf16[256,2048]{1,0:T(8,128)(2,1)S(1)} %fusion.10.back.refs_4_), channel_id=1, source_target_pairs={{0,8},{4,12},{8,0},{12,4},{16,24},{20,28},{24,16},{28,20},{1,9},{5... | collective-permute-start | bytes 3145736 | tf_op jit(solution)/shard_map/ppermute | solution.py:615
  103.1 26.7 %collective-permute-start.8 = (bf16[256,2048]{1,0:T(8,128)(2,1)S(1)}, bf16[256,2048]{1,0:T(8,128)(2,1)S(1)}, u32[]{:S(2)}, u32[]{:S(2)}) collective-permute-start(bf16[256,2048]{1,0:T(8,128)(2,1)S(1)} %fusion.10.back.refs_4_), channel_id=1, source_target_pairs={{8,16},{12,20},{16,8},{20,12},{9,17},{13,21},{17,9},{21,13},{10,18... | collective-permute-start | bytes 3145736 | tf_op jit(solution)/shard_map/ppermute | solution.py:615
  129.9 12.6 %collective-permute-start.14 = (f32[1,3,320]{2,1,0:T(4,128)S(1)}, f32[1,3,320]{2,1,0:T(4,128)S(1)}, u32[]{:S(2)}, u32[]{:S(2)}) collective-permute-start(f32[1,3,320]{2,1,0:T(4,128)S(1)} %get-tuple-element.605), channel_id=1, source_target_pairs={{0,4},{4,0},{8,12},{12,8},{16,20},{20,16},{24,28},{28,24},{1,5},{5... | collective-permute-start | bytes 11528 | tf_op jit(solution)/shard_map/ppermute | solution.py:601
  130.5 11.4 %collective-permute-start.13 = (f32[1,320]{1,0:T(1,128)S(1)}, f32[1,320]{1,0:T(1,128)S(1)}, u32[]{:S(2)}, u32[]{:S(2)}) collective-permute-start(f32[1,320]{1,0:T(1,128)S(1)} %get-tuple-element.607), channel_id=1, source_target_pairs={{0,4},{4,0},{8,12},{12,8},{16,20},{20,16},{24,28},{28,24},{1,5},{5... | collective-permute-start | bytes 3848 | tf_op jit(solution)/shard_map/ppermute | solution.py:601
  130.6 26.8 %collective-permute-start.11 = (bf16[256,2048]{1,0:T(8,128)(2,1)S(1)}, bf16[256,2048]{1,0:T(8,128)(2,1)S(1)}, u32[]{:S(2)}, u32[]{:S(2)}) collective-permute-start(bf16[256,2048]{1,0:T(8,128)(2,1)S(1)} %broadcast_select_fusion.12), channel_id=1, source_target_pairs={{0,8},{4,12},{8,0},{12,4},{16,24},{20,28},{24,16},{28,20},{1,9},{5... | collective-permute-start | bytes 3145736 | tf_op jit(solution)/shard_map/ppermute | solution.py:615
  133.9 23.6 %collective-permute-start.12 = (bf16[256,2048]{1,0:T(8,128)(2,1)S(1)}, bf16[256,2048]{1,0:T(8,128)(2,1)S(1)}, u32[]{:S(2)}, u32[]{:S(2)}) collective-permute-start(bf16[256,2048]{1,0:T(8,128)(2,1)S(1)} %collective-permute-done.7), channel_id=1, source_target_pairs={{8,16},{12,20},{16,8},{20,12},{9,17},{13,21},{17,9},{21,13},{10,18... | collective-permute-start | bytes 3145736 | tf_op jit(solution)/shard_map/ppermute | solution.py:615
  160.0 26.8 %collective-permute-start.15 = (bf16[256,2048]{1,0:T(8,128)(2,1)}, bf16[256,2048]{1,0:T(8,128)(2,1)S(1)}, u32[]{:S(2)}, u32[]{:S(2)}) collective-permute-start(bf16[256,2048]{1,0:T(8,128)(2,1)} %get-tuple-element.292), channel_id=1, source_target_pairs={{0,8},{4,12},{8,0},{12,4},{16,24},{20,28},{24,16},{28,20},{1,9},{5... | collective-permute-start | bytes 3145736 | tf_op jit(solution)/shard_map/ppermute | solution.py:615
  163.8 23.0 %collective-permute-start.16 = (bf16[256,2048]{1,0:T(8,128)(2,1)}, bf16[256,2048]{1,0:T(8,128)(2,1)}, u32[]{:S(2)}, u32[]{:S(2)}) collective-permute-start(bf16[256,2048]{1,0:T(8,128)(2,1)} %get-tuple-element.294), channel_id=1, source_target_pairs={{8,16},{12,20},{16,8},{20,12},{9,17},{13,21},{17,9},{21,13},{10,18... | collective-permute-start | bytes 3145736 | tf_op jit(solution)/shard_map/ppermute | solution.py:615
  186.8 46.2 %collective-permute-start.20 = (bf16[2,2048,768]{2,1,0:T(8,128)(2,1)}, bf16[2,2048,768]{2,1,0:T(8,128)(2,1)}, u32[]{:S(2)}, u32[]{:S(2)}) collective-permute-start(bf16[2,2048,768]{2,1,0:T(8,128)(2,1)} %all-gather.9.cloned.1.call-done.own_in), channel_id=1, source_target_pairs={{0,4},{4,0},{8,12},{12,8},{16,20},{20,16},{24,28},{28,24},{1,5},{5... | collective-permute-start | bytes 18874376 | tf_op jit(solution)/shard_map/ppermute | solution.py:601
  193.9 27.6 %collective-permute-start.17 = (bf16[256,2048]{1,0:T(8,128)(2,1)}, bf16[256,2048]{1,0:T(8,128)(2,1)}, u32[]{:S(2)}, u32[]{:S(2)}) collective-permute-start(bf16[256,2048]{1,0:T(8,128)(2,1)} %get-tuple-element.304), channel_id=1, source_target_pairs={{0,8},{4,12},{8,0},{12,4},{16,24},{20,28},{24,16},{28,20},{1,9},{5... | collective-permute-start | bytes 3145736 | tf_op jit(solution)/shard_map/ppermute | solution.py:615
  197.3 24.2 %collective-permute-start.18 = (bf16[256,2048]{1,0:T(8,128)(2,1)}, bf16[256,2048]{1,0:T(8,128)(2,1)}, u32[]{:S(2)}, u32[]{:S(2)}) collective-permute-start(bf16[256,2048]{1,0:T(8,128)(2,1)} %get-tuple-element.307), channel_id=1, source_target_pairs={{8,16},{12,20},{16,8},{20,12},{9,17},{13,21},{17,9},{21,13},{10,18... | collective-permute-start | bytes 3145736 | tf_op jit(solution)/shard_map/ppermute | solution.py:615
  227.3 5.7 collective-permute-start.21
  227.3 27.8 %collective-permute-start.19 = (bf16[256,2048]{1,0:T(8,128)(2,1)S(1)}, bf16[256,2048]{1,0:T(8,128)(2,1)S(1)}, u32[]{:S(2)}, u32[]{:S(2)}) collective-permute-start(bf16[256,2048]{1,0:T(8,128)(2,1)S(1)} %multiply_convert_fusion.rows.refs_4_), channel_id=1, source_target_pairs={{0,8},{4,12},{8,16},{12,20},{16,24},{20,28},{24,0},{28,4},{1,9},{5... | collective-permute-start | bytes 3145736 | tf_op jit(solution)/shard_map/ppermute | solution.py:615
  255.1 26.6 %collective-permute-start.22 = (bf16[256,2048]{1,0:T(8,128)(2,1)S(1)}, bf16[256,2048]{1,0:T(8,128)(2,1)S(1)}, u32[]{:S(2)}, u32[]{:S(2)}) collective-permute-start(bf16[256,2048]{1,0:T(8,128)(2,1)S(1)} %collective-permute-done.19.rows.refs_5_), channel_id=1, source_target_pairs={{0,8},{4,12},{8,16},{12,20},{16,24},{20,28},{24,0},{28,4},{1,9},{5... | collective-permute-start | bytes 3145736 | tf_op jit(solution)/shard_map/ppermute | solution.py:615
  283.4 27.9 %collective-permute-start.24 = (bf16[256,2048]{1,0:T(8,128)(2,1)S(1)}, bf16[256,2048]{1,0:T(8,128)(2,1)S(1)}, u32[]{:S(2)}, u32[]{:S(2)}) collective-permute-start(bf16[256,2048]{1,0:T(8,128)(2,1)S(1)} %convert_element_type.138), channel_id=1, source_target_pairs={{0,8},{4,12},{8,16},{12,20},{16,24},{20,28},{24,0},{28,4},{1,9},{5... | collective-permute-start | bytes 3145736 | tf_op jit(solution)/shard_map/ppermute | solution.py:615
  283.8 47.9 %collective-permute-start.23 = (bf16[256,2048]{1,0:T(8,128)(2,1)S(1)}, bf16[256,2048]{1,0:T(8,128)(2,1)S(1)}, u32[]{:S(2)}, u32[]{:S(2)}) collective-permute-start(bf16[256,2048]{1,0:T(8,128)(2,1)S(1)} %collective-permute-done.22.rows.refs_6_), channel_id=1, source_target_pairs={{0,8},{4,12},{8,16},{12,20},{16,24},{20,28},{24,0},{28,4},{1,9},{5... | collective-permute-start | bytes 3145736 | tf_op jit(solution)/shard_map/ppermute | solution.py:615
  333.6 24.8 %collective-permute-start.25 = (bf16[256,2048]{1,0:T(8,128)(2,1)S(1)}, bf16[256,2048]{1,0:T(8,128)(2,1)S(1)}, u32[]{:S(2)}, u32[]{:S(2)}) collective-permute-start(bf16[256,2048]{1,0:T(8,128)(2,1)S(1)} %add_convert_fusion.2), channel_id=1, source_target_pairs={{0,8},{4,12},{8,16},{12,20},{16,24},{20,28},{24,0},{28,4},{1,9},{5... | collective-permute-start | bytes 3145736 | tf_op jit(solution)/shard_map/ppermute | solution.py:615
  360.5 24.1 %collective-permute-start.26 = (bf16[256,2048]{1,0:T(8,128)(2,1)S(1)}, bf16[256,2048]{1,0:T(8,128)(2,1)S(1)}, u32[]{:S(2)}, u32[]{:S(2)}) collective-permute-start(bf16[256,2048]{1,0:T(8,128)(2,1)S(1)} %add_convert_fusion.1), channel_id=1, source_target_pairs={{0,8},{4,12},{8,16},{12,20},{16,24},{20,28},{24,0},{28,4},{1,9},{5... | collective-permute-start | bytes 3145736 | tf_op jit(solution)/shard_map/ppermute | solution.py:615
  384.6 28.7 %collective-permute-start.29 = (bf16[768,2048]{1,0:T(8,128)(2,1)S(1)}, bf16[768,2048]{1,0:T(8,128)(2,1)S(1)}, u32[]{:S(2)}, u32[]{:S(2)}) collective-permute-start(bf16[768,2048]{1,0:T(8,128)(2,1)S(1)} %copy-done.104), channel_id=1, source_target_pairs={{0,4},{4,0},{8,12},{12,8},{16,20},{20,16},{24,28},{28,24},{1,5},{5... | collective-permute-start | bytes 9437192 | tf_op jit(solution)/shard_map/ppermute | solution.py:601
  384.6 28.7 %collective-permute-start.30 = (bf16[768,2048]{1,0:T(8,128)(2,1)}, bf16[768,2048]{1,0:T(8,128)(2,1)S(1)}, u32[]{:S(2)}, u32[]{:S(2)}) collective-permute-start(bf16[768,2048]{1,0:T(8,128)(2,1)} %get-tuple-element.394), channel_id=1, source_target_pairs={{0,4},{4,0},{8,12},{12,8},{16,20},{20,16},{24,28},{28,24},{1,5},{5... | collective-permute-start | bytes 9437192 | tf_op jit(solution)/shard_map/ppermute | solution.py:601
  388.1 25.3 %collective-permute-start.27 = (bf16[256,2048]{1,0:T(8,128)(2,1)S(1)}, bf16[256,2048]{1,0:T(8,128)(2,1)}, u32[]{:S(2)}, u32[]{:S(2)}) collective-permute-start(bf16[256,2048]{1,0:T(8,128)(2,1)S(1)} %get-tuple-element.384.refs_4_), channel_id=1, source_target_pairs={{0,8},{4,12},{8,0},{12,4},{16,24},{20,28},{24,16},{28,20},{1,9},{5... | collective-permute-start | bytes 3145736 | tf_op jit(solution)/shard_map/ppermute | solution.py:615
  388.1 25.2 %collective-permute-start.28 = (bf16[256,2048]{1,0:T(8,128)(2,1)S(1)}, bf16[256,2048]{1,0:T(8,128)(2,1)S(1)}, u32[]{:S(2)}, u32[]{:S(2)}) collective-permute-start(bf16[256,2048]{1,0:T(8,128)(2,1)S(1)} %get-tuple-element.384.refs_4_), channel_id=1, source_target_pairs={{8,16},{12,20},{16,8},{20,12},{9,17},{13,21},{17,9},{21,13},{10,18... | collective-permute-start | bytes 3145736 | tf_op jit(solution)/shard_map/ppermute | solution.py:615
  413.4 28.8 %collective-permute-start.33 = (bf16[768,2048]{1,0:T(8,128)(2,1)}, bf16[768,2048]{1,0:T(8,128)(2,1)}, u32[]{:S(2)}, u32[]{:S(2)}) collective-permute-start(bf16[768,2048]{1,0:T(8,128)(2,1)} %get-tuple-element.407), channel_id=1, source_target_pairs={{0,4},{4,0},{8,12},{12,8},{16,20},{20,16},{24,28},{28,24},{1,5},{5... | collective-permute-start | bytes 9437192 | tf_op jit(solution)/shard_map/ppermute | solution.py:601
  415.5 26.7 %collective-permute-start.31 = (bf16[256,2048]{1,0:T(8,128)(2,1)}, bf16[256,2048]{1,0:T(8,128)(2,1)S(1)}, u32[]{:S(2)}, u32[]{:S(2)}) collective-permute-start(bf16[256,2048]{1,0:T(8,128)(2,1)} %broadcast_select_fusion.9), channel_id=1, source_target_pairs={{0,8},{4,12},{8,0},{12,4},{16,24},{20,28},{24,16},{28,20},{1,9},{5... | collective-permute-start | bytes 3145736 | tf_op jit(solution)/shard_map/ppermute | solution.py:615
  419.0 23.1 %collective-permute-start.32 = (bf16[256,2048]{1,0:T(8,128)(2,1)}, bf16[256,2048]{1,0:T(8,128)(2,1)S(1)}, u32[]{:S(2)}, u32[]{:S(2)}) collective-permute-start(bf16[256,2048]{1,0:T(8,128)(2,1)} %collective-permute-done.27), channel_id=1, source_target_pairs={{8,16},{12,20},{16,8},{20,12},{9,17},{13,21},{17,9},{21,13},{10,18... | collective-permute-start | bytes 3145736 | tf_op jit(solution)/shard_map/ppermute | solution.py:615
  442.2 154.8 %reduce-scatter.5.cloned.1.call-start = ((), (), s32[]{:S(2)}) async-start(), calls=%async_computation.7 | async-start | bytes 7864320 | tf_op jit(solution)/shard_map/reduce_scatter | solution.py:578
  446.6 25.9 %collective-permute-start.34 = (bf16[256,2048]{1,0:T(8,128)(2,1)}, bf16[256,2048]{1,0:T(8,128)(2,1)}, u32[]{:S(2)}, u32[]{:S(2)}) collective-permute-start(bf16[256,2048]{1,0:T(8,128)(2,1)} %get-tuple-element.413), channel_id=1, source_target_pairs={{0,8},{4,12},{8,0},{12,4},{16,24},{20,28},{24,16},{28,20},{1,9},{5... | collective-permute-start | bytes 3145736 | tf_op jit(solution)/shard_map/ppermute | solution.py:615
  450.2 22.3 %collective-permute-start.35 = (bf16[256,2048]{1,0:T(8,128)(2,1)}, bf16[256,2048]{1,0:T(8,128)(2,1)}, u32[]{:S(2)}, u32[]{:S(2)}) collective-permute-start(bf16[256,2048]{1,0:T(8,128)(2,1)} %get-tuple-element.415), channel_id=1, source_target_pairs={{8,16},{12,20},{16,8},{20,12},{9,17},{13,21},{17,9},{21,13},{10,18... | collective-permute-start | bytes 3145736 | tf_op jit(solution)/shard_map/ppermute | solution.py:615
  481.7 33.0 %collective-permute-start.36 = (bf16[256,2048]{1,0:T(8,128)(2,1)}, bf16[256,2048]{1,0:T(8,128)(2,1)S(1)}, u32[]{:S(2)}, u32[]{:S(2)}) collective-permute-start(bf16[256,2048]{1,0:T(8,128)(2,1)} %get-tuple-element.427), channel_id=1, source_target_pairs={{0,8},{4,12},{8,0},{12,4},{16,24},{20,28},{24,16},{28,20},{1,9},{5... | collective-permute-start | bytes 3145736 | tf_op jit(solution)/shard_map/ppermute | solution.py:615
  485.4 30.3 %collective-permute-start.37 = (bf16[256,2048]{1,0:T(8,128)(2,1)}, bf16[256,2048]{1,0:T(8,128)(2,1)}, u32[]{:S(2)}, u32[]{:S(2)}) collective-permute-start(bf16[256,2048]{1,0:T(8,128)(2,1)} %get-tuple-element.430), channel_id=1, source_target_pairs={{8,16},{12,20},{16,8},{20,12},{9,17},{13,21},{17,9},{21,13},{10,18... | collective-permute-start | bytes 3145736 | tf_op jit(solution)/shard_map/ppermute | solution.py:615
  517.0 2.2 collective-permute-start.39
  517.1 27.7 %collective-permute-start.38 = (bf16[256,2048]{1,0:T(8,128)(2,1)}, bf16[256,2048]{1,0:T(8,128)(2,1)}, u32[]{:S(2)}, u32[]{:S(2)}) collective-permute-start(bf16[256,2048]{1,0:T(8,128)(2,1)} %row_dot.4), channel_id=1, source_target_pairs={{0,8},{4,12},{8,16},{12,20},{16,24},{20,28},{24,0},{28,4},{1,9},{5... | collective-permute-start | bytes 3145736 | tf_op jit(solution)/shard_map/ppermute | solution.py:615
  519.4 20.1 %collective-permute-start.40 = (bf16[656,160]{1,0:T(8,128)(2,1)S(1)}, bf16[656,160]{1,0:T(8,128)(2,1)S(1)}, u32[]{:S(2)}, u32[]{:S(2)}) collective-permute-start(bf16[656,160]{1,0:T(8,128)(2,1)S(1)} %fusion.17), channel_id=1, source_target_pairs={{0,1},{1,0},{2,3},{3,2},{4,5},{5,4},{6,7},{7,6},{8,9},{9,8},{10,11... | collective-permute-start | bytes 629768 | tf_op jit(solution)/shard_map/ppermute | solution.py:754
  549.4 3.4 collective-permute-start.43
  549.4 5.2 collective-permute-start.44
  549.9 6.6 %collective-permute-start.45 = (bf16[320,2048]{1,0:T(8,128)(2,1)}, bf16[320,2048]{1,0:T(8,128)(2,1)}, u32[]{:S(2)}, u32[]{:S(2)}) collective-permute-start(bf16[320,2048]{1,0:T(8,128)(2,1)} %get-tuple-element.479), channel_id=1, source_target_pairs={{0,4},{4,0},{8,12},{12,8},{16,20},{20,16},{24,28},{28,24},{1,5},{5... | collective-permute-start | bytes 3932168 | tf_op jit(solution)/shard_map/ppermute | solution.py:601
  549.9 28.0 %collective-permute-start.41 = (bf16[256,2048]{1,0:T(8,128)(2,1)}, bf16[256,2048]{1,0:T(8,128)(2,1)}, u32[]{:S(2)}, u32[]{:S(2)}) collective-permute-start(bf16[256,2048]{1,0:T(8,128)(2,1)} %row_dot.5), channel_id=1, source_target_pairs={{0,8},{4,12},{8,16},{12,20},{16,24},{20,28},{24,0},{28,4},{1,9},{5... | collective-permute-start | bytes 3145736 | tf_op jit(solution)/shard_map/ppermute | solution.py:615
  571.1 25.8 %collective-permute-start.49 = (bf16[960,512]{1,0:T(8,128)(2,1)}, bf16[960,512]{1,0:T(8,128)(2,1)}, u32[]{:S(2)}, u32[]{:S(2)}) collective-permute-start(bf16[960,512]{1,0:T(8,128)(2,1)} %get-tuple-element.571), channel_id=1, source_target_pairs={{0,1},{1,0},{2,3},{3,2},{4,5},{5,4},{6,7},{7,6},{8,9},{9,8},{10,11... | collective-permute-start | bytes 2949128 | tf_op jit(solution)/shard_map/ppermute | solution.py:594
  572.4 24.5 %collective-permute-start.50 = (bf16[960,512]{1,0:T(8,128)(2,1)}, bf16[960,512]{1,0:T(8,128)(2,1)}, u32[]{:S(2)}, u32[]{:S(2)}) collective-permute-start(bf16[960,512]{1,0:T(8,128)(2,1)} %get-tuple-element.570), channel_id=1, source_target_pairs={{0,2},{1,3},{2,0},{3,1},{4,6},{5,7},{6,4},{7,5},{8,10},{9,11},{10,... | collective-permute-start | bytes 2949128 | tf_op jit(solution)/shard_map/ppermute | solution.py:594
  574.0 21.6 %collective-permute-start.46 = (f32[2,2048]{1,0:T(2,128)S(1)}, f32[2,2048]{1,0:T(2,128)S(1)}, u32[]{:S(2)}, u32[]{:S(2)}) collective-permute-start(f32[2,2048]{1,0:T(2,128)S(1)} %pad_maximum_fusion.8), channel_id=1, source_target_pairs={{0,1},{1,0},{2,3},{3,2},{4,5},{5,4},{6,7},{7,6},{8,9},{9,8},{10,11... | collective-permute-start | bytes 49160 | tf_op jit(solution)/shard_map/ppermute | solution.py:760
  574.5 22.4 %collective-permute-start.47 = (f32[2,2048]{1,0:T(2,128)S(1)}, f32[2,2048]{1,0:T(2,128)S(1)}, u32[]{:S(2)}, u32[]{:S(2)}) collective-permute-start(f32[2,2048]{1,0:T(2,128)S(1)} %pad_maximum_fusion.8), channel_id=1, source_target_pairs={{0,2},{1,3},{2,0},{3,1},{4,6},{5,7},{6,4},{7,5},{8,10},{9,11},{10,... | collective-permute-start | bytes 49160 | tf_op jit(solution)/shard_map/ppermute | solution.py:760
  577.9 19.0 %collective-permute-start.48 = (f32[2,2048]{1,0:T(2,128)S(1)}, f32[2,2048]{1,0:T(2,128)S(1)}, u32[]{:S(2)}, u32[]{:S(2)}) collective-permute-start(f32[2,2048]{1,0:T(2,128)S(1)} %pad_maximum_fusion.8), channel_id=1, source_target_pairs={{0,3},{1,2},{2,1},{3,0},{4,7},{5,6},{6,5},{7,4},{8,11},{9,10},{10,... | collective-permute-start | bytes 49160 | tf_op jit(solution)/shard_map/ppermute | solution.py:760
  595.7 26.3 %collective-permute-start.42 = (bf16[256,2048]{1,0:T(8,128)(2,1)}, bf16[256,2048]{1,0:T(8,128)(2,1)S(1)}, u32[]{:S(2)}, u32[]{:S(2)}) collective-permute-start(bf16[256,2048]{1,0:T(8,128)(2,1)} %row_dot.6), channel_id=1, source_target_pairs={{0,8},{4,12},{8,16},{12,20},{16,24},{20,28},{24,0},{28,4},{1,9},{5... | collective-permute-start | bytes 3145736 | tf_op jit(solution)/shard_map/ppermute | solution.py:615
  599.2 23.7 %collective-permute-start.53 = (bf16[960,512]{1,0:T(8,128)(2,1)}, bf16[960,512]{1,0:T(8,128)(2,1)}, u32[]{:S(2)}, u32[]{:S(2)}) collective-permute-start(bf16[960,512]{1,0:T(8,128)(2,1)} %constant_dynamic-slice_fusion), channel_id=1, source_target_pairs={{0,3},{1,2},{2,1},{3,0},{4,7},{5,6},{6,5},{7,4},{8,11},{9,10},{10,... | collective-permute-start | bytes 2949128 | tf_op jit(solution)/shard_map/ppermute | solution.py:594
  604.4 5.7 collective-permute-start.51
  604.4 5.6 collective-permute-start.52
  628.9 6.1 collective-permute-start.55
  628.9 6.1 collective-permute-start.56
  632.2 5.5 collective-permute-start.57
  633.2 7.2 %collective-permute-start.58 = (bf16[656,160]{1,0:T(8,128)(2,1)S(1)}, bf16[656,160]{1,0:T(8,128)(2,1)S(1)}, u32[]{:S(2)}, u32[]{:S(2)}) collective-permute-start(bf16[656,160]{1,0:T(8,128)(2,1)S(1)} %add.194), channel_id=1, source_target_pairs={{0,2},{1,3},{2,0},{3,1},{4,6},{5,7},{6,4},{7,5},{8,10},{9,11},{10,... | collective-permute-start | bytes 629768 | tf_op jit(solution)/shard_map/ppermute | solution.py:754
  634.9 9.8 %collective-permute-start.54 = (bf16[128,2048]{1,0:T(8,128)(2,1)S(1)}, bf16[128,2048]{1,0:T(8,128)(2,1)S(1)}, u32[]{:S(2)}, u32[]{:S(2)}) collective-permute-start(bf16[128,2048]{1,0:T(8,128)(2,1)S(1)} %get-tuple-element.579), channel_id=1, source_target_pairs={{0,4},{4,0},{8,12},{12,8},{16,20},{20,16},{24,28},{28,24},{1,5},{5... | collective-permute-start | bytes 1572872 | tf_op jit(solution)/shard_map/ppermute | solution.py:601
  (117 other events, 1265.6 us)
Sparse Core Ops, SparseCore 0:
  9.9 42.1 all-gather.4
  53.9 28.6 all-gather.6
  84.5 70.1 all-gather.8
  156.3 43.8 all-gather.10
  442.3 45.3 reduce-scatter.2
  490.6 77.2 reduce-scatter.4
